TPU v7x, 32 devices: a whole 2x2x4 slice. The times are simulated.
32 devices in a mesh: row: 4 (over z), kv: 8 (over y, x, core).
Axes of the slice: x: 2, y: 2, z: 4, core: 2. Of those that a mesh axis runs over, the one named last changes fastest.
Arguments:
- hidden: bfloat16 [64, 5120], P(None, 'kv'), may hold values from -6 to 6
- query_weight: bfloat16 [5120, 8192], P('kv', 'row'), may hold values from -0.078125 to 0.078125
- adapter_down_weight: bfloat16 [32, 5120, 16], P(None, 'kv'), may hold values from -0.078125 to 0.078125
- adapter_up_weight: float32 [32, 16, 8192], P(None, None, 'row'), may hold values from -1.5 to 1.5
- query_norm_gain: float32 [128], replicated, may hold values from 0.1 to 1.9
- paged_key_cache: bfloat16 [1024, 128, 8, 128], P('kv', None, 'row'), may hold values from -400 to 400
- paged_value_cache: bfloat16 [1024, 128, 8, 128], P('kv', None, 'row'), may hold values from -6 to 6
- output_weight: bfloat16 [8192, 5120], P('row', 'kv'), may hold values from -0.0625 to 0.0625
- holder: int32 [64, 32], P('kv'), may hold values from 0 to 7, as said below
- holder_block_index: int32 [64, 32], P('kv'), may hold values from 0 to 127
- block_used_length: int32 [64, 32], P('kv'), may hold values from 1 to 128
- tenant: int32 [64], replicated, may hold values from 0 to 63
- tenant_adapter: int32 [64], replicated, may hold values from 0 to 31
Outputs:
- projected: bfloat16 [64, 5120], P('row', 'kv')
Inputs may be any that keep to these rules, and one draw needn't show every extreme that they name: At most 64 of the 8 x 32 slots of the rows of one index of kv name one holder; in every draw one holder is named exactly 64 times by the slots of every index.
All inputs are finite; a program needn't handle non-finite values.
Results may differ from a plain program's by a relative error of at most 0.0159.
The roundings to bfloat16 on the way count: a program that leaves them out, or rounds other values in their place, can miss the bound.
Values may be sent and summed in bfloat16 or wider, within the bound.
No kernel may reach another device: no remote copies, remote signals or barrier semaphores. Data moves between devices by JAX's collectives and lax.ppermute only.
A program may use at most 256 MiB of HBM per device.

v0:
```python
import math

import jax
import jax.numpy as jnp
from jax import lax
from jax.sharding import PartitionSpec as P

ADAPTER_SCALE = 0.5
ROPE_BASE = 1000000.0
EPSILON = 1e-06
NEG_FILL = -1e30


def rotate_half(query, position):
    half_width = query.shape[-1] // 2
    frequency = ROPE_BASE ** (-(jnp.arange(half_width, dtype=jnp.float32) * 2.0) / query.shape[-1])
    angles = position[:, None] * frequency[None, :]
    cosine = jnp.concatenate([jnp.cos(angles), jnp.cos(angles)], axis=-1)[:, None, :]
    sine_part = jnp.concatenate([jnp.sin(angles), jnp.sin(angles)], axis=-1)[:, None, :]
    first_half = query[..., :half_width]
    second_half = query[..., half_width:]
    turned = jnp.concatenate([-second_half, first_half], axis=-1)
    return query * cosine + turned * sine_part


def prepare_queries(query_linear, query_norm_gain, block_used_length):
    row_count = query_linear.shape[0]
    head_size = query_norm_gain.shape[0]
    query = query_linear.reshape(row_count, query_linear.shape[1] // head_size, head_size)
    squares = jnp.mean(query * query, axis=-1, keepdims=True)
    query = query * lax.rsqrt(squares + EPSILON) * query_norm_gain
    position = (jnp.sum(block_used_length, axis=1) - 1).astype(jnp.float32)
    return rotate_half(query, position).astype(jnp.bfloat16)


def merge_blocks(block_out, block_top, block_total, axis):
    overall = jnp.max(block_top, axis=axis, keepdims=True)
    factors = jnp.exp(block_top - overall)
    numerator = jnp.sum(factors[..., None] * block_out, axis=axis)
    denominator = jnp.sum(factors * block_total, axis=axis)
    return numerator / denominator[..., None]


def local(
    hidden,
    query_weight,
    adapter_down_weight,
    adapter_up_weight,
    query_norm_gain,
    paged_key_cache,
    paged_value_cache,
    output_weight,
    holder,
    holder_block_index,
    block_used_length,
    tenant,
    tenant_adapter,
):
    own_rows = holder.shape[0]
    slot_count = holder.shape[1]
    kv_count = lax.axis_size("kv")
    my_index = lax.axis_index("kv")
    adapter_total = adapter_down_weight.shape[0]
    adapter_rank_size = adapter_down_weight.shape[2]
    query_width = query_weight.shape[1]
    head_size = query_norm_gain.shape[0]
    local_blocks = paged_key_cache.shape[0]
    kv_local = paged_key_cache.shape[2]
    block_size = paged_key_cache.shape[1]
    group_size = query_width // (kv_local * head_size)
    flat_keys = paged_key_cache.reshape(local_blocks, block_size * kv_local * head_size)
    flat_values = paged_value_cache.reshape(local_blocks, block_size * kv_local * head_size)
    tenant_match = tenant[:, None] == jnp.arange(tenant_adapter.shape[0], dtype=jnp.int32)[None, :]
    adapter_per_row = jnp.sum(jnp.where(tenant_match, tenant_adapter[None, :], 0), axis=1)
    adapter_match = (
        adapter_per_row[:, None] == jnp.arange(adapter_total, dtype=jnp.int32)[None, :]
    ).astype(jnp.float32)
    up_weight_flat = adapter_up_weight.reshape(adapter_total * adapter_rank_size, query_width)
    query_linear = lax.psum_scatter(
        jnp.dot(hidden, query_weight, preferred_element_type=jnp.float32),
        "kv",
        scatter_dimension=0,
        tiled=True,
    )
    partial_low = jnp.sum(
        jnp.einsum("ib,xbz->ixz", hidden, adapter_down_weight, preferred_element_type=jnp.float32)
        * adapter_match[:, :, None],
        axis=1,
    )
    own_low = lax.psum_scatter(partial_low, "kv", scatter_dimension=0, tiled=True)
    own_match = lax.dynamic_slice_in_dim(adapter_match, my_index * own_rows, own_rows, 0)
    spread = (own_low[:, None, :] * own_match[:, :, None]).reshape(
        own_rows, adapter_total * adapter_rank_size
    )
    query_linear = query_linear + ADAPTER_SCALE * jnp.dot(
        spread, up_weight_flat, precision=lax.Precision.HIGHEST, preferred_element_type=jnp.float32
    )
    queries = prepare_queries(query_linear, query_norm_gain, block_used_length).reshape(
        own_rows, query_width
    )
    entry_count = own_rows * slot_count
    capacity = 2 * entry_count // kv_count
    slot_total = kv_count * capacity
    slot_ids = jnp.arange(slot_total, dtype=jnp.int32)
    destination = holder.reshape(entry_count)
    dest_match = (destination[:, None] == jnp.arange(kv_count, dtype=jnp.int32)[None, :]).astype(
        jnp.int32
    )
    earlier = jnp.cumsum(dest_match, axis=0) - dest_match
    position = jnp.sum(earlier * dest_match, axis=1)
    slot_index = destination * capacity + position
    slot_match = slot_index[None, :] == slot_ids[:, None]
    row_pick = jnp.any(slot_match.reshape(slot_total, own_rows, slot_count), axis=2).astype(
        jnp.bfloat16
    )
    sent_queries = jnp.dot(row_pick, queries, preferred_element_type=jnp.bfloat16).reshape(
        kv_count, capacity, query_width
    )
    entry_fields = jnp.stack(
        [holder_block_index.reshape(entry_count), block_used_length.reshape(entry_count)], axis=1
    )
    sent_fields = jnp.sum(
        jnp.where(slot_match[:, :, None], entry_fields[None, :, :], 0), axis=1
    ).reshape(kv_count, capacity, 2)
    received_queries = lax.all_to_all(sent_queries, "kv", split_axis=0, concat_axis=0, tiled=True)
    received_fields = lax.all_to_all(sent_fields, "kv", split_axis=0, concat_axis=0, tiled=True)
    source_count = received_queries.shape[0]
    item_count = received_queries.shape[1]
    total_items = source_count * item_count
    blocks = received_fields[..., 0].reshape(total_items)
    lengths = received_fields[..., 1].reshape(total_items)
    block_pick = (blocks[:, None] == jnp.arange(local_blocks, dtype=jnp.int32)[None, :]).astype(
        jnp.bfloat16
    )
    keys = jnp.dot(block_pick, flat_keys, preferred_element_type=jnp.bfloat16).reshape(
        total_items, block_size, kv_local, head_size
    )
    values = jnp.dot(block_pick, flat_values, preferred_element_type=jnp.bfloat16).reshape(
        total_items, block_size, kv_local, head_size
    )
    grouped = received_queries.reshape(total_items, kv_local, group_size, head_size)
    scores = jnp.einsum("rajd,rtad->rajt", grouped, keys, preferred_element_type=jnp.float32) * (
        1.0 / math.sqrt(head_size)
    )
    token_mask = (jnp.arange(block_size, dtype=jnp.int32)[None, :] < lengths[:, None])[
        :, None, None, :
    ]
    block_top = jnp.max(jnp.where(token_mask, scores, NEG_FILL), axis=-1)
    weights = jnp.where(token_mask, jnp.exp(scores - block_top[..., None]), 0.0)
    block_total = jnp.sum(weights, axis=-1)
    block_out = jnp.einsum(
        "rajt,rtad->rajd", weights.astype(jnp.bfloat16), values, preferred_element_type=jnp.float32
    )
    lead = (source_count, item_count, kv_local, group_size)
    block_out, block_top, block_total = (
        block_out.reshape(lead + (head_size,)),
        block_top.reshape(lead),
        block_total.reshape(lead),
    )
    returned = (
        lax.all_to_all(block_out, "kv", split_axis=0, concat_axis=0, tiled=True),
        lax.all_to_all(block_top, "kv", split_axis=0, concat_axis=0, tiled=True),
        lax.all_to_all(block_total, "kv", split_axis=0, concat_axis=0, tiled=True),
    )
    slot_weight = slot_match.astype(jnp.float32)
    picked = []
    for piece in returned:
        trailing = piece.shape[2:]
        flat_piece = piece.reshape(slot_total, -1)
        chosen = jnp.dot(
            slot_weight.T,
            flat_piece,
            precision=lax.Precision.HIGHEST,
            preferred_element_type=jnp.float32,
        )
        picked.append(chosen.reshape((own_rows, slot_count) + trailing))
    attended = merge_blocks(picked[0], picked[1], picked[2], 1)
    attention = attended.reshape(own_rows, query_width).astype(jnp.bfloat16)
    terms = jnp.dot(
        lax.all_gather(attention, "kv", axis=0, tiled=True),
        output_weight,
        preferred_element_type=jnp.float32,
    )
    return lax.psum_scatter(terms.astype(jnp.bfloat16), "row", scatter_dimension=0, tiled=True)


def solution(mesh):
    return jax.shard_map(
        local,
        mesh=mesh,
        in_specs=(
            P(None, "kv"),
            P("kv", "row"),
            P(None, "kv", None),
            P(None, None, "row"),
            P(),
            P("kv", None, "row", None),
            P("kv", None, "row", None),
            P("row", "kv"),
            P("kv", None),
            P("kv", None),
            P("kv", None),
            P(),
            P(),
        ),
        out_specs=P("row", "kv"),
        check_vma=False,
    )
```

profile of v0, /device:TPU:0, one launch (start us, length us, event | category | flops | bytes accessed | tf_op | source)
XLA Modules:
  0.0 405.8 jit_solution(6399942681598203111)
XLA Ops:
  6.6 1.9 copy-done
  8.5 2.3 fusion.71
  16.0 5.2 %all-to-all-start = ((s32[8,1,128]{2,1,0:T(1,128)}), s32[8,1,128]{2,1,0:T(1,128)S(1)}, u32[]{:S(2)}, u32[]{:S(2)}) async-start(s32[8,1,128]{2,1,0:T(1,128)} %reshape.256), calls=%async_computation | async-start | bytes 8192 | tf_op jit(solution)/shard_map/all_to_all | solution.py:126
  22.1 0.8 select_reduce_fusion.2
  23.4 14.8 %all-reduce = f32[64,16]{0,1:T(8,128)S(1)} all-reduce(f32[64,16]{0,1:T(8,128)S(1)} %fusion.22), channel_id=3, replica_groups=mesh['row'=4,'kv'=8] {'kv'}, use_global_device_ids=true, to_apply=%region_8.9.clone | all-reduce | flops 1024 | bytes 8192
  40.2 14.5 %reshape.223 = bf16[128,32768]{1,0:T(8,128)(2,1)} reshape(bf16[128,128,2,128]{3,2,1,0:T(2,128)(2,1)} %param.18) | data formatting | bytes 16777216 | tf_op jit(solution)/shard_map/reshape | solution.py:71
  54.7 11.9 %copy.71 = bf16[32768,128]{1,0:T(8,128)(2,1)} copy(bf16[32768,128]{0,1:T(8,128)(2,1)} %bitcast.145) | data formatting | bytes 16777216 | tf_op jit(solution)/shard_map/dot_general | solution.py:135
  66.6 14.4 %reshape.226 = bf16[128,32768]{1,0:T(8,128)(2,1)} reshape(bf16[128,128,2,128]{3,2,1,0:T(2,128)(2,1)} %param.19) | data formatting | bytes 16777216 | tf_op jit(solution)/shard_map/reshape | solution.py:72
  81.1 11.9 %copy.76 = bf16[32768,128]{1,0:T(8,128)(2,1)} copy(bf16[32768,128]{0,1:T(8,128)(2,1)} %bitcast.146) | data formatting | bytes 16777216 | tf_op jit(solution)/shard_map/dot_general | solution.py:138
  94.6 7.5 %fusion.47 = (f32[8,16]{0,1:T(8,128)S(1)}, f32[8,2048]{1,0:T(8,128)S(1)}) fusion(f32[8,2048]{1,0:T(8,128)} %reduce-scatter.4.cloned.1.call-done, f32[32,16,2048]{2,1,0:T(8,128)} %param.16, f32[8,32]{1,0:T(8,128)S(1)} %copy.68, f32[8,16]{0,1:T(8,128)S(1)} %constant_dynamic-slice_fusion), kind=kOutput, calls=%fused_computation.53 | convolution fusion | flops 100732800 | bytes 4327424 | tf_op jit(solution)/shard_map/dot_general | solution.py:95
  102.3 2.1 fusion.51
  104.4 3.6 all-to-all-start.1
  108.0 17.0 %fusion.38 = bf16[512,128,2,128]{3,0,2,1:T(8,128)(2,1)} fusion(bf16[128,2,128,128]{3,2,1,0:T(8,128)(2,1)} %bitcast.144, s32[512]{0:T(512)S(1)} %eq.138), kind=kOutput, calls=%fused_computation.39 | convolution fusion | flops 4295032832 | bytes 41945088 | tf_op jit(solution)/shard_map/dot_general | solution.py:135
  125.0 9.5 %all-to-all-done.1 = bf16[8,64,2048]{2,1,0:T(8,128)(2,1)S(1)} async-done(((bf16[8,64,2048]{2,1,0:T(8,128)(2,1)}), bf16[8,64,2048]{2,1,0:T(8,128)(2,1)S(1)}, u32[]{:S(2)}, u32[]{:S(2)}) %all-to-all-start.1) | async-done | bytes 2097184 | tf_op jit(solution)/shard_map/all_to_all | solution.py:125
  134.5 1.4 copy-done.2
  135.9 2.2 copy.88
  138.1 85.0 %select_reduce_fusion = (f32[512,2,8]{2,1,0:T(2,128)S(1)}, f32[512,2,8,128]{3,2,1,0:T(8,128)}) fusion(pred[512,128]{1,0:T(8,128)(4,1)S(1)} %iota_compare_fusion.4, bf16[512,2,8,128]{3,2,1,0:T(8,128)(2,1)S(1)} %bitcast.147, bf16[512,128,2,128]{3,0,2,1:T(8,128)(2,1)} %fusion.38), kind=kOutput, calls=%fused_computation.7 | convolution fusion | flops 271572992 | bytes 39944192 | tf_op jit(solution)/shard_map/rajd,rtad->rajt/dot_general | solution.py:142
  223.1 15.7 %fusion.6 = f32[512,2,8]{2,1,0:T(2,128)S(1)} fusion(f32[512,2,8,128]{3,2,1,0:T(8,128)} %get-tuple-element.14, f32[512,2,8]{2,1,0:T(2,128)S(1)} %get-tuple-element.13, pred[512,128]{1,0:T(8,128)(4,1)S(1)} %iota_compare_fusion.4), kind=kLoop, calls=%fused_computation.8 | loop fusion | flops 4186112 | bytes 4325376 | tf_op jit(solution)/shard_map/reduce_sum | solution.py:150
  239.7 3.3 all-to-all-start.4
  243.0 17.0 %fusion.36 = bf16[512,128,2,128]{3,0,2,1:T(8,128)(2,1)} fusion(bf16[128,2,128,128]{3,2,1,0:T(8,128)(2,1)} %bitcast.143, s32[512]{0:T(512)S(1)} %eq.138), kind=kOutput, calls=%fused_computation.38 | convolution fusion | flops 4295032832 | bytes 41945088 | tf_op jit(solution)/shard_map/dot_general | solution.py:138
  261.0 4.1 %all-to-all-start.2 = ((f32[8,1,1024]{2,1,0:T(1,128)}), f32[8,1,1024]{2,1,0:T(1,128)S(1)}, u32[]{:S(2)}, u32[]{:S(2)}) async-start(f32[8,1,1024]{2,1,0:T(1,128)} %reshape.258), calls=%async_computation.3 | async-start | bytes 65536 | tf_op jit(solution)/shard_map/all_to_all | solution.py:162
  265.1 35.6 %fusion = f32[512,2,8,128]{3,2,1,0:T(8,128)} fusion(bf16[512,128,2,128]{3,0,2,1:T(8,128)(2,1)} %fusion.36, f32[512,2,8,128]{3,2,1,0:T(8,128)} %get-tuple-element.14, f32[512,2,8]{2,1,0:T(2,128)S(1)} %get-tuple-element.13, pred[512,128]{1,0:T(8,128)(4,1)S(1)} %iota_compare_fusion.4), kind=kOutput, calls=%fused_computation | convolution fusion | flops 272629760 | bytes 42041344 | tf_op jit(solution)/shard_map/rajt,rtad->rajd/dot_general | solution.py:151
  300.6 4.5 %all-to-all-start.3 = ((f32[8,64,2,8,128]{4,3,2,1,0:T(8,128)}), f32[8,64,2,8,128]{4,3,2,1,0:T(8,128)}, u32[]{:S(2)}, u32[]{:S(2)}) async-start(f32[8,64,2,8,128]{4,3,2,1,0:T(8,128)} %bitcast.150), calls=%async_computation.4 | async-start | bytes 8388608 | tf_op jit(solution)/shard_map/all_to_all | solution.py:161
  308.3 1.5 subtract_exponential_fusion
  309.8 0.8 fusion.23
  310.6 43.7 %all-to-all-done.3 = f32[8,64,2,8,128]{4,3,2,1,0:T(8,128)} async-done(((f32[8,64,2,8,128]{4,3,2,1,0:T(8,128)}), f32[8,64,2,8,128]{4,3,2,1,0:T(8,128)}, u32[]{:S(2)}, u32[]{:S(2)}) %all-to-all-start.3) | async-done | bytes 4194336 | tf_op jit(solution)/shard_map/all_to_all | solution.py:161
  354.3 4.9 %reshape.228 = f32[512,2048]{1,0:T(8,128)} reshape(f32[8,64,2,8,128]{4,3,2,1,0:T(8,128)} %all-to-all-done.3) | data formatting | bytes 8388608 | tf_op jit(solution)/shard_map/reshape | solution.py:169
  359.2 5.3 %copy.78 = f32[512,2048]{0,1:T(8,128)} copy(f32[512,2048]{1,0:T(8,128)} %reshape.228) | data formatting | bytes 8388608 | tf_op jit(solution)/shard_map/reshape | solution.py:169
  364.6 4.9 %multiply_reduce_fusion = f32[8,2,8,128]{3,2,1,0:T(8,128)S(1)} fusion(f32[2,8,128,512,1]{3,2,1,0,4:T(8,128)} %bitcast.151, f32[8,32,2,8]{1,3,2,0:T(8,128)S(1)} %subtract_exponential_fusion, s32[8,32]{1,0:T(8,128)S(1)} %multiply_add_fusion), kind=kOutput, calls=%fused_computation.13 | convolution fusion | flops 3222388736 | bytes 4277248 | tf_op jit(solution)/shard_map/dot_general | solution.py:170
  369.6 8.4 %all_gather.3 = bf16[64,2048]{1,0:T(8,128)(2,1)S(1)} all-gather(bf16[8,2048]{1,0:T(8,128)(2,1)S(1)} %bitcast.157), channel_id=1, replica_groups=mesh['row'=4,'kv'=8] {'kv'}, dimensions={0}, use_global_device_ids=true | all-gather | bytes 294912 | tf_op jit(solution)/shard_map/all_gather | solution.py:180
  377.9 1.2 convolution_convert_fusion
  379.1 19.6 %reduce-scatter.6.cloned.1.call-done = bf16[16,640]{1,0:T(8,128)(2,1)} async-done(((bf16[64,640]{1,0:T(8,128)(2,1)}), bf16[16,640]{1,0:T(8,128)(2,1)}) %reduce-scatter.6.cloned.1.call-update) | async-done | bytes 20496 | tf_op jit(solution)/shard_map/reduce_scatter | solution.py:184
  (83 shorter events, 14.5 us)
Async XLA Ops:
  6.5 2.0 copy-start
  6.5 31.9 %copy-start.8 = (u32[32]{0:T(128)S(1)}, u32[32]{0:T(128)}, u32[]{:S(2)}) copy-start(u32[32]{0:T(128)} %constant.45) | copy-start | bytes 388
  6.5 16.5 %copy-start.4 = (bf16[64,640]{1,0:T(8,128)(2,1)S(1)}, bf16[64,640]{1,0:T(8,128)(2,1)}, u32[]{:S(2)}) copy-start(bf16[64,640]{1,0:T(8,128)(2,1)} %param.13) | copy-start | bytes 245764
  6.5 31.7 %copy-start.5 = (s32[8,32]{1,0:T(8,128)S(1)}, s32[8,32]{1,0:T(8,128)}, u32[]{:S(2)}) copy-start(s32[8,32]{1,0:T(8,128)} %param.21) | copy-start | bytes 3076
  6.5 16.5 %copy-start.7 = (bf16[32,640,16]{1,2,0:T(8,128)(2,1)S(1)}, bf16[32,640,16]{1,2,0:T(8,128)(2,1)}, u32[]{:S(2)}) copy-start(bf16[32,640,16]{1,2,0:T(8,128)(2,1)} %param.15) | copy-start | bytes 1966084
  6.5 31.9 %copy-start.6 = (f32[128]{0:T(128)S(1)}, f32[128]{0:T(128)}, u32[]{:S(2)}) copy-start(f32[128]{0:T(128)} %param.17) | copy-start | bytes 1540
  6.6 88.0 %reduce-scatter.4.cloned.1.call-start = ((), (), s32[]{:S(2)}) async-start(), calls=%async_computation.7 | async-start | bytes 589824 | tf_op jit(solution)/shard_map/reduce_scatter | solution.py:79
  16.0 77.0 %all-to-all-start = ((s32[8,1,128]{2,1,0:T(1,128)}), s32[8,1,128]{2,1,0:T(1,128)S(1)}, u32[]{:S(2)}, u32[]{:S(2)}) async-start(s32[8,1,128]{2,1,0:T(1,128)} %reshape.256), calls=%async_computation | async-start | bytes 8192 | tf_op jit(solution)/shard_map/all_to_all | solution.py:126
  104.4 30.2 %all-to-all-start.1 = ((bf16[8,64,2048]{2,1,0:T(8,128)(2,1)}), bf16[8,64,2048]{2,1,0:T(8,128)(2,1)S(1)}, u32[]{:S(2)}, u32[]{:S(2)}) async-start(bf16[8,64,2048]{2,1,0:T(8,128)(2,1)} %fusion.51), calls=%async_computation.2 | async-start | bytes 4194304 | tf_op jit(solution)/shard_map/all_to_all | solution.py:125
  134.5 1.4 copy-start.2
  239.7 21.3 %all-to-all-start.4 = ((f32[8,1,1024]{2,1,0:T(1,128)}), f32[8,1,1024]{2,1,0:T(1,128)S(1)}, u32[]{:S(2)}, u32[]{:S(2)}) async-start(f32[8,1,1024]{2,1,0:T(1,128)} %reshape.260), calls=%async_computation.5 | async-start | bytes 65536 | tf_op jit(solution)/shard_map/all_to_all | solution.py:163
  261.0 39.7 %all-to-all-start.2 = ((f32[8,1,1024]{2,1,0:T(1,128)}), f32[8,1,1024]{2,1,0:T(1,128)S(1)}, u32[]{:S(2)}, u32[]{:S(2)}) async-start(f32[8,1,1024]{2,1,0:T(1,128)} %reshape.258), calls=%async_computation.3 | async-start | bytes 65536 | tf_op jit(solution)/shard_map/all_to_all | solution.py:162
  300.6 53.7 %all-to-all-start.3 = ((f32[8,64,2,8,128]{4,3,2,1,0:T(8,128)}), f32[8,64,2,8,128]{4,3,2,1,0:T(8,128)}, u32[]{:S(2)}, u32[]{:S(2)}) async-start(f32[8,64,2,8,128]{4,3,2,1,0:T(8,128)} %bitcast.150), calls=%async_computation.4 | async-start | bytes 8388608 | tf_op jit(solution)/shard_map/all_to_all | solution.py:161
  305.2 93.5 %reduce-scatter.6.cloned.1.call-start = ((), (), s32[]{:S(2)}) async-start(), calls=%async_computation.8 | async-start | bytes 102400 | tf_op jit(solution)/shard_map/reduce_scatter | solution.py:184
  364.6 13.3 %copy-start.3 = (bf16[2048,640]{1,0:T(8,128)(2,1)S(1)}, bf16[2048,640]{1,0:T(8,128)(2,1)}, u32[]{:S(2)}) copy-start(bf16[2048,640]{1,0:T(8,128)(2,1)} %param.20) | copy-start | bytes 7864324
  364.6 34.1 %copy-start.1 = (bf16[640,2048]{1,0:T(8,128)(2,1)S(1)}, bf16[640,2048]{1,0:T(8,128)(2,1)}, u32[]{:S(2)}) copy-start(bf16[640,2048]{1,0:T(8,128)(2,1)} %param.14) | copy-start | bytes 7864324
Sparse Core Ops, SparseCore 0:
  11.0 36.8 reduce-scatter.3
  379.2 19.4 reduce-scatter.5
where the time goes:
time: 410 us; the launch traced here: 406 us
  matrix products  174 us (42%)
  local copies, waits for them, and re-layouts  77.1 us (19%)
  waiting for transfers between devices  72.8 us (18%)
  blocking collectives  23.2 us (6%)
  other arithmetic  22.8 us (6%)
  starting transfers between devices  20.8 us (5%)
  between operations  14.6 us (4%)
    dot_general x1, matrix products, local(): jnp.einsum('rajd,rtad->rajt', grouped, keys, preferred_element_type=jnp.f...  85 us
    all_to_all x1, waiting for transfers between devices, local(): lax.all_to_all(block_out, 'kv', split_axis=0, concat_axis=0, tiled=True)  43.7 us
    dot_general x1, matrix products, local(): jnp.einsum('rajt,rtad->rajd', weights.astype(jnp.bfloat16), values, prefe...  35.6 us
    reduce_scatter x1, waiting for transfers between devices, local(): lax.psum_scatter(terms.astype(jnp.bfloat16), 'row', scatter_dimension=0,...  19.6 us
    dot_general x1, matrix products, local(): jnp.dot(block_pick, flat_keys, preferred_element_type=jnp.bfloat16)  17 us
    dot_general x1, matrix products, local(): jnp.dot(block_pick, flat_values, preferred_element_type=jnp.bfloat16)  17 us
    reduce_sum x1, other arithmetic, local(): block_total = jnp.sum(weights, axis=-1)  15.7 us
    unnamed x1, blocking collectives  14.8 us
  transfers between devices with their start and end apart: 7, of which 3 were waited for; matrix products, arithmetic and copies ran while one was open for 34% of the time, Pallas kernels for 0%

commit v1 on v0

v1 whole, which is shorter than its diff:
```python
import functools
import math

import jax
import jax.numpy as jnp
from jax import lax
from jax.experimental import pallas as pl
from jax.experimental.pallas import tpu as pltpu
from jax.sharding import PartitionSpec as P

ADAPTER_SCALE = 0.5
ROPE_BASE = 1000000.0
EPSILON = 1e-06
NEG_FILL = -1e30
LANES = 128
COLUMN_TILE = 256
UNROLL = 8
LOG2E = math.log2(math.e)
MIB = 1024 * 1024


def params(mib):
    return pltpu.CompilerParams(vmem_limit_bytes=mib * MIB)


def vmem_spec():
    return pl.BlockSpec(memory_space=pltpu.VMEM)


def smem_spec():
    return pl.BlockSpec(memory_space=pltpu.SMEM)


def split2(x):
    high = x.astype(jnp.bfloat16)
    return high, (x - high.astype(jnp.float32)).astype(jnp.bfloat16)


def split3(x):
    high = x.astype(jnp.bfloat16).astype(jnp.float32)
    rest = x - high
    middle = rest.astype(jnp.bfloat16).astype(jnp.float32)
    return high, middle, (rest - middle).astype(jnp.bfloat16).astype(jnp.float32)


def to_column(row, count):
    shape = (count, count)
    eye = lax.broadcasted_iota(jnp.int32, shape, 0) == lax.broadcasted_iota(jnp.int32, shape, 1)
    return jnp.sum(jnp.where(eye, row.astype(jnp.float32), 0.0), axis=1, keepdims=True)


def project_kernel(
    rank, tenant_ref, adapter_ref, slots_ref, hidden_ref, weight_ref, down_ref, up_ref, out_ref, high_ref, low_ref
):
    step = pl.program_id(0)
    rows = hidden_ref.shape[0]
    width = pl.num_programs(0) * weight_ref.shape[1]
    nt = (((1,), (1,)), ((), ()))

    @pl.when(step == 0)
    def _():
        tenants = adapter_ref.shape[1]
        tenant = to_column(tenant_ref[...], rows)
        pick = lax.broadcasted_iota(jnp.int32, (rows, tenants), 1).astype(jnp.float32) == tenant
        adapter = jnp.sum(
            jnp.where(pick, adapter_ref[...].astype(jnp.float32), 0.0), axis=1, keepdims=True
        ).astype(jnp.int32)
        low = lax.dot_general(hidden_ref[...], down_ref[...], nt, preferred_element_type=jnp.float32)
        column = lax.broadcasted_iota(jnp.int32, low.shape, 1)
        match = (column >= adapter * rank) & (column < adapter * rank + rank)
        high_part, low_part = split2(jnp.where(match, ADAPTER_SCALE * low, 0.0))
        high_ref[...] = high_part
        low_ref[...] = low_part
        own = slots_ref.shape[0]
        for start in range(0, rows, own):
            out_ref[start : start + own, width:] = slots_ref[...]

    up_high, up_low = split2(up_ref[...])
    total = jnp.dot(hidden_ref[...], weight_ref[...], preferred_element_type=jnp.float32)
    total += jnp.dot(low_ref[...], up_high, preferred_element_type=jnp.float32)
    total += jnp.dot(high_ref[...], up_low, preferred_element_type=jnp.float32)
    total += jnp.dot(high_ref[...], up_high, preferred_element_type=jnp.float32)
    tile = weight_ref.shape[1]
    out_ref[:, pl.ds(pl.multiple_of(step * tile, tile), tile)] = total


def project(hidden, query_weight, down, up, tenant, tenant_adapter, slots, rank):
    rows, depth = hidden.shape
    width = query_weight.shape[1]
    low_width = down.shape[0]
    whole = lambda shape: pl.BlockSpec(shape, lambda i: (0,) * len(shape))
    return pl.pallas_call(
        functools.partial(project_kernel, rank),
        grid=(width // COLUMN_TILE,),
        in_specs=[
            whole(tenant.shape),
            whole(tenant_adapter.shape),
            whole(slots.shape),
            whole(hidden.shape),
            pl.BlockSpec((depth, COLUMN_TILE), lambda i: (0, i)),
            whole(down.shape),
            pl.BlockSpec((low_width, COLUMN_TILE), lambda i: (0, i)),
        ],
        out_specs=whole((rows, width + LANES)),
        out_shape=jax.ShapeDtypeStruct((rows, width + LANES), jnp.float32),
        scratch_shapes=[
            pltpu.VMEM((rows, low_width), jnp.bfloat16),
            pltpu.VMEM((rows, low_width), jnp.bfloat16),
        ],
        compiler_params=params(16),
        cost_estimate=pl.CostEstimate(
            flops=2 * rows * width * (depth + 3 * low_width),
            bytes_accessed=2 * depth * width + 4 * low_width * width,
            transcendentals=0,
        ),
        name="project",
    )(tenant, tenant_adapter, slots, hidden, query_weight, down, up)


def queries_kernel(parts_ref, cosine_ref, sine_ref, gain_ref, out_ref, turned_ref):
    heads = turned_ref.shape[1]
    copies = out_ref.shape[0]
    cosine, sine, gain = cosine_ref[...], sine_ref[...], gain_ref[...]
    for h in range(heads):
        columns = slice(h * LANES, (h + 1) * LANES)
        query = parts_ref[0, :, columns]
        for s in range(1, parts_ref.shape[0]):
            query = query + parts_ref[s, :, columns]
        square = jnp.mean(query * query, axis=-1, keepdims=True)
        query = query * lax.rsqrt(square + EPSILON) * gain
        turned_ref[:, h, :] = query * cosine + pltpu.roll(query, LANES // 2, 1) * sine
    result = turned_ref[...].astype(jnp.bfloat16)
    for c in range(copies):
        out_ref[c] = result


def make_queries(parts, cosine, sine, gain, heads):
    count, own, _ = parts.shape
    return pl.pallas_call(
        queries_kernel,
        in_specs=[vmem_spec()] * 4,
        out_specs=vmem_spec(),
        out_shape=jax.ShapeDtypeStruct((count, own, heads, LANES), jnp.bfloat16),
        scratch_shapes=[pltpu.VMEM((own, heads, LANES), jnp.float32)],
        compiler_params=params(16),
        name="queries",
    )(parts, cosine, sine, gain)


def list_kernel(block_size, slots, packed_ref, list_ref, count_ref):
    total = packed_ref.shape[0]
    capacity = list_ref.shape[0]
    rows = total // slots
    shift = block_size * LANES

    def step(i, position):
        for j in range(UNROLL):
            entry = i * UNROLL + j
            value = packed_ref[entry]
            list_ref[position] = value + (entry // slots) * shift
            position = position + (value >= 0).astype(jnp.int32)
        return position

    count = lax.fori_loop(0, total // UNROLL, step, jnp.int32(0))
    count_ref[0] = count

    def fill(i, carry):
        list_ref[count + i] = rows * shift
        return carry

    lax.fori_loop(0, UNROLL, fill, 0)


def make_list(packed, capacity, block_size, slots):
    return pl.pallas_call(
        functools.partial(list_kernel, block_size, slots),
        in_specs=[smem_spec()],
        out_specs=[smem_spec(), smem_spec()],
        out_shape=[
            jax.ShapeDtypeStruct((capacity,), jnp.int32),
            jax.ShapeDtypeStruct((1,), jnp.int32),
        ],
        compiler_params=params(16),
        cost_estimate=pl.CostEstimate(flops=10**8, bytes_accessed=10**7, transcendentals=0),
        name="slot_list",
    )(packed)


def attend_kernel(
    scale, group, kv_local, list_ref, count_ref, query_ref, key_ref, value_ref, out_ref, top_ref, total_ref, sum_ref
):
    rows, heads, _ = query_ref.shape
    tokens = key_ref.shape[1]
    block_size = tokens // kv_local
    shift = block_size * LANES
    factor = scale * LOG2E
    top_ref[...] = jnp.full(top_ref.shape, NEG_FILL, jnp.float32)
    total_ref[...] = jnp.zeros(total_ref.shape, jnp.float32)
    sum_ref[...] = jnp.zeros(sum_ref.shape, jnp.float32)
    head = lax.broadcasted_iota(jnp.int32, (heads, tokens), 0) // group
    place = lax.broadcasted_iota(jnp.int32, (heads, tokens), 1)
    token = jnp.where(place % kv_local == head, place // kv_local, block_size)
    nt = (((1,), (1,)), ((), ()))

    def chunk(i, carry):
        before, top, total, acc = carry
        row, block, length = [], [], []
        for j in range(UNROLL):
            entry = list_ref[i * UNROLL + j]
            row.append(entry // shift)
            block.append((entry // block_size) % LANES)
            length.append(entry % block_size + 1)
        scores = [
            lax.dot_general(
                query_ref[jnp.minimum(row[j], rows - 1)], key_ref[block[j]], nt, preferred_element_type=jnp.float32
            )
            for j in range(UNROLL)
        ]
        scores = [jnp.where(token < length[j], scores[j], NEG_FILL) for j in range(UNROLL)]
        tops = [jnp.max(s, axis=1, keepdims=True) for s in scores]
        weights = [jnp.exp2((scores[j] - tops[j]) * factor) for j in range(UNROLL)]
        totals = [jnp.sum(w, axis=1, keepdims=True) for w in weights]
        outs = [
            jnp.dot(weights[j].astype(jnp.bfloat16), value_ref[block[j]], preferred_element_type=jnp.float32)
            for j in range(UNROLL)
        ]
        for j in range(UNROLL):
            fresh = row[j] != before
            top = jnp.where(fresh, NEG_FILL, top)
            total = jnp.where(fresh, 0.0, total)
            acc = jnp.where(fresh, 0.0, acc)
            high = jnp.maximum(top, tops[j])
            old = jnp.exp2((top - high) * factor)
            new = jnp.exp2((tops[j] - high) * factor)
            total = total * old + totals[j] * new
            acc = acc * old + outs[j] * new
            top = high
            before = row[j]
            top_ref[row[j]] = top
            total_ref[row[j]] = total
            sum_ref[row[j]] = acc
        return before, top, total, acc

    wide = jnp.zeros((heads, LANES), jnp.float32)
    count = count_ref[0]
    lax.fori_loop(0, (count + UNROLL - 1) // UNROLL, chunk, (jnp.int32(-1), wide, wide, wide))

    copies, sections, _, _ = out_ref.shape
    own = sections - 1
    square = (own * heads, LANES)
    eye = lax.broadcasted_iota(jnp.int32, square, 0) == lax.broadcasted_iota(jnp.int32, square, 1)
    line = lax.broadcasted_iota(jnp.int32, (heads, LANES), 0)
    for c in range(copies):
        stats = jnp.zeros((heads, LANES), jnp.float32)
        position = 0
        for ref in (top_ref, total_ref):
            flat = jnp.sum(
                jnp.where(eye, ref[c * own : (c + 1) * own].reshape(square), 0.0), axis=0, keepdims=True
            )
            for piece in split3(flat):
                stats = jnp.where(line == position, piece, stats)
                position += 1
        for r in range(own):
            out_ref[c, r] = sum_ref[c * own + r].astype(jnp.bfloat16)
        out_ref[c, own] = stats.astype(jnp.bfloat16)


def attend(items, count, queries, keys, values, copies, kv_local, scale):
    rows, heads, _ = queries.shape
    own = rows // copies
    keys = pltpu.with_memory_space_constraint(keys, pltpu.VMEM)
    values = pltpu.with_memory_space_constraint(values, pltpu.VMEM)
    state = pltpu.VMEM((rows + 1, heads, LANES), jnp.float32)
    return pl.pallas_call(
        functools.partial(attend_kernel, scale, heads // kv_local, kv_local),
        in_specs=[smem_spec(), smem_spec(), vmem_spec(), vmem_spec(), vmem_spec()],
        out_specs=vmem_spec(),
        out_shape=jax.ShapeDtypeStruct((copies, own + 1, heads, LANES), jnp.bfloat16),
        scratch_shapes=[state, state, state],
        compiler_params=params(28),
        name="attend",
    )(items, count, queries, keys, values)


def merge_kernel(scale, parts_ref, out_ref, wide_ref):
    count, sections, heads, _ = parts_ref.shape
    own = sections - 1
    factor = scale * LOG2E
    stats = [parts_ref[s, own].astype(jnp.float32) for s in range(count)]
    tops = jnp.concatenate([s[0:1] + s[1:2] + s[2:3] for s in stats], axis=0)
    totals = jnp.concatenate([s[3:4] + s[4:5] + s[5:6] for s in stats], axis=0)
    weights = jnp.exp2((tops - jnp.max(tops, axis=0, keepdims=True)) * factor)
    weights = weights / jnp.sum(weights * totals, axis=0, keepdims=True)
    columns = weights.T
    acc = jnp.zeros((own * heads, LANES), jnp.float32)
    for s in range(count):
        part = parts_ref[s, :own].astype(jnp.float32).reshape(own * heads, LANES)
        acc = acc + part * columns[:, s : s + 1]
    wide_ref[...] = acc
    pieces = [wide_ref[pl.ds(h, own, stride=heads), :] for h in range(heads)]
    result = jnp.concatenate(pieces, axis=1).astype(jnp.bfloat16)
    for c in range(out_ref.shape[0]):
        out_ref[c] = result


def merge(parts, scale):
    count, sections, heads, _ = parts.shape
    own = sections - 1
    return pl.pallas_call(
        functools.partial(merge_kernel, scale),
        in_specs=[vmem_spec()],
        out_specs=vmem_spec(),
        out_shape=jax.ShapeDtypeStruct((count, own, heads * LANES), jnp.bfloat16),
        scratch_shapes=[pltpu.VMEM((own * heads, LANES), jnp.float32)],
        compiler_params=params(16),
        name="merge",
    )(parts)


def swap(x, axis):
    return lax.all_to_all(x, axis, split_axis=0, concat_axis=0, tiled=True)


def local(
    hidden,
    query_weight,
    adapter_down_weight,
    adapter_up_weight,
    query_norm_gain,
    paged_key_cache,
    paged_value_cache,
    output_weight,
    holder,
    holder_block_index,
    block_used_length,
    tenant,
    tenant_adapter,
):
    own, slots = holder.shape
    rows, depth = hidden.shape
    kv_count = lax.axis_size("kv")
    row_count = lax.axis_size("row")
    adapters, _, rank = adapter_down_weight.shape
    width = query_weight.shape[1]
    head_size = query_norm_gain.shape[0]
    heads = width // head_size
    blocks, block_size, kv_local, _ = paged_key_cache.shape
    scale = 1.0 / math.sqrt(head_size)

    fields = jnp.concatenate(
        [holder, holder_block_index, block_used_length, jnp.zeros((own, LANES - 3 * slots), jnp.int32)], axis=1
    ).astype(jnp.float32)
    down = jnp.swapaxes(adapter_down_weight, 1, 2).reshape(adapters * rank, depth)
    up = adapter_up_weight.reshape(adapters * rank, width)
    partial = project(
        hidden, query_weight, down, up, tenant.reshape(1, rows), tenant_adapter.reshape(1, -1), fields, rank
    )
    parts = swap(partial.reshape(kv_count, own, width + LANES), "kv")

    position = (jnp.sum(block_used_length, axis=1) - 1).astype(jnp.float32)
    half = head_size // 2
    frequency = ROPE_BASE ** (-(jnp.arange(half, dtype=jnp.float32) * 2.0) / head_size)
    angles = position[:, None] * frequency[None, :]
    cosine = jnp.concatenate([jnp.cos(angles), jnp.cos(angles)], axis=-1)
    sine = jnp.concatenate([-jnp.sin(angles), jnp.sin(angles)], axis=-1)
    queries = make_queries(parts, cosine, sine, query_norm_gain.reshape(1, head_size), heads)
    queries = swap(queries, "kv").reshape(rows, heads, head_size)

    numbers = parts[:, :, width:].astype(jnp.int32).reshape(rows, LANES)
    holders, numbers, lengths = (numbers[:, i * slots : (i + 1) * slots] for i in range(3))
    packed = jnp.where(
        holders == lax.axis_index("kv"), numbers * block_size + lengths - 1, -rows * block_size * LANES
    ).reshape(rows * slots)
    entries = own * slots
    capacity = 2 * entries // kv_count * kv_count + 2 * UNROLL
    items, count = make_list(packed, capacity, block_size, slots)

    keys = paged_key_cache.reshape(blocks, block_size * kv_local, head_size)
    values = paged_value_cache.reshape(blocks, block_size * kv_local, head_size)
    partial_out = attend(items, count, queries, keys, values, kv_count, kv_local, scale)
    attention = merge(swap(partial_out, "kv"), scale)
    attention = swap(attention, "kv").reshape(rows, width)
    terms = jnp.dot(attention, output_weight, preferred_element_type=jnp.float32).astype(jnp.bfloat16)
    terms = swap(terms.reshape(row_count, rows // row_count, -1), "row")
    return jnp.sum(terms.astype(jnp.float32), axis=0).astype(jnp.bfloat16)


def solution(mesh):
    return jax.shard_map(
        local,
        mesh=mesh,
        in_specs=(
            P(None, "kv"),
            P("kv", "row"),
            P(None, "kv", None),
            P(None, None, "row"),
            P(),
            P("kv", None, "row", None),
            P("kv", None, "row", None),
            P("row", "kv"),
            P("kv", None),
            P("kv", None),
            P("kv", None),
            P(),
            P(),
        ),
        out_specs=P("row", "kv"),
        check_vma=False,
    )
```

time: 410 us -> 119 us (0.29)
  matrix products: 174 us -> 0.54 us
  waiting for transfers between devices: 72.8 us -> 9.76 us
  local copies, waits for them, and re-layouts: 77.1 us -> 15.6 us
  Pallas kernels: 0 us -> 51.9 us
  other arithmetic: 22.8 us -> 1.98 us
  between operations: 14.6 us -> 0.13 us
  starting transfers between devices: 20.8 us -> 8.58 us
  blocking collectives: 23.2 us -> 29.5 us
    dot_general x12 -> x1, matrix products: 174 us -> 0.54 us  [local(): jnp.dot(attention, output_weight, preferred_element_type=jnp.float32)]
    pallas_call x0 -> x5, Pallas kernels: none -> 51.9 us  [the longest x1 31.4 us: attend(): pl.pallas_call(functools.partial(attend_kernel, scale, heads // kv_local,...]
    all_to_all x5 -> x2, waiting for transfers between devices: 53.2 us -> 9.76 us  [swap(): return lax.all_to_all(x, axis, split_axis=0, concat_axis=0, tiled=True)]
    reshape x11 -> x1, local copies, waits for them, and re-layouts: 40.5 us -> 0.07 us  [local(): packed = jnp.where(holders == lax.axis_index('kv'), numbers * block_size...]
    all_to_all x0 -> x3, blocking collectives: none -> 29.5 us  [swap(): return lax.all_to_all(x, axis, split_axis=0, concat_axis=0, tiled=True)]
    dot_general x3 -> x0, local copies, waits for them, and re-layouts: 23.9 us -> none  [the longest x1 11.9 us: local(): jnp.dot(block_pick, flat_values, preferred_element_type=jnp.bfloat16)]
    reduce_scatter x2 -> x0, waiting for transfers between devices: 19.6 us -> none  [the longest x1 19.6 us: local(): lax.psum_scatter(terms.astype(jnp.bfloat16), 'row', scatter_dimension=0,...]
    reduce_sum x5 -> x2, other arithmetic: 17.7 us -> 0.74 us  [the longest x1 0.62 us: local(): return jnp.sum(terms.astype(jnp.float32), axis=0).astype(jnp.bfloat16)]
  transfers between devices with their start and end apart: 7 -> 2, of which waited for: 3 -> 1; matrix products, arithmetic and copies ran while one was open for 34% -> 0% of each run, Pallas kernels for 0% -> 14%
where the time goes in v1:
time: 119 us; the launch traced here: 118 us
  Pallas kernels  51.9 us (44%)
  blocking collectives  29.5 us (25%)
  local copies, waits for them, and re-layouts  15.6 us (13%)
  waiting for transfers between devices  9.76 us (8%)
  starting transfers between devices  8.58 us (7%)
  other arithmetic  1.98 us (2%)
    pallas_call x1, Pallas kernels, attend(): pl.pallas_call(functools.partial(attend_kernel, scale, heads // kv_local,...  31.4 us
    all_to_all x3, blocking collectives, swap(): return lax.all_to_all(x, axis, split_axis=0, concat_axis=0, tiled=True)  29.5 us
    pallas_call x1, Pallas kernels, make_list(): pl.pallas_call(functools.partial(list_kernel, block_size, slots), in_spec...  16.4 us
    unnamed x26, local copies, waits for them, and re-layouts  15.5 us
    all_to_all x2, waiting for transfers between devices, swap(): return lax.all_to_all(x, axis, split_axis=0, concat_axis=0, tiled=True)  9.76 us
    all_to_all x2, starting transfers between devices, swap(): return lax.all_to_all(x, axis, split_axis=0, concat_axis=0, tiled=True)  8.58 us
    pallas_call x1, Pallas kernels, project(): pl.pallas_call(functools.partial(project_kernel, rank), grid=(width // CO...  3.39 us
  transfers between devices with their start and end apart: 2, of which 1 were waited for; matrix products, arithmetic and copies ran while one was open for 0% of the time, Pallas kernels for 14%

profile of v1, /device:TPU:0, one launch (start us, length us, event | category | flops | bytes accessed | tf_op | source)
XLA Modules:
  0.0 118.0 jit_solution(11004517466594849745)
XLA Ops:
  0.0 0.1 pad.7.clone
  0.1 0.9 add_convert_fusion.slots_ref
  1.0 2.2 %copy-done.3 = f32[32,16,2048]{2,1,0:T(8,128)S(1)} copy-done((f32[32,16,2048]{2,1,0:T(8,128)S(1)}, f32[32,16,2048]{2,1,0:T(8,128)}, u32[]{:S(2)}) %copy-start.3) | copy-done | bytes 4194328
  3.2 1.7 %copy-done.4 = bf16[640,2048]{1,0:T(8,128)(2,1)S(1)} copy-done((bf16[640,2048]{1,0:T(8,128)(2,1)S(1)}, bf16[640,2048]{1,0:T(8,128)(2,1)}, u32[]{:S(2)}) %copy-start.4) | copy-done | bytes 2621464
  5.0 1.1 copy-done.7
  6.0 0.9 copy-done.8
  6.9 0.7 copy-done.9
  7.6 0.7 copy-done.10
  8.2 3.4 %project.1 = f32[64,2176]{1,0:T(8,128)S(1)} custom-call(s32[1,64]{1,0:T(1,128)S(1)} %bitcast.24, s32[1,64]{1,0:T(1,128)S(1)} %bitcast.25, f32[8,128]{1,0:T(8,128)S(1)} %add_convert_fusion.slots_ref, bf16[64,640]{1,0:T(8,128)(2,1)S(1)} %copy-done.8, bf16[640,2048]{1,0:T(8,128)(2,1)S(1)} %copy-done.4, bf16[512,640]{1,0:T(8,128)(2,1)S(1)} %bitcast.23, ...), custom_call_target="tpu_custom_call" | custom-call | flops 570425344 | bytes 6815744 | tf_op jit(solution)/shard_map/project/pallas_call | solution.py:92
  11.7 0.8 copy-done.5
  12.5 5.2 %all-to-all-start = ((f32[8,8,2176]{2,1,0:T(8,128)}), f32[8,8,2176]{2,1,0:T(8,128)S(1)}, u32[]{:S(2)}, u32[]{:S(2)}) async-start(f32[8,8,2176]{2,1,0:T(8,128)} %bitcast.21), calls=%async_computation | async-start | bytes 1114112 | tf_op jit(solution)/shard_map/all_to_all | solution.py:321
  17.6 0.1 reduce_sum.21
  17.8 0.1 fusion.4
  17.9 0.1 pad_maximum_fusion
  18.0 9.8 %all-to-all-done.parts_ref = f32[8,8,2176]{2,1,0:T(8,128)S(1)} async-done(((f32[8,8,2176]{2,1,0:T(8,128)}), f32[8,8,2176]{2,1,0:T(8,128)S(1)}, u32[]{:S(2)}, u32[]{:S(2)}) %all-to-all-start) | async-done | bytes 557088 | tf_op jit(solution)/shard_map/all_to_all | solution.py:321
  27.7 0.3 queries.1
  28.0 0.7 copy-done.6
  28.7 3.4 %all-to-all-start.1 = ((bf16[8,8,16,128]{3,2,1,0:T(8,128)(2,1)}), bf16[8,8,16,128]{3,2,1,0:T(8,128)(2,1)S(1)}, u32[]{:S(2)}, u32[]{:S(2)}) async-start(bf16[8,8,16,128]{3,2,1,0:T(8,128)(2,1)} %copy-done.6), calls=%async_computation.1 | async-start | bytes 524288 | tf_op jit(solution)/shard_map/all_to_all | solution.py:321
  32.2 0.1 fusion.2
  32.3 0.1 reshape.56.packed_ref
  32.3 16.4 %slot_list.1 = (s32[528]{0:T(1024)S(1)}, s32[1]{0:T(128)}) custom-call(s32[2048]{0:T(1024)S(1)} %reshape.56.packed_ref), custom_call_target="tpu_custom_call" | custom-call | flops 100000000 | bytes 10000000 | tf_op jit(solution)/shard_map/slot_list/pallas_call | solution.py:175
  48.8 0.0 all-to-all-done.1
  48.8 0.0 copy-start.1
  48.8 3.4 %copy-done.1 = bf16[128,128,2,128]{3,2,1,0:T(2,128)(2,1)S(1)} copy-done((bf16[128,128,2,128]{3,2,1,0:T(2,128)(2,1)S(1)}, bf16[128,128,2,128]{3,2,1,0:T(2,128)(2,1)}, u32[]{:S(2)}) %copy-start.1) | copy-done | bytes 8388632
  52.2 3.4 %copy-done.2 = bf16[128,128,2,128]{3,2,1,0:T(2,128)(2,1)S(1)} copy-done((bf16[128,128,2,128]{3,2,1,0:T(2,128)(2,1)S(1)}, bf16[128,128,2,128]{3,2,1,0:T(2,128)(2,1)}, u32[]{:S(2)}) %copy-start.2) | copy-done | bytes 8388632
  55.6 31.4 %attend.1 = bf16[8,9,16,128]{3,2,1,0:T(8,128)(2,1)S(1)} custom-call(s32[528]{0:T(1024)S(1)} %get-tuple-element.7.list_ref, s32[1]{0:T(128)} %get-tuple-element.8.count_ref, bf16[64,16,128]{2,1,0:T(8,128)(2,1)S(1)} %bitcast.22, bf16[128,256,128]{2,1,0:T(8,128)(2,1)S(1)} %bitcast.18, bf16[128,256,128]{2,1,0:T(8,128)(2,1)S(1)} %bitcast.19), custom_call_target="tpu_custom_call" | custom-call | tf_op jit(solution)/shard_map/attend/pallas_call | solution.py:274
  87.0 9.7 %all_to_all.25.parts_ref = bf16[8,9,16,128]{3,2,1,0:T(8,128)(2,1)S(1)} all-to-all(bf16[8,9,16,128]{3,2,1,0:T(8,128)(2,1)S(1)} %attend.1), channel_id=1, replica_groups=mesh['row'=4,'kv'=8] {'kv'}, dimensions={0} | all-to-all | bytes 589824 | tf_op jit(solution)/shard_map/all_to_all | solution.py:321
  96.6 0.4 merge.1
  97.0 9.3 %all_to_all.26 = bf16[8,8,2048]{2,1,0:T(8,128)(2,1)S(1)} all-to-all(bf16[8,8,2048]{2,1,0:T(8,128)(2,1)S(1)} %merge.1), channel_id=1, replica_groups=mesh['row'=4,'kv'=8] {'kv'}, dimensions={0} | all-to-all | bytes 524288 | tf_op jit(solution)/shard_map/all_to_all | solution.py:321
  106.4 0.5 convolution_convert_fusion
  106.9 10.5 %all_to_all.27 = bf16[4,16,640]{2,1,0:T(8,128)(2,1)S(1)} all-to-all(bf16[4,16,640]{2,1,0:T(8,128)(2,1)S(1)} %bitcast.27), channel_id=1, replica_groups=mesh['row'=4,'kv'=8] {'row'}, dimensions={0} | all-to-all | bytes 163840 | tf_op jit(solution)/shard_map/all_to_all | solution.py:321
  117.4 0.6 reduce_sum.22
  (19 shorter events, 0.1 us)
Async XLA Ops:
  0.0 106.4 %copy-start = (bf16[2048,640]{1,0:T(8,128)(2,1)S(1)}, bf16[2048,640]{1,0:T(8,128)(2,1)}, u32[]{:S(2)}) copy-start(bf16[2048,640]{1,0:T(8,128)(2,1)} %param.20) | copy-start | bytes 7864324
  1.0 2.2 %copy-start.3 = (f32[32,16,2048]{2,1,0:T(8,128)S(1)}, f32[32,16,2048]{2,1,0:T(8,128)}, u32[]{:S(2)}) copy-start(f32[32,16,2048]{2,1,0:T(8,128)} %param.16) | copy-start | bytes 12582916
  3.2 1.7 %copy-start.4 = (bf16[640,2048]{1,0:T(8,128)(2,1)S(1)}, bf16[640,2048]{1,0:T(8,128)(2,1)}, u32[]{:S(2)}) copy-start(bf16[640,2048]{1,0:T(8,128)(2,1)} %weight_ref.1) | copy-start | bytes 7864324
  5.0 1.1 copy-start.7
  6.0 0.9 copy-start.8
  6.9 0.7 copy-start.9
  7.6 0.7 copy-start.10
  8.2 9.4 %copy-start.12 = (s32[8,32]{1,0:T(8,128)S(1)}, s32[8,32]{1,0:T(8,128)}, u32[]{:S(2)}) copy-start(s32[8,32]{1,0:T(8,128)} %param.23) | copy-start | bytes 3076
  8.2 19.5 %copy-start.11 = (f32[128]{0:T(128)S(1)}, f32[128]{0:T(128)}, u32[]{:S(2)}) copy-start(f32[128]{0:T(128)} %param.17) | copy-start | bytes 1540
  11.7 0.8 copy-start.5
  12.5 15.3 %all-to-all-start = ((f32[8,8,2176]{2,1,0:T(8,128)}), f32[8,8,2176]{2,1,0:T(8,128)S(1)}, u32[]{:S(2)}, u32[]{:S(2)}) async-start(f32[8,8,2176]{2,1,0:T(8,128)} %bitcast.21), calls=%async_computation | async-start | bytes 1114112 | tf_op jit(solution)/shard_map/all_to_all | solution.py:321
  28.0 0.7 copy-start.6
  28.7 20.0 %all-to-all-start.1 = ((bf16[8,8,16,128]{3,2,1,0:T(8,128)(2,1)}), bf16[8,8,16,128]{3,2,1,0:T(8,128)(2,1)S(1)}, u32[]{:S(2)}, u32[]{:S(2)}) async-start(bf16[8,8,16,128]{3,2,1,0:T(8,128)(2,1)} %copy-done.6), calls=%async_computation.1 | async-start | bytes 524288 | tf_op jit(solution)/shard_map/all_to_all | solution.py:321
  48.8 3.4 %copy-start.1 = (bf16[128,128,2,128]{3,2,1,0:T(2,128)(2,1)S(1)}, bf16[128,128,2,128]{3,2,1,0:T(2,128)(2,1)}, u32[]{:S(2)}) copy-start(bf16[128,128,2,128]{3,2,1,0:T(2,128)(2,1)} %param.18) | copy-start | bytes 25165828
  52.2 3.4 %copy-start.2 = (bf16[128,128,2,128]{3,2,1,0:T(2,128)(2,1)S(1)}, bf16[128,128,2,128]{3,2,1,0:T(2,128)(2,1)}, u32[]{:S(2)}) copy-start(bf16[128,128,2,128]{3,2,1,0:T(2,128)(2,1)} %param.19) | copy-start | bytes 25165828

commit v2 on v1

v2 whole, which is shorter than its diff:
```python
import functools
import math

import jax
import jax.numpy as jnp
from jax import lax
from jax.experimental import pallas as pl
from jax.experimental.pallas import tpu as pltpu
from jax.sharding import PartitionSpec as P

ADAPTER_SCALE = 0.5
ROPE_BASE = 1000000.0
EPSILON = 1e-06
NEG_FILL = -1e30
LANES = 128
COLUMN_TILE = 256
UNROLL = 16
PHASES = 4
LOG2E = math.log2(math.e)
MIB = 1024 * 1024


def params(mib):
    return pltpu.CompilerParams(vmem_limit_bytes=mib * MIB)


def vmem_spec():
    return pl.BlockSpec(memory_space=pltpu.VMEM)


def in_hbm(*arrays):
    return [pltpu.with_memory_space_constraint(x, pltpu.HBM) for x in arrays]


def smem_spec():
    return pl.BlockSpec(memory_space=pltpu.SMEM)


def split2(x):
    high = x.astype(jnp.bfloat16)
    return high, (x - high.astype(jnp.float32)).astype(jnp.bfloat16)


def split3(x):
    high = x.astype(jnp.bfloat16).astype(jnp.float32)
    rest = x - high
    middle = rest.astype(jnp.bfloat16).astype(jnp.float32)
    return high, middle, (rest - middle).astype(jnp.bfloat16).astype(jnp.float32)


def to_column(row, count):
    shape = (count, count)
    eye = lax.broadcasted_iota(jnp.int32, shape, 0) == lax.broadcasted_iota(jnp.int32, shape, 1)
    return jnp.sum(jnp.where(eye, row.astype(jnp.float32), 0.0), axis=1, keepdims=True)


def project_kernel(
    rank,
    tenant_ref,
    adapter_ref,
    holder_ref,
    block_ref,
    length_ref,
    hidden_ref,
    weight_ref,
    down_ref,
    up_ref,
    out_ref,
    high_ref,
    low_ref,
):
    step = pl.program_id(0)
    rows = hidden_ref.shape[0]
    width = pl.num_programs(0) * weight_ref.shape[1]
    nt = (((1,), (1,)), ((), ()))

    @pl.when(step == 0)
    def _():
        tenants = adapter_ref.shape[1]
        tenant = to_column(tenant_ref[...], rows)
        pick = lax.broadcasted_iota(jnp.int32, (rows, tenants), 1).astype(jnp.float32) == tenant
        adapter = jnp.sum(
            jnp.where(pick, adapter_ref[...].astype(jnp.float32), 0.0), axis=1, keepdims=True
        ).astype(jnp.int32)
        low = lax.dot_general(hidden_ref[...], down_ref[...], nt, preferred_element_type=jnp.float32)
        column = lax.broadcasted_iota(jnp.int32, low.shape, 1)
        match = (column >= adapter * rank) & (column < adapter * rank + rank)
        high_part, low_part = split2(jnp.where(match, ADAPTER_SCALE * low, 0.0))
        high_ref[...] = high_part
        low_ref[...] = low_part
        own, slots = holder_ref.shape
        numbers = [holder_ref[...], block_ref[...], length_ref[...], jnp.zeros((own, LANES - 3 * slots), jnp.int32)]
        numbers = jnp.concatenate(numbers, axis=1).astype(jnp.float32)
        for start in range(0, rows, own):
            out_ref[start : start + own, width:] = numbers

    up_high, up_low = split2(up_ref[...])
    total = jnp.dot(hidden_ref[...], weight_ref[...], preferred_element_type=jnp.float32)
    total += jnp.dot(low_ref[...], up_high, preferred_element_type=jnp.float32)
    total += jnp.dot(high_ref[...], up_low, preferred_element_type=jnp.float32)
    total += jnp.dot(high_ref[...], up_high, preferred_element_type=jnp.float32)
    tile = weight_ref.shape[1]
    out_ref[:, pl.ds(pl.multiple_of(step * tile, tile), tile)] = total


def project(tenant, tenant_adapter, holder, block, length, hidden, query_weight, down, up, rank):
    rows, depth = hidden.shape
    width = query_weight.shape[1]
    low_width = down.shape[0]
    whole = lambda shape: pl.BlockSpec(shape, lambda i: (0,) * len(shape))
    operands = in_hbm(tenant, tenant_adapter, holder, block, length, hidden, query_weight, down, up)
    specs = [whole(x.shape) for x in operands]
    specs[6] = pl.BlockSpec((depth, COLUMN_TILE), lambda i: (0, i))
    specs[8] = pl.BlockSpec((low_width, COLUMN_TILE), lambda i: (0, i))
    return pl.pallas_call(
        functools.partial(project_kernel, rank),
        grid=(width // COLUMN_TILE,),
        in_specs=specs,
        out_specs=whole((rows, width + LANES)),
        out_shape=pltpu.HBM((rows, width + LANES), jnp.float32),
        scratch_shapes=[
            pltpu.VMEM((rows, low_width), jnp.bfloat16),
            pltpu.VMEM((rows, low_width), jnp.bfloat16),
        ],
        compiler_params=params(16),
        cost_estimate=pl.CostEstimate(
            flops=2 * rows * width * (depth + 3 * low_width),
            bytes_accessed=2 * depth * width + 4 * low_width * width,
            transcendentals=0,
        ),
        name="project",
    )(*operands)


def queries_kernel(parts_ref, cosine_ref, sine_ref, gain_ref, out_ref, turned_ref):
    heads = turned_ref.shape[1]
    copies = out_ref.shape[0]
    cosine, sine, gain = cosine_ref[...], sine_ref[...], gain_ref[...]
    for h in range(heads):
        columns = slice(h * LANES, (h + 1) * LANES)
        query = parts_ref[0, :, columns]
        for s in range(1, parts_ref.shape[0]):
            query = query + parts_ref[s, :, columns]
        square = jnp.mean(query * query, axis=-1, keepdims=True)
        query = query * lax.rsqrt(square + EPSILON) * gain
        turned_ref[:, h, :] = query * cosine + pltpu.roll(query, LANES // 2, 1) * sine
    result = turned_ref[...].astype(jnp.bfloat16)
    for c in range(copies):
        out_ref[c] = result


def make_queries(parts, cosine, sine, gain, heads):
    count, own, _ = parts.shape
    shape = (count, own, heads, LANES)
    return pl.pallas_call(
        queries_kernel,
        grid=(1,),
        in_specs=[vmem_spec()] * 4,
        out_specs=pl.BlockSpec(shape, lambda i: (0, 0, 0, 0)),
        out_shape=pltpu.HBM(shape, jnp.bfloat16),
        scratch_shapes=[pltpu.VMEM((own, heads, LANES), jnp.float32)],
        compiler_params=params(16),
        name="queries",
    )(parts, cosine, sine, gain)


def list_kernel(blocks, block_size, slots, numbers_ref, list_ref, bound_ref, place_ref, value_ref):
    rows = place_ref.shape[0]
    capacity = list_ref.shape[1]
    me = lax.axis_index("kv").astype(jnp.float32)
    numbers = numbers_ref[...].reshape(rows, LANES)
    holder, block, length = (numbers[:, i * slots : (i + 1) * slots] for i in range(3))
    row = lax.broadcasted_iota(jnp.int32, (rows, slots), 0).astype(jnp.float32)
    spare = float(rows * blocks * block_size)
    value_ref[...] = (row * blocks + block) * block_size + (length - 1.0) - spare

    def before(count, axis):
        first = lax.broadcasted_iota(jnp.int32, (count, count), axis)
        return jnp.where(first < lax.broadcasted_iota(jnp.int32, (count, count), 1 - axis), 1.0, 0.0).astype(
            jnp.bfloat16
        )

    slot_before, row_before = before(slots, 0), before(rows, 1)
    place = jnp.full((rows, slots), -1.0, jnp.float32)
    base = jnp.zeros((1, 1), jnp.float32)
    lane = lax.broadcasted_iota(jnp.int32, (1, LANES), 1)
    bounds = jnp.zeros((1, LANES), jnp.float32)
    size = blocks // PHASES
    for part in range(PHASES):
        inside = (holder == me) & (block >= part * size) & (block < (part + 1) * size)
        ones = jnp.where(inside, 1.0, 0.0)
        flags = ones.astype(jnp.bfloat16)
        within = jnp.dot(flags, slot_before, preferred_element_type=jnp.float32)
        above = jnp.sum(jnp.dot(row_before, flags, preferred_element_type=jnp.float32), axis=1, keepdims=True)
        place = jnp.where(inside, base + above + within, place)
        count = jnp.sum(jnp.sum(ones, axis=1, keepdims=True), axis=0, keepdims=True)
        base = base + jnp.ceil(count * (1.0 / UNROLL)) * UNROLL
        bounds = jnp.where(lane == part + 1, base * (1.0 / UNROLL), bounds)
    bound_ref[...] = bounds.astype(jnp.int32)
    place_ref[...] = place
    target = lax.broadcasted_iota(jnp.int32, (8, capacity), 1).astype(jnp.float32)

    def tile(t, total):
        here = pl.ds(pl.multiple_of(t * 8, 8), 8)
        places, values = place_ref[here, :], value_ref[here, :]
        for j in range(slots):
            total = total + jnp.where(places[:, j : j + 1] == target, values[:, j : j + 1], 0.0)
        return total

    total = lax.fori_loop(0, rows // 8, tile, jnp.zeros((8, capacity), jnp.float32))
    list_ref[...] = (jnp.sum(total, axis=0, keepdims=True) + spare).astype(jnp.int32)


def make_list(parts, slots, blocks, block_size):
    count, own, width = parts.shape
    rows = count * own
    most = 2 * own * slots // count * count + (PHASES + 2) * UNROLL
    capacity = -(-most // LANES) * LANES
    last = width // LANES - 1
    return pl.pallas_call(
        functools.partial(list_kernel, blocks, block_size, slots),
        grid=(1,),
        in_specs=[pl.BlockSpec((count, own, LANES), lambda i: (0, 0, last))],
        out_specs=[
            pl.BlockSpec((1, capacity), lambda i: (0, 0)),
            pl.BlockSpec((1, LANES), lambda i: (0, 0)),
        ],
        out_shape=[
            jax.ShapeDtypeStruct((1, capacity), jnp.int32),
            jax.ShapeDtypeStruct((1, LANES), jnp.int32),
        ],
        scratch_shapes=[pltpu.VMEM((rows, slots), jnp.float32), pltpu.VMEM((rows, slots), jnp.float32)],
        compiler_params=params(16),
        cost_estimate=pl.CostEstimate(flops=10**8, bytes_accessed=10**7, transcendentals=0),
        name="slot_list",
    )(parts)


def attend_kernel(
    scale,
    group,
    kv_local,
    list_ref,
    bound_ref,
    query_ref,
    key_hbm,
    value_hbm,
    out_ref,
    key_ref,
    value_ref,
    top_ref,
    total_ref,
    sum_ref,
    score_ref,
    part_top_ref,
    part_total_ref,
    part_sum_ref,
    sems,
):
    rows, heads, _ = query_ref.shape
    blocks, tokens, _ = key_ref.shape
    block_size = tokens // kv_local
    size = blocks // PHASES
    length_bits = (block_size - 1).bit_length()
    block_bits = (blocks - 1).bit_length()
    copies = []
    for part in range(PHASES):
        here = pl.ds(part * size, size)
        pair = (
            pltpu.make_async_copy(key_hbm.at[here], key_ref.at[here], sems.at[0, part]),
            pltpu.make_async_copy(value_hbm.at[here], value_ref.at[here], sems.at[1, part]),
        )
        for copy in pair:
            copy.start()
        copies.append(pair)

    factor = scale * LOG2E
    top_ref[...] = jnp.full(top_ref.shape, NEG_FILL, jnp.float32)
    for ref in (total_ref, sum_ref, score_ref, part_top_ref, part_total_ref, part_sum_ref):
        ref[...] = jnp.zeros(ref.shape, jnp.float32)
    head = lax.broadcasted_iota(jnp.int32, (heads, tokens), 0) // group
    place = lax.broadcasted_iota(jnp.int32, (heads, tokens), 1)
    token = jnp.where(place % kv_local == head, place // kv_local, block_size)
    nt = (((1,), (1,)), ((), ()))
    wide = (heads, LANES)

    def entries(chunk):
        return [list_ref[0, chunk * UNROLL + j] for j in range(UNROLL)]

    def row_of(entry):
        return entry >> (length_bits + block_bits)

    def block_of(entry):
        return (entry >> length_bits) & (blocks - 1)

    def turn(i, carry):
        before, top, total, acc = carry
        row = [jnp.where(i >= 2, row_of(e), rows) for e in entries(jnp.maximum(i - 2, 0))]
        states = [(top_ref[r], total_ref[r], sum_ref[r]) for r in row]
        for j in range(UNROLL):
            fresh = row[j] != before
            top, total, acc = (jnp.where(fresh, x, y) for x, y in zip(states[j], (top, total, acc)))
            part_top = part_top_ref[j]
            high = jnp.maximum(top, part_top)
            old = jnp.exp2((top - high) * factor)
            new = jnp.exp2((part_top - high) * factor)
            total = total * old + part_total_ref[j] * new
            acc = acc * old + part_sum_ref[j] * new
            top, before = high, row[j]
            top_ref[row[j]] = top
            total_ref[row[j]] = total
            sum_ref[row[j]] = acc

        for j, entry in enumerate(entries(jnp.maximum(i - 1, 0))):
            scores = jnp.where(token <= (entry & (block_size - 1)), score_ref[j], NEG_FILL)
            high = jnp.max(scores, axis=1, keepdims=True)
            weights = jnp.exp2((scores - high) * factor)
            part_top_ref[j] = jnp.broadcast_to(high, wide)
            part_total_ref[j] = jnp.broadcast_to(jnp.sum(weights, axis=1, keepdims=True), wide)
            part_sum_ref[j] = jnp.dot(
                weights.astype(jnp.bfloat16), value_ref[block_of(entry)], preferred_element_type=jnp.float32
            )

        for j, entry in enumerate(entries(i)):
            score_ref[j] = lax.dot_general(
                query_ref[jnp.minimum(row_of(entry), rows - 1)],
                key_ref[block_of(entry)],
                nt,
                preferred_element_type=jnp.float32,
            )
        return before, top, total, acc

    zero = jnp.zeros(wide, jnp.float32)
    carry = (jnp.int32(-1), zero, zero, zero)
    for part in range(PHASES):
        for copy in copies[part]:
            copy.wait()
        carry = lax.fori_loop(bound_ref[0, part], bound_ref[0, part + 1], turn, carry)
    last = bound_ref[0, PHASES]
    lax.fori_loop(last, last + 2, turn, carry)

    count, sections, _, _ = out_ref.shape
    own = sections - 1
    square = (own * heads, LANES)
    eye = lax.broadcasted_iota(jnp.int32, square, 0) == lax.broadcasted_iota(jnp.int32, square, 1)
    line = lax.broadcasted_iota(jnp.int32, wide, 0)
    for c in range(count):
        stats = jnp.zeros(wide, jnp.float32)
        position = 0
        for ref in (top_ref, total_ref):
            flat = jnp.sum(
                jnp.where(eye, ref[c * own : (c + 1) * own].reshape(square), 0.0), axis=0, keepdims=True
            )
            for piece in split3(flat):
                stats = jnp.where(line == position, piece, stats)
                position += 1
        for r in range(own):
            out_ref[c, r] = sum_ref[c * own + r].astype(jnp.bfloat16)
        out_ref[c, own] = stats.astype(jnp.bfloat16)


def attend(items, bounds, queries, keys, values, count, kv_local, scale):
    rows, heads, _ = queries.shape
    own = rows // count
    tokens = keys.shape[1]
    keys, values = in_hbm(keys, values)
    state = pltpu.VMEM((rows + 1, heads, LANES), jnp.float32)
    part = pltpu.VMEM((UNROLL, heads, LANES), jnp.float32)
    hbm = pl.BlockSpec(memory_space=pltpu.HBM)
    return pl.pallas_call(
        functools.partial(attend_kernel, scale, heads // kv_local, kv_local),
        in_specs=[smem_spec(), smem_spec(), vmem_spec(), hbm, hbm],
        out_specs=vmem_spec(),
        out_shape=jax.ShapeDtypeStruct((count, own + 1, heads, LANES), jnp.bfloat16),
        scratch_shapes=[
            pltpu.VMEM(keys.shape, keys.dtype),
            pltpu.VMEM(values.shape, values.dtype),
            state,
            state,
            state,
            pltpu.VMEM((UNROLL, heads, tokens), jnp.float32),
            part,
            part,
            part,
            pltpu.SemaphoreType.DMA((2, PHASES)),
        ],
        compiler_params=params(40),
        name="attend",
    )(items, bounds, queries, keys, values)


def merge_kernel(scale, parts_ref, out_ref, wide_ref):
    count, sections, heads, _ = parts_ref.shape
    own = sections - 1
    factor = scale * LOG2E
    stats = [parts_ref[s, own].astype(jnp.float32) for s in range(count)]
    tops = jnp.concatenate([s[0:1] + s[1:2] + s[2:3] for s in stats], axis=0)
    totals = jnp.concatenate([s[3:4] + s[4:5] + s[5:6] for s in stats], axis=0)
    weights = jnp.exp2((tops - jnp.max(tops, axis=0, keepdims=True)) * factor)
    weights = weights / jnp.sum(weights * totals, axis=0, keepdims=True)
    columns = weights.T
    acc = jnp.zeros((own * heads, LANES), jnp.float32)
    for s in range(count):
        part = parts_ref[s, :own].astype(jnp.float32).reshape(own * heads, LANES)
        acc = acc + part * columns[:, s : s + 1]
    wide_ref[...] = acc
    pieces = [wide_ref[pl.ds(h, own, stride=heads), :] for h in range(heads)]
    out_ref[...] = jnp.concatenate(pieces, axis=1).astype(jnp.bfloat16)


def merge(parts, scale):
    count, sections, heads, _ = parts.shape
    own = sections - 1
    return pl.pallas_call(
        functools.partial(merge_kernel, scale),
        in_specs=[vmem_spec()],
        out_specs=vmem_spec(),
        out_shape=jax.ShapeDtypeStruct((own, heads * LANES), jnp.bfloat16),
        scratch_shapes=[pltpu.VMEM((own * heads, LANES), jnp.float32)],
        compiler_params=params(16),
        name="merge",
    )(parts)


def output_kernel(count, row_count, *refs):
    pieces, weight_ref = refs[:count], refs[count]
    own_ref, sends = refs[count + 1], refs[count + 2 : count + 1 + row_count]
    rows_ref, terms_ref = refs[count + 1 + row_count :]
    own = pieces[0].shape[0]
    me = lax.axis_index("kv")
    for s in range(count):
        start = pl.multiple_of(jnp.bitwise_xor(me, s) * own, own)
        rows_ref[pl.ds(start, own), :] = pieces[s][...].astype(jnp.float32)
    terms_ref[...] = jnp.dot(
        rows_ref[...].astype(jnp.bfloat16), weight_ref[...], preferred_element_type=jnp.float32
    )
    me = lax.axis_index("row")
    part = own_ref.shape[0]
    for s, ref in enumerate((own_ref, *sends)):
        start = pl.multiple_of(jnp.bitwise_xor(me, s) * part, part)
        ref[...] = terms_ref[pl.ds(start, part), :].astype(ref.dtype)


def project_out(pieces, weight, row_count):
    count = len(pieces)
    own, width = pieces[0].shape
    rows, columns = count * own, weight.shape[1]
    part = rows // row_count
    send = jax.ShapeDtypeStruct((part, columns), jnp.bfloat16)
    return pl.pallas_call(
        functools.partial(output_kernel, count, row_count),
        in_specs=[vmem_spec()] * (count + 1),
        out_specs=[vmem_spec()] * row_count,
        out_shape=[jax.ShapeDtypeStruct((part, columns), jnp.float32)] + [send] * (row_count - 1),
        scratch_shapes=[pltpu.VMEM((rows, width), jnp.float32), pltpu.VMEM((rows, columns), jnp.float32)],
        compiler_params=params(24),
        name="project_out",
    )(*pieces, weight)


def swap(x, axis):
    return lax.all_to_all(x, axis, split_axis=0, concat_axis=0, tiled=True)


def exchange(x, axis, s):
    count = lax.axis_size(axis)
    return lax.ppermute(x, axis, [(i, i ^ s) for i in range(count)])


def local(
    hidden,
    query_weight,
    adapter_down_weight,
    adapter_up_weight,
    query_norm_gain,
    paged_key_cache,
    paged_value_cache,
    output_weight,
    holder,
    holder_block_index,
    block_used_length,
    tenant,
    tenant_adapter,
):
    own, slots = holder.shape
    rows, depth = hidden.shape
    kv_count = lax.axis_size("kv")
    row_count = lax.axis_size("row")
    adapters, _, rank = adapter_down_weight.shape
    width = query_weight.shape[1]
    head_size = query_norm_gain.shape[0]
    heads = width // head_size
    blocks, block_size, kv_local, _ = paged_key_cache.shape
    scale = 1.0 / math.sqrt(head_size)

    partial = project(
        tenant.reshape(1, rows),
        tenant_adapter.reshape(1, -1),
        holder,
        holder_block_index,
        block_used_length,
        hidden,
        query_weight,
        jnp.swapaxes(adapter_down_weight, 1, 2).reshape(adapters * rank, depth),
        adapter_up_weight.reshape(adapters * rank, width),
        rank,
    )
    parts = swap(partial.reshape(kv_count, own, width + LANES), "kv")

    position = (jnp.sum(block_used_length, axis=1) - 1).astype(jnp.float32)
    half = head_size // 2
    frequency = ROPE_BASE ** (-(jnp.arange(half, dtype=jnp.float32) * 2.0) / head_size)
    angles = position[:, None] * frequency[None, :]
    cosine = jnp.concatenate([jnp.cos(angles), jnp.cos(angles)], axis=-1)
    sine = jnp.concatenate([-jnp.sin(angles), jnp.sin(angles)], axis=-1)
    queries = make_queries(parts, cosine, sine, query_norm_gain.reshape(1, head_size), heads)
    queries = swap(queries, "kv").reshape(rows, heads, head_size)
    items, bounds = make_list(parts, slots, blocks, block_size)

    keys = paged_key_cache.reshape(blocks, block_size * kv_local, head_size)
    values = paged_value_cache.reshape(blocks, block_size * kv_local, head_size)
    partial_out = attend(items, bounds, queries, keys, values, kv_count, kv_local, scale)
    attention = merge(swap(partial_out, "kv"), scale)
    pieces = [attention] + [exchange(attention, "kv", s) for s in range(1, kv_count)]
    terms = project_out(pieces, output_weight, row_count)
    total = terms[0]
    for s in range(1, row_count):
        total = total + exchange(terms[s], "row", s).astype(jnp.float32)
    return total.astype(jnp.bfloat16)


def solution(mesh):
    return jax.shard_map(
        local,
        mesh=mesh,
        in_specs=(
            P(None, "kv"),
            P("kv", "row"),
            P(None, "kv", None),
            P(None, None, "row"),
            P(),
            P("kv", None, "row", None),
            P("kv", None, "row", None),
            P("row", "kv"),
            P("kv", None),
            P("kv", None),
            P("kv", None),
            P(),
            P(),
        ),
        out_specs=P("row", "kv"),
        check_vma=False,
    )
```

time: 119 us -> 88 us (0.74); the launches traced: 118 us -> 88.6 us
  blocking collectives: 29.5 us -> 9.66 us
  local copies, waits for them, and re-layouts: 15.6 us -> 0.01 us
  Pallas kernels: 51.9 us -> 37.2 us
  waiting for transfers between devices: 9.76 us -> 21.6 us
  starting transfers between devices: 8.58 us -> 19.2 us
    all_to_all x3 -> x1, blocking collectives: 29.5 us -> 9.66 us  [swap(): return lax.all_to_all(x, axis, split_axis=0, concat_axis=0, tiled=True)]
    unnamed x26 -> x6, local copies, waits for them, and re-layouts: 15.5 us -> 0.01 us
    pallas_call x2 -> x3, Pallas kernels: 16.7 us -> 3.39 us  [the longest x1 1.76 us: make_list(): pl.pallas_call(functools.partial(list_kernel, blocks, block_size, slots),...]
    ppermute x0 -> x10, starting transfers between devices: none -> 10.6 us  [exchange(): return lax.ppermute(x, axis, [(i, i ^ s) for i in range(count)])]
    ppermute x0 -> x10, waiting for transfers between devices: none -> 6.73 us  [exchange(): return lax.ppermute(x, axis, [(i, i ^ s) for i in range(count)])]
    pallas_call x1, Pallas kernels: 31.4 us -> 25.6 us  [attend(): pl.pallas_call(functools.partial(attend_kernel, scale, heads // kv_local,...]
    all_to_all x2, waiting for transfers between devices: 9.76 us -> 14.9 us  [swap(): return lax.all_to_all(x, axis, split_axis=0, concat_axis=0, tiled=True)]
    pallas_call x1, Pallas kernels: 3.39 us -> 7.77 us  [project(): pl.pallas_call(functools.partial(project_kernel, rank), grid=(width // CO...]
  transfers between devices with their start and end apart: 2 -> 12, of which waited for: 1 -> 7; matrix products, arithmetic and copies ran while one was open for 0% -> 0% of each run, Pallas kernels for 14% -> 2%
where the time goes in v2:
time: 88 us; the launch traced here: 88.6 us
  Pallas kernels  37.2 us (42%)
  waiting for transfers between devices  21.6 us (25%)
  starting transfers between devices  19.2 us (22%)
  blocking collectives  9.66 us (11%)
  other arithmetic  0.95 us (1%)
    pallas_call x1, Pallas kernels, attend(): pl.pallas_call(functools.partial(attend_kernel, scale, heads // kv_local,...  25.6 us
    all_to_all x2, waiting for transfers between devices, swap(): return lax.all_to_all(x, axis, split_axis=0, concat_axis=0, tiled=True)  14.9 us
    ppermute x10, starting transfers between devices, exchange(): return lax.ppermute(x, axis, [(i, i ^ s) for i in range(count)])  10.6 us
    all_to_all x1, blocking collectives, swap(): return lax.all_to_all(x, axis, split_axis=0, concat_axis=0, tiled=True)  9.66 us
    all_to_all x2, starting transfers between devices, swap(): return lax.all_to_all(x, axis, split_axis=0, concat_axis=0, tiled=True)  8.58 us
    pallas_call x1, Pallas kernels, project(): pl.pallas_call(functools.partial(project_kernel, rank), grid=(width // CO...  7.77 us
    ppermute x10, waiting for transfers between devices, exchange(): return lax.ppermute(x, axis, [(i, i ^ s) for i in range(count)])  6.73 us
    pallas_call x1, Pallas kernels, make_list(): pl.pallas_call(functools.partial(list_kernel, blocks, block_size, slots),...  1.76 us
  transfers between devices with their start and end apart: 12, of which 7 were waited for; matrix products, arithmetic and copies ran while one was open for 0% of the time, Pallas kernels for 2%

profile of v2, /device:TPU:0, one launch (start us, length us, event | category | flops | bytes accessed | tf_op | source)
XLA Modules:
  0.0 88.6 jit_solution(13853937629574687703)
XLA Ops:
  0.0 7.8 %project.1 = f32[64,2176]{1,0:T(8,128)} custom-call(s32[1,64]{1,0:T(1,128)} %bitcast.18, s32[1,64]{1,0:T(1,128)} %bitcast.19, s32[8,32]{1,0:T(8,128)} %holder_ref.1, s32[8,32]{1,0:T(8,128)} %block_ref.1, s32[8,32]{1,0:T(8,128)} %length_ref.1, bf16[64,640]{1,0:T(8,128)(2,1)} %hidden_ref.1, bf16[640,2048]{1,0:T(8,128)(2,1)} %weight_ref.1, ...), custom_call_target="tpu_custom_call" | custom-call | flops 570425344 | bytes 6815744 | tf_op jit(solution)/shard_map/project/pallas_call | solution.py:115
  7.8 5.2 %all-to-all-start = ((f32[8,8,2176]{2,1,0:T(8,128)}), f32[8,8,2176]{2,1,0:T(8,128)S(1)}, u32[]{:S(2)}, u32[]{:S(2)}) async-start(f32[8,8,2176]{2,1,0:T(8,128)} %bitcast.16), calls=%async_computation | async-start | bytes 1114112 | tf_op jit(solution)/shard_map/all_to_all | solution.py:462
  13.0 0.1 reduce_sum.9
  13.1 0.1 fusion
  13.2 0.1 pad_maximum_fusion
  13.3 9.8 %all-to-all-done.numbers_ref.parts_ref = f32[8,8,2176]{2,1,0:T(8,128)S(1)} async-done(((f32[8,8,2176]{2,1,0:T(8,128)}), f32[8,8,2176]{2,1,0:T(8,128)S(1)}, u32[]{:S(2)}, u32[]{:S(2)}) %all-to-all-start) | async-done | bytes 557088 | tf_op jit(solution)/shard_map/all_to_all | solution.py:462
  23.0 1.0 %queries.1 = bf16[8,8,16,128]{3,2,1,0:T(8,128)(2,1)} custom-call(f32[8,8,2176]{2,1,0:T(8,128)S(1)} %all-to-all-done.numbers_ref.parts_ref, f32[8,128]{1,0:T(8,128)S(1)} %get-tuple-element.20.cosine_ref, f32[8,128]{1,0:T(8,128)S(1)} %get-tuple-element.21.sine_ref, f32[1,128]{1,0:T(1,128)S(1)} %bitcast.12), custom_call_target="tpu_custom_call" | custom-call | tf_op jit(solution)/shard_map/queries/pallas_call | solution.py:155
  24.1 3.4 %all-to-all-start.1 = ((bf16[8,8,16,128]{3,2,1,0:T(8,128)(2,1)}), bf16[8,8,16,128]{3,2,1,0:T(8,128)(2,1)S(1)}, u32[]{:S(2)}, u32[]{:S(2)}) async-start(bf16[8,8,16,128]{3,2,1,0:T(8,128)(2,1)} %queries.1), calls=%async_computation.1 | async-start | bytes 524288 | tf_op jit(solution)/shard_map/all_to_all | solution.py:462
  27.5 1.8 %slot_list.1 = (s32[1,640]{1,0:T(1,128)S(1)}, s32[1,128]{1,0:T(1,128)S(1)}) custom-call(f32[8,8,2176]{2,1,0:T(8,128)S(1)} %all-to-all-done.numbers_ref.parts_ref), custom_call_target="tpu_custom_call" | custom-call | flops 100000000 | bytes 10000000 | tf_op jit(solution)/shard_map/slot_list/pallas_call | solution.py:220
  29.3 5.1 %all-to-all-done.1 = bf16[8,8,16,128]{3,2,1,0:T(8,128)(2,1)S(1)} async-done(((bf16[8,8,16,128]{3,2,1,0:T(8,128)(2,1)}), bf16[8,8,16,128]{3,2,1,0:T(8,128)(2,1)S(1)}, u32[]{:S(2)}, u32[]{:S(2)}) %all-to-all-start.1) | async-done | bytes 262176 | tf_op jit(solution)/shard_map/all_to_all | solution.py:462
  34.4 25.6 %attend.1 = bf16[8,9,16,128]{3,2,1,0:T(8,128)(2,1)S(1)} custom-call(s32[1,640]{1,0:T(1,128)S(1)} %get-tuple-element.11.list_ref, s32[1,128]{1,0:T(1,128)S(1)} %get-tuple-element.12.bound_ref, bf16[64,16,128]{2,1,0:T(8,128)(2,1)S(1)} %bitcast.11, bf16[128,256,128]{2,1,0:T(8,128)(2,1)} %bitcast.13, bf16[128,256,128]{2,1,0:T(8,128)(2,1)} %bitcast.14), custom_call_target="tpu_custom_call" | custom-call | tf_op jit(solution)/shard_map/attend/pallas_call | solution.py:370
  60.0 9.7 %all_to_all.15.parts_ref = bf16[8,9,16,128]{3,2,1,0:T(8,128)(2,1)S(1)} all-to-all(bf16[8,9,16,128]{3,2,1,0:T(8,128)(2,1)S(1)} %attend.1), channel_id=1, replica_groups=mesh['row'=4,'kv'=8] {'kv'}, dimensions={0} | all-to-all | bytes 589824 | tf_op jit(solution)/shard_map/all_to_all | solution.py:462
  69.7 0.4 merge.1.refs_0_
  70.1 0.1 collective-permute-start
  70.1 0.6 collective-permute-start.1
  70.8 1.2 %collective-permute-start.2 = (bf16[8,2048]{1,0:T(8,128)(2,1)S(1)}, bf16[8,2048]{1,0:T(8,128)(2,1)S(1)}, u32[]{:S(2)}, u32[]{:S(2)}) collective-permute-start(bf16[8,2048]{1,0:T(8,128)(2,1)S(1)} %merge.1.refs_0_), channel_id=1, source_target_pairs={{0,3},{1,2},{2,1},{3,0},{4,7},{5,6},{6,5},{7,4},{8,11},{9,10},{10,... | collective-permute-start | bytes 98312 | tf_op jit(solution)/shard_map/ppermute | solution.py:467
  72.0 0.6 collective-permute-start.3
  72.5 1.1 %collective-permute-start.4 = (bf16[8,2048]{1,0:T(8,128)(2,1)S(1)}, bf16[8,2048]{1,0:T(8,128)(2,1)S(1)}, u32[]{:S(2)}, u32[]{:S(2)}) collective-permute-start(bf16[8,2048]{1,0:T(8,128)(2,1)S(1)} %merge.1.refs_0_), channel_id=1, source_target_pairs={{0,5},{1,4},{2,7},{3,6},{4,1},{5,0},{6,3},{7,2},{8,13},{9,12},{10,... | collective-permute-start | bytes 98312 | tf_op jit(solution)/shard_map/ppermute | solution.py:467
  73.7 0.0 collective-permute-done.refs_1_
  73.7 0.6 collective-permute-start.5
  74.3 0.2 collective-permute-done.1.refs_2_
  74.4 1.9 %collective-permute-start.6 = (bf16[8,2048]{1,0:T(8,128)(2,1)S(1)}, bf16[8,2048]{1,0:T(8,128)(2,1)S(1)}, u32[]{:S(2)}, u32[]{:S(2)}) collective-permute-start(bf16[8,2048]{1,0:T(8,128)(2,1)S(1)} %merge.1.refs_0_), channel_id=1, source_target_pairs={{0,7},{1,6},{2,5},{3,4},{4,3},{5,2},{6,1},{7,0},{8,15},{9,14},{10,... | collective-permute-start | bytes 98312 | tf_op jit(solution)/shard_map/ppermute | solution.py:467
  76.4 0.0 collective-permute-done.2.refs_3_
  76.4 0.0 collective-permute-done.3.refs_4_
  76.4 2.3 %collective-permute-done.5.refs_6_ = bf16[8,2048]{1,0:T(8,128)(2,1)S(1)} collective-permute-done((bf16[8,2048]{1,0:T(8,128)(2,1)S(1)}, bf16[8,2048]{1,0:T(8,128)(2,1)S(1)}, u32[]{:S(2)}, u32[]{:S(2)}) %collective-permute-start.5) | collective-permute-done | bytes 32800 | tf_op jit(solution)/shard_map/ppermute | solution.py:467
  78.7 0.4 collective-permute-done.6.refs_7_
  79.0 0.6 project_out.1
  79.6 3.7 %collective-permute-start.9 = (bf16[16,640]{1,0:T(8,128)(2,1)S(1)}, bf16[16,640]{1,0:T(8,128)(2,1)S(1)}, u32[]{:S(2)}, u32[]{:S(2)}) collective-permute-start(bf16[16,640]{1,0:T(8,128)(2,1)S(1)} %get-tuple-element.16), channel_id=1, source_target_pairs={{0,24},{8,16},{16,8},{24,0},{1,25},{9,17},{17,9},{25,1},{2,26},{10... | collective-permute-start | bytes 61448 | tf_op jit(solution)/shard_map/ppermute | solution.py:467
  83.3 0.8 collective-permute-start.7
  84.1 1.2 %collective-permute-done.9 = bf16[16,640]{1,0:T(8,128)(2,1)S(1)} collective-permute-done((bf16[16,640]{1,0:T(8,128)(2,1)S(1)}, bf16[16,640]{1,0:T(8,128)(2,1)S(1)}, u32[]{:S(2)}, u32[]{:S(2)}) %collective-permute-start.9) | collective-permute-done | bytes 20512 | tf_op jit(solution)/shard_map/ppermute | solution.py:467
  85.3 2.7 %collective-permute-done.8 = bf16[16,640]{1,0:T(8,128)(2,1)S(1)} collective-permute-done((bf16[16,640]{1,0:T(8,128)(2,1)S(1)}, bf16[16,640]{1,0:T(8,128)(2,1)S(1)}, u32[]{:S(2)}, u32[]{:S(2)}) %collective-permute-start.8) | collective-permute-done | bytes 20512 | tf_op jit(solution)/shard_map/ppermute | solution.py:467
  88.0 0.6 add_convert_fusion
  (11 shorter events, 0.0 us)
Async XLA Ops:
  0.0 12.9 %copy-start.2 = (s32[8,32]{1,0:T(8,128)S(1)}, s32[8,32]{1,0:T(8,128)}, u32[]{:S(2)}) copy-start(s32[8,32]{1,0:T(8,128)} %length_ref.1) | copy-start | bytes 3076
  0.0 23.0 %copy-start.1 = (f32[128]{0:T(128)S(1)}, f32[128]{0:T(128)}, u32[]{:S(2)}) copy-start(f32[128]{0:T(128)} %param.17) | copy-start | bytes 1540
  7.8 15.3 %all-to-all-start = ((f32[8,8,2176]{2,1,0:T(8,128)}), f32[8,8,2176]{2,1,0:T(8,128)S(1)}, u32[]{:S(2)}, u32[]{:S(2)}) async-start(f32[8,8,2176]{2,1,0:T(8,128)} %bitcast.16), calls=%async_computation | async-start | bytes 1114112 | tf_op jit(solution)/shard_map/all_to_all | solution.py:462
  24.1 10.3 %all-to-all-start.1 = ((bf16[8,8,16,128]{3,2,1,0:T(8,128)(2,1)}), bf16[8,8,16,128]{3,2,1,0:T(8,128)(2,1)S(1)}, u32[]{:S(2)}, u32[]{:S(2)}) async-start(bf16[8,8,16,128]{3,2,1,0:T(8,128)(2,1)} %queries.1), calls=%async_computation.1 | async-start | bytes 524288 | tf_op jit(solution)/shard_map/all_to_all | solution.py:462
  34.4 44.7 %copy-start = (bf16[2048,640]{1,0:T(8,128)(2,1)S(1)}, bf16[2048,640]{1,0:T(8,128)(2,1)}, u32[]{:S(2)}) copy-start(bf16[2048,640]{1,0:T(8,128)(2,1)} %refs_8_.1) | copy-start | bytes 7864324
  70.1 3.6 %collective-permute-start = (bf16[8,2048]{1,0:T(8,128)(2,1)S(1)}, bf16[8,2048]{1,0:T(8,128)(2,1)S(1)}, u32[]{:S(2)}, u32[]{:S(2)}) collective-permute-start(bf16[8,2048]{1,0:T(8,128)(2,1)S(1)} %merge.1.refs_0_), channel_id=1, source_target_pairs={{0,1},{1,0},{2,3},{3,2},{4,5},{5,4},{6,7},{7,6},{8,9},{9,8},{10,11... | collective-permute-start | bytes 98312 | tf_op jit(solution)/shard_map/ppermute | solution.py:467
  70.1 4.3 %collective-permute-start.1 = (bf16[8,2048]{1,0:T(8,128)(2,1)S(1)}, bf16[8,2048]{1,0:T(8,128)(2,1)S(1)}, u32[]{:S(2)}, u32[]{:S(2)}) collective-permute-start(bf16[8,2048]{1,0:T(8,128)(2,1)S(1)} %merge.1.refs_0_), channel_id=1, source_target_pairs={{0,2},{1,3},{2,0},{3,1},{4,6},{5,7},{6,4},{7,5},{8,10},{9,11},{10,... | collective-permute-start | bytes 98312 | tf_op jit(solution)/shard_map/ppermute | solution.py:467
  70.8 5.6 %collective-permute-start.2 = (bf16[8,2048]{1,0:T(8,128)(2,1)S(1)}, bf16[8,2048]{1,0:T(8,128)(2,1)S(1)}, u32[]{:S(2)}, u32[]{:S(2)}) collective-permute-start(bf16[8,2048]{1,0:T(8,128)(2,1)S(1)} %merge.1.refs_0_), channel_id=1, source_target_pairs={{0,3},{1,2},{2,1},{3,0},{4,7},{5,6},{6,5},{7,4},{8,11},{9,10},{10,... | collective-permute-start | bytes 98312 | tf_op jit(solution)/shard_map/ppermute | solution.py:467
  72.0 4.4 %collective-permute-start.3 = (bf16[8,2048]{1,0:T(8,128)(2,1)S(1)}, bf16[8,2048]{1,0:T(8,128)(2,1)S(1)}, u32[]{:S(2)}, u32[]{:S(2)}) collective-permute-start(bf16[8,2048]{1,0:T(8,128)(2,1)S(1)} %merge.1.refs_0_), channel_id=1, source_target_pairs={{0,4},{1,5},{2,6},{3,7},{4,0},{5,1},{6,2},{7,3},{8,12},{9,13},{10,... | collective-permute-start | bytes 98312 | tf_op jit(solution)/shard_map/ppermute | solution.py:467
  72.5 3.9 %collective-permute-start.4 = (bf16[8,2048]{1,0:T(8,128)(2,1)S(1)}, bf16[8,2048]{1,0:T(8,128)(2,1)S(1)}, u32[]{:S(2)}, u32[]{:S(2)}) collective-permute-start(bf16[8,2048]{1,0:T(8,128)(2,1)S(1)} %merge.1.refs_0_), channel_id=1, source_target_pairs={{0,5},{1,4},{2,7},{3,6},{4,1},{5,0},{6,3},{7,2},{8,13},{9,12},{10,... | collective-permute-start | bytes 98312 | tf_op jit(solution)/shard_map/ppermute | solution.py:467
  73.7 5.0 %collective-permute-start.5 = (bf16[8,2048]{1,0:T(8,128)(2,1)S(1)}, bf16[8,2048]{1,0:T(8,128)(2,1)S(1)}, u32[]{:S(2)}, u32[]{:S(2)}) collective-permute-start(bf16[8,2048]{1,0:T(8,128)(2,1)S(1)} %merge.1.refs_0_), channel_id=1, source_target_pairs={{0,6},{1,7},{2,4},{3,5},{4,2},{5,3},{6,0},{7,1},{8,14},{9,15},{10,... | collective-permute-start | bytes 98312 | tf_op jit(solution)/shard_map/ppermute | solution.py:467
  74.4 4.6 %collective-permute-start.6 = (bf16[8,2048]{1,0:T(8,128)(2,1)S(1)}, bf16[8,2048]{1,0:T(8,128)(2,1)S(1)}, u32[]{:S(2)}, u32[]{:S(2)}) collective-permute-start(bf16[8,2048]{1,0:T(8,128)(2,1)S(1)} %merge.1.refs_0_), channel_id=1, source_target_pairs={{0,7},{1,6},{2,5},{3,4},{4,3},{5,2},{6,1},{7,0},{8,15},{9,14},{10,... | collective-permute-start | bytes 98312 | tf_op jit(solution)/shard_map/ppermute | solution.py:467
  79.6 5.6 %collective-permute-start.9 = (bf16[16,640]{1,0:T(8,128)(2,1)S(1)}, bf16[16,640]{1,0:T(8,128)(2,1)S(1)}, u32[]{:S(2)}, u32[]{:S(2)}) collective-permute-start(bf16[16,640]{1,0:T(8,128)(2,1)S(1)} %get-tuple-element.16), channel_id=1, source_target_pairs={{0,24},{8,16},{16,8},{24,0},{1,25},{9,17},{17,9},{25,1},{2,26},{10... | collective-permute-start | bytes 61448 | tf_op jit(solution)/shard_map/ppermute | solution.py:467
  83.3 4.7 %collective-permute-start.8 = (bf16[16,640]{1,0:T(8,128)(2,1)S(1)}, bf16[16,640]{1,0:T(8,128)(2,1)S(1)}, u32[]{:S(2)}, u32[]{:S(2)}) collective-permute-start(bf16[16,640]{1,0:T(8,128)(2,1)S(1)} %get-tuple-element.15), channel_id=1, source_target_pairs={{0,16},{8,24},{16,0},{24,8},{1,17},{9,25},{17,1},{25,9},{2,18},{10... | collective-permute-start | bytes 61448 | tf_op jit(solution)/shard_map/ppermute | solution.py:467
  83.3 4.7 %collective-permute-start.7 = (bf16[16,640]{1,0:T(8,128)(2,1)S(1)}, bf16[16,640]{1,0:T(8,128)(2,1)S(1)}, u32[]{:S(2)}, u32[]{:S(2)}) collective-permute-start(bf16[16,640]{1,0:T(8,128)(2,1)S(1)} %get-tuple-element.14), channel_id=1, source_target_pairs={{0,8},{8,0},{16,24},{24,16},{1,9},{9,1},{17,25},{25,17},{2,10},{10... | collective-permute-start | bytes 61448 | tf_op jit(solution)/shard_map/ppermute | solution.py:467

commit v3 on v2

v3 whole, which is shorter than its diff:
```python
import functools
import math

import jax
import jax.numpy as jnp
from jax import lax
from jax.experimental import pallas as pl
from jax.experimental.pallas import tpu as pltpu
from jax.sharding import PartitionSpec as P

ADAPTER_SCALE = 0.5
ROPE_BASE = 1000000.0
EPSILON = 1e-06
NEG_FILL = -1e30
LANES = 128
COLUMN_TILE = 256
PAIR = 2
TASKS = 8
CHUNK = PAIR * TASKS
PHASES = 8
LOG2E = math.log2(math.e)
MIB = 1024 * 1024


def params(mib):
    return pltpu.CompilerParams(vmem_limit_bytes=mib * MIB)


def vmem_spec():
    return pl.BlockSpec(memory_space=pltpu.VMEM)


def in_hbm(*arrays):
    return [pltpu.with_memory_space_constraint(x, pltpu.HBM) for x in arrays]


def hbm_spec():
    return pl.BlockSpec(memory_space=pltpu.HBM)


def smem_spec():
    return pl.BlockSpec(memory_space=pltpu.SMEM)


def split2(x):
    high = x.astype(jnp.bfloat16)
    return high, (x - high.astype(jnp.float32)).astype(jnp.bfloat16)


def split3(x):
    high = x.astype(jnp.bfloat16).astype(jnp.float32)
    rest = x - high
    middle = rest.astype(jnp.bfloat16).astype(jnp.float32)
    return high, middle, (rest - middle).astype(jnp.bfloat16).astype(jnp.float32)


def to_column(row, count):
    shape = (count, count)
    eye = lax.broadcasted_iota(jnp.int32, shape, 0) == lax.broadcasted_iota(jnp.int32, shape, 1)
    return jnp.sum(jnp.where(eye, row.astype(jnp.float32), 0.0), axis=1, keepdims=True)


def project_kernel(
    rank,
    tenant_ref,
    adapter_ref,
    holder_ref,
    block_ref,
    length_ref,
    hidden_hbm,
    weight_hbm,
    down_hbm,
    up_hbm,
    keep_ref,
    send_ref,
    hidden_ref,
    weight_ref,
    down_ref,
    up_ref,
    sems,
    tile_sems,
):
    chips, own, _ = keep_ref.shape
    rows = hidden_ref.shape[0]
    width = weight_ref.shape[1]
    tiles = width // COLUMN_TILE
    first = [
        pltpu.make_async_copy(hidden_hbm, hidden_ref, sems.at[0]),
        pltpu.make_async_copy(down_hbm, down_ref, sems.at[1]),
    ]
    for copy in first:
        copy.start()
    copies = []
    for i in range(tiles):
        columns = pl.ds(i * COLUMN_TILE, COLUMN_TILE)
        pair = (
            pltpu.make_async_copy(weight_hbm.at[:, columns], weight_ref.at[:, columns], tile_sems.at[0, i]),
            pltpu.make_async_copy(up_hbm.at[:, columns], up_ref.at[:, columns], tile_sems.at[1, i]),
        )
        for copy in pair:
            copy.start()
        copies.append(pair)

    slots = holder_ref.shape[1]
    numbers = [holder_ref[...], block_ref[...], length_ref[...], jnp.zeros((own, LANES - 3 * slots), jnp.int32)]
    numbers = jnp.concatenate(numbers, axis=1).astype(jnp.float32)
    for c in range(chips):
        keep_ref[c, :, width:] = numbers
        send_ref[c, :, width:] = numbers
    tenants = adapter_ref.shape[1]
    tenant = to_column(tenant_ref[...], rows)
    pick = lax.broadcasted_iota(jnp.int32, (rows, tenants), 1).astype(jnp.float32) == tenant
    adapter = jnp.sum(jnp.where(pick, adapter_ref[...].astype(jnp.float32), 0.0), axis=1, keepdims=True).astype(
        jnp.int32
    )
    for copy in first:
        copy.wait()
    hidden = hidden_ref[...]
    low = lax.dot_general(hidden, down_ref[...], (((1,), (1,)), ((), ())), preferred_element_type=jnp.float32)
    column = lax.broadcasted_iota(jnp.int32, low.shape, 1)
    match = (column >= adapter * rank) & (column < adapter * rank + rank)
    high, low = split2(jnp.where(match, ADAPTER_SCALE * low, 0.0))
    even = lax.axis_index("kv") % PAIR == 0
    for i in range(tiles):
        columns = slice(i * COLUMN_TILE, (i + 1) * COLUMN_TILE)
        for copy in copies[i]:
            copy.wait()
        up_high, up_low = split2(up_ref[:, columns])
        total = jnp.dot(hidden, weight_ref[:, columns], preferred_element_type=jnp.float32)
        total += jnp.dot(low, up_high, preferred_element_type=jnp.float32)
        total += jnp.dot(high, up_low, preferred_element_type=jnp.float32)
        total += jnp.dot(high, up_high, preferred_element_type=jnp.float32)
        total = total.reshape(chips, PAIR, own, COLUMN_TILE)
        keep_ref[:, :, columns] = jnp.where(even, total[:, 0], total[:, 1])
        send_ref[:, :, columns] = jnp.where(even, total[:, 1], total[:, 0])


def project(tenant, tenant_adapter, holder, block, length, hidden, query_weight, down, up, rank, chips):
    rows, _ = hidden.shape
    width = query_weight.shape[1]
    out = jax.ShapeDtypeStruct((chips, rows // chips // PAIR, width + LANES), jnp.float32)
    operands = in_hbm(tenant, tenant_adapter, holder, block, length, hidden, query_weight, down, up)
    large = operands[5:]
    return pl.pallas_call(
        functools.partial(project_kernel, rank),
        in_specs=[vmem_spec()] * 5 + [hbm_spec()] * 4,
        out_specs=[vmem_spec()] * 2,
        out_shape=[out] * 2,
        scratch_shapes=[pltpu.VMEM(x.shape, x.dtype) for x in large]
        + [pltpu.SemaphoreType.DMA((2,)), pltpu.SemaphoreType.DMA((2, width // COLUMN_TILE))],
        compiler_params=params(24),
        name="project",
    )(*operands)


def pair_kernel(keep_ref, got_ref, *out_refs):
    width = keep_ref.shape[2] - LANES
    chip = lax.axis_index("kv") // PAIR
    for s, ref in enumerate(out_refs):
        c = jnp.bitwise_xor(chip, s)
        ref[:, :width] = keep_ref[c, :, :width] + got_ref[c, :, :width]
        ref[:, width : width + LANES] = keep_ref[0, :, width:]
        ref[:, width + LANES :] = got_ref[0, :, width:]


def add_pair(keep, got):
    chips, own, width = keep.shape
    return pl.pallas_call(
        pair_kernel,
        in_specs=[vmem_spec()] * 2,
        out_specs=[vmem_spec()] * chips,
        out_shape=[jax.ShapeDtypeStruct((own, width + LANES), jnp.float32)] * chips,
        compiler_params=params(16),
        name="add_pair",
    )(keep, got)


def queries_kernel(*refs):
    parts, (cosine_ref, sine_ref, gain_ref, out_ref, turned_ref) = refs[:-5], refs[-5:]
    heads = turned_ref.shape[1]
    cosine, sine, gain = cosine_ref[...], sine_ref[...], gain_ref[...]
    for h in range(heads):
        columns = slice(h * LANES, (h + 1) * LANES)
        query = parts[0][:, columns]
        for part in parts[1:]:
            query = query + part[:, columns]
        square = jnp.mean(query * query, axis=-1, keepdims=True)
        query = query * lax.rsqrt(square + EPSILON) * gain
        turned_ref[:, h, :] = query * cosine + pltpu.roll(query, LANES // 2, 1) * sine
    out_ref[...] = turned_ref[...].astype(jnp.bfloat16)


def make_queries(parts, cosine, sine, gain, heads):
    own = parts[0].shape[0]
    shape = (own, heads, LANES)
    return pl.pallas_call(
        queries_kernel,
        in_specs=[vmem_spec()] * (len(parts) + 3),
        out_specs=vmem_spec(),
        out_shape=jax.ShapeDtypeStruct(shape, jnp.bfloat16),
        scratch_shapes=[pltpu.VMEM(shape, jnp.float32)],
        compiler_params=params(16),
        name="queries",
    )(*parts, cosine, sine, gain)


def list_kernel(blocks, block_size, slots, *refs):
    pieces, (list_ref, bound_ref, place_ref, value_ref) = refs[:-4], refs[-4:]
    rows = place_ref.shape[0]
    capacity = list_ref.shape[1]
    me = lax.axis_index("kv").astype(jnp.float32)
    numbers = jnp.concatenate([p[:, i * LANES : (i + 1) * LANES] for p in pieces for i in range(PAIR)], axis=0)
    holder, block, length = (numbers[:, i * slots : (i + 1) * slots] for i in range(3))
    row = lax.broadcasted_iota(jnp.int32, (rows, slots), 0).astype(jnp.float32)
    spare = float(rows * blocks * block_size)
    value_ref[...] = (row * blocks + block) * block_size + (length - 1.0) - spare
    mine = holder == me
    key = jnp.where(mine, block, -1.0)

    def before(count, axis):
        first = lax.broadcasted_iota(jnp.int32, (count, count), axis)
        return jnp.where(first < lax.broadcasted_iota(jnp.int32, (count, count), 1 - axis), 1.0, 0.0).astype(
            jnp.bfloat16
        )

    lane = lax.broadcasted_iota(jnp.int32, (rows, blocks), 1).astype(jnp.float32)
    picks = [jnp.where(key[:, j : j + 1] == lane, 1.0, 0.0) for j in range(slots)]
    count = jnp.sum(functools.reduce(jnp.add, picks), axis=0, keepdims=True)
    tasks = jnp.floor((count + (PAIR - 1)) * (1.0 / PAIR))
    earlier = jnp.dot(
        jnp.broadcast_to(tasks, (8, blocks)).astype(jnp.bfloat16),
        before(blocks, 0),
        preferred_element_type=jnp.float32,
    )[:1]
    base = earlier * PAIR
    row_before = before(rows, 1)
    slot = lax.broadcasted_iota(jnp.int32, (rows, slots), 1)
    place = jnp.full((rows, slots), -1.0, jnp.float32)
    for j in range(slots):
        above = jnp.dot(row_before, picks[j].astype(jnp.bfloat16), preferred_element_type=jnp.float32)
        here = jnp.sum(picks[j] * (above + base), axis=1, keepdims=True)
        place = jnp.where((slot == j) & mine, here, place)
        base = base + jnp.sum(picks[j], axis=0, keepdims=True)
    place_ref[...] = place
    size = blocks // PHASES
    end = earlier + tasks
    block_lane = lax.broadcasted_iota(jnp.int32, (1, blocks), 1)
    bound_lane = lax.broadcasted_iota(jnp.int32, (1, LANES), 1)
    bounds = jnp.zeros((1, LANES), jnp.float32)
    for part in range(PHASES):
        done = jnp.sum(jnp.where(block_lane == (part + 1) * size - 1, end, 0.0), axis=1, keepdims=True)
        done = done * (1.0 / TASKS)
        done = jnp.ceil(done) if part == PHASES - 1 else jnp.floor(done)
        bounds = jnp.where(bound_lane == part + 1, done, bounds)
    bound_ref[...] = bounds.astype(jnp.int32)
    target = lax.broadcasted_iota(jnp.int32, (8, capacity), 1).astype(jnp.float32)

    def tile(t, total):
        here = pl.ds(pl.multiple_of(t * 8, 8), 8)
        places, values = place_ref[here, :], value_ref[here, :]
        for j in range(slots):
            total = total + jnp.where(places[:, j : j + 1] == target, values[:, j : j + 1], 0.0)
        return total

    total = lax.fori_loop(0, rows // 8, tile, jnp.zeros((8, capacity), jnp.float32))
    list_ref[...] = (jnp.sum(total, axis=0, keepdims=True) + spare).astype(jnp.int32)


def make_list(parts, slots, blocks, block_size, count):
    own, width = parts[0].shape
    rows = count * own
    most = 2 * own * slots // count * count + (PAIR - 1) * blocks + 3 * CHUNK
    capacity = -(-most // LANES) * LANES
    last = width // (PAIR * LANES) - 1
    return pl.pallas_call(
        functools.partial(list_kernel, blocks, block_size, slots),
        grid=(1,),
        in_specs=[pl.BlockSpec((own, PAIR * LANES), lambda i: (0, last))] * len(parts),
        out_specs=[
            pl.BlockSpec((1, capacity), lambda i: (0, 0)),
            pl.BlockSpec((1, LANES), lambda i: (0, 0)),
        ],
        out_shape=[
            jax.ShapeDtypeStruct((1, capacity), jnp.int32),
            jax.ShapeDtypeStruct((1, LANES), jnp.int32),
        ],
        scratch_shapes=[pltpu.VMEM((rows, slots), jnp.float32), pltpu.VMEM((rows, slots), jnp.float32)],
        compiler_params=params(16),
        cost_estimate=pl.CostEstimate(flops=10**8, bytes_accessed=10**7, transcendentals=0),
        name="slot_list",
    )(*parts)


def attend_kernel(scale, group, kv_local, count, list_ref, bound_ref, *refs):
    queries, refs = refs[: count // PAIR], refs[count // PAIR :]
    (key_hbm, value_hbm, out_ref, query_ref, key_ref, value_ref, top_ref, total_ref, sum_ref) = refs[:9]
    (score_ref, part_top_ref, part_total_ref, part_sum_ref, sems) = refs[9:]
    heads = query_ref.shape[1]
    rows = query_ref.shape[0] - 1
    own = rows // count
    blocks, tokens, _ = key_ref.shape
    block_size = tokens // kv_local
    size = blocks // PHASES
    length_bits = (block_size - 1).bit_length()
    block_bits = (blocks - 1).bit_length()
    copies = []
    for part in range(PHASES):
        here = pl.ds(part * size, size)
        pair = (
            pltpu.make_async_copy(key_hbm.at[here], key_ref.at[here], sems.at[0, part]),
            pltpu.make_async_copy(value_hbm.at[here], value_ref.at[here], sems.at[1, part]),
        )
        for copy in pair:
            copy.start()
        copies.append(pair)

    factor = scale * LOG2E
    for s, piece in enumerate(queries):
        for t in range(PAIR):
            start = (PAIR * s + t) * own
            query_ref[start : start + own] = piece[t]
    query_ref[rows] = jnp.zeros((heads, LANES), jnp.bfloat16)
    top_ref[...] = jnp.full(top_ref.shape, NEG_FILL, jnp.float32)
    for ref in (total_ref, sum_ref, score_ref, part_top_ref, part_total_ref, part_sum_ref):
        ref[...] = jnp.zeros(ref.shape, jnp.float32)
    head = lax.broadcasted_iota(jnp.int32, (heads, tokens), 0) // group
    place = lax.broadcasted_iota(jnp.int32, (heads, tokens), 1)
    token = jnp.where(place % kv_local == head, place // kv_local, block_size)
    wide = (heads, LANES)

    def entries(chunk):
        return [list_ref[0, chunk * CHUNK + j] for j in range(CHUNK)]

    def row_of(entry):
        return entry >> (length_bits + block_bits)

    def block_of(entry):
        return (entry >> length_bits) & (blocks - 1)

    def turn(i, carry):
        row = [jnp.where(i >= 2, row_of(e), rows) for e in entries(jnp.maximum(i - 2, 0))]
        shares = []
        for j in range(CHUNK):
            top, part_top = top_ref[row[j]], part_top_ref[j]
            high = jnp.maximum(top, part_top)
            top_ref[row[j]] = high
            shares.append((jnp.exp2((top - high) * factor), jnp.exp2((part_top - high) * factor)))
        for j, (old, new) in enumerate(shares):
            t, k = divmod(j, PAIR)
            total_ref[row[j]] = total_ref[row[j]] * old + part_total_ref[j] * new
            sum_ref[row[j]] = sum_ref[row[j]] * old + part_sum_ref[t, k * heads : (k + 1) * heads] * new

        items = entries(jnp.maximum(i - 1, 0))
        for t in range(TASKS):
            pieces = []
            for k in range(PAIR):
                j = t * PAIR + k
                length = items[j] & (block_size - 1)
                scores = jnp.where(token <= length, score_ref[t, k * heads : (k + 1) * heads], NEG_FILL)
                high = jnp.max(scores, axis=1, keepdims=True)
                weights = jnp.exp2((scores - high) * factor)
                part_top_ref[j] = jnp.broadcast_to(high, wide)
                part_total_ref[j] = jnp.broadcast_to(jnp.sum(weights, axis=1, keepdims=True), wide)
                pieces.append(weights.astype(jnp.bfloat16))
            part_sum_ref[t] = jnp.dot(
                jnp.concatenate(pieces, axis=0),
                value_ref[block_of(items[t * PAIR])],
                preferred_element_type=jnp.float32,
            )

        items = entries(i)
        for t in range(TASKS):
            task = items[t * PAIR : (t + 1) * PAIR]
            score_ref[t] = lax.dot_general(
                jnp.concatenate([query_ref[row_of(e)] for e in task], axis=0),
                key_ref[block_of(task[0])],
                (((1,), (1,)), ((), ())),
                preferred_element_type=jnp.float32,
            )
        return carry

    for part in range(PHASES):
        for copy in copies[part]:
            copy.wait()
        lax.fori_loop(bound_ref[0, part], bound_ref[0, part + 1], turn, 0)
    last = bound_ref[0, PHASES]
    lax.fori_loop(last, last + 2, turn, 0)

    me = lax.axis_index("kv")
    square = (own * heads, LANES)
    eye = lax.broadcasted_iota(jnp.int32, square, 0) == lax.broadcasted_iota(jnp.int32, square, 1)
    line = lax.broadcasted_iota(jnp.int32, wide, 0)
    for c in range(count):
        stats = jnp.zeros(wide, jnp.float32)
        position = 0
        for ref in (top_ref, total_ref):
            flat = jnp.sum(
                jnp.where(eye, ref[c * own : (c + 1) * own].reshape(square), 0.0), axis=0, keepdims=True
            )
            for piece in split3(flat):
                stats = jnp.where(line == position, piece, stats)
                position += 1
        owner = jnp.bitwise_xor(me, c)
        for r in range(own):
            out_ref[owner, r] = sum_ref[c * own + r].astype(jnp.bfloat16)
        out_ref[owner, own] = stats.astype(jnp.bfloat16)


def attend(items, bounds, queries, keys, values, kv_local, scale):
    _, own, heads, _ = queries[0].shape
    count = len(queries) * PAIR
    rows = count * own
    tokens = keys.shape[1]
    keys, values = in_hbm(keys, values)
    state = pltpu.VMEM((rows + 1, heads, LANES), jnp.float32)
    part = pltpu.VMEM((CHUNK, heads, LANES), jnp.float32)
    return pl.pallas_call(
        functools.partial(attend_kernel, scale, heads // kv_local, kv_local, count),
        in_specs=[smem_spec(), smem_spec()] + [vmem_spec()] * len(queries) + [hbm_spec()] * 2,
        out_specs=vmem_spec(),
        out_shape=jax.ShapeDtypeStruct((count, own + 1, heads, LANES), jnp.bfloat16),
        scratch_shapes=[
            pltpu.VMEM((rows + 1, heads, LANES), jnp.bfloat16),
            pltpu.VMEM(keys.shape, keys.dtype),
            pltpu.VMEM(values.shape, values.dtype),
            state,
            state,
            state,
            pltpu.VMEM((TASKS, PAIR * heads, tokens), jnp.float32),
            part,
            part,
            pltpu.VMEM((TASKS, PAIR * heads, LANES), jnp.float32),
            pltpu.SemaphoreType.DMA((2, PHASES)),
        ],
        compiler_params=params(40),
        name="attend",
    )(items, bounds, *queries, keys, values)


def merge_kernel(scale, parts_ref, out_ref, wide_ref):
    count, sections, heads, _ = parts_ref.shape
    own = sections - 1
    factor = scale * LOG2E
    stats = [parts_ref[s, own].astype(jnp.float32) for s in range(count)]
    tops = jnp.concatenate([s[0:1] + s[1:2] + s[2:3] for s in stats], axis=0)
    totals = jnp.concatenate([s[3:4] + s[4:5] + s[5:6] for s in stats], axis=0)
    weights = jnp.exp2((tops - jnp.max(tops, axis=0, keepdims=True)) * factor)
    weights = weights / jnp.sum(weights * totals, axis=0, keepdims=True)
    columns = weights.T
    acc = jnp.zeros((own * heads, LANES), jnp.float32)
    for s in range(count):
        part = parts_ref[s, :own].astype(jnp.float32).reshape(own * heads, LANES)
        acc = acc + part * columns[:, s : s + 1]
    wide_ref[...] = acc
    pieces = [wide_ref[pl.ds(h, own, stride=heads), :] for h in range(heads)]
    out_ref[...] = jnp.concatenate(pieces, axis=1).astype(jnp.bfloat16)


def merge(parts, scale):
    count, sections, heads, _ = parts.shape
    own = sections - 1
    return pl.pallas_call(
        functools.partial(merge_kernel, scale),
        in_specs=[vmem_spec()],
        out_specs=vmem_spec(),
        out_shape=jax.ShapeDtypeStruct((own, heads * LANES), jnp.bfloat16),
        scratch_shapes=[pltpu.VMEM((own * heads, LANES), jnp.float32)],
        compiler_params=params(16),
        name="merge",
    )(parts)


def output_kernel(chips, row_count, *refs):
    pieces, weight_ref = refs[:chips], refs[chips]
    own_ref, sends = refs[chips + 1], refs[chips + 2 : chips + 1 + row_count]
    rows_ref, terms_ref = refs[chips + 1 + row_count :]
    own = pieces[0].shape[0] // PAIR
    me = lax.axis_index("kv")
    for s in range(chips):
        piece = pieces[s][...].astype(jnp.float32)
        for t in range(PAIR):
            start = pl.multiple_of(jnp.bitwise_xor(me, PAIR * s + t) * own, own)
            rows_ref[pl.ds(start, own), :] = piece[t * own : (t + 1) * own]
    terms_ref[...] = jnp.dot(
        rows_ref[...].astype(jnp.bfloat16), weight_ref[...], preferred_element_type=jnp.float32
    )
    me = lax.axis_index("row")
    part = own_ref.shape[0]
    for s, ref in enumerate((own_ref, *sends)):
        start = pl.multiple_of(jnp.bitwise_xor(me, s) * part, part)
        ref[...] = terms_ref[pl.ds(start, part), :].astype(ref.dtype)


def project_out(pieces, weight, row_count):
    chips = len(pieces)
    pair_rows, width = pieces[0].shape
    rows, columns = chips * pair_rows, weight.shape[1]
    part = rows // row_count
    send = jax.ShapeDtypeStruct((part, columns), jnp.bfloat16)
    return pl.pallas_call(
        functools.partial(output_kernel, chips, row_count),
        in_specs=[vmem_spec()] * (chips + 1),
        out_specs=[vmem_spec()] * row_count,
        out_shape=[jax.ShapeDtypeStruct((part, columns), jnp.float32)] + [send] * (row_count - 1),
        scratch_shapes=[pltpu.VMEM((rows, width), jnp.float32), pltpu.VMEM((rows, columns), jnp.float32)],
        compiler_params=params(24),
        name="project_out",
    )(*pieces, weight)


def swap(x, axis):
    return lax.all_to_all(x, axis, split_axis=0, concat_axis=0, tiled=True)


def exchange(x, axis, s):
    count = lax.axis_size(axis)
    return lax.ppermute(x, axis, [(i, i ^ s) for i in range(count)])


def gather_pairs(x):
    pair = jnp.concatenate([x, exchange(x, "kv", 1)], axis=0)
    return [pair] + [exchange(pair, "kv", s) for s in range(PAIR, lax.axis_size("kv"), PAIR)]


def local(
    hidden,
    query_weight,
    adapter_down_weight,
    adapter_up_weight,
    query_norm_gain,
    paged_key_cache,
    paged_value_cache,
    output_weight,
    holder,
    holder_block_index,
    block_used_length,
    tenant,
    tenant_adapter,
):
    own, slots = holder.shape
    rows, depth = hidden.shape
    kv_count = lax.axis_size("kv")
    row_count = lax.axis_size("row")
    adapters, _, rank = adapter_down_weight.shape
    width = query_weight.shape[1]
    head_size = query_norm_gain.shape[0]
    heads = width // head_size
    blocks, block_size, kv_local, _ = paged_key_cache.shape
    scale = 1.0 / math.sqrt(head_size)

    chips = kv_count // PAIR
    keep, send = project(
        tenant.reshape(1, rows),
        tenant_adapter.reshape(1, -1),
        holder,
        holder_block_index,
        block_used_length,
        hidden,
        query_weight,
        jnp.swapaxes(adapter_down_weight, 1, 2).reshape(adapters * rank, depth),
        adapter_up_weight.reshape(adapters * rank, width),
        rank,
        chips,
    )
    parts = add_pair(keep, exchange(send, "kv", 1))
    parts = [parts[0]] + [exchange(parts[s], "kv", PAIR * s) for s in range(1, chips)]

    position = (jnp.sum(block_used_length, axis=1) - 1).astype(jnp.float32)
    half = head_size // 2
    frequency = ROPE_BASE ** (-(jnp.arange(half, dtype=jnp.float32) * 2.0) / head_size)
    angles = position[:, None] * frequency[None, :]
    cosine = jnp.concatenate([jnp.cos(angles), jnp.cos(angles)], axis=-1)
    sine = jnp.concatenate([-jnp.sin(angles), jnp.sin(angles)], axis=-1)
    queries = make_queries(parts, cosine, sine, query_norm_gain.reshape(1, head_size), heads)
    queries = [q.reshape(PAIR, own, heads, head_size) for q in gather_pairs(queries)]
    items, bounds = make_list(parts, slots, blocks, block_size, kv_count)

    keys = paged_key_cache.reshape(blocks, block_size * kv_local, head_size)
    values = paged_value_cache.reshape(blocks, block_size * kv_local, head_size)
    partial_out = attend(items, bounds, queries, keys, values, kv_local, scale)
    attention = merge(swap(partial_out, "kv"), scale)
    terms = project_out(gather_pairs(attention), output_weight, row_count)
    total = terms[0]
    for s in range(1, row_count):
        total = total + exchange(terms[s], "row", s).astype(jnp.float32)
    return total.astype(jnp.bfloat16)


def solution(mesh):
    return jax.shard_map(
        local,
        mesh=mesh,
        in_specs=(
            P(None, "kv"),
            P("kv", "row"),
            P(None, "kv", None),
            P(None, None, "row"),
            P(),
            P("kv", None, "row", None),
            P("kv", None, "row", None),
            P("row", "kv"),
            P("kv", None),
            P("kv", None),
            P("kv", None),
            P(),
            P(),
        ),
        out_specs=P("row", "kv"),
        check_vma=False,
    )
```

time: 88 us -> 73.3 us (0.83)
  waiting for transfers between devices: 21.6 us -> 15.6 us
  Pallas kernels: 37.2 us -> 31.6 us
  starting transfers between devices: 19.2 us -> 16.6 us
    all_to_all x2 -> x0, waiting for transfers between devices: 14.9 us -> none  [swap(): return lax.all_to_all(x, axis, split_axis=0, concat_axis=0, tiled=True)]
    ppermute x10 -> x15, waiting for transfers between devices: 6.73 us -> 15.6 us  [exchange(): return lax.ppermute(x, axis, [(i, i ^ s) for i in range(count)])]
    all_to_all x2 -> x0, starting transfers between devices: 8.58 us -> none  [swap(): return lax.all_to_all(x, axis, split_axis=0, concat_axis=0, tiled=True)]
    ppermute x10 -> x15, starting transfers between devices: 10.6 us -> 16.6 us  [exchange(): return lax.ppermute(x, axis, [(i, i ^ s) for i in range(count)])]
    pallas_call x1, Pallas kernels: 25.6 us -> 19.9 us  [attend(): pl.pallas_call(functools.partial(attend_kernel, scale, heads // kv_local,...]
    pallas_call x3 -> x4, Pallas kernels: 9.4 us -> 8.88 us  [the longest x1 7.94 us: project(): pl.pallas_call(functools.partial(project_kernel, rank), in_specs=[vmem_sp...]
  transfers between devices with their start and end apart: 12 -> 15, of which waited for: 7 -> 12; matrix products, arithmetic and copies ran while one was open for 0% -> 0% of each run, Pallas kernels for 2% -> 3%
where the time goes in v3:
time: 73.3 us; the launch traced here: 74.6 us
  Pallas kernels  31.6 us (43%)
  starting transfers between devices  16.6 us (23%)
  waiting for transfers between devices  15.6 us (21%)
  blocking collectives  9.66 us (13%)
  other arithmetic  0.96 us (1%)
    pallas_call x1, Pallas kernels, attend(): pl.pallas_call(functools.partial(attend_kernel, scale, heads // kv_local,...  19.9 us
    ppermute x15, starting transfers between devices, exchange(): return lax.ppermute(x, axis, [(i, i ^ s) for i in range(count)])  16.6 us
    ppermute x15, waiting for transfers between devices, exchange(): return lax.ppermute(x, axis, [(i, i ^ s) for i in range(count)])  15.6 us
    all_to_all x1, blocking collectives, swap(): return lax.all_to_all(x, axis, split_axis=0, concat_axis=0, tiled=True)  9.66 us
    pallas_call x1, Pallas kernels, project(): pl.pallas_call(functools.partial(project_kernel, rank), in_specs=[vmem_sp...  7.94 us
    pallas_call x1, Pallas kernels, make_list(): pl.pallas_call(functools.partial(list_kernel, blocks, block_size, slots),...  2.42 us
  transfers between devices with their start and end apart: 15, of which 12 were waited for; matrix products, arithmetic and copies ran while one was open for 0% of the time, Pallas kernels for 3%

profile of v3, /device:TPU:0, one launch (start us, length us, event | category | flops | bytes accessed | tf_op | source)
XLA Modules:
  0.0 74.6 jit_solution(4485333535372042476)
XLA Ops:
  0.0 7.9 %project.1 = (f32[4,8,2176]{2,1,0:T(8,128)S(1)}, f32[4,8,2176]{2,1,0:T(8,128)S(1)}) custom-call(s32[1,64]{1,0:T(1,128)} %bitcast.22, s32[1,64]{1,0:T(1,128)} %bitcast.23, s32[8,32]{1,0:T(8,128)} %holder_ref.1, s32[8,32]{1,0:T(8,128)} %block_ref.1, s32[8,32]{1,0:T(8,128)} %length_ref.1, bf16[64,640]{1,0:T(8,128)(2,1)} %hidden_hbm.1, ...), custom_call_target="tpu_custom_call" | custom-call | tf_op jit(solution)/shard_map/project/pallas_call | solution.py:144
  8.0 0.5 collective-permute-start
  8.5 0.1 reduce_sum.9
  8.7 0.9 %collective-permute-done.got_ref = f32[4,8,2176]{2,1,0:T(8,128)S(1)} collective-permute-done((f32[4,8,2176]{2,1,0:T(8,128)S(1)}, f32[4,8,2176]{2,1,0:T(8,128)S(1)}, u32[]{:S(2)}, u32[]{:S(2)}) %collective-permute-start) | collective-permute-done | bytes 278560 | tf_op jit(solution)/shard_map/ppermute | solution.py:517
  9.7 2.9 %collective-permute-start.1 = (f32[8,2304]{1,0:T(8,128)S(1)}, f32[8,2304]{1,0:T(8,128)S(1)}, u32[]{:S(2)}, u32[]{:S(2)}) collective-permute-start(f32[8,2304]{1,0:T(8,128)S(1)} %get-tuple-element.20), channel_id=1, source_target_pairs={{0,2},{1,3},{2,0},{3,1},{4,6},{5,7},{6,4},{7,5},{8,10},{9,11},{10,... | collective-permute-start | bytes 221192 | tf_op jit(solution)/shard_map/ppermute | solution.py:517
  12.6 1.5 %collective-permute-start.2 = (f32[8,2304]{1,0:T(8,128)S(1)}, f32[8,2304]{1,0:T(8,128)S(1)}, u32[]{:S(2)}, u32[]{:S(2)}) collective-permute-start(f32[8,2304]{1,0:T(8,128)S(1)} %get-tuple-element.21), channel_id=1, source_target_pairs={{0,4},{1,5},{2,6},{3,7},{4,0},{5,1},{6,2},{7,3},{8,12},{9,13},{10,... | collective-permute-start | bytes 221192 | tf_op jit(solution)/shard_map/ppermute | solution.py:517
  14.2 1.0 %collective-permute-done.1.refs_1_ = f32[8,2304]{1,0:T(8,128)S(1)} collective-permute-done((f32[8,2304]{1,0:T(8,128)S(1)}, f32[8,2304]{1,0:T(8,128)S(1)}, u32[]{:S(2)}, u32[]{:S(2)}) %collective-permute-start.1) | collective-permute-done | bytes 73760 | tf_op jit(solution)/shard_map/ppermute | solution.py:517
  15.2 1.8 %collective-permute-done.2.refs_2_ = f32[8,2304]{1,0:T(8,128)S(1)} collective-permute-done((f32[8,2304]{1,0:T(8,128)S(1)}, f32[8,2304]{1,0:T(8,128)S(1)}, u32[]{:S(2)}, u32[]{:S(2)}) %collective-permute-start.2) | collective-permute-done | bytes 73760 | tf_op jit(solution)/shard_map/ppermute | solution.py:517
  17.0 2.4 %collective-permute-done.3.refs_3_ = f32[8,2304]{1,0:T(8,128)S(1)} collective-permute-done((f32[8,2304]{1,0:T(8,128)S(1)}, f32[8,2304]{1,0:T(8,128)S(1)}, u32[]{:S(2)}, u32[]{:S(2)}) %collective-permute-start.3) | collective-permute-done | bytes 73760 | tf_op jit(solution)/shard_map/ppermute | solution.py:517
  19.4 0.3 queries.1
  19.8 1.2 %collective-permute-done.4 = bf16[8,16,128]{2,1,0:T(8,128)(2,1)S(1)} collective-permute-done((bf16[8,16,128]{2,1,0:T(8,128)(2,1)S(1)}, bf16[8,16,128]{2,1,0:T(8,128)(2,1)S(1)}, u32[]{:S(2)}, u32[]{:S(2)}) %collective-permute-start.4) | collective-permute-done | bytes 32800 | tf_op jit(solution)/shard_map/ppermute | solution.py:517
  21.0 0.6 collective-permute-start.5
  21.6 0.6 collective-permute-start.6
  22.1 2.4 %collective-permute-start.7 = (bf16[16,16,128]{2,1,0:T(8,128)(2,1)S(1)}, bf16[16,16,128]{2,1,0:T(8,128)(2,1)S(1)}, u32[]{:S(2)}, u32[]{:S(2)}) collective-permute-start(bf16[16,16,128]{2,1,0:T(8,128)(2,1)S(1)} %pad_maximum_fusion), channel_id=1, source_target_pairs={{0,6},{1,7},{2,4},{3,5},{4,2},{5,3},{6,0},{7,1},{8,14},{9,15},{10,... | collective-permute-start | bytes 196616 | tf_op jit(solution)/shard_map/ppermute | solution.py:517
  24.5 2.4 %slot_list.1 = (s32[1,768]{1,0:T(1,128)S(1)}, s32[1,128]{1,0:T(1,128)S(1)}) custom-call(f32[8,2304]{1,0:T(8,128)S(1)} %get-tuple-element.19.refs_0_, f32[8,2304]{1,0:T(8,128)S(1)} %collective-permute-done.1.refs_1_, f32[8,2304]{1,0:T(8,128)S(1)} %collective-permute-done.2.refs_2_, f32[8,2304]{1,0:T(8,128)S(1)} %collective-permute-done.3.refs_3_), custom_call_target="tpu_custom_call" | custom-call | flops 100000000 | bytes 10000000 | tf_op jit(solution)/shard_map/slot_list/pallas_call | solution.py:275
  27.0 0.3 collective-permute-done.7
  27.3 19.9 %attend.1 = bf16[8,9,16,128]{3,2,1,0:T(8,128)(2,1)S(1)} custom-call(s32[1,768]{1,0:T(1,128)S(1)} %get-tuple-element.23.list_ref, s32[1,128]{1,0:T(1,128)S(1)} %get-tuple-element.24.bound_ref, bf16[2,8,16,128]{3,2,1,0:T(8,128)(2,1)S(1)} %bitcast.13, bf16[2,8,16,128]{3,2,1,0:T(8,128)(2,1)S(1)} %bitcast.14, bf16[2,8,16,128]{3,2,1,0:T(8,128)(2,1)S(1)} %bitcast.15, ...), custom_call_target="tpu_custom_call" | custom-call | tf_op jit(solution)/shard_map/attend/pallas_call | solution.py:417
  47.2 9.7 %all_to_all.5.parts_ref = bf16[8,9,16,128]{3,2,1,0:T(8,128)(2,1)S(1)} all-to-all(bf16[8,9,16,128]{3,2,1,0:T(8,128)(2,1)S(1)} %attend.1), channel_id=1, replica_groups=mesh['row'=4,'kv'=8] {'kv'}, dimensions={0} | all-to-all | bytes 589824 | tf_op jit(solution)/shard_map/all_to_all | solution.py:512
  56.9 0.4 merge.1
  57.4 1.2 %collective-permute-done.8 = bf16[8,2048]{1,0:T(8,128)(2,1)S(1)} collective-permute-done((bf16[8,2048]{1,0:T(8,128)(2,1)S(1)}, bf16[8,2048]{1,0:T(8,128)(2,1)S(1)}, u32[]{:S(2)}, u32[]{:S(2)}) %collective-permute-start.8) | collective-permute-done | bytes 32800 | tf_op jit(solution)/shard_map/ppermute | solution.py:517
  58.6 0.6 collective-permute-start.9
  59.1 0.6 collective-permute-start.10
  59.7 2.4 %collective-permute-start.11 = (bf16[16,2048]{1,0:T(8,128)(2,1)S(1)}, bf16[16,2048]{1,0:T(8,128)(2,1)S(1)}, u32[]{:S(2)}, u32[]{:S(2)}) collective-permute-start(bf16[16,2048]{1,0:T(8,128)(2,1)S(1)} %pad_maximum_fusion.1.refs_0_), channel_id=1, source_target_pairs={{0,6},{1,7},{2,4},{3,5},{4,2},{5,3},{6,0},{7,1},{8,14},{9,15},{10,... | collective-permute-start | bytes 196616 | tf_op jit(solution)/shard_map/ppermute | solution.py:517
  62.0 0.9 %collective-permute-done.9.refs_1_ = bf16[16,2048]{1,0:T(8,128)(2,1)S(1)} collective-permute-done((bf16[16,2048]{1,0:T(8,128)(2,1)S(1)}, bf16[16,2048]{1,0:T(8,128)(2,1)S(1)}, u32[]{:S(2)}, u32[]{:S(2)}) %collective-permute-start.9) | collective-permute-done | bytes 65568 | tf_op jit(solution)/shard_map/ppermute | solution.py:517
  62.9 1.2 %collective-permute-done.10.refs_2_ = bf16[16,2048]{1,0:T(8,128)(2,1)S(1)} collective-permute-done((bf16[16,2048]{1,0:T(8,128)(2,1)S(1)}, bf16[16,2048]{1,0:T(8,128)(2,1)S(1)}, u32[]{:S(2)}, u32[]{:S(2)}) %collective-permute-start.10) | collective-permute-done | bytes 65568 | tf_op jit(solution)/shard_map/ppermute | solution.py:517
  64.1 0.8 %collective-permute-done.11.refs_3_ = bf16[16,2048]{1,0:T(8,128)(2,1)S(1)} collective-permute-done((bf16[16,2048]{1,0:T(8,128)(2,1)S(1)}, bf16[16,2048]{1,0:T(8,128)(2,1)S(1)}, u32[]{:S(2)}, u32[]{:S(2)}) %collective-permute-start.11) | collective-permute-done | bytes 65568 | tf_op jit(solution)/shard_map/ppermute | solution.py:517
  64.8 0.6 project_out.1
  65.5 3.8 %collective-permute-start.14 = (bf16[16,640]{1,0:T(8,128)(2,1)S(1)}, bf16[16,640]{1,0:T(8,128)(2,1)S(1)}, u32[]{:S(2)}, u32[]{:S(2)}) collective-permute-start(bf16[16,640]{1,0:T(8,128)(2,1)S(1)} %get-tuple-element.28), channel_id=1, source_target_pairs={{0,24},{8,16},{16,8},{24,0},{1,25},{9,17},{17,9},{25,1},{2,26},{10... | collective-permute-start | bytes 61448 | tf_op jit(solution)/shard_map/ppermute | solution.py:517
  69.3 0.7 collective-permute-start.12
  69.9 1.2 %collective-permute-done.14 = bf16[16,640]{1,0:T(8,128)(2,1)S(1)} collective-permute-done((bf16[16,640]{1,0:T(8,128)(2,1)S(1)}, bf16[16,640]{1,0:T(8,128)(2,1)S(1)}, u32[]{:S(2)}, u32[]{:S(2)}) %collective-permute-start.14) | collective-permute-done | bytes 20512 | tf_op jit(solution)/shard_map/ppermute | solution.py:517
  71.1 2.8 %collective-permute-done.13 = bf16[16,640]{1,0:T(8,128)(2,1)S(1)} collective-permute-done((bf16[16,640]{1,0:T(8,128)(2,1)S(1)}, bf16[16,640]{1,0:T(8,128)(2,1)S(1)}, u32[]{:S(2)}, u32[]{:S(2)}) %collective-permute-start.13) | collective-permute-done | bytes 20512 | tf_op jit(solution)/shard_map/ppermute | solution.py:517
  73.9 0.6 add_convert_fusion
  (20 shorter events, 0.4 us)
Async XLA Ops:
  0.0 8.5 %copy-start.2 = (s32[8,32]{1,0:T(8,128)S(1)}, s32[8,32]{1,0:T(8,128)}, u32[]{:S(2)}) copy-start(s32[8,32]{1,0:T(8,128)} %length_ref.1) | copy-start | bytes 3076
  0.0 19.4 %copy-start.1 = (f32[128]{0:T(128)S(1)}, f32[128]{0:T(128)}, u32[]{:S(2)}) copy-start(f32[128]{0:T(128)} %param.17) | copy-start | bytes 1540
  8.0 1.7 %collective-permute-start = (f32[4,8,2176]{2,1,0:T(8,128)S(1)}, f32[4,8,2176]{2,1,0:T(8,128)S(1)}, u32[]{:S(2)}, u32[]{:S(2)}) collective-permute-start(f32[4,8,2176]{2,1,0:T(8,128)S(1)} %get-tuple-element.18), channel_id=1, source_target_pairs={{0,1},{1,0},{2,3},{3,2},{4,5},{5,4},{6,7},{7,6},{8,9},{9,8},{10,11... | collective-permute-start | bytes 835592 | tf_op jit(solution)/shard_map/ppermute | solution.py:517
  9.7 5.5 %collective-permute-start.1 = (f32[8,2304]{1,0:T(8,128)S(1)}, f32[8,2304]{1,0:T(8,128)S(1)}, u32[]{:S(2)}, u32[]{:S(2)}) collective-permute-start(f32[8,2304]{1,0:T(8,128)S(1)} %get-tuple-element.20), channel_id=1, source_target_pairs={{0,2},{1,3},{2,0},{3,1},{4,6},{5,7},{6,4},{7,5},{8,10},{9,11},{10,... | collective-permute-start | bytes 221192 | tf_op jit(solution)/shard_map/ppermute | solution.py:517
  12.6 4.4 %collective-permute-start.2 = (f32[8,2304]{1,0:T(8,128)S(1)}, f32[8,2304]{1,0:T(8,128)S(1)}, u32[]{:S(2)}, u32[]{:S(2)}) collective-permute-start(f32[8,2304]{1,0:T(8,128)S(1)} %get-tuple-element.21), channel_id=1, source_target_pairs={{0,4},{1,5},{2,6},{3,7},{4,0},{5,1},{6,2},{7,3},{8,12},{9,13},{10,... | collective-permute-start | bytes 221192 | tf_op jit(solution)/shard_map/ppermute | solution.py:517
  14.1 5.3 %collective-permute-start.3 = (f32[8,2304]{1,0:T(8,128)S(1)}, f32[8,2304]{1,0:T(8,128)S(1)}, u32[]{:S(2)}, u32[]{:S(2)}) collective-permute-start(f32[8,2304]{1,0:T(8,128)S(1)} %get-tuple-element.22), channel_id=1, source_target_pairs={{0,6},{1,7},{2,4},{3,5},{4,2},{5,3},{6,0},{7,1},{8,14},{9,15},{10,... | collective-permute-start | bytes 221192 | tf_op jit(solution)/shard_map/ppermute | solution.py:517
  19.7 1.3 %collective-permute-start.4 = (bf16[8,16,128]{2,1,0:T(8,128)(2,1)S(1)}, bf16[8,16,128]{2,1,0:T(8,128)(2,1)S(1)}, u32[]{:S(2)}, u32[]{:S(2)}) collective-permute-start(bf16[8,16,128]{2,1,0:T(8,128)(2,1)S(1)} %queries.1), channel_id=1, source_target_pairs={{0,1},{1,0},{2,3},{3,2},{4,5},{5,4},{6,7},{7,6},{8,9},{9,8},{10,11... | collective-permute-start | bytes 98312 | tf_op jit(solution)/shard_map/ppermute | solution.py:517
  21.0 6.0 %collective-permute-start.5 = (bf16[16,16,128]{2,1,0:T(8,128)(2,1)S(1)}, bf16[16,16,128]{2,1,0:T(8,128)(2,1)S(1)}, u32[]{:S(2)}, u32[]{:S(2)}) collective-permute-start(bf16[16,16,128]{2,1,0:T(8,128)(2,1)S(1)} %pad_maximum_fusion), channel_id=1, source_target_pairs={{0,2},{1,3},{2,0},{3,1},{4,6},{5,7},{6,4},{7,5},{8,10},{9,11},{10,... | collective-permute-start | bytes 196616 | tf_op jit(solution)/shard_map/ppermute | solution.py:517
  21.6 5.4 %collective-permute-start.6 = (bf16[16,16,128]{2,1,0:T(8,128)(2,1)S(1)}, bf16[16,16,128]{2,1,0:T(8,128)(2,1)S(1)}, u32[]{:S(2)}, u32[]{:S(2)}) collective-permute-start(bf16[16,16,128]{2,1,0:T(8,128)(2,1)S(1)} %pad_maximum_fusion), channel_id=1, source_target_pairs={{0,4},{1,5},{2,6},{3,7},{4,0},{5,1},{6,2},{7,3},{8,12},{9,13},{10,... | collective-permute-start | bytes 196616 | tf_op jit(solution)/shard_map/ppermute | solution.py:517
  22.1 5.2 %collective-permute-start.7 = (bf16[16,16,128]{2,1,0:T(8,128)(2,1)S(1)}, bf16[16,16,128]{2,1,0:T(8,128)(2,1)S(1)}, u32[]{:S(2)}, u32[]{:S(2)}) collective-permute-start(bf16[16,16,128]{2,1,0:T(8,128)(2,1)S(1)} %pad_maximum_fusion), channel_id=1, source_target_pairs={{0,6},{1,7},{2,4},{3,5},{4,2},{5,3},{6,0},{7,1},{8,14},{9,15},{10,... | collective-permute-start | bytes 196616 | tf_op jit(solution)/shard_map/ppermute | solution.py:517
  27.3 37.5 %copy-start = (bf16[2048,640]{1,0:T(8,128)(2,1)S(1)}, bf16[2048,640]{1,0:T(8,128)(2,1)}, u32[]{:S(2)}) copy-start(bf16[2048,640]{1,0:T(8,128)(2,1)} %refs_4_.1) | copy-start | bytes 7864324
  57.3 1.3 %collective-permute-start.8 = (bf16[8,2048]{1,0:T(8,128)(2,1)S(1)}, bf16[8,2048]{1,0:T(8,128)(2,1)S(1)}, u32[]{:S(2)}, u32[]{:S(2)}) collective-permute-start(bf16[8,2048]{1,0:T(8,128)(2,1)S(1)} %merge.1), channel_id=1, source_target_pairs={{0,1},{1,0},{2,3},{3,2},{4,5},{5,4},{6,7},{7,6},{8,9},{9,8},{10,11... | collective-permute-start | bytes 98312 | tf_op jit(solution)/shard_map/ppermute | solution.py:517
  58.6 4.4 %collective-permute-start.9 = (bf16[16,2048]{1,0:T(8,128)(2,1)S(1)}, bf16[16,2048]{1,0:T(8,128)(2,1)S(1)}, u32[]{:S(2)}, u32[]{:S(2)}) collective-permute-start(bf16[16,2048]{1,0:T(8,128)(2,1)S(1)} %pad_maximum_fusion.1.refs_0_), channel_id=1, source_target_pairs={{0,2},{1,3},{2,0},{3,1},{4,6},{5,7},{6,4},{7,5},{8,10},{9,11},{10,... | collective-permute-start | bytes 196616 | tf_op jit(solution)/shard_map/ppermute | solution.py:517
  59.1 5.0 %collective-permute-start.10 = (bf16[16,2048]{1,0:T(8,128)(2,1)S(1)}, bf16[16,2048]{1,0:T(8,128)(2,1)S(1)}, u32[]{:S(2)}, u32[]{:S(2)}) collective-permute-start(bf16[16,2048]{1,0:T(8,128)(2,1)S(1)} %pad_maximum_fusion.1.refs_0_), channel_id=1, source_target_pairs={{0,4},{1,5},{2,6},{3,7},{4,0},{5,1},{6,2},{7,3},{8,12},{9,13},{10,... | collective-permute-start | bytes 196616 | tf_op jit(solution)/shard_map/ppermute | solution.py:517
  59.7 5.2 %collective-permute-start.11 = (bf16[16,2048]{1,0:T(8,128)(2,1)S(1)}, bf16[16,2048]{1,0:T(8,128)(2,1)S(1)}, u32[]{:S(2)}, u32[]{:S(2)}) collective-permute-start(bf16[16,2048]{1,0:T(8,128)(2,1)S(1)} %pad_maximum_fusion.1.refs_0_), channel_id=1, source_target_pairs={{0,6},{1,7},{2,4},{3,5},{4,2},{5,3},{6,0},{7,1},{8,14},{9,15},{10,... | collective-permute-start | bytes 196616 | tf_op jit(solution)/shard_map/ppermute | solution.py:517
  65.5 5.7 %collective-permute-start.14 = (bf16[16,640]{1,0:T(8,128)(2,1)S(1)}, bf16[16,640]{1,0:T(8,128)(2,1)S(1)}, u32[]{:S(2)}, u32[]{:S(2)}) collective-permute-start(bf16[16,640]{1,0:T(8,128)(2,1)S(1)} %get-tuple-element.28), channel_id=1, source_target_pairs={{0,24},{8,16},{16,8},{24,0},{1,25},{9,17},{17,9},{25,1},{2,26},{10... | collective-permute-start | bytes 61448 | tf_op jit(solution)/shard_map/ppermute | solution.py:517
  69.3 4.7 %collective-permute-start.13 = (bf16[16,640]{1,0:T(8,128)(2,1)S(1)}, bf16[16,640]{1,0:T(8,128)(2,1)S(1)}, u32[]{:S(2)}, u32[]{:S(2)}) collective-permute-start(bf16[16,640]{1,0:T(8,128)(2,1)S(1)} %get-tuple-element.27), channel_id=1, source_target_pairs={{0,16},{8,24},{16,0},{24,8},{1,17},{9,25},{17,1},{25,9},{2,18},{10... | collective-permute-start | bytes 61448 | tf_op jit(solution)/shard_map/ppermute | solution.py:517
  69.3 4.7 %collective-permute-start.12 = (bf16[16,640]{1,0:T(8,128)(2,1)S(1)}, bf16[16,640]{1,0:T(8,128)(2,1)S(1)}, u32[]{:S(2)}, u32[]{:S(2)}) collective-permute-start(bf16[16,640]{1,0:T(8,128)(2,1)S(1)} %get-tuple-element.26), channel_id=1, source_target_pairs={{0,8},{8,0},{16,24},{24,16},{1,9},{9,1},{17,25},{25,17},{2,10},{10... | collective-permute-start | bytes 61448 | tf_op jit(solution)/shard_map/ppermute | solution.py:517

commit v4 on v3

--- a/solution.py
+++ b/solution.py
@@ -15,9 +15,11 @@
 LANES = 128
 COLUMN_TILE = 256
 PAIR = 2
-TASKS = 8
+TASKS = 16
 CHUNK = PAIR * TASKS
 PHASES = 8
+AHEAD = 3
+DEPTH = 256
 LOG2E = math.log2(math.e)
 MIB = 1024 * 1024
 
@@ -77,29 +79,37 @@
     weight_ref,
     down_ref,
     up_ref,
+    total_ref,
     sems,
-    tile_sems,
 ):
     chips, own, _ = keep_ref.shape
-    rows = hidden_ref.shape[0]
+    rows, depth = hidden_ref.shape
+    low_width = down_ref.shape[0]
     width = weight_ref.shape[1]
     tiles = width // COLUMN_TILE
-    first = [
-        pltpu.make_async_copy(hidden_hbm, hidden_ref, sems.at[0]),
-        pltpu.make_async_copy(down_hbm, down_ref, sems.at[1]),
-    ]
-    for copy in first:
-        copy.start()
-    copies = []
-    for i in range(tiles):
-        columns = pl.ds(i * COLUMN_TILE, COLUMN_TILE)
-        pair = (
-            pltpu.make_async_copy(weight_hbm.at[:, columns], weight_ref.at[:, columns], tile_sems.at[0, i]),
-            pltpu.make_async_copy(up_hbm.at[:, columns], up_ref.at[:, columns], tile_sems.at[1, i]),
-        )
-        for copy in pair:
+
+    def start(copies):
+        for copy in copies:
             copy.start()
-        copies.append(pair)
+        return copies
+
+    def chunks(hbm, ref, offset):
+        spans = [slice(i, min(i + DEPTH, ref.shape[0])) for i in range(0, ref.shape[0], DEPTH)]
+        return [
+            (span, pltpu.make_async_copy(hbm.at[span], ref.at[span], sems.at[offset + i]))
+            for i, span in enumerate(spans)
+        ]
+
+    first = start(
+        [
+            pltpu.make_async_copy(hidden_hbm, hidden_ref, sems.at[0]),
+            pltpu.make_async_copy(down_hbm, down_ref, sems.at[1]),
+        ]
+    )
+    up_chunks = chunks(up_hbm, up_ref, 2)
+    weight_chunks = chunks(weight_hbm, weight_ref, 2 + len(up_chunks))
+    waiting = [copy for _, copy in up_chunks + weight_chunks]
+    start(waiting[:1])
 
     slots = holder_ref.shape[1]
     numbers = [holder_ref[...], block_ref[...], length_ref[...], jnp.zeros((own, LANES - 3 * slots), jnp.int32)]
@@ -115,28 +125,41 @@
     )
     for copy in first:
         copy.wait()
+    start(waiting[1:3])
     hidden = hidden_ref[...]
     low = lax.dot_general(hidden, down_ref[...], (((1,), (1,)), ((), ())), preferred_element_type=jnp.float32)
-    column = lax.broadcasted_iota(jnp.int32, low.shape, 1)
+    column = lax.broadcasted_iota(jnp.int32, (rows, low_width), 1)
     match = (column >= adapter * rank) & (column < adapter * rank + rank)
     high, low = split2(jnp.where(match, ADAPTER_SCALE * low, 0.0))
+    both = jnp.concatenate([high, low], axis=0)
+    columns = [slice(i * COLUMN_TILE, (i + 1) * COLUMN_TILE) for i in range(tiles)]
+    for i, (span, copy) in enumerate(up_chunks):
+        copy.wait()
+        start(waiting[i + 3 : i + 4])
+        for tile in columns:
+            up_high, up_low = split2(up_ref[span, tile])
+            twice = jnp.dot(both[:, span], up_high, preferred_element_type=jnp.float32)
+            total = jnp.dot(high[:, span], up_low, preferred_element_type=jnp.float32)
+            total = (total + twice[rows:]) + twice[:rows]
+            total_ref[:, tile] = total if i == 0 else total_ref[:, tile] + total
     even = lax.axis_index("kv") % PAIR == 0
-    for i in range(tiles):
-        columns = slice(i * COLUMN_TILE, (i + 1) * COLUMN_TILE)
-        for copy in copies[i]:
-            copy.wait()
-        up_high, up_low = split2(up_ref[:, columns])
-        total = jnp.dot(hidden, weight_ref[:, columns], preferred_element_type=jnp.float32)
-        total += jnp.dot(low, up_high, preferred_element_type=jnp.float32)
-        total += jnp.dot(high, up_low, preferred_element_type=jnp.float32)
-        total += jnp.dot(high, up_high, preferred_element_type=jnp.float32)
-        total = total.reshape(chips, PAIR, own, COLUMN_TILE)
-        keep_ref[:, :, columns] = jnp.where(even, total[:, 0], total[:, 1])
-        send_ref[:, :, columns] = jnp.where(even, total[:, 1], total[:, 0])
+    for i, (span, copy) in enumerate(weight_chunks):
+        copy.wait()
+        start(waiting[i + len(up_chunks) + 3 : i + len(up_chunks) + 4])
+        for tile in columns:
+            total = total_ref[:, tile] + jnp.dot(
+                hidden[:, span], weight_ref[span, tile], preferred_element_type=jnp.float32
+            )
+            if i < len(weight_chunks) - 1:
+                total_ref[:, tile] = total
+            else:
+                total = total.reshape(chips, PAIR, own, COLUMN_TILE)
+                keep_ref[:, :, tile] = jnp.where(even, total[:, 0], total[:, 1])
+                send_ref[:, :, tile] = jnp.where(even, total[:, 1], total[:, 0])
 
 
 def project(tenant, tenant_adapter, holder, block, length, hidden, query_weight, down, up, rank, chips):
-    rows, _ = hidden.shape
+    rows, depth = hidden.shape
     width = query_weight.shape[1]
     out = jax.ShapeDtypeStruct((chips, rows // chips // PAIR, width + LANES), jnp.float32)
     operands = in_hbm(tenant, tenant_adapter, holder, block, length, hidden, query_weight, down, up)
@@ -147,7 +170,10 @@
         out_specs=[vmem_spec()] * 2,
         out_shape=[out] * 2,
         scratch_shapes=[pltpu.VMEM(x.shape, x.dtype) for x in large]
-        + [pltpu.SemaphoreType.DMA((2,)), pltpu.SemaphoreType.DMA((2, width // COLUMN_TILE))],
+        + [
+            pltpu.VMEM((rows, width), jnp.float32),
+            pltpu.SemaphoreType.DMA((2 + pl.cdiv(depth, DEPTH) + pl.cdiv(down.shape[0], DEPTH),)),
+        ],
         compiler_params=params(24),
         name="project",
     )(*operands)
@@ -293,8 +319,8 @@
 
 def attend_kernel(scale, group, kv_local, count, list_ref, bound_ref, *refs):
     queries, refs = refs[: count // PAIR], refs[count // PAIR :]
-    (key_hbm, value_hbm, out_ref, query_ref, key_ref, value_ref, top_ref, total_ref, sum_ref) = refs[:9]
-    (score_ref, part_top_ref, part_total_ref, part_sum_ref, sems) = refs[9:]
+    (key_hbm, value_hbm, keep_ref, send_ref, query_ref, key_ref, value_ref, top_ref, total_ref, sum_ref) = refs[:10]
+    (score_ref, part_top_ref, part_total_ref, part_sum_ref, sems) = refs[10:]
     heads = query_ref.shape[1]
     rows = query_ref.shape[0] - 1
     own = rows // count
@@ -306,13 +332,15 @@
     copies = []
     for part in range(PHASES):
         here = pl.ds(part * size, size)
-        pair = (
-            pltpu.make_async_copy(key_hbm.at[here], key_ref.at[here], sems.at[0, part]),
-            pltpu.make_async_copy(value_hbm.at[here], value_ref.at[here], sems.at[1, part]),
+        copies.append(
+            (
+                pltpu.make_async_copy(key_hbm.at[here], key_ref.at[here], sems.at[0, part]),
+                pltpu.make_async_copy(value_hbm.at[here], value_ref.at[here], sems.at[1, part]),
+            )
         )
+    for pair in copies[:AHEAD]:
         for copy in pair:
             copy.start()
-        copies.append(pair)
 
     factor = scale * LOG2E
     for s, piece in enumerate(queries):
@@ -337,43 +365,39 @@
     def block_of(entry):
         return (entry >> length_bits) & (blocks - 1)
 
+    def merge_item(row, t, k):
+        j = t * PAIR + k
+        top, part_top = top_ref[row], part_top_ref[j]
+        high = jnp.maximum(top, part_top)
+        top_ref[row] = high
+        old, new = jnp.exp2((top - high) * factor), jnp.exp2((part_top - high) * factor)
+        total_ref[row] = total_ref[row] * old + part_total_ref[j] * new
+        sum_ref[row] = sum_ref[row] * old + part_sum_ref[t, k * heads : (k + 1) * heads] * new
+
+    def weigh_item(entry, t, k):
+        j = t * PAIR + k
+        scores = jnp.where(token <= (entry & (block_size - 1)), score_ref[t, k * heads : (k + 1) * heads], NEG_FILL)
+        high = jnp.max(scores, axis=1, keepdims=True)
+        weights = jnp.exp2((scores - high) * factor)
+        part_top_ref[j] = jnp.broadcast_to(high, wide)
+        part_total_ref[j] = jnp.broadcast_to(jnp.sum(weights, axis=1, keepdims=True), wide)
+        return weights.astype(jnp.bfloat16)
+
     def turn(i, carry):
-        row = [jnp.where(i >= 2, row_of(e), rows) for e in entries(jnp.maximum(i - 2, 0))]
-        shares = []
-        for j in range(CHUNK):
-            top, part_top = top_ref[row[j]], part_top_ref[j]
-            high = jnp.maximum(top, part_top)
-            top_ref[row[j]] = high
-            shares.append((jnp.exp2((top - high) * factor), jnp.exp2((part_top - high) * factor)))
-        for j, (old, new) in enumerate(shares):
-            t, k = divmod(j, PAIR)
-            total_ref[row[j]] = total_ref[row[j]] * old + part_total_ref[j] * new
-            sum_ref[row[j]] = sum_ref[row[j]] * old + part_sum_ref[t, k * heads : (k + 1) * heads] * new
-
-        items = entries(jnp.maximum(i - 1, 0))
+        merged, weighed, scored = (entries(jnp.maximum(i - back, 0)) for back in (2, 1, 0))
         for t in range(TASKS):
-            pieces = []
-            for k in range(PAIR):
-                j = t * PAIR + k
-                length = items[j] & (block_size - 1)
-                scores = jnp.where(token <= length, score_ref[t, k * heads : (k + 1) * heads], NEG_FILL)
-                high = jnp.max(scores, axis=1, keepdims=True)
-                weights = jnp.exp2((scores - high) * factor)
-                part_top_ref[j] = jnp.broadcast_to(high, wide)
-                part_total_ref[j] = jnp.broadcast_to(jnp.sum(weights, axis=1, keepdims=True), wide)
-                pieces.append(weights.astype(jnp.bfloat16))
+            task = slice(t * PAIR, (t + 1) * PAIR)
+            for k, entry in enumerate(merged[task]):
+                merge_item(jnp.where(i >= 2, row_of(entry), rows), t, k)
+            weights = [weigh_item(entry, t, k) for k, entry in enumerate(weighed[task])]
             part_sum_ref[t] = jnp.dot(
-                jnp.concatenate(pieces, axis=0),
-                value_ref[block_of(items[t * PAIR])],
+                jnp.concatenate(weights, axis=0),
+                value_ref[block_of(weighed[task][0])],
                 preferred_element_type=jnp.float32,
             )
-
-        items = entries(i)
-        for t in range(TASKS):
-            task = items[t * PAIR : (t + 1) * PAIR]
             score_ref[t] = lax.dot_general(
-                jnp.concatenate([query_ref[row_of(e)] for e in task], axis=0),
-                key_ref[block_of(task[0])],
+                jnp.concatenate([query_ref[row_of(entry)] for entry in scored[task]], axis=0),
+                key_ref[block_of(scored[task][0])],
                 (((1,), (1,)), ((), ())),
                 preferred_element_type=jnp.float32,
             )
@@ -382,28 +406,25 @@
     for part in range(PHASES):
         for copy in copies[part]:
             copy.wait()
+        for pair in copies[part + AHEAD : part + AHEAD + 1]:
+            for copy in pair:
+                copy.start()
         lax.fori_loop(bound_ref[0, part], bound_ref[0, part + 1], turn, 0)
     last = bound_ref[0, PHASES]
     lax.fori_loop(last, last + 2, turn, 0)
 
-    me = lax.axis_index("kv")
     square = (own * heads, LANES)
     eye = lax.broadcasted_iota(jnp.int32, square, 0) == lax.broadcasted_iota(jnp.int32, square, 1)
     line = lax.broadcasted_iota(jnp.int32, wide, 0)
-    for c in range(count):
-        stats = jnp.zeros(wide, jnp.float32)
-        position = 0
-        for ref in (top_ref, total_ref):
-            flat = jnp.sum(
-                jnp.where(eye, ref[c * own : (c + 1) * own].reshape(square), 0.0), axis=0, keepdims=True
-            )
-            for piece in split3(flat):
-                stats = jnp.where(line == position, piece, stats)
-                position += 1
-        owner = jnp.bitwise_xor(me, c)
-        for r in range(own):
-            out_ref[owner, r] = sum_ref[c * own + r].astype(jnp.bfloat16)
-        out_ref[owner, own] = stats.astype(jnp.bfloat16)
+    for q in range(count):
+        ref = (keep_ref, send_ref)[q % PAIR]
+        mine = slice(q * own, (q + 1) * own)
+        top, total = (
+            jnp.sum(jnp.where(eye, state[mine].reshape(square), 0.0), axis=0, keepdims=True)
+            for state in (top_ref, total_ref)
+        )
+        ref[q // PAIR, :own] = sum_ref[mine]
+        ref[q // PAIR, own] = jnp.where(line == 0, top, jnp.where(line == 1, total, 0.0))
 
 
 def attend(items, bounds, queries, keys, values, kv_local, scale):
@@ -417,8 +438,8 @@
     return pl.pallas_call(
         functools.partial(attend_kernel, scale, heads // kv_local, kv_local, count),
         in_specs=[smem_spec(), smem_spec()] + [vmem_spec()] * len(queries) + [hbm_spec()] * 2,
-        out_specs=vmem_spec(),
-        out_shape=jax.ShapeDtypeStruct((count, own + 1, heads, LANES), jnp.bfloat16),
+        out_specs=[vmem_spec()] * PAIR,
+        out_shape=[jax.ShapeDtypeStruct((count // PAIR, own + 1, heads, LANES), jnp.float32)] * PAIR,
         scratch_shapes=[
             pltpu.VMEM((rows + 1, heads, LANES), jnp.bfloat16),
             pltpu.VMEM(keys.shape, keys.dtype),
@@ -437,50 +458,90 @@
     )(items, bounds, *queries, keys, values)
 
 
-def merge_kernel(scale, parts_ref, out_ref, wide_ref):
-    count, sections, heads, _ = parts_ref.shape
+def merge_pair_kernel(scale, keep_ref, got_ref, out_ref):
+    chips, sections, heads, _ = keep_ref.shape
     own = sections - 1
     factor = scale * LOG2E
-    stats = [parts_ref[s, own].astype(jnp.float32) for s in range(count)]
-    tops = jnp.concatenate([s[0:1] + s[1:2] + s[2:3] for s in stats], axis=0)
-    totals = jnp.concatenate([s[3:4] + s[4:5] + s[5:6] for s in stats], axis=0)
-    weights = jnp.exp2((tops - jnp.max(tops, axis=0, keepdims=True)) * factor)
-    weights = weights / jnp.sum(weights * totals, axis=0, keepdims=True)
-    columns = weights.T
-    acc = jnp.zeros((own * heads, LANES), jnp.float32)
-    for s in range(count):
-        part = parts_ref[s, :own].astype(jnp.float32).reshape(own * heads, LANES)
-        acc = acc + part * columns[:, s : s + 1]
-    wide_ref[...] = acc
-    pieces = [wide_ref[pl.ds(h, own, stride=heads), :] for h in range(heads)]
-    out_ref[...] = jnp.concatenate(pieces, axis=1).astype(jnp.bfloat16)
-
-
-def merge(parts, scale):
-    count, sections, heads, _ = parts.shape
+    line = lax.broadcasted_iota(jnp.int32, (heads, LANES), 0)
+    shares, stats = [], []
+    for s in range(chips):
+        keep, got = keep_ref[s, own], got_ref[s, own]
+        high = jnp.maximum(keep[0:1], got[0:1])
+        pair = [jnp.exp2((x[0:1] - high) * factor) for x in (keep, got)]
+        shares += pair
+        total = pair[0] * keep[1:2] + pair[1] * got[1:2]
+        stat = jnp.zeros((heads, LANES), jnp.float32)
+        for position, piece in enumerate(split3(high) + split3(total)):
+            stat = jnp.where(line == position, piece, stat)
+        stats.append(stat)
+    columns = jnp.concatenate(shares, axis=0).T
+    flat = (own * heads, LANES)
+    for s in range(chips):
+        total = keep_ref[s, :own].reshape(flat) * columns[:, PAIR * s : PAIR * s + 1]
+        total = total + got_ref[s, :own].reshape(flat) * columns[:, PAIR * s + 1 : PAIR * s + 2]
+        out_ref[s, :own] = total.astype(jnp.bfloat16).reshape(own, heads, LANES)
+        out_ref[s, own] = stats[s].astype(jnp.bfloat16)
+
+
+def merge_pair(keep, got, scale):
+    return pl.pallas_call(
+        functools.partial(merge_pair_kernel, scale),
+        in_specs=[vmem_spec()] * 2,
+        out_specs=vmem_spec(),
+        out_shape=jax.ShapeDtypeStruct(keep.shape, jnp.bfloat16),
+        compiler_params=params(16),
+        name="merge_pair",
+    )(keep, got)
+
+
+def merge_kernel(scale, *refs):
+    pieces, (out_ref, wide_ref) = refs[:-2], refs[-2:]
+    chips, sections, heads, _ = pieces[0].shape
     own = sections - 1
+    factor = scale * LOG2E
+    shares = []
+    for s in range(chips):
+        stats = [pieces[j][s ^ j, own].astype(jnp.float32) for j in range(chips)]
+        tops = jnp.concatenate([x[0:1] + x[1:2] + x[2:3] for x in stats], axis=0)
+        totals = jnp.concatenate([x[3:4] + x[4:5] + x[5:6] for x in stats], axis=0)
+        weights = jnp.exp2((tops - jnp.max(tops, axis=0, keepdims=True)) * factor)
+        shares.append(weights / jnp.sum(weights * totals, axis=0, keepdims=True))
+    columns = jnp.concatenate(shares, axis=0).T
+    flat = own * heads
+    for s in range(chips):
+        total = jnp.zeros((flat, LANES), jnp.float32)
+        for j in range(chips):
+            part = pieces[j][s ^ j, :own].astype(jnp.float32).reshape(flat, LANES)
+            total = total + part * columns[:, s * chips + j : s * chips + j + 1]
+        wide_ref[s * flat : (s + 1) * flat, :] = total
+    rows = [wide_ref[pl.ds(h, chips * own, stride=heads), :] for h in range(heads)]
+    out_ref[...] = jnp.concatenate(rows, axis=1).astype(jnp.bfloat16)
+
+
+def merge(pieces, scale):
+    chips, sections, heads, _ = pieces[0].shape
+    own = sections - 1
     return pl.pallas_call(
         functools.partial(merge_kernel, scale),
-        in_specs=[vmem_spec()],
+        in_specs=[vmem_spec()] * chips,
         out_specs=vmem_spec(),
-        out_shape=jax.ShapeDtypeStruct((own, heads * LANES), jnp.bfloat16),
-        scratch_shapes=[pltpu.VMEM((own * heads, LANES), jnp.float32)],
-        compiler_params=params(16),
+        out_shape=jax.ShapeDtypeStruct((chips * own, heads * LANES), jnp.bfloat16),
+        scratch_shapes=[pltpu.VMEM((chips * own * heads, LANES), jnp.float32)],
+        compiler_params=params(32),
         name="merge",
-    )(parts)
-
-
-def output_kernel(chips, row_count, *refs):
-    pieces, weight_ref = refs[:chips], refs[chips]
-    own_ref, sends = refs[chips + 1], refs[chips + 2 : chips + 1 + row_count]
-    rows_ref, terms_ref = refs[chips + 1 + row_count :]
-    own = pieces[0].shape[0] // PAIR
+    )(*pieces)
+
+
+def output_kernel(own, row_count, *refs):
+    pieces, weight_ref = refs[:PAIR], refs[PAIR]
+    own_ref, sends = refs[PAIR + 1], refs[PAIR + 2 : PAIR + 1 + row_count]
+    rows_ref, terms_ref = refs[PAIR + 1 + row_count :]
     me = lax.axis_index("kv")
-    for s in range(chips):
-        piece = pieces[s][...].astype(jnp.float32)
-        for t in range(PAIR):
+    for t in range(PAIR):
+        piece = pieces[t][...].astype(jnp.float32)
+        for s in range(piece.shape[0] // own):
             start = pl.multiple_of(jnp.bitwise_xor(me, PAIR * s + t) * own, own)
-            rows_ref[pl.ds(start, own), :] = piece[t * own : (t + 1) * own]
+            rows_ref[pl.ds(start, own), :] = piece[s * own : (s + 1) * own]
     terms_ref[...] = jnp.dot(
         rows_ref[...].astype(jnp.bfloat16), weight_ref[...], preferred_element_type=jnp.float32
     )
@@ -491,15 +552,14 @@
         ref[...] = terms_ref[pl.ds(start, part), :].astype(ref.dtype)
 
 
-def project_out(pieces, weight, row_count):
-    chips = len(pieces)
-    pair_rows, width = pieces[0].shape
-    rows, columns = chips * pair_rows, weight.shape[1]
+def project_out(pieces, weight, own, row_count):
+    half, width = pieces[0].shape
+    rows, columns = PAIR * half, weight.shape[1]
     part = rows // row_count
     send = jax.ShapeDtypeStruct((part, columns), jnp.bfloat16)
     return pl.pallas_call(
-        functools.partial(output_kernel, chips, row_count),
-        in_specs=[vmem_spec()] * (chips + 1),
+        functools.partial(output_kernel, own, row_count),
+        in_specs=[vmem_spec()] * (PAIR + 1),
         out_specs=[vmem_spec()] * row_count,
         out_shape=[jax.ShapeDtypeStruct((part, columns), jnp.float32)] + [send] * (row_count - 1),
         scratch_shapes=[pltpu.VMEM((rows, width), jnp.float32), pltpu.VMEM((rows, columns), jnp.float32)],
@@ -508,18 +568,17 @@
     )(*pieces, weight)
 
 
-def swap(x, axis):
-    return lax.all_to_all(x, axis, split_axis=0, concat_axis=0, tiled=True)
-
-
 def exchange(x, axis, s):
     count = lax.axis_size(axis)
     return lax.ppermute(x, axis, [(i, i ^ s) for i in range(count)])
 
 
+def gather_chips(x):
+    return [x] + [exchange(x, "kv", s) for s in range(PAIR, lax.axis_size("kv"), PAIR)]
+
+
 def gather_pairs(x):
-    pair = jnp.concatenate([x, exchange(x, "kv", 1)], axis=0)
-    return [pair] + [exchange(pair, "kv", s) for s in range(PAIR, lax.axis_size("kv"), PAIR)]
+    return gather_chips(jnp.concatenate([x, exchange(x, "kv", 1)], axis=0))
 
 
 def local(
@@ -577,9 +636,10 @@
 
     keys = paged_key_cache.reshape(blocks, block_size * kv_local, head_size)
     values = paged_value_cache.reshape(blocks, block_size * kv_local, head_size)
-    partial_out = attend(items, bounds, queries, keys, values, kv_local, scale)
-    attention = merge(swap(partial_out, "kv"), scale)
-    terms = project_out(gather_pairs(attention), output_weight, row_count)
+    keep, send = attend(items, bounds, queries, keys, values, kv_local, scale)
+    merged = merge_pair(keep, exchange(send, "kv", 1), scale)
+    attention = merge(gather_chips(merged), scale)
+    terms = project_out([attention, exchange(attention, "kv", 1)], output_weight, own, row_count)
     total = terms[0]
     for s in range(1, row_count):
         total = total + exchange(terms[s], "row", s).astype(jnp.float32)

time: 73.3 us -> 65.9 us (0.90); the launches traced: 74.6 us -> 66.2 us
  Pallas kernels: 31.6 us -> 20.5 us
  blocking collectives: 9.66 us -> 0 us
  waiting for transfers between devices: 15.6 us -> 21.9 us
  starting transfers between devices: 16.6 us -> 22.7 us
    all_to_all x1 -> x0, blocking collectives: 9.66 us -> none  [swap(): return lax.all_to_all(x, axis, split_axis=0, concat_axis=0, tiled=True)]
    pallas_call x1, Pallas kernels: 19.9 us -> 11.1 us  [attend(): pl.pallas_call(functools.partial(attend_kernel, scale, heads // kv_local,...]
    ppermute x15 -> x16, waiting for transfers between devices: 15.6 us -> 21.9 us  [exchange(): return lax.ppermute(x, axis, [(i, i ^ s) for i in range(count)])]
    ppermute x15 -> x16, starting transfers between devices: 16.6 us -> 22.7 us  [exchange(): return lax.ppermute(x, axis, [(i, i ^ s) for i in range(count)])]
    pallas_call x1, Pallas kernels: 7.94 us -> 5.14 us  [project(): pl.pallas_call(functools.partial(project_kernel, rank), in_specs=[vmem_sp...]
  transfers between devices with their start and end apart: 15 -> 16, of which waited for: 12 -> 12; matrix products, arithmetic and copies ran while one was open for 0% -> 0% of each run, Pallas kernels for 3% -> 4%
where the time goes in v4:
time: 65.9 us; the launch traced here: 66.2 us
  starting transfers between devices  22.7 us (34%)
  waiting for transfers between devices  21.9 us (33%)
  Pallas kernels  20.5 us (31%)
  other arithmetic  0.95 us (1%)
    ppermute x16, starting transfers between devices, exchange(): return lax.ppermute(x, axis, [(i, i ^ s) for i in range(count)])  22.7 us
    ppermute x16, waiting for transfers between devices, exchange(): return lax.ppermute(x, axis, [(i, i ^ s) for i in range(count)])  21.9 us
    pallas_call x1, Pallas kernels, attend(): pl.pallas_call(functools.partial(attend_kernel, scale, heads // kv_local,...  11.1 us
    pallas_call x1, Pallas kernels, project(): pl.pallas_call(functools.partial(project_kernel, rank), in_specs=[vmem_sp...  5.14 us
    pallas_call x1, Pallas kernels, make_list(): pl.pallas_call(functools.partial(list_kernel, blocks, block_size, slots),...  2.42 us
  transfers between devices with their start and end apart: 16, of which 12 were waited for; matrix products, arithmetic and copies ran while one was open for 0% of the time, Pallas kernels for 4%

profile of v4, /device:TPU:0, one launch (start us, length us, event | category | flops | bytes accessed | tf_op | source)
XLA Modules:
  0.0 66.2 jit_solution(1312208310868660088)
XLA Ops:
  0.0 5.1 %project.1 = (f32[4,8,2176]{2,1,0:T(8,128)S(1)}, f32[4,8,2176]{2,1,0:T(8,128)S(1)}) custom-call(s32[1,64]{1,0:T(1,128)} %bitcast.22, s32[1,64]{1,0:T(1,128)} %bitcast.23, s32[8,32]{1,0:T(8,128)} %holder_ref.1, s32[8,32]{1,0:T(8,128)} %block_ref.1, s32[8,32]{1,0:T(8,128)} %length_ref.1, bf16[64,640]{1,0:T(8,128)(2,1)} %hidden_hbm.1, ...), custom_call_target="tpu_custom_call" | custom-call | tf_op jit(solution)/shard_map/project/pallas_call | solution.py:167
  5.2 0.5 collective-permute-start
  5.7 0.1 reduce_sum.9
  5.9 0.9 %collective-permute-done.got_ref = f32[4,8,2176]{2,1,0:T(8,128)S(1)} collective-permute-done((f32[4,8,2176]{2,1,0:T(8,128)S(1)}, f32[4,8,2176]{2,1,0:T(8,128)S(1)}, u32[]{:S(2)}, u32[]{:S(2)}) %collective-permute-start) | collective-permute-done | bytes 278560 | tf_op jit(solution)/shard_map/ppermute | solution.py:573
  6.9 2.9 %collective-permute-start.1 = (f32[8,2304]{1,0:T(8,128)S(1)}, f32[8,2304]{1,0:T(8,128)S(1)}, u32[]{:S(2)}, u32[]{:S(2)}) collective-permute-start(f32[8,2304]{1,0:T(8,128)S(1)} %get-tuple-element.22), channel_id=1, source_target_pairs={{0,2},{1,3},{2,0},{3,1},{4,6},{5,7},{6,4},{7,5},{8,10},{9,11},{10,... | collective-permute-start | bytes 221192 | tf_op jit(solution)/shard_map/ppermute | solution.py:573
  9.8 1.5 %collective-permute-start.2 = (f32[8,2304]{1,0:T(8,128)S(1)}, f32[8,2304]{1,0:T(8,128)S(1)}, u32[]{:S(2)}, u32[]{:S(2)}) collective-permute-start(f32[8,2304]{1,0:T(8,128)S(1)} %get-tuple-element.23), channel_id=1, source_target_pairs={{0,4},{1,5},{2,6},{3,7},{4,0},{5,1},{6,2},{7,3},{8,12},{9,13},{10,... | collective-permute-start | bytes 221192 | tf_op jit(solution)/shard_map/ppermute | solution.py:573
  11.4 1.0 %collective-permute-done.1.refs_1_ = f32[8,2304]{1,0:T(8,128)S(1)} collective-permute-done((f32[8,2304]{1,0:T(8,128)S(1)}, f32[8,2304]{1,0:T(8,128)S(1)}, u32[]{:S(2)}, u32[]{:S(2)}) %collective-permute-start.1) | collective-permute-done | bytes 73760 | tf_op jit(solution)/shard_map/ppermute | solution.py:573
  12.4 1.8 %collective-permute-done.2.refs_2_ = f32[8,2304]{1,0:T(8,128)S(1)} collective-permute-done((f32[8,2304]{1,0:T(8,128)S(1)}, f32[8,2304]{1,0:T(8,128)S(1)}, u32[]{:S(2)}, u32[]{:S(2)}) %collective-permute-start.2) | collective-permute-done | bytes 73760 | tf_op jit(solution)/shard_map/ppermute | solution.py:573
  14.2 2.4 %collective-permute-done.3.refs_3_ = f32[8,2304]{1,0:T(8,128)S(1)} collective-permute-done((f32[8,2304]{1,0:T(8,128)S(1)}, f32[8,2304]{1,0:T(8,128)S(1)}, u32[]{:S(2)}, u32[]{:S(2)}) %collective-permute-start.3) | collective-permute-done | bytes 73760 | tf_op jit(solution)/shard_map/ppermute | solution.py:573
  16.6 0.3 queries.1
  17.0 1.2 %collective-permute-done.4 = bf16[8,16,128]{2,1,0:T(8,128)(2,1)S(1)} collective-permute-done((bf16[8,16,128]{2,1,0:T(8,128)(2,1)S(1)}, bf16[8,16,128]{2,1,0:T(8,128)(2,1)S(1)}, u32[]{:S(2)}, u32[]{:S(2)}) %collective-permute-start.4) | collective-permute-done | bytes 32800 | tf_op jit(solution)/shard_map/ppermute | solution.py:573
  18.2 0.6 collective-permute-start.7
  18.8 1.5 %collective-permute-start.6 = (bf16[16,16,128]{2,1,0:T(8,128)(2,1)S(1)}, bf16[16,16,128]{2,1,0:T(8,128)(2,1)S(1)}, u32[]{:S(2)}, u32[]{:S(2)}) collective-permute-start(bf16[16,16,128]{2,1,0:T(8,128)(2,1)S(1)} %pad_maximum_fusion), channel_id=1, source_target_pairs={{0,4},{1,5},{2,6},{3,7},{4,0},{5,1},{6,2},{7,3},{8,12},{9,13},{10,... | collective-permute-start | bytes 196616 | tf_op jit(solution)/shard_map/ppermute | solution.py:573
  20.2 1.5 %collective-permute-start.5 = (bf16[16,16,128]{2,1,0:T(8,128)(2,1)S(1)}, bf16[16,16,128]{2,1,0:T(8,128)(2,1)S(1)}, u32[]{:S(2)}, u32[]{:S(2)}) collective-permute-start(bf16[16,16,128]{2,1,0:T(8,128)(2,1)S(1)} %pad_maximum_fusion), channel_id=1, source_target_pairs={{0,2},{1,3},{2,0},{3,1},{4,6},{5,7},{6,4},{7,5},{8,10},{9,11},{10,... | collective-permute-start | bytes 196616 | tf_op jit(solution)/shard_map/ppermute | solution.py:573
  21.7 2.4 %slot_list.1 = (s32[1,768]{1,0:T(1,128)S(1)}, s32[1,128]{1,0:T(1,128)S(1)}) custom-call(f32[8,2304]{1,0:T(8,128)S(1)} %get-tuple-element.21.refs_0_, f32[8,2304]{1,0:T(8,128)S(1)} %collective-permute-done.1.refs_1_, f32[8,2304]{1,0:T(8,128)S(1)} %collective-permute-done.2.refs_2_, f32[8,2304]{1,0:T(8,128)S(1)} %collective-permute-done.3.refs_3_), custom_call_target="tpu_custom_call" | custom-call | flops 100000000 | bytes 10000000 | tf_op jit(solution)/shard_map/slot_list/pallas_call | solution.py:301
  24.2 0.3 collective-permute-done.5
  24.5 11.1 %attend.1 = (f32[4,9,16,128]{3,2,1,0:T(8,128)S(1)}, f32[4,9,16,128]{3,2,1,0:T(8,128)S(1)}) custom-call(s32[1,768]{1,0:T(1,128)S(1)} %get-tuple-element.25.list_ref, s32[1,128]{1,0:T(1,128)S(1)} %get-tuple-element.26.bound_ref, bf16[2,8,16,128]{3,2,1,0:T(8,128)(2,1)S(1)} %bitcast.13, bf16[2,8,16,128]{3,2,1,0:T(8,128)(2,1)S(1)} %bitcast.16, ...), custom_call_target="tpu_custom_call" | custom-call | tf_op jit(solution)/shard_map/attend/pallas_call | solution.py:438
  35.7 1.6 %collective-permute-done.8.got_ref = f32[4,9,16,128]{3,2,1,0:T(8,128)S(1)} collective-permute-done((f32[4,9,16,128]{3,2,1,0:T(8,128)S(1)}, f32[4,9,16,128]{3,2,1,0:T(8,128)S(1)}, u32[]{:S(2)}, u32[]{:S(2)}) %collective-permute-start.8) | collective-permute-done | bytes 294944 | tf_op jit(solution)/shard_map/ppermute | solution.py:573
  37.2 0.3 merge_pair.1.refs_0_
  37.6 1.7 %collective-permute-start.11 = (bf16[4,9,16,128]{3,2,1,0:T(8,128)(2,1)S(1)}, bf16[4,9,16,128]{3,2,1,0:T(8,128)(2,1)S(1)}, u32[]{:S(2)}, u32[]{:S(2)}) collective-permute-start(bf16[4,9,16,128]{3,2,1,0:T(8,128)(2,1)S(1)} %merge_pair.1.refs_0_), channel_id=1, source_target_pairs={{0,6},{1,7},{2,4},{3,5},{4,2},{5,3},{6,0},{7,1},{8,14},{9,15},{10,... | collective-permute-start | bytes 442376 | tf_op jit(solution)/shard_map/ppermute | solution.py:573
  39.3 7.8 %collective-permute-start.10 = (bf16[4,9,16,128]{3,2,1,0:T(8,128)(2,1)S(1)}, bf16[4,9,16,128]{3,2,1,0:T(8,128)(2,1)S(1)}, u32[]{:S(2)}, u32[]{:S(2)}) collective-permute-start(bf16[4,9,16,128]{3,2,1,0:T(8,128)(2,1)S(1)} %merge_pair.1.refs_0_), channel_id=1, source_target_pairs={{0,4},{1,5},{2,6},{3,7},{4,0},{5,1},{6,2},{7,3},{8,12},{9,13},{10,... | collective-permute-start | bytes 442376 | tf_op jit(solution)/shard_map/ppermute | solution.py:573
  47.1 5.0 %collective-permute-done.10.refs_2_ = bf16[4,9,16,128]{3,2,1,0:T(8,128)(2,1)S(1)} collective-permute-done((bf16[4,9,16,128]{3,2,1,0:T(8,128)(2,1)S(1)}, bf16[4,9,16,128]{3,2,1,0:T(8,128)(2,1)S(1)}, u32[]{:S(2)}, u32[]{:S(2)}) %collective-permute-start.10) | collective-permute-done | bytes 147488 | tf_op jit(solution)/shard_map/ppermute | solution.py:573
  52.2 1.0 %collective-permute-done.9.refs_1_ = bf16[4,9,16,128]{3,2,1,0:T(8,128)(2,1)S(1)} collective-permute-done((bf16[4,9,16,128]{3,2,1,0:T(8,128)(2,1)S(1)}, bf16[4,9,16,128]{3,2,1,0:T(8,128)(2,1)S(1)}, u32[]{:S(2)}, u32[]{:S(2)}) %collective-permute-start.9) | collective-permute-done | bytes 147488 | tf_op jit(solution)/shard_map/ppermute | solution.py:573
  53.2 0.6 merge.1.refs_0_
  53.8 1.3 %collective-permute-done.12.refs_1_ = bf16[32,2048]{1,0:T(8,128)(2,1)S(1)} collective-permute-done((bf16[32,2048]{1,0:T(8,128)(2,1)S(1)}, bf16[32,2048]{1,0:T(8,128)(2,1)S(1)}, u32[]{:S(2)}, u32[]{:S(2)}) %collective-permute-start.12) | collective-permute-done | bytes 131104 | tf_op jit(solution)/shard_map/ppermute | solution.py:573
  55.2 0.6 project_out.1
  55.8 1.6 %collective-permute-start.13 = (bf16[16,640]{1,0:T(8,128)(2,1)S(1)}, bf16[16,640]{1,0:T(8,128)(2,1)S(1)}, u32[]{:S(2)}, u32[]{:S(2)}) collective-permute-start(bf16[16,640]{1,0:T(8,128)(2,1)S(1)} %get-tuple-element.30), channel_id=1, source_target_pairs={{0,8},{8,0},{16,24},{24,16},{1,9},{9,1},{17,25},{25,17},{2,10},{10... | collective-permute-start | bytes 61448 | tf_op jit(solution)/shard_map/ppermute | solution.py:573
  57.4 2.6 %collective-permute-start.14 = (bf16[16,640]{1,0:T(8,128)(2,1)S(1)}, bf16[16,640]{1,0:T(8,128)(2,1)S(1)}, u32[]{:S(2)}, u32[]{:S(2)}) collective-permute-start(bf16[16,640]{1,0:T(8,128)(2,1)S(1)} %get-tuple-element.31), channel_id=1, source_target_pairs={{0,16},{8,24},{16,0},{24,8},{1,17},{9,25},{17,1},{25,9},{2,18},{10... | collective-permute-start | bytes 61448 | tf_op jit(solution)/shard_map/ppermute | solution.py:573
  60.0 0.2 collective-permute-start.15
  60.2 2.1 %collective-permute-done.14 = bf16[16,640]{1,0:T(8,128)(2,1)S(1)} collective-permute-done((bf16[16,640]{1,0:T(8,128)(2,1)S(1)}, bf16[16,640]{1,0:T(8,128)(2,1)S(1)}, u32[]{:S(2)}, u32[]{:S(2)}) %collective-permute-start.14) | collective-permute-done | bytes 20512 | tf_op jit(solution)/shard_map/ppermute | solution.py:573
  62.3 3.2 %collective-permute-done.15 = bf16[16,640]{1,0:T(8,128)(2,1)S(1)} collective-permute-done((bf16[16,640]{1,0:T(8,128)(2,1)S(1)}, bf16[16,640]{1,0:T(8,128)(2,1)S(1)}, u32[]{:S(2)}, u32[]{:S(2)}) %collective-permute-start.15) | collective-permute-done | bytes 20512 | tf_op jit(solution)/shard_map/ppermute | solution.py:573
  65.6 0.6 add_convert_fusion
  (21 shorter events, 0.5 us)
Async XLA Ops:
  0.0 5.7 %copy-start.2 = (s32[8,32]{1,0:T(8,128)S(1)}, s32[8,32]{1,0:T(8,128)}, u32[]{:S(2)}) copy-start(s32[8,32]{1,0:T(8,128)} %length_ref.1) | copy-start | bytes 3076
  0.0 16.6 %copy-start.1 = (f32[128]{0:T(128)S(1)}, f32[128]{0:T(128)}, u32[]{:S(2)}) copy-start(f32[128]{0:T(128)} %param.17) | copy-start | bytes 1540
  5.2 1.7 %collective-permute-start = (f32[4,8,2176]{2,1,0:T(8,128)S(1)}, f32[4,8,2176]{2,1,0:T(8,128)S(1)}, u32[]{:S(2)}, u32[]{:S(2)}) collective-permute-start(f32[4,8,2176]{2,1,0:T(8,128)S(1)} %get-tuple-element.20), channel_id=1, source_target_pairs={{0,1},{1,0},{2,3},{3,2},{4,5},{5,4},{6,7},{7,6},{8,9},{9,8},{10,11... | collective-permute-start | bytes 835592 | tf_op jit(solution)/shard_map/ppermute | solution.py:573
  6.9 5.5 %collective-permute-start.1 = (f32[8,2304]{1,0:T(8,128)S(1)}, f32[8,2304]{1,0:T(8,128)S(1)}, u32[]{:S(2)}, u32[]{:S(2)}) collective-permute-start(f32[8,2304]{1,0:T(8,128)S(1)} %get-tuple-element.22), channel_id=1, source_target_pairs={{0,2},{1,3},{2,0},{3,1},{4,6},{5,7},{6,4},{7,5},{8,10},{9,11},{10,... | collective-permute-start | bytes 221192 | tf_op jit(solution)/shard_map/ppermute | solution.py:573
  9.8 4.4 %collective-permute-start.2 = (f32[8,2304]{1,0:T(8,128)S(1)}, f32[8,2304]{1,0:T(8,128)S(1)}, u32[]{:S(2)}, u32[]{:S(2)}) collective-permute-start(f32[8,2304]{1,0:T(8,128)S(1)} %get-tuple-element.23), channel_id=1, source_target_pairs={{0,4},{1,5},{2,6},{3,7},{4,0},{5,1},{6,2},{7,3},{8,12},{9,13},{10,... | collective-permute-start | bytes 221192 | tf_op jit(solution)/shard_map/ppermute | solution.py:573
  11.3 5.3 %collective-permute-start.3 = (f32[8,2304]{1,0:T(8,128)S(1)}, f32[8,2304]{1,0:T(8,128)S(1)}, u32[]{:S(2)}, u32[]{:S(2)}) collective-permute-start(f32[8,2304]{1,0:T(8,128)S(1)} %get-tuple-element.24), channel_id=1, source_target_pairs={{0,6},{1,7},{2,4},{3,5},{4,2},{5,3},{6,0},{7,1},{8,14},{9,15},{10,... | collective-permute-start | bytes 221192 | tf_op jit(solution)/shard_map/ppermute | solution.py:573
  16.9 1.3 %collective-permute-start.4 = (bf16[8,16,128]{2,1,0:T(8,128)(2,1)S(1)}, bf16[8,16,128]{2,1,0:T(8,128)(2,1)S(1)}, u32[]{:S(2)}, u32[]{:S(2)}) collective-permute-start(bf16[8,16,128]{2,1,0:T(8,128)(2,1)S(1)} %queries.1), channel_id=1, source_target_pairs={{0,1},{1,0},{2,3},{3,2},{4,5},{5,4},{6,7},{7,6},{8,9},{9,8},{10,11... | collective-permute-start | bytes 98312 | tf_op jit(solution)/shard_map/ppermute | solution.py:573
  18.2 6.0 %collective-permute-start.7 = (bf16[16,16,128]{2,1,0:T(8,128)(2,1)S(1)}, bf16[16,16,128]{2,1,0:T(8,128)(2,1)S(1)}, u32[]{:S(2)}, u32[]{:S(2)}) collective-permute-start(bf16[16,16,128]{2,1,0:T(8,128)(2,1)S(1)} %pad_maximum_fusion), channel_id=1, source_target_pairs={{0,6},{1,7},{2,4},{3,5},{4,2},{5,3},{6,0},{7,1},{8,14},{9,15},{10,... | collective-permute-start | bytes 196616 | tf_op jit(solution)/shard_map/ppermute | solution.py:573
  18.8 5.4 %collective-permute-start.6 = (bf16[16,16,128]{2,1,0:T(8,128)(2,1)S(1)}, bf16[16,16,128]{2,1,0:T(8,128)(2,1)S(1)}, u32[]{:S(2)}, u32[]{:S(2)}) collective-permute-start(bf16[16,16,128]{2,1,0:T(8,128)(2,1)S(1)} %pad_maximum_fusion), channel_id=1, source_target_pairs={{0,4},{1,5},{2,6},{3,7},{4,0},{5,1},{6,2},{7,3},{8,12},{9,13},{10,... | collective-permute-start | bytes 196616 | tf_op jit(solution)/shard_map/ppermute | solution.py:573
  20.2 4.3 %collective-permute-start.5 = (bf16[16,16,128]{2,1,0:T(8,128)(2,1)S(1)}, bf16[16,16,128]{2,1,0:T(8,128)(2,1)S(1)}, u32[]{:S(2)}, u32[]{:S(2)}) collective-permute-start(bf16[16,16,128]{2,1,0:T(8,128)(2,1)S(1)} %pad_maximum_fusion), channel_id=1, source_target_pairs={{0,2},{1,3},{2,0},{3,1},{4,6},{5,7},{6,4},{7,5},{8,10},{9,11},{10,... | collective-permute-start | bytes 196616 | tf_op jit(solution)/shard_map/ppermute | solution.py:573
  24.5 30.7 %copy-start = (bf16[2048,640]{1,0:T(8,128)(2,1)S(1)}, bf16[2048,640]{1,0:T(8,128)(2,1)}, u32[]{:S(2)}) copy-start(bf16[2048,640]{1,0:T(8,128)(2,1)} %refs_2_.1) | copy-start | bytes 7864324
  35.6 1.6 %collective-permute-start.8 = (f32[4,9,16,128]{3,2,1,0:T(8,128)S(1)}, f32[4,9,16,128]{3,2,1,0:T(8,128)S(1)}, u32[]{:S(2)}, u32[]{:S(2)}) collective-permute-start(f32[4,9,16,128]{3,2,1,0:T(8,128)S(1)} %get-tuple-element.28), channel_id=1, source_target_pairs={{0,1},{1,0},{2,3},{3,2},{4,5},{5,4},{6,7},{7,6},{8,9},{9,8},{10,11... | collective-permute-start | bytes 884744 | tf_op jit(solution)/shard_map/ppermute | solution.py:573
  37.6 9.5 %collective-permute-start.11 = (bf16[4,9,16,128]{3,2,1,0:T(8,128)(2,1)S(1)}, bf16[4,9,16,128]{3,2,1,0:T(8,128)(2,1)S(1)}, u32[]{:S(2)}, u32[]{:S(2)}) collective-permute-start(bf16[4,9,16,128]{3,2,1,0:T(8,128)(2,1)S(1)} %merge_pair.1.refs_0_), channel_id=1, source_target_pairs={{0,6},{1,7},{2,4},{3,5},{4,2},{5,3},{6,0},{7,1},{8,14},{9,15},{10,... | collective-permute-start | bytes 442376 | tf_op jit(solution)/shard_map/ppermute | solution.py:573
  39.3 12.9 %collective-permute-start.10 = (bf16[4,9,16,128]{3,2,1,0:T(8,128)(2,1)S(1)}, bf16[4,9,16,128]{3,2,1,0:T(8,128)(2,1)S(1)}, u32[]{:S(2)}, u32[]{:S(2)}) collective-permute-start(bf16[4,9,16,128]{3,2,1,0:T(8,128)(2,1)S(1)} %merge_pair.1.refs_0_), channel_id=1, source_target_pairs={{0,4},{1,5},{2,6},{3,7},{4,0},{5,1},{6,2},{7,3},{8,12},{9,13},{10,... | collective-permute-start | bytes 442376 | tf_op jit(solution)/shard_map/ppermute | solution.py:573
  47.1 6.1 %collective-permute-start.9 = (bf16[4,9,16,128]{3,2,1,0:T(8,128)(2,1)S(1)}, bf16[4,9,16,128]{3,2,1,0:T(8,128)(2,1)S(1)}, u32[]{:S(2)}, u32[]{:S(2)}) collective-permute-start(bf16[4,9,16,128]{3,2,1,0:T(8,128)(2,1)S(1)} %merge_pair.1.refs_0_), channel_id=1, source_target_pairs={{0,2},{1,3},{2,0},{3,1},{4,6},{5,7},{6,4},{7,5},{8,10},{9,11},{10,... | collective-permute-start | bytes 442376 | tf_op jit(solution)/shard_map/ppermute | solution.py:573
  53.7 1.4 %collective-permute-start.12 = (bf16[32,2048]{1,0:T(8,128)(2,1)S(1)}, bf16[32,2048]{1,0:T(8,128)(2,1)S(1)}, u32[]{:S(2)}, u32[]{:S(2)}) collective-permute-start(bf16[32,2048]{1,0:T(8,128)(2,1)S(1)} %merge.1.refs_0_), channel_id=1, source_target_pairs={{0,1},{1,0},{2,3},{3,2},{4,5},{5,4},{6,7},{7,6},{8,9},{9,8},{10,11... | collective-permute-start | bytes 393224 | tf_op jit(solution)/shard_map/ppermute | solution.py:573
  55.8 4.5 %collective-permute-start.13 = (bf16[16,640]{1,0:T(8,128)(2,1)S(1)}, bf16[16,640]{1,0:T(8,128)(2,1)S(1)}, u32[]{:S(2)}, u32[]{:S(2)}) collective-permute-start(bf16[16,640]{1,0:T(8,128)(2,1)S(1)} %get-tuple-element.30), channel_id=1, source_target_pairs={{0,8},{8,0},{16,24},{24,16},{1,9},{9,1},{17,25},{25,17},{2,10},{10... | collective-permute-start | bytes 61448 | tf_op jit(solution)/shard_map/ppermute | solution.py:573
  57.4 4.9 %collective-permute-start.14 = (bf16[16,640]{1,0:T(8,128)(2,1)S(1)}, bf16[16,640]{1,0:T(8,128)(2,1)S(1)}, u32[]{:S(2)}, u32[]{:S(2)}) collective-permute-start(bf16[16,640]{1,0:T(8,128)(2,1)S(1)} %get-tuple-element.31), channel_id=1, source_target_pairs={{0,16},{8,24},{16,0},{24,8},{1,17},{9,25},{17,1},{25,9},{2,18},{10... | collective-permute-start | bytes 61448 | tf_op jit(solution)/shard_map/ppermute | solution.py:573
  60.0 5.6 %collective-permute-start.15 = (bf16[16,640]{1,0:T(8,128)(2,1)S(1)}, bf16[16,640]{1,0:T(8,128)(2,1)S(1)}, u32[]{:S(2)}, u32[]{:S(2)}) collective-permute-start(bf16[16,640]{1,0:T(8,128)(2,1)S(1)} %get-tuple-element.32), channel_id=1, source_target_pairs={{0,24},{8,16},{16,8},{24,0},{1,25},{9,17},{17,9},{25,1},{2,26},{10... | collective-permute-start | bytes 61448 | tf_op jit(solution)/shard_map/ppermute | solution.py:573

commit v5 on v4

--- a/solution.py
+++ b/solution.py
@@ -15,8 +15,9 @@
 LANES = 128
 COLUMN_TILE = 256
 PAIR = 2
-TASKS = 16
-CHUNK = PAIR * TASKS
+GROUP = 4
+TASKS = 8
+CHUNK = GROUP * TASKS
 PHASES = 8
 AHEAD = 3
 DEPTH = 256
@@ -252,13 +253,13 @@
     lane = lax.broadcasted_iota(jnp.int32, (rows, blocks), 1).astype(jnp.float32)
     picks = [jnp.where(key[:, j : j + 1] == lane, 1.0, 0.0) for j in range(slots)]
     count = jnp.sum(functools.reduce(jnp.add, picks), axis=0, keepdims=True)
-    tasks = jnp.floor((count + (PAIR - 1)) * (1.0 / PAIR))
+    tasks = jnp.floor((count + (GROUP - 1)) * (1.0 / GROUP))
     earlier = jnp.dot(
         jnp.broadcast_to(tasks, (8, blocks)).astype(jnp.bfloat16),
         before(blocks, 0),
         preferred_element_type=jnp.float32,
     )[:1]
-    base = earlier * PAIR
+    base = earlier * GROUP
     row_before = before(rows, 1)
     slot = lax.broadcasted_iota(jnp.int32, (rows, slots), 1)
     place = jnp.full((rows, slots), -1.0, jnp.float32)
@@ -295,7 +296,7 @@
 def make_list(parts, slots, blocks, block_size, count):
     own, width = parts[0].shape
     rows = count * own
-    most = 2 * own * slots // count * count + (PAIR - 1) * blocks + 3 * CHUNK
+    most = 2 * own * slots // count * count + (GROUP - 1) * blocks + 3 * CHUNK
     capacity = -(-most // LANES) * LANES
     last = width // (PAIR * LANES) - 1
     return pl.pallas_call(
@@ -366,7 +367,7 @@
         return (entry >> length_bits) & (blocks - 1)
 
     def merge_item(row, t, k):
-        j = t * PAIR + k
+        j = t * GROUP + k
         top, part_top = top_ref[row], part_top_ref[j]
         high = jnp.maximum(top, part_top)
         top_ref[row] = high
@@ -375,7 +376,7 @@
         sum_ref[row] = sum_ref[row] * old + part_sum_ref[t, k * heads : (k + 1) * heads] * new
 
     def weigh_item(entry, t, k):
-        j = t * PAIR + k
+        j = t * GROUP + k
         scores = jnp.where(token <= (entry & (block_size - 1)), score_ref[t, k * heads : (k + 1) * heads], NEG_FILL)
         high = jnp.max(scores, axis=1, keepdims=True)
         weights = jnp.exp2((scores - high) * factor)
@@ -386,7 +387,7 @@
     def turn(i, carry):
         merged, weighed, scored = (entries(jnp.maximum(i - back, 0)) for back in (2, 1, 0))
         for t in range(TASKS):
-            task = slice(t * PAIR, (t + 1) * PAIR)
+            task = slice(t * GROUP, (t + 1) * GROUP)
             for k, entry in enumerate(merged[task]):
                 merge_item(jnp.where(i >= 2, row_of(entry), rows), t, k)
             weights = [weigh_item(entry, t, k) for k, entry in enumerate(weighed[task])]
@@ -447,10 +448,10 @@
             state,
             state,
             state,
-            pltpu.VMEM((TASKS, PAIR * heads, tokens), jnp.float32),
+            pltpu.VMEM((TASKS, GROUP * heads, tokens), jnp.float32),
             part,
             part,
-            pltpu.VMEM((TASKS, PAIR * heads, LANES), jnp.float32),
+            pltpu.VMEM((TASKS, GROUP * heads, LANES), jnp.float32),
             pltpu.SemaphoreType.DMA((2, PHASES)),
         ],
         compiler_params=params(40),
@@ -534,8 +535,7 @@
 
 def output_kernel(own, row_count, *refs):
     pieces, weight_ref = refs[:PAIR], refs[PAIR]
-    own_ref, sends = refs[PAIR + 1], refs[PAIR + 2 : PAIR + 1 + row_count]
-    rows_ref, terms_ref = refs[PAIR + 1 + row_count :]
+    keep_ref, send_ref, rows_ref, terms_ref = refs[PAIR + 1 :]
     me = lax.axis_index("kv")
     for t in range(PAIR):
         piece = pieces[t][...].astype(jnp.float32)
@@ -546,22 +546,22 @@
         rows_ref[...].astype(jnp.bfloat16), weight_ref[...], preferred_element_type=jnp.float32
     )
     me = lax.axis_index("row")
-    part = own_ref.shape[0]
-    for s, ref in enumerate((own_ref, *sends)):
+    part = keep_ref.shape[1]
+    for s in range(row_count):
         start = pl.multiple_of(jnp.bitwise_xor(me, s) * part, part)
-        ref[...] = terms_ref[pl.ds(start, part), :].astype(ref.dtype)
+        ref = (keep_ref, send_ref)[s % PAIR]
+        ref[s // PAIR] = terms_ref[pl.ds(start, part), :].astype(ref.dtype)
 
 
 def project_out(pieces, weight, own, row_count):
     half, width = pieces[0].shape
     rows, columns = PAIR * half, weight.shape[1]
-    part = rows // row_count
-    send = jax.ShapeDtypeStruct((part, columns), jnp.bfloat16)
+    shape = (row_count // PAIR, rows // row_count, columns)
     return pl.pallas_call(
         functools.partial(output_kernel, own, row_count),
         in_specs=[vmem_spec()] * (PAIR + 1),
-        out_specs=[vmem_spec()] * row_count,
-        out_shape=[jax.ShapeDtypeStruct((part, columns), jnp.float32)] + [send] * (row_count - 1),
+        out_specs=[vmem_spec()] * PAIR,
+        out_shape=[jax.ShapeDtypeStruct(shape, jnp.float32), jax.ShapeDtypeStruct(shape, jnp.bfloat16)],
         scratch_shapes=[pltpu.VMEM((rows, width), jnp.float32), pltpu.VMEM((rows, columns), jnp.float32)],
         compiler_params=params(24),
         name="project_out",
@@ -639,11 +639,14 @@
     keep, send = attend(items, bounds, queries, keys, values, kv_local, scale)
     merged = merge_pair(keep, exchange(send, "kv", 1), scale)
     attention = merge(gather_chips(merged), scale)
-    terms = project_out([attention, exchange(attention, "kv", 1)], output_weight, own, row_count)
-    total = terms[0]
-    for s in range(1, row_count):
-        total = total + exchange(terms[s], "row", s).astype(jnp.float32)
-    return total.astype(jnp.bfloat16)
+    keep, send = project_out([attention, exchange(attention, "kv", 1)], output_weight, own, row_count)
+    step = 1
+    while True:
+        total = keep + exchange(send, "row", step).astype(jnp.float32)
+        step *= 2
+        if step == row_count:
+            return total[0].astype(jnp.bfloat16)
+        keep, send = total[0::2], total[1::2]
 
 
 def solution(mesh):

time: 65.9 us -> 63.5 us (0.964); the launches traced: 66.2 us -> 62.9 us
  starting transfers between devices: 22.7 us -> 19.2 us
  Pallas kernels: 20.5 us -> 21.3 us
    ppermute x16 -> x15, starting transfers between devices: 22.7 us -> 19.2 us  [exchange(): return lax.ppermute(x, axis, [(i, i ^ s) for i in range(count)])]
    pallas_call x1, Pallas kernels: 11.1 us -> 11.9 us  [attend(): pl.pallas_call(functools.partial(attend_kernel, scale, heads // kv_local,...]
    ppermute x16 -> x15, waiting for transfers between devices: 21.9 us -> 21.3 us  [exchange(): return lax.ppermute(x, axis, [(i, i ^ s) for i in range(count)])]
  transfers between devices with their start and end apart: 16 -> 15, of which waited for: 12 -> 13; matrix products, arithmetic and copies ran while one was open for 0% -> 1% of each run, Pallas kernels for 4% -> 4%
where the time goes in v5:
time: 63.5 us; the launch traced here: 62.9 us
  Pallas kernels  21.3 us (34%)
  waiting for transfers between devices  21.3 us (34%)
  starting transfers between devices  19.2 us (30%)
  other arithmetic  0.95 us (1%)
    ppermute x15, waiting for transfers between devices, exchange(): return lax.ppermute(x, axis, [(i, i ^ s) for i in range(count)])  21.3 us
    ppermute x15, starting transfers between devices, exchange(): return lax.ppermute(x, axis, [(i, i ^ s) for i in range(count)])  19.2 us
    pallas_call x1, Pallas kernels, attend(): pl.pallas_call(functools.partial(attend_kernel, scale, heads // kv_local,...  11.9 us
    pallas_call x1, Pallas kernels, project(): pl.pallas_call(functools.partial(project_kernel, rank), in_specs=[vmem_sp...  5.14 us
    pallas_call x1, Pallas kernels, make_list(): pl.pallas_call(functools.partial(list_kernel, blocks, block_size, slots),...  2.44 us
  transfers between devices with their start and end apart: 15, of which 13 were waited for; matrix products, arithmetic and copies ran while one was open for 1% of the time, Pallas kernels for 4%

profile of v5, /device:TPU:0, one launch (start us, length us, event | category | flops | bytes accessed | tf_op | source)
XLA Modules:
  0.0 62.9 jit_solution(11262043577742036086)
XLA Ops:
  0.0 5.1 %project.1 = (f32[4,8,2176]{2,1,0:T(8,128)S(1)}, f32[4,8,2176]{2,1,0:T(8,128)S(1)}) custom-call(s32[1,64]{1,0:T(1,128)} %bitcast.24, s32[1,64]{1,0:T(1,128)} %bitcast.25, s32[8,32]{1,0:T(8,128)} %holder_ref.1, s32[8,32]{1,0:T(8,128)} %block_ref.1, s32[8,32]{1,0:T(8,128)} %length_ref.1, bf16[64,640]{1,0:T(8,128)(2,1)} %hidden_hbm.1, ...), custom_call_target="tpu_custom_call" | custom-call | tf_op jit(solution)/shard_map/project/pallas_call | solution.py:168
  5.2 0.5 collective-permute-start
  5.7 0.1 reduce_sum.9
  5.9 0.9 %collective-permute-done.got_ref = f32[4,8,2176]{2,1,0:T(8,128)S(1)} collective-permute-done((f32[4,8,2176]{2,1,0:T(8,128)S(1)}, f32[4,8,2176]{2,1,0:T(8,128)S(1)}, u32[]{:S(2)}, u32[]{:S(2)}) %collective-permute-start) | collective-permute-done | bytes 278560 | tf_op jit(solution)/shard_map/ppermute | solution.py:573
  6.9 2.9 %collective-permute-start.1 = (f32[8,2304]{1,0:T(8,128)S(1)}, f32[8,2304]{1,0:T(8,128)S(1)}, u32[]{:S(2)}, u32[]{:S(2)}) collective-permute-start(f32[8,2304]{1,0:T(8,128)S(1)} %get-tuple-element.20), channel_id=1, source_target_pairs={{0,2},{1,3},{2,0},{3,1},{4,6},{5,7},{6,4},{7,5},{8,10},{9,11},{10,... | collective-permute-start | bytes 221192 | tf_op jit(solution)/shard_map/ppermute | solution.py:573
  9.8 1.5 %collective-permute-start.2 = (f32[8,2304]{1,0:T(8,128)S(1)}, f32[8,2304]{1,0:T(8,128)S(1)}, u32[]{:S(2)}, u32[]{:S(2)}) collective-permute-start(f32[8,2304]{1,0:T(8,128)S(1)} %get-tuple-element.21), channel_id=1, source_target_pairs={{0,4},{1,5},{2,6},{3,7},{4,0},{5,1},{6,2},{7,3},{8,12},{9,13},{10,... | collective-permute-start | bytes 221192 | tf_op jit(solution)/shard_map/ppermute | solution.py:573
  11.4 1.0 %collective-permute-done.1.refs_1_ = f32[8,2304]{1,0:T(8,128)S(1)} collective-permute-done((f32[8,2304]{1,0:T(8,128)S(1)}, f32[8,2304]{1,0:T(8,128)S(1)}, u32[]{:S(2)}, u32[]{:S(2)}) %collective-permute-start.1) | collective-permute-done | bytes 73760 | tf_op jit(solution)/shard_map/ppermute | solution.py:573
  12.4 1.8 %collective-permute-done.2.refs_2_ = f32[8,2304]{1,0:T(8,128)S(1)} collective-permute-done((f32[8,2304]{1,0:T(8,128)S(1)}, f32[8,2304]{1,0:T(8,128)S(1)}, u32[]{:S(2)}, u32[]{:S(2)}) %collective-permute-start.2) | collective-permute-done | bytes 73760 | tf_op jit(solution)/shard_map/ppermute | solution.py:573
  14.2 2.4 %collective-permute-done.3.refs_3_ = f32[8,2304]{1,0:T(8,128)S(1)} collective-permute-done((f32[8,2304]{1,0:T(8,128)S(1)}, f32[8,2304]{1,0:T(8,128)S(1)}, u32[]{:S(2)}, u32[]{:S(2)}) %collective-permute-start.3) | collective-permute-done | bytes 73760 | tf_op jit(solution)/shard_map/ppermute | solution.py:573
  16.6 0.3 queries.1
  17.0 1.2 %collective-permute-done.4 = bf16[8,16,128]{2,1,0:T(8,128)(2,1)S(1)} collective-permute-done((bf16[8,16,128]{2,1,0:T(8,128)(2,1)S(1)}, bf16[8,16,128]{2,1,0:T(8,128)(2,1)S(1)}, u32[]{:S(2)}, u32[]{:S(2)}) %collective-permute-start.4) | collective-permute-done | bytes 32800 | tf_op jit(solution)/shard_map/ppermute | solution.py:573
  18.2 0.6 collective-permute-start.7
  18.8 1.5 %collective-permute-start.6 = (bf16[16,16,128]{2,1,0:T(8,128)(2,1)S(1)}, bf16[16,16,128]{2,1,0:T(8,128)(2,1)S(1)}, u32[]{:S(2)}, u32[]{:S(2)}) collective-permute-start(bf16[16,16,128]{2,1,0:T(8,128)(2,1)S(1)} %pad_maximum_fusion), channel_id=1, source_target_pairs={{0,4},{1,5},{2,6},{3,7},{4,0},{5,1},{6,2},{7,3},{8,12},{9,13},{10,... | collective-permute-start | bytes 196616 | tf_op jit(solution)/shard_map/ppermute | solution.py:573
  20.2 1.5 %collective-permute-start.5 = (bf16[16,16,128]{2,1,0:T(8,128)(2,1)S(1)}, bf16[16,16,128]{2,1,0:T(8,128)(2,1)S(1)}, u32[]{:S(2)}, u32[]{:S(2)}) collective-permute-start(bf16[16,16,128]{2,1,0:T(8,128)(2,1)S(1)} %pad_maximum_fusion), channel_id=1, source_target_pairs={{0,2},{1,3},{2,0},{3,1},{4,6},{5,7},{6,4},{7,5},{8,10},{9,11},{10,... | collective-permute-start | bytes 196616 | tf_op jit(solution)/shard_map/ppermute | solution.py:573
  21.7 2.4 %slot_list.1 = (s32[1,1024]{1,0:T(1,128)S(1)}, s32[1,128]{1,0:T(1,128)S(1)}) custom-call(f32[8,2304]{1,0:T(8,128)S(1)} %get-tuple-element.19.refs_0_, f32[8,2304]{1,0:T(8,128)S(1)} %collective-permute-done.1.refs_1_, f32[8,2304]{1,0:T(8,128)S(1)} %collective-permute-done.2.refs_2_, f32[8,2304]{1,0:T(8,128)S(1)} %collective-permute-done.3.refs_3_), custom_call_target="tpu_custom_call" | custom-call | flops 100000000 | bytes 10000000 | tf_op jit(solution)/shard_map/slot_list/pallas_call | solution.py:302
  24.2 0.3 collective-permute-done.5
  24.5 11.9 %attend.1 = (f32[4,9,16,128]{3,2,1,0:T(8,128)S(1)}, f32[4,9,16,128]{3,2,1,0:T(8,128)S(1)}) custom-call(s32[1,1024]{1,0:T(1,128)S(1)} %get-tuple-element.23.list_ref, s32[1,128]{1,0:T(1,128)S(1)} %get-tuple-element.24.bound_ref, bf16[2,8,16,128]{3,2,1,0:T(8,128)(2,1)S(1)} %bitcast.15, bf16[2,8,16,128]{3,2,1,0:T(8,128)(2,1)S(1)} %bitcast.18, ...), custom_call_target="tpu_custom_call" | custom-call | tf_op jit(solution)/shard_map/attend/pallas_call | solution.py:439
  36.5 1.6 %collective-permute-done.8.got_ref = f32[4,9,16,128]{3,2,1,0:T(8,128)S(1)} collective-permute-done((f32[4,9,16,128]{3,2,1,0:T(8,128)S(1)}, f32[4,9,16,128]{3,2,1,0:T(8,128)S(1)}, u32[]{:S(2)}, u32[]{:S(2)}) %collective-permute-start.8) | collective-permute-done | bytes 294944 | tf_op jit(solution)/shard_map/ppermute | solution.py:573
  38.0 0.3 merge_pair.1.refs_0_
  38.4 1.7 %collective-permute-start.11 = (bf16[4,9,16,128]{3,2,1,0:T(8,128)(2,1)S(1)}, bf16[4,9,16,128]{3,2,1,0:T(8,128)(2,1)S(1)}, u32[]{:S(2)}, u32[]{:S(2)}) collective-permute-start(bf16[4,9,16,128]{3,2,1,0:T(8,128)(2,1)S(1)} %merge_pair.1.refs_0_), channel_id=1, source_target_pairs={{0,6},{1,7},{2,4},{3,5},{4,2},{5,3},{6,0},{7,1},{8,14},{9,15},{10,... | collective-permute-start | bytes 442376 | tf_op jit(solution)/shard_map/ppermute | solution.py:573
  40.1 4.5 %collective-permute-start.10 = (bf16[4,9,16,128]{3,2,1,0:T(8,128)(2,1)S(1)}, bf16[4,9,16,128]{3,2,1,0:T(8,128)(2,1)S(1)}, u32[]{:S(2)}, u32[]{:S(2)}) collective-permute-start(bf16[4,9,16,128]{3,2,1,0:T(8,128)(2,1)S(1)} %merge_pair.1.refs_0_), channel_id=1, source_target_pairs={{0,4},{1,5},{2,6},{3,7},{4,0},{5,1},{6,2},{7,3},{8,12},{9,13},{10,... | collective-permute-start | bytes 442376 | tf_op jit(solution)/shard_map/ppermute | solution.py:573
  44.6 0.7 %collective-permute-done.11.refs_3_ = bf16[4,9,16,128]{3,2,1,0:T(8,128)(2,1)S(1)} collective-permute-done((bf16[4,9,16,128]{3,2,1,0:T(8,128)(2,1)S(1)}, bf16[4,9,16,128]{3,2,1,0:T(8,128)(2,1)S(1)}, u32[]{:S(2)}, u32[]{:S(2)}) %collective-permute-start.11) | collective-permute-done | bytes 147488 | tf_op jit(solution)/shard_map/ppermute | solution.py:573
  45.2 4.4 %collective-permute-done.10.refs_2_ = bf16[4,9,16,128]{3,2,1,0:T(8,128)(2,1)S(1)} collective-permute-done((bf16[4,9,16,128]{3,2,1,0:T(8,128)(2,1)S(1)}, bf16[4,9,16,128]{3,2,1,0:T(8,128)(2,1)S(1)}, u32[]{:S(2)}, u32[]{:S(2)}) %collective-permute-start.10) | collective-permute-done | bytes 147488 | tf_op jit(solution)/shard_map/ppermute | solution.py:573
  49.6 1.0 %collective-permute-done.9.refs_1_ = bf16[4,9,16,128]{3,2,1,0:T(8,128)(2,1)S(1)} collective-permute-done((bf16[4,9,16,128]{3,2,1,0:T(8,128)(2,1)S(1)}, bf16[4,9,16,128]{3,2,1,0:T(8,128)(2,1)S(1)}, u32[]{:S(2)}, u32[]{:S(2)}) %collective-permute-start.9) | collective-permute-done | bytes 147488 | tf_op jit(solution)/shard_map/ppermute | solution.py:573
  50.6 0.6 merge.1.refs_0_
  51.3 1.3 %collective-permute-done.12.refs_1_ = bf16[32,2048]{1,0:T(8,128)(2,1)S(1)} collective-permute-done((bf16[32,2048]{1,0:T(8,128)(2,1)S(1)}, bf16[32,2048]{1,0:T(8,128)(2,1)S(1)}, u32[]{:S(2)}, u32[]{:S(2)}) %collective-permute-start.12) | collective-permute-done | bytes 131104 | tf_op jit(solution)/shard_map/ppermute | solution.py:573
  52.6 0.6 project_out.1
  53.2 1.6 %collective-permute-start.13 = (bf16[2,16,640]{2,1,0:T(8,128)(2,1)S(1)}, bf16[2,16,640]{2,1,0:T(8,128)(2,1)S(1)}, u32[]{:S(2)}, u32[]{:S(2)}) collective-permute-start(bf16[2,16,640]{2,1,0:T(8,128)(2,1)S(1)} %get-tuple-element.28), channel_id=1, source_target_pairs={{0,8},{8,0},{16,24},{24,16},{1,9},{9,1},{17,25},{25,17},{2,10},{10... | collective-permute-start | bytes 122888 | tf_op jit(solution)/shard_map/ppermute | solution.py:573
  54.9 2.4 %collective-permute-done.13 = bf16[2,16,640]{2,1,0:T(8,128)(2,1)S(1)} collective-permute-done((bf16[2,16,640]{2,1,0:T(8,128)(2,1)S(1)}, bf16[2,16,640]{2,1,0:T(8,128)(2,1)S(1)}, u32[]{:S(2)}, u32[]{:S(2)}) %collective-permute-start.13) | collective-permute-done | bytes 40992 | tf_op jit(solution)/shard_map/ppermute | solution.py:573
  57.3 2.6 %collective-permute-start.14 = (f32[1,16,640]{2,1,0:T(8,128)S(1)}, f32[1,16,640]{2,1,0:T(8,128)S(1)}, u32[]{:S(2)}, u32[]{:S(2)}) collective-permute-start(f32[1,16,640]{2,1,0:T(8,128)S(1)} %slice.11), channel_id=1, source_target_pairs={{0,16},{8,24},{16,0},{24,8},{1,17},{9,25},{17,1},{25,9},{2,18},{10... | collective-permute-start | bytes 122888 | tf_op jit(solution)/shard_map/ppermute | solution.py:573
  60.0 2.3 %collective-permute-done.14 = f32[1,16,640]{2,1,0:T(8,128)S(1)} collective-permute-done((f32[1,16,640]{2,1,0:T(8,128)S(1)}, f32[1,16,640]{2,1,0:T(8,128)S(1)}, u32[]{:S(2)}, u32[]{:S(2)}) %collective-permute-start.14) | collective-permute-done | bytes 40992 | tf_op jit(solution)/shard_map/ppermute | solution.py:573
  62.3 0.6 fusion.1
  (21 shorter events, 0.5 us)
Async XLA Ops:
  0.0 5.7 %copy-start.2 = (s32[8,32]{1,0:T(8,128)S(1)}, s32[8,32]{1,0:T(8,128)}, u32[]{:S(2)}) copy-start(s32[8,32]{1,0:T(8,128)} %length_ref.1) | copy-start | bytes 3076
  0.0 16.6 %copy-start.1 = (f32[128]{0:T(128)S(1)}, f32[128]{0:T(128)}, u32[]{:S(2)}) copy-start(f32[128]{0:T(128)} %param.17) | copy-start | bytes 1540
  5.2 1.7 %collective-permute-start = (f32[4,8,2176]{2,1,0:T(8,128)S(1)}, f32[4,8,2176]{2,1,0:T(8,128)S(1)}, u32[]{:S(2)}, u32[]{:S(2)}) collective-permute-start(f32[4,8,2176]{2,1,0:T(8,128)S(1)} %get-tuple-element.18), channel_id=1, source_target_pairs={{0,1},{1,0},{2,3},{3,2},{4,5},{5,4},{6,7},{7,6},{8,9},{9,8},{10,11... | collective-permute-start | bytes 835592 | tf_op jit(solution)/shard_map/ppermute | solution.py:573
  6.9 5.5 %collective-permute-start.1 = (f32[8,2304]{1,0:T(8,128)S(1)}, f32[8,2304]{1,0:T(8,128)S(1)}, u32[]{:S(2)}, u32[]{:S(2)}) collective-permute-start(f32[8,2304]{1,0:T(8,128)S(1)} %get-tuple-element.20), channel_id=1, source_target_pairs={{0,2},{1,3},{2,0},{3,1},{4,6},{5,7},{6,4},{7,5},{8,10},{9,11},{10,... | collective-permute-start | bytes 221192 | tf_op jit(solution)/shard_map/ppermute | solution.py:573
  9.8 4.4 %collective-permute-start.2 = (f32[8,2304]{1,0:T(8,128)S(1)}, f32[8,2304]{1,0:T(8,128)S(1)}, u32[]{:S(2)}, u32[]{:S(2)}) collective-permute-start(f32[8,2304]{1,0:T(8,128)S(1)} %get-tuple-element.21), channel_id=1, source_target_pairs={{0,4},{1,5},{2,6},{3,7},{4,0},{5,1},{6,2},{7,3},{8,12},{9,13},{10,... | collective-permute-start | bytes 221192 | tf_op jit(solution)/shard_map/ppermute | solution.py:573
  11.3 5.3 %collective-permute-start.3 = (f32[8,2304]{1,0:T(8,128)S(1)}, f32[8,2304]{1,0:T(8,128)S(1)}, u32[]{:S(2)}, u32[]{:S(2)}) collective-permute-start(f32[8,2304]{1,0:T(8,128)S(1)} %get-tuple-element.22), channel_id=1, source_target_pairs={{0,6},{1,7},{2,4},{3,5},{4,2},{5,3},{6,0},{7,1},{8,14},{9,15},{10,... | collective-permute-start | bytes 221192 | tf_op jit(solution)/shard_map/ppermute | solution.py:573
  16.9 1.3 %collective-permute-start.4 = (bf16[8,16,128]{2,1,0:T(8,128)(2,1)S(1)}, bf16[8,16,128]{2,1,0:T(8,128)(2,1)S(1)}, u32[]{:S(2)}, u32[]{:S(2)}) collective-permute-start(bf16[8,16,128]{2,1,0:T(8,128)(2,1)S(1)} %queries.1), channel_id=1, source_target_pairs={{0,1},{1,0},{2,3},{3,2},{4,5},{5,4},{6,7},{7,6},{8,9},{9,8},{10,11... | collective-permute-start | bytes 98312 | tf_op jit(solution)/shard_map/ppermute | solution.py:573
  18.2 6.0 %collective-permute-start.7 = (bf16[16,16,128]{2,1,0:T(8,128)(2,1)S(1)}, bf16[16,16,128]{2,1,0:T(8,128)(2,1)S(1)}, u32[]{:S(2)}, u32[]{:S(2)}) collective-permute-start(bf16[16,16,128]{2,1,0:T(8,128)(2,1)S(1)} %pad_maximum_fusion), channel_id=1, source_target_pairs={{0,6},{1,7},{2,4},{3,5},{4,2},{5,3},{6,0},{7,1},{8,14},{9,15},{10,... | collective-permute-start | bytes 196616 | tf_op jit(solution)/shard_map/ppermute | solution.py:573
  18.8 5.4 %collective-permute-start.6 = (bf16[16,16,128]{2,1,0:T(8,128)(2,1)S(1)}, bf16[16,16,128]{2,1,0:T(8,128)(2,1)S(1)}, u32[]{:S(2)}, u32[]{:S(2)}) collective-permute-start(bf16[16,16,128]{2,1,0:T(8,128)(2,1)S(1)} %pad_maximum_fusion), channel_id=1, source_target_pairs={{0,4},{1,5},{2,6},{3,7},{4,0},{5,1},{6,2},{7,3},{8,12},{9,13},{10,... | collective-permute-start | bytes 196616 | tf_op jit(solution)/shard_map/ppermute | solution.py:573
  20.2 4.3 %collective-permute-start.5 = (bf16[16,16,128]{2,1,0:T(8,128)(2,1)S(1)}, bf16[16,16,128]{2,1,0:T(8,128)(2,1)S(1)}, u32[]{:S(2)}, u32[]{:S(2)}) collective-permute-start(bf16[16,16,128]{2,1,0:T(8,128)(2,1)S(1)} %pad_maximum_fusion), channel_id=1, source_target_pairs={{0,2},{1,3},{2,0},{3,1},{4,6},{5,7},{6,4},{7,5},{8,10},{9,11},{10,... | collective-permute-start | bytes 196616 | tf_op jit(solution)/shard_map/ppermute | solution.py:573
  24.5 28.1 %copy-start = (bf16[2048,640]{1,0:T(8,128)(2,1)S(1)}, bf16[2048,640]{1,0:T(8,128)(2,1)}, u32[]{:S(2)}) copy-start(bf16[2048,640]{1,0:T(8,128)(2,1)} %refs_2_.1) | copy-start | bytes 7864324
  36.4 1.6 %collective-permute-start.8 = (f32[4,9,16,128]{3,2,1,0:T(8,128)S(1)}, f32[4,9,16,128]{3,2,1,0:T(8,128)S(1)}, u32[]{:S(2)}, u32[]{:S(2)}) collective-permute-start(f32[4,9,16,128]{3,2,1,0:T(8,128)S(1)} %get-tuple-element.26), channel_id=1, source_target_pairs={{0,1},{1,0},{2,3},{3,2},{4,5},{5,4},{6,7},{7,6},{8,9},{9,8},{10,11... | collective-permute-start | bytes 884744 | tf_op jit(solution)/shard_map/ppermute | solution.py:573
  38.4 6.9 %collective-permute-start.11 = (bf16[4,9,16,128]{3,2,1,0:T(8,128)(2,1)S(1)}, bf16[4,9,16,128]{3,2,1,0:T(8,128)(2,1)S(1)}, u32[]{:S(2)}, u32[]{:S(2)}) collective-permute-start(bf16[4,9,16,128]{3,2,1,0:T(8,128)(2,1)S(1)} %merge_pair.1.refs_0_), channel_id=1, source_target_pairs={{0,6},{1,7},{2,4},{3,5},{4,2},{5,3},{6,0},{7,1},{8,14},{9,15},{10,... | collective-permute-start | bytes 442376 | tf_op jit(solution)/shard_map/ppermute | solution.py:573
  40.1 9.6 %collective-permute-start.10 = (bf16[4,9,16,128]{3,2,1,0:T(8,128)(2,1)S(1)}, bf16[4,9,16,128]{3,2,1,0:T(8,128)(2,1)S(1)}, u32[]{:S(2)}, u32[]{:S(2)}) collective-permute-start(bf16[4,9,16,128]{3,2,1,0:T(8,128)(2,1)S(1)} %merge_pair.1.refs_0_), channel_id=1, source_target_pairs={{0,4},{1,5},{2,6},{3,7},{4,0},{5,1},{6,2},{7,3},{8,12},{9,13},{10,... | collective-permute-start | bytes 442376 | tf_op jit(solution)/shard_map/ppermute | solution.py:573
  44.6 6.1 %collective-permute-start.9 = (bf16[4,9,16,128]{3,2,1,0:T(8,128)(2,1)S(1)}, bf16[4,9,16,128]{3,2,1,0:T(8,128)(2,1)S(1)}, u32[]{:S(2)}, u32[]{:S(2)}) collective-permute-start(bf16[4,9,16,128]{3,2,1,0:T(8,128)(2,1)S(1)} %merge_pair.1.refs_0_), channel_id=1, source_target_pairs={{0,2},{1,3},{2,0},{3,1},{4,6},{5,7},{6,4},{7,5},{8,10},{9,11},{10,... | collective-permute-start | bytes 442376 | tf_op jit(solution)/shard_map/ppermute | solution.py:573
  51.2 1.4 %collective-permute-start.12 = (bf16[32,2048]{1,0:T(8,128)(2,1)S(1)}, bf16[32,2048]{1,0:T(8,128)(2,1)S(1)}, u32[]{:S(2)}, u32[]{:S(2)}) collective-permute-start(bf16[32,2048]{1,0:T(8,128)(2,1)S(1)} %merge.1.refs_0_), channel_id=1, source_target_pairs={{0,1},{1,0},{2,3},{3,2},{4,5},{5,4},{6,7},{7,6},{8,9},{9,8},{10,11... | collective-permute-start | bytes 393224 | tf_op jit(solution)/shard_map/ppermute | solution.py:573
  53.2 4.1 %collective-permute-start.13 = (bf16[2,16,640]{2,1,0:T(8,128)(2,1)S(1)}, bf16[2,16,640]{2,1,0:T(8,128)(2,1)S(1)}, u32[]{:S(2)}, u32[]{:S(2)}) collective-permute-start(bf16[2,16,640]{2,1,0:T(8,128)(2,1)S(1)} %get-tuple-element.28), channel_id=1, source_target_pairs={{0,8},{8,0},{16,24},{24,16},{1,9},{9,1},{17,25},{25,17},{2,10},{10... | collective-permute-start | bytes 122888 | tf_op jit(solution)/shard_map/ppermute | solution.py:573
  57.3 5.0 %collective-permute-start.14 = (f32[1,16,640]{2,1,0:T(8,128)S(1)}, f32[1,16,640]{2,1,0:T(8,128)S(1)}, u32[]{:S(2)}, u32[]{:S(2)}) collective-permute-start(f32[1,16,640]{2,1,0:T(8,128)S(1)} %slice.11), channel_id=1, source_target_pairs={{0,16},{8,24},{16,0},{24,8},{1,17},{9,25},{17,1},{25,9},{2,18},{10... | collective-permute-start | bytes 122888 | tf_op jit(solution)/shard_map/ppermute | solution.py:573

commit v6 on v5

--- a/solution.py
+++ b/solution.py
@@ -18,8 +18,8 @@
 GROUP = 4
 TASKS = 8
 CHUNK = GROUP * TASKS
-PHASES = 8
-AHEAD = 3
+PHASES = 16
+AHEAD = 6
 DEPTH = 256
 LOG2E = math.log2(math.e)
 MIB = 1024 * 1024
@@ -39,10 +39,6 @@
 
 def hbm_spec():
     return pl.BlockSpec(memory_space=pltpu.HBM)
-
-
-def smem_spec():
-    return pl.BlockSpec(memory_space=pltpu.SMEM)
 
 
 def split2(x):
@@ -318,10 +314,10 @@
     )(*parts)
 
 
-def attend_kernel(scale, group, kv_local, count, list_ref, bound_ref, *refs):
+def attend_kernel(scale, kv_local, count, list_vmem, bound_vmem, *refs):
     queries, refs = refs[: count // PAIR], refs[count // PAIR :]
-    (key_hbm, value_hbm, keep_ref, send_ref, query_ref, key_ref, value_ref, top_ref, total_ref, sum_ref) = refs[:10]
-    (score_ref, part_top_ref, part_total_ref, part_sum_ref, sems) = refs[10:]
+    (key_hbm, value_hbm, keep_ref, send_ref, list_ref, bound_ref, query_ref, key_ref, value_ref) = refs[:9]
+    (top_ref, total_ref, sum_ref, score_ref, part_top_ref, part_total_ref, part_sum_ref, number_sems, sems) = refs[9:]
     heads = query_ref.shape[1]
     rows = query_ref.shape[0] - 1
     own = rows // count
@@ -339,7 +335,11 @@
                 pltpu.make_async_copy(value_hbm.at[here], value_ref.at[here], sems.at[1, part]),
             )
         )
-    for pair in copies[:AHEAD]:
+    numbers = (
+        pltpu.make_async_copy(list_vmem, list_ref, number_sems.at[0]),
+        pltpu.make_async_copy(bound_vmem, bound_ref, number_sems.at[1]),
+    )
+    for pair in (copies[0], numbers, *copies[1:AHEAD]):
         for copy in pair:
             copy.start()
 
@@ -352,10 +352,11 @@
     top_ref[...] = jnp.full(top_ref.shape, NEG_FILL, jnp.float32)
     for ref in (total_ref, sum_ref, score_ref, part_top_ref, part_total_ref, part_sum_ref):
         ref[...] = jnp.zeros(ref.shape, jnp.float32)
-    head = lax.broadcasted_iota(jnp.int32, (heads, tokens), 0) // group
-    place = lax.broadcasted_iota(jnp.int32, (heads, tokens), 1)
-    token = jnp.where(place % kv_local == head, place // kv_local, block_size)
+    group = heads // kv_local
+    column = lax.broadcasted_iota(jnp.int32, (group, tokens), 1)
+    first = column % kv_local == 0
     wide = (heads, LANES)
+    narrow = (group, LANES)
 
     def entries(chunk):
         return [list_ref[0, chunk * CHUNK + j] for j in range(CHUNK)]
@@ -369,50 +370,67 @@
     def merge_item(row, t, k):
         j = t * GROUP + k
         top, part_top = top_ref[row], part_top_ref[j]
-        high = jnp.maximum(top, part_top)
-        top_ref[row] = high
-        old, new = jnp.exp2((top - high) * factor), jnp.exp2((part_top - high) * factor)
+        top_ref[row] = jnp.maximum(top, part_top)
+        share = jnp.exp2(-jnp.abs(top - part_top) * factor)
+        lower = top < part_top
+        old, new = jnp.where(lower, share, 1.0), jnp.where(lower, 1.0, share)
         total_ref[row] = total_ref[row] * old + part_total_ref[j] * new
         sum_ref[row] = sum_ref[row] * old + part_sum_ref[t, k * heads : (k + 1) * heads] * new
 
     def weigh_item(entry, t, k):
         j = t * GROUP + k
-        scores = jnp.where(token <= (entry & (block_size - 1)), score_ref[t, k * heads : (k + 1) * heads], NEG_FILL)
-        high = jnp.max(scores, axis=1, keepdims=True)
-        weights = jnp.exp2((scores - high) * factor)
-        part_top_ref[j] = jnp.broadcast_to(high, wide)
-        part_total_ref[j] = jnp.broadcast_to(jnp.sum(weights, axis=1, keepdims=True), wide)
-        return weights.astype(jnp.bfloat16)
-
-    def turn(i, carry):
+        start = k * heads
+        scores = jnp.where(
+            first, score_ref[t, start : start + group], score_ref[t, start + group : start + heads]
+        )
+        length = (entry & (block_size - 1)) + 1
+        scores = jnp.where(column < length * kv_local, scores, NEG_FILL)
+        tops = [
+            jnp.max(x, axis=1, keepdims=True)
+            for x in (jnp.where(first, scores, NEG_FILL), jnp.where(first, NEG_FILL, scores))
+        ]
+        weights = jnp.exp2((scores - jnp.where(first, tops[0], tops[1])) * factor)
+        weights = (jnp.where(first, weights, 0.0), jnp.where(first, 0.0, weights))
+        for a in range(kv_local):
+            here = slice(a * group, (a + 1) * group)
+            part_top_ref[j, here] = jnp.broadcast_to(tops[a], narrow)
+            part_total_ref[j, here] = jnp.broadcast_to(jnp.sum(weights[a], axis=1, keepdims=True), narrow)
+        return jnp.concatenate(weights, axis=0).astype(jnp.bfloat16)
+
+    def turn(stages, i, carry):
         merged, weighed, scored = (entries(jnp.maximum(i - back, 0)) for back in (2, 1, 0))
         for t in range(TASKS):
             task = slice(t * GROUP, (t + 1) * GROUP)
             for k, entry in enumerate(merged[task]):
                 merge_item(jnp.where(i >= 2, row_of(entry), rows), t, k)
-            weights = [weigh_item(entry, t, k) for k, entry in enumerate(weighed[task])]
-            part_sum_ref[t] = jnp.dot(
-                jnp.concatenate(weights, axis=0),
-                value_ref[block_of(weighed[task][0])],
-                preferred_element_type=jnp.float32,
-            )
-            score_ref[t] = lax.dot_general(
-                jnp.concatenate([query_ref[row_of(entry)] for entry in scored[task]], axis=0),
-                key_ref[block_of(scored[task][0])],
-                (((1,), (1,)), ((), ())),
-                preferred_element_type=jnp.float32,
-            )
+            if stages > 1:
+                weights = [weigh_item(entry, t, k) for k, entry in enumerate(weighed[task])]
+                part_sum_ref[t] = jnp.dot(
+                    jnp.concatenate(weights, axis=0),
+                    value_ref[block_of(weighed[task][0])],
+                    preferred_element_type=jnp.float32,
+                )
+            if stages > 2:
+                score_ref[t] = lax.dot_general(
+                    jnp.concatenate([query_ref[row_of(entry)] for entry in scored[task]], axis=0),
+                    key_ref[block_of(scored[task][0])],
+                    (((1,), (1,)), ((), ())),
+                    preferred_element_type=jnp.float32,
+                )
         return carry
 
+    for copy in numbers:
+        copy.wait()
     for part in range(PHASES):
         for copy in copies[part]:
             copy.wait()
         for pair in copies[part + AHEAD : part + AHEAD + 1]:
             for copy in pair:
                 copy.start()
-        lax.fori_loop(bound_ref[0, part], bound_ref[0, part + 1], turn, 0)
+        lax.fori_loop(bound_ref[0, part], bound_ref[0, part + 1], functools.partial(turn, 3), 0)
     last = bound_ref[0, PHASES]
-    lax.fori_loop(last, last + 2, turn, 0)
+    turn(2, last, 0)
+    turn(1, last + 1, 0)
 
     square = (own * heads, LANES)
     eye = lax.broadcasted_iota(jnp.int32, square, 0) == lax.broadcasted_iota(jnp.int32, square, 1)
@@ -437,11 +455,13 @@
     state = pltpu.VMEM((rows + 1, heads, LANES), jnp.float32)
     part = pltpu.VMEM((CHUNK, heads, LANES), jnp.float32)
     return pl.pallas_call(
-        functools.partial(attend_kernel, scale, heads // kv_local, kv_local, count),
-        in_specs=[smem_spec(), smem_spec()] + [vmem_spec()] * len(queries) + [hbm_spec()] * 2,
+        functools.partial(attend_kernel, scale, kv_local, count),
+        in_specs=[vmem_spec()] * (2 + len(queries)) + [hbm_spec()] * 2,
         out_specs=[vmem_spec()] * PAIR,
         out_shape=[jax.ShapeDtypeStruct((count // PAIR, own + 1, heads, LANES), jnp.float32)] * PAIR,
         scratch_shapes=[
+            pltpu.SMEM(items.shape, items.dtype),
+            pltpu.SMEM(bounds.shape, bounds.dtype),
             pltpu.VMEM((rows + 1, heads, LANES), jnp.bfloat16),
             pltpu.VMEM(keys.shape, keys.dtype),
             pltpu.VMEM(values.shape, values.dtype),
@@ -452,6 +472,7 @@
             part,
             part,
             pltpu.VMEM((TASKS, GROUP * heads, LANES), jnp.float32),
+            pltpu.SemaphoreType.DMA((2,)),
             pltpu.SemaphoreType.DMA((2, PHASES)),
         ],
         compiler_params=params(40),
@@ -533,9 +554,9 @@
     )(*pieces)
 
 
-def output_kernel(own, row_count, *refs):
+def output_kernel(own, *refs):
     pieces, weight_ref = refs[:PAIR], refs[PAIR]
-    keep_ref, send_ref, rows_ref, terms_ref = refs[PAIR + 1 :]
+    outs, (rows_ref, terms_ref) = refs[PAIR + 1 : -2], refs[-2:]
     me = lax.axis_index("kv")
     for t in range(PAIR):
         piece = pieces[t][...].astype(jnp.float32)
@@ -546,22 +567,22 @@
         rows_ref[...].astype(jnp.bfloat16), weight_ref[...], preferred_element_type=jnp.float32
     )
     me = lax.axis_index("row")
-    part = keep_ref.shape[1]
-    for s in range(row_count):
+    part = outs[0].shape[0]
+    for s, ref in enumerate(outs):
         start = pl.multiple_of(jnp.bitwise_xor(me, s) * part, part)
-        ref = (keep_ref, send_ref)[s % PAIR]
-        ref[s // PAIR] = terms_ref[pl.ds(start, part), :].astype(ref.dtype)
+        ref[...] = terms_ref[pl.ds(start, part), :].astype(ref.dtype)
 
 
 def project_out(pieces, weight, own, row_count):
     half, width = pieces[0].shape
     rows, columns = PAIR * half, weight.shape[1]
-    shape = (row_count // PAIR, rows // row_count, columns)
-    return pl.pallas_call(
-        functools.partial(output_kernel, own, row_count),
+    shape = (rows // row_count, columns)
+    send = jax.ShapeDtypeStruct(shape, jnp.bfloat16)
+    return pl.pallas_call(
+        functools.partial(output_kernel, own),
         in_specs=[vmem_spec()] * (PAIR + 1),
-        out_specs=[vmem_spec()] * PAIR,
-        out_shape=[jax.ShapeDtypeStruct(shape, jnp.float32), jax.ShapeDtypeStruct(shape, jnp.bfloat16)],
+        out_specs=[vmem_spec()] * row_count,
+        out_shape=[jax.ShapeDtypeStruct(shape, jnp.float32)] + [send] * (row_count - 1),
         scratch_shapes=[pltpu.VMEM((rows, width), jnp.float32), pltpu.VMEM((rows, columns), jnp.float32)],
         compiler_params=params(24),
         name="project_out",
@@ -639,14 +660,11 @@
     keep, send = attend(items, bounds, queries, keys, values, kv_local, scale)
     merged = merge_pair(keep, exchange(send, "kv", 1), scale)
     attention = merge(gather_chips(merged), scale)
-    keep, send = project_out([attention, exchange(attention, "kv", 1)], output_weight, own, row_count)
-    step = 1
-    while True:
-        total = keep + exchange(send, "row", step).astype(jnp.float32)
-        step *= 2
-        if step == row_count:
-            return total[0].astype(jnp.bfloat16)
-        keep, send = total[0::2], total[1::2]
+    terms = project_out([attention, exchange(attention, "kv", 1)], output_weight, own, row_count)
+    total = terms[0]
+    for s in range(1, row_count):
+        total = total + exchange(terms[s], "row", s).astype(jnp.float32)
+    return total.astype(jnp.bfloat16)
 
 
 def solution(mesh):

time: 63.5 us -> 63.4 us (level); the launches traced: 62.9 us -> 63.5 us
  waiting for transfers between devices: 21.3 us -> 22.9 us
  Pallas kernels: 21.3 us -> 20.1 us
    ppermute x15 -> x16, waiting for transfers between devices: 21.3 us -> 22.9 us  [exchange(): return lax.ppermute(x, axis, [(i, i ^ s) for i in range(count)])]
    pallas_call x2, Pallas kernels: 12.5 us -> 11.3 us  [the longest x1 10.6 us: attend(): pl.pallas_call(functools.partial(attend_kernel, scale, kv_local, count),...]
    ppermute x15 -> x16, starting transfers between devices: 19.2 us -> 19.4 us  [exchange(): return lax.ppermute(x, axis, [(i, i ^ s) for i in range(count)])]
  transfers between devices with their start and end apart: 15 -> 16, of which waited for: 13 -> 13; matrix products, arithmetic and copies ran while one was open for 1% -> 1% of each run, Pallas kernels for 4% -> 4%
where the time goes in v6:
time: 63.4 us; the launch traced here: 63.5 us
  waiting for transfers between devices  22.9 us (36%)
  Pallas kernels  20.1 us (32%)
  starting transfers between devices  19.4 us (31%)
  other arithmetic  0.95 us (1%)
    ppermute x16, waiting for transfers between devices, exchange(): return lax.ppermute(x, axis, [(i, i ^ s) for i in range(count)])  22.9 us
    ppermute x16, starting transfers between devices, exchange(): return lax.ppermute(x, axis, [(i, i ^ s) for i in range(count)])  19.4 us
    pallas_call x1, Pallas kernels, attend(): pl.pallas_call(functools.partial(attend_kernel, scale, kv_local, count),...  10.6 us
    pallas_call x1, Pallas kernels, project(): pl.pallas_call(functools.partial(project_kernel, rank), in_specs=[vmem_sp...  5.14 us
    pallas_call x1, Pallas kernels, make_list(): pl.pallas_call(functools.partial(list_kernel, blocks, block_size, slots),...  2.44 us
  transfers between devices with their start and end apart: 16, of which 13 were waited for; matrix products, arithmetic and copies ran while one was open for 1% of the time, Pallas kernels for 4%

profile of v6, /device:TPU:0, one launch (start us, length us, event | category | flops | bytes accessed | tf_op | source)
XLA Modules:
  0.0 63.5 jit_solution(2871240473180085845)
XLA Ops:
  0.0 5.1 %project.1 = (f32[4,8,2176]{2,1,0:T(8,128)S(1)}, f32[4,8,2176]{2,1,0:T(8,128)S(1)}) custom-call(s32[1,64]{1,0:T(1,128)} %bitcast.22, s32[1,64]{1,0:T(1,128)} %bitcast.23, s32[8,32]{1,0:T(8,128)} %holder_ref.1, s32[8,32]{1,0:T(8,128)} %block_ref.1, s32[8,32]{1,0:T(8,128)} %length_ref.1, bf16[64,640]{1,0:T(8,128)(2,1)} %hidden_hbm.1, ...), custom_call_target="tpu_custom_call" | custom-call | tf_op jit(solution)/shard_map/project/pallas_call | solution.py:164
  5.2 0.5 collective-permute-start
  5.9 0.9 %collective-permute-done.got_ref = f32[4,8,2176]{2,1,0:T(8,128)S(1)} collective-permute-done((f32[4,8,2176]{2,1,0:T(8,128)S(1)}, f32[4,8,2176]{2,1,0:T(8,128)S(1)}, u32[]{:S(2)}, u32[]{:S(2)}) %collective-permute-start) | collective-permute-done | bytes 278560 | tf_op jit(solution)/shard_map/ppermute | solution.py:594
  6.9 2.9 %collective-permute-start.1 = (f32[8,2304]{1,0:T(8,128)S(1)}, f32[8,2304]{1,0:T(8,128)S(1)}, u32[]{:S(2)}, u32[]{:S(2)}) collective-permute-start(f32[8,2304]{1,0:T(8,128)S(1)} %get-tuple-element.22), channel_id=1, source_target_pairs={{0,2},{1,3},{2,0},{3,1},{4,6},{5,7},{6,4},{7,5},{8,10},{9,11},{10,... | collective-permute-start | bytes 221192 | tf_op jit(solution)/shard_map/ppermute | solution.py:594
  9.8 1.5 %collective-permute-start.2 = (f32[8,2304]{1,0:T(8,128)S(1)}, f32[8,2304]{1,0:T(8,128)S(1)}, u32[]{:S(2)}, u32[]{:S(2)}) collective-permute-start(f32[8,2304]{1,0:T(8,128)S(1)} %get-tuple-element.23), channel_id=1, source_target_pairs={{0,4},{1,5},{2,6},{3,7},{4,0},{5,1},{6,2},{7,3},{8,12},{9,13},{10,... | collective-permute-start | bytes 221192 | tf_op jit(solution)/shard_map/ppermute | solution.py:594
  11.4 1.0 %collective-permute-done.1.refs_1_ = f32[8,2304]{1,0:T(8,128)S(1)} collective-permute-done((f32[8,2304]{1,0:T(8,128)S(1)}, f32[8,2304]{1,0:T(8,128)S(1)}, u32[]{:S(2)}, u32[]{:S(2)}) %collective-permute-start.1) | collective-permute-done | bytes 73760 | tf_op jit(solution)/shard_map/ppermute | solution.py:594
  12.4 1.8 %collective-permute-done.2.refs_2_ = f32[8,2304]{1,0:T(8,128)S(1)} collective-permute-done((f32[8,2304]{1,0:T(8,128)S(1)}, f32[8,2304]{1,0:T(8,128)S(1)}, u32[]{:S(2)}, u32[]{:S(2)}) %collective-permute-start.2) | collective-permute-done | bytes 73760 | tf_op jit(solution)/shard_map/ppermute | solution.py:594
  14.2 2.4 %collective-permute-done.3.refs_3_ = f32[8,2304]{1,0:T(8,128)S(1)} collective-permute-done((f32[8,2304]{1,0:T(8,128)S(1)}, f32[8,2304]{1,0:T(8,128)S(1)}, u32[]{:S(2)}, u32[]{:S(2)}) %collective-permute-start.3) | collective-permute-done | bytes 73760 | tf_op jit(solution)/shard_map/ppermute | solution.py:594
  16.6 0.3 queries.1
  17.0 1.2 %collective-permute-done.4 = bf16[8,16,128]{2,1,0:T(8,128)(2,1)S(1)} collective-permute-done((bf16[8,16,128]{2,1,0:T(8,128)(2,1)S(1)}, bf16[8,16,128]{2,1,0:T(8,128)(2,1)S(1)}, u32[]{:S(2)}, u32[]{:S(2)}) %collective-permute-start.4) | collective-permute-done | bytes 32800 | tf_op jit(solution)/shard_map/ppermute | solution.py:594
  18.2 0.6 collective-permute-start.7
  18.8 1.5 %collective-permute-start.6 = (bf16[16,16,128]{2,1,0:T(8,128)(2,1)S(1)}, bf16[16,16,128]{2,1,0:T(8,128)(2,1)S(1)}, u32[]{:S(2)}, u32[]{:S(2)}) collective-permute-start(bf16[16,16,128]{2,1,0:T(8,128)(2,1)S(1)} %pad_maximum_fusion), channel_id=1, source_target_pairs={{0,4},{1,5},{2,6},{3,7},{4,0},{5,1},{6,2},{7,3},{8,12},{9,13},{10,... | collective-permute-start | bytes 196616 | tf_op jit(solution)/shard_map/ppermute | solution.py:594
  20.2 1.5 %collective-permute-start.5 = (bf16[16,16,128]{2,1,0:T(8,128)(2,1)S(1)}, bf16[16,16,128]{2,1,0:T(8,128)(2,1)S(1)}, u32[]{:S(2)}, u32[]{:S(2)}) collective-permute-start(bf16[16,16,128]{2,1,0:T(8,128)(2,1)S(1)} %pad_maximum_fusion), channel_id=1, source_target_pairs={{0,2},{1,3},{2,0},{3,1},{4,6},{5,7},{6,4},{7,5},{8,10},{9,11},{10,... | collective-permute-start | bytes 196616 | tf_op jit(solution)/shard_map/ppermute | solution.py:594
  21.7 2.4 %slot_list.1 = (s32[1,1024]{1,0:T(1,128)S(1)}, s32[1,128]{1,0:T(1,128)S(1)}) custom-call(f32[8,2304]{1,0:T(8,128)S(1)} %get-tuple-element.21.refs_0_, f32[8,2304]{1,0:T(8,128)S(1)} %collective-permute-done.1.refs_1_, f32[8,2304]{1,0:T(8,128)S(1)} %collective-permute-done.2.refs_2_, f32[8,2304]{1,0:T(8,128)S(1)} %collective-permute-done.3.refs_3_), custom_call_target="tpu_custom_call" | custom-call | flops 100000000 | bytes 10000000 | tf_op jit(solution)/shard_map/slot_list/pallas_call | solution.py:298
  24.2 0.3 collective-permute-done.5
  24.5 10.6 %attend.1 = (f32[4,9,16,128]{3,2,1,0:T(8,128)S(1)}, f32[4,9,16,128]{3,2,1,0:T(8,128)S(1)}) custom-call(s32[1,1024]{1,0:T(1,128)S(1)} %get-tuple-element.25.list_vmem, s32[1,128]{1,0:T(1,128)S(1)} %get-tuple-element.26.bound_vmem, bf16[2,8,16,128]{3,2,1,0:T(8,128)(2,1)S(1)} %bitcast.13, bf16[2,8,16,128]{3,2,1,0:T(8,128)(2,1)S(1)} %bitcast.16, ...), custom_call_target="tpu_custom_call" | custom-call | tf_op jit(solution)/shard_map/attend/pallas_call | solution.py:457
  35.2 1.6 %collective-permute-done.8.got_ref = f32[4,9,16,128]{3,2,1,0:T(8,128)S(1)} collective-permute-done((f32[4,9,16,128]{3,2,1,0:T(8,128)S(1)}, f32[4,9,16,128]{3,2,1,0:T(8,128)S(1)}, u32[]{:S(2)}, u32[]{:S(2)}) %collective-permute-start.8) | collective-permute-done | bytes 294944 | tf_op jit(solution)/shard_map/ppermute | solution.py:594
  36.8 0.3 merge_pair.1.refs_0_
  37.2 1.7 %collective-permute-start.11 = (bf16[4,9,16,128]{3,2,1,0:T(8,128)(2,1)S(1)}, bf16[4,9,16,128]{3,2,1,0:T(8,128)(2,1)S(1)}, u32[]{:S(2)}, u32[]{:S(2)}) collective-permute-start(bf16[4,9,16,128]{3,2,1,0:T(8,128)(2,1)S(1)} %merge_pair.1.refs_0_), channel_id=1, source_target_pairs={{0,6},{1,7},{2,4},{3,5},{4,2},{5,3},{6,0},{7,1},{8,14},{9,15},{10,... | collective-permute-start | bytes 442376 | tf_op jit(solution)/shard_map/ppermute | solution.py:594
  38.9 3.1 %collective-permute-start.10 = (bf16[4,9,16,128]{3,2,1,0:T(8,128)(2,1)S(1)}, bf16[4,9,16,128]{3,2,1,0:T(8,128)(2,1)S(1)}, u32[]{:S(2)}, u32[]{:S(2)}) collective-permute-start(bf16[4,9,16,128]{3,2,1,0:T(8,128)(2,1)S(1)} %merge_pair.1.refs_0_), channel_id=1, source_target_pairs={{0,4},{1,5},{2,6},{3,7},{4,0},{5,1},{6,2},{7,3},{8,12},{9,13},{10,... | collective-permute-start | bytes 442376 | tf_op jit(solution)/shard_map/ppermute | solution.py:594
  42.0 1.4 %collective-permute-start.9 = (bf16[4,9,16,128]{3,2,1,0:T(8,128)(2,1)S(1)}, bf16[4,9,16,128]{3,2,1,0:T(8,128)(2,1)S(1)}, u32[]{:S(2)}, u32[]{:S(2)}) collective-permute-start(bf16[4,9,16,128]{3,2,1,0:T(8,128)(2,1)S(1)} %merge_pair.1.refs_0_), channel_id=1, source_target_pairs={{0,2},{1,3},{2,0},{3,1},{4,6},{5,7},{6,4},{7,5},{8,10},{9,11},{10,... | collective-permute-start | bytes 442376 | tf_op jit(solution)/shard_map/ppermute | solution.py:594
  43.4 0.7 %collective-permute-done.11.refs_3_ = bf16[4,9,16,128]{3,2,1,0:T(8,128)(2,1)S(1)} collective-permute-done((bf16[4,9,16,128]{3,2,1,0:T(8,128)(2,1)S(1)}, bf16[4,9,16,128]{3,2,1,0:T(8,128)(2,1)S(1)}, u32[]{:S(2)}, u32[]{:S(2)}) %collective-permute-start.11) | collective-permute-done | bytes 147488 | tf_op jit(solution)/shard_map/ppermute | solution.py:594
  44.1 4.4 %collective-permute-done.10.refs_2_ = bf16[4,9,16,128]{3,2,1,0:T(8,128)(2,1)S(1)} collective-permute-done((bf16[4,9,16,128]{3,2,1,0:T(8,128)(2,1)S(1)}, bf16[4,9,16,128]{3,2,1,0:T(8,128)(2,1)S(1)}, u32[]{:S(2)}, u32[]{:S(2)}) %collective-permute-start.10) | collective-permute-done | bytes 147488 | tf_op jit(solution)/shard_map/ppermute | solution.py:594
  48.6 1.9 %collective-permute-done.9.refs_1_ = bf16[4,9,16,128]{3,2,1,0:T(8,128)(2,1)S(1)} collective-permute-done((bf16[4,9,16,128]{3,2,1,0:T(8,128)(2,1)S(1)}, bf16[4,9,16,128]{3,2,1,0:T(8,128)(2,1)S(1)}, u32[]{:S(2)}, u32[]{:S(2)}) %collective-permute-start.9) | collective-permute-done | bytes 147488 | tf_op jit(solution)/shard_map/ppermute | solution.py:594
  50.4 0.6 merge.1.refs_0_
  51.1 1.3 %collective-permute-done.12.refs_1_ = bf16[32,2048]{1,0:T(8,128)(2,1)S(1)} collective-permute-done((bf16[32,2048]{1,0:T(8,128)(2,1)S(1)}, bf16[32,2048]{1,0:T(8,128)(2,1)S(1)}, u32[]{:S(2)}, u32[]{:S(2)}) %collective-permute-start.12) | collective-permute-done | bytes 131104 | tf_op jit(solution)/shard_map/ppermute | solution.py:594
  52.4 0.6 project_out.1
  53.0 1.6 %collective-permute-start.13 = (bf16[16,640]{1,0:T(8,128)(2,1)S(1)}, bf16[16,640]{1,0:T(8,128)(2,1)S(1)}, u32[]{:S(2)}, u32[]{:S(2)}) collective-permute-start(bf16[16,640]{1,0:T(8,128)(2,1)S(1)} %get-tuple-element.30), channel_id=1, source_target_pairs={{0,8},{8,0},{16,24},{24,16},{1,9},{9,1},{17,25},{25,17},{2,10},{10... | collective-permute-start | bytes 61448 | tf_op jit(solution)/shard_map/ppermute | solution.py:594
  54.7 2.6 %collective-permute-start.14 = (bf16[16,640]{1,0:T(8,128)(2,1)S(1)}, bf16[16,640]{1,0:T(8,128)(2,1)S(1)}, u32[]{:S(2)}, u32[]{:S(2)}) collective-permute-start(bf16[16,640]{1,0:T(8,128)(2,1)S(1)} %get-tuple-element.31), channel_id=1, source_target_pairs={{0,16},{8,24},{16,0},{24,8},{1,17},{9,25},{17,1},{25,9},{2,18},{10... | collective-permute-start | bytes 61448 | tf_op jit(solution)/shard_map/ppermute | solution.py:594
  57.5 2.1 %collective-permute-done.14 = bf16[16,640]{1,0:T(8,128)(2,1)S(1)} collective-permute-done((bf16[16,640]{1,0:T(8,128)(2,1)S(1)}, bf16[16,640]{1,0:T(8,128)(2,1)S(1)}, u32[]{:S(2)}, u32[]{:S(2)}) %collective-permute-start.14) | collective-permute-done | bytes 20512 | tf_op jit(solution)/shard_map/ppermute | solution.py:594
  59.6 3.3 %collective-permute-done.15 = bf16[16,640]{1,0:T(8,128)(2,1)S(1)} collective-permute-done((bf16[16,640]{1,0:T(8,128)(2,1)S(1)}, bf16[16,640]{1,0:T(8,128)(2,1)S(1)}, u32[]{:S(2)}, u32[]{:S(2)}) %collective-permute-start.15) | collective-permute-done | bytes 20512 | tf_op jit(solution)/shard_map/ppermute | solution.py:594
  62.9 0.6 add_convert_fusion
  (21 shorter events, 0.8 us)
Async XLA Ops:
  0.0 5.7 %copy-start.2 = (s32[8,32]{1,0:T(8,128)S(1)}, s32[8,32]{1,0:T(8,128)}, u32[]{:S(2)}) copy-start(s32[8,32]{1,0:T(8,128)} %length_ref.1) | copy-start | bytes 3076
  0.0 16.6 %copy-start.1 = (f32[128]{0:T(128)S(1)}, f32[128]{0:T(128)}, u32[]{:S(2)}) copy-start(f32[128]{0:T(128)} %param.17) | copy-start | bytes 1540
  5.2 1.7 %collective-permute-start = (f32[4,8,2176]{2,1,0:T(8,128)S(1)}, f32[4,8,2176]{2,1,0:T(8,128)S(1)}, u32[]{:S(2)}, u32[]{:S(2)}) collective-permute-start(f32[4,8,2176]{2,1,0:T(8,128)S(1)} %get-tuple-element.20), channel_id=1, source_target_pairs={{0,1},{1,0},{2,3},{3,2},{4,5},{5,4},{6,7},{7,6},{8,9},{9,8},{10,11... | collective-permute-start | bytes 835592 | tf_op jit(solution)/shard_map/ppermute | solution.py:594
  6.9 5.5 %collective-permute-start.1 = (f32[8,2304]{1,0:T(8,128)S(1)}, f32[8,2304]{1,0:T(8,128)S(1)}, u32[]{:S(2)}, u32[]{:S(2)}) collective-permute-start(f32[8,2304]{1,0:T(8,128)S(1)} %get-tuple-element.22), channel_id=1, source_target_pairs={{0,2},{1,3},{2,0},{3,1},{4,6},{5,7},{6,4},{7,5},{8,10},{9,11},{10,... | collective-permute-start | bytes 221192 | tf_op jit(solution)/shard_map/ppermute | solution.py:594
  9.8 4.4 %collective-permute-start.2 = (f32[8,2304]{1,0:T(8,128)S(1)}, f32[8,2304]{1,0:T(8,128)S(1)}, u32[]{:S(2)}, u32[]{:S(2)}) collective-permute-start(f32[8,2304]{1,0:T(8,128)S(1)} %get-tuple-element.23), channel_id=1, source_target_pairs={{0,4},{1,5},{2,6},{3,7},{4,0},{5,1},{6,2},{7,3},{8,12},{9,13},{10,... | collective-permute-start | bytes 221192 | tf_op jit(solution)/shard_map/ppermute | solution.py:594
  11.3 5.3 %collective-permute-start.3 = (f32[8,2304]{1,0:T(8,128)S(1)}, f32[8,2304]{1,0:T(8,128)S(1)}, u32[]{:S(2)}, u32[]{:S(2)}) collective-permute-start(f32[8,2304]{1,0:T(8,128)S(1)} %get-tuple-element.24), channel_id=1, source_target_pairs={{0,6},{1,7},{2,4},{3,5},{4,2},{5,3},{6,0},{7,1},{8,14},{9,15},{10,... | collective-permute-start | bytes 221192 | tf_op jit(solution)/shard_map/ppermute | solution.py:594
  16.9 1.3 %collective-permute-start.4 = (bf16[8,16,128]{2,1,0:T(8,128)(2,1)S(1)}, bf16[8,16,128]{2,1,0:T(8,128)(2,1)S(1)}, u32[]{:S(2)}, u32[]{:S(2)}) collective-permute-start(bf16[8,16,128]{2,1,0:T(8,128)(2,1)S(1)} %queries.1), channel_id=1, source_target_pairs={{0,1},{1,0},{2,3},{3,2},{4,5},{5,4},{6,7},{7,6},{8,9},{9,8},{10,11... | collective-permute-start | bytes 98312 | tf_op jit(solution)/shard_map/ppermute | solution.py:594
  18.2 6.0 %collective-permute-start.7 = (bf16[16,16,128]{2,1,0:T(8,128)(2,1)S(1)}, bf16[16,16,128]{2,1,0:T(8,128)(2,1)S(1)}, u32[]{:S(2)}, u32[]{:S(2)}) collective-permute-start(bf16[16,16,128]{2,1,0:T(8,128)(2,1)S(1)} %pad_maximum_fusion), channel_id=1, source_target_pairs={{0,6},{1,7},{2,4},{3,5},{4,2},{5,3},{6,0},{7,1},{8,14},{9,15},{10,... | collective-permute-start | bytes 196616 | tf_op jit(solution)/shard_map/ppermute | solution.py:594
  18.8 5.4 %collective-permute-start.6 = (bf16[16,16,128]{2,1,0:T(8,128)(2,1)S(1)}, bf16[16,16,128]{2,1,0:T(8,128)(2,1)S(1)}, u32[]{:S(2)}, u32[]{:S(2)}) collective-permute-start(bf16[16,16,128]{2,1,0:T(8,128)(2,1)S(1)} %pad_maximum_fusion), channel_id=1, source_target_pairs={{0,4},{1,5},{2,6},{3,7},{4,0},{5,1},{6,2},{7,3},{8,12},{9,13},{10,... | collective-permute-start | bytes 196616 | tf_op jit(solution)/shard_map/ppermute | solution.py:594
  20.2 4.3 %collective-permute-start.5 = (bf16[16,16,128]{2,1,0:T(8,128)(2,1)S(1)}, bf16[16,16,128]{2,1,0:T(8,128)(2,1)S(1)}, u32[]{:S(2)}, u32[]{:S(2)}) collective-permute-start(bf16[16,16,128]{2,1,0:T(8,128)(2,1)S(1)} %pad_maximum_fusion), channel_id=1, source_target_pairs={{0,2},{1,3},{2,0},{3,1},{4,6},{5,7},{6,4},{7,5},{8,10},{9,11},{10,... | collective-permute-start | bytes 196616 | tf_op jit(solution)/shard_map/ppermute | solution.py:594
  24.5 27.9 %copy-start = (bf16[2048,640]{1,0:T(8,128)(2,1)S(1)}, bf16[2048,640]{1,0:T(8,128)(2,1)}, u32[]{:S(2)}) copy-start(bf16[2048,640]{1,0:T(8,128)(2,1)} %refs_2_.1) | copy-start | bytes 7864324
  35.2 1.6 %collective-permute-start.8 = (f32[4,9,16,128]{3,2,1,0:T(8,128)S(1)}, f32[4,9,16,128]{3,2,1,0:T(8,128)S(1)}, u32[]{:S(2)}, u32[]{:S(2)}) collective-permute-start(f32[4,9,16,128]{3,2,1,0:T(8,128)S(1)} %get-tuple-element.28), channel_id=1, source_target_pairs={{0,1},{1,0},{2,3},{3,2},{4,5},{5,4},{6,7},{7,6},{8,9},{9,8},{10,11... | collective-permute-start | bytes 884744 | tf_op jit(solution)/shard_map/ppermute | solution.py:594
  37.2 7.0 %collective-permute-start.11 = (bf16[4,9,16,128]{3,2,1,0:T(8,128)(2,1)S(1)}, bf16[4,9,16,128]{3,2,1,0:T(8,128)(2,1)S(1)}, u32[]{:S(2)}, u32[]{:S(2)}) collective-permute-start(bf16[4,9,16,128]{3,2,1,0:T(8,128)(2,1)S(1)} %merge_pair.1.refs_0_), channel_id=1, source_target_pairs={{0,6},{1,7},{2,4},{3,5},{4,2},{5,3},{6,0},{7,1},{8,14},{9,15},{10,... | collective-permute-start | bytes 442376 | tf_op jit(solution)/shard_map/ppermute | solution.py:594
  38.9 9.7 %collective-permute-start.10 = (bf16[4,9,16,128]{3,2,1,0:T(8,128)(2,1)S(1)}, bf16[4,9,16,128]{3,2,1,0:T(8,128)(2,1)S(1)}, u32[]{:S(2)}, u32[]{:S(2)}) collective-permute-start(bf16[4,9,16,128]{3,2,1,0:T(8,128)(2,1)S(1)} %merge_pair.1.refs_0_), channel_id=1, source_target_pairs={{0,4},{1,5},{2,6},{3,7},{4,0},{5,1},{6,2},{7,3},{8,12},{9,13},{10,... | collective-permute-start | bytes 442376 | tf_op jit(solution)/shard_map/ppermute | solution.py:594
  42.0 8.5 %collective-permute-start.9 = (bf16[4,9,16,128]{3,2,1,0:T(8,128)(2,1)S(1)}, bf16[4,9,16,128]{3,2,1,0:T(8,128)(2,1)S(1)}, u32[]{:S(2)}, u32[]{:S(2)}) collective-permute-start(bf16[4,9,16,128]{3,2,1,0:T(8,128)(2,1)S(1)} %merge_pair.1.refs_0_), channel_id=1, source_target_pairs={{0,2},{1,3},{2,0},{3,1},{4,6},{5,7},{6,4},{7,5},{8,10},{9,11},{10,... | collective-permute-start | bytes 442376 | tf_op jit(solution)/shard_map/ppermute | solution.py:594
  51.0 1.4 %collective-permute-start.12 = (bf16[32,2048]{1,0:T(8,128)(2,1)S(1)}, bf16[32,2048]{1,0:T(8,128)(2,1)S(1)}, u32[]{:S(2)}, u32[]{:S(2)}) collective-permute-start(bf16[32,2048]{1,0:T(8,128)(2,1)S(1)} %merge.1.refs_0_), channel_id=1, source_target_pairs={{0,1},{1,0},{2,3},{3,2},{4,5},{5,4},{6,7},{7,6},{8,9},{9,8},{10,11... | collective-permute-start | bytes 393224 | tf_op jit(solution)/shard_map/ppermute | solution.py:594
  53.0 4.5 %collective-permute-start.13 = (bf16[16,640]{1,0:T(8,128)(2,1)S(1)}, bf16[16,640]{1,0:T(8,128)(2,1)S(1)}, u32[]{:S(2)}, u32[]{:S(2)}) collective-permute-start(bf16[16,640]{1,0:T(8,128)(2,1)S(1)} %get-tuple-element.30), channel_id=1, source_target_pairs={{0,8},{8,0},{16,24},{24,16},{1,9},{9,1},{17,25},{25,17},{2,10},{10... | collective-permute-start | bytes 61448 | tf_op jit(solution)/shard_map/ppermute | solution.py:594
  54.7 4.9 %collective-permute-start.14 = (bf16[16,640]{1,0:T(8,128)(2,1)S(1)}, bf16[16,640]{1,0:T(8,128)(2,1)S(1)}, u32[]{:S(2)}, u32[]{:S(2)}) collective-permute-start(bf16[16,640]{1,0:T(8,128)(2,1)S(1)} %get-tuple-element.31), channel_id=1, source_target_pairs={{0,16},{8,24},{16,0},{24,8},{1,17},{9,25},{17,1},{25,9},{2,18},{10... | collective-permute-start | bytes 61448 | tf_op jit(solution)/shard_map/ppermute | solution.py:594
  57.3 5.6 %collective-permute-start.15 = (bf16[16,640]{1,0:T(8,128)(2,1)S(1)}, bf16[16,640]{1,0:T(8,128)(2,1)S(1)}, u32[]{:S(2)}, u32[]{:S(2)}) collective-permute-start(bf16[16,640]{1,0:T(8,128)(2,1)S(1)} %get-tuple-element.32), channel_id=1, source_target_pairs={{0,24},{8,16},{16,8},{24,0},{1,25},{9,17},{17,9},{25,1},{2,26},{10... | collective-permute-start | bytes 61448 | tf_op jit(solution)/shard_map/ppermute | solution.py:594

commit v7 on v6

--- a/solution.py
+++ b/solution.py
@@ -18,8 +18,8 @@
 GROUP = 4
 TASKS = 8
 CHUNK = GROUP * TASKS
-PHASES = 16
-AHEAD = 6
+PHASES = 8
+AHEAD = 4
 DEPTH = 256
 LOG2E = math.log2(math.e)
 MIB = 1024 * 1024
@@ -39,11 +39,6 @@
 
 def hbm_spec():
     return pl.BlockSpec(memory_space=pltpu.HBM)
-
-
-def split2(x):
-    high = x.astype(jnp.bfloat16)
-    return high, (x - high.astype(jnp.float32)).astype(jnp.bfloat16)
 
 
 def split3(x):
@@ -69,127 +64,135 @@
     hidden_hbm,
     weight_hbm,
     down_hbm,
-    up_hbm,
     keep_ref,
     send_ref,
     hidden_ref,
     weight_ref,
     down_ref,
-    up_ref,
     total_ref,
     sems,
 ):
     chips, own, _ = keep_ref.shape
     rows, depth = hidden_ref.shape
-    low_width = down_ref.shape[0]
     width = weight_ref.shape[1]
-    tiles = width // COLUMN_TILE
-
-    def start(copies):
-        for copy in copies:
-            copy.start()
-        return copies
-
-    def chunks(hbm, ref, offset):
-        spans = [slice(i, min(i + DEPTH, ref.shape[0])) for i in range(0, ref.shape[0], DEPTH)]
-        return [
-            (span, pltpu.make_async_copy(hbm.at[span], ref.at[span], sems.at[offset + i]))
-            for i, span in enumerate(spans)
-        ]
-
-    first = start(
-        [
-            pltpu.make_async_copy(hidden_hbm, hidden_ref, sems.at[0]),
-            pltpu.make_async_copy(down_hbm, down_ref, sems.at[1]),
-        ]
-    )
-    up_chunks = chunks(up_hbm, up_ref, 2)
-    weight_chunks = chunks(weight_hbm, weight_ref, 2 + len(up_chunks))
-    waiting = [copy for _, copy in up_chunks + weight_chunks]
-    start(waiting[:1])
+    spans = [slice(i, min(i + DEPTH, depth)) for i in range(0, depth, DEPTH)]
+    first = [
+        pltpu.make_async_copy(hidden_hbm, hidden_ref, sems.at[0]),
+        pltpu.make_async_copy(down_hbm, down_ref, sems.at[1]),
+    ]
+    chunks = [
+        pltpu.make_async_copy(weight_hbm.at[span], weight_ref.at[span], sems.at[2 + i])
+        for i, span in enumerate(spans)
+    ]
+    for copy in first + chunks:
+        copy.start()
 
     slots = holder_ref.shape[1]
     numbers = [holder_ref[...], block_ref[...], length_ref[...], jnp.zeros((own, LANES - 3 * slots), jnp.int32)]
     numbers = jnp.concatenate(numbers, axis=1).astype(jnp.float32)
-    for c in range(chips):
-        keep_ref[c, :, width:] = numbers
-        send_ref[c, :, width:] = numbers
     tenants = adapter_ref.shape[1]
     tenant = to_column(tenant_ref[...], rows)
     pick = lax.broadcasted_iota(jnp.int32, (rows, tenants), 1).astype(jnp.float32) == tenant
     adapter = jnp.sum(jnp.where(pick, adapter_ref[...].astype(jnp.float32), 0.0), axis=1, keepdims=True).astype(
         jnp.int32
     )
+    even = lax.axis_index("kv") % PAIR == 0
+
+    def store(columns, total):
+        total = total.reshape(chips, PAIR, own, total.shape[1])
+        keep_ref[:, :, columns] = jnp.where(even, total[:, 0], total[:, 1])
+        send_ref[:, :, columns] = jnp.where(even, total[:, 1], total[:, 0])
+
     for copy in first:
         copy.wait()
-    start(waiting[1:3])
     hidden = hidden_ref[...]
     low = lax.dot_general(hidden, down_ref[...], (((1,), (1,)), ((), ())), preferred_element_type=jnp.float32)
-    column = lax.broadcasted_iota(jnp.int32, (rows, low_width), 1)
-    match = (column >= adapter * rank) & (column < adapter * rank + rank)
-    high, low = split2(jnp.where(match, ADAPTER_SCALE * low, 0.0))
-    both = jnp.concatenate([high, low], axis=0)
-    columns = [slice(i * COLUMN_TILE, (i + 1) * COLUMN_TILE) for i in range(tiles)]
-    for i, (span, copy) in enumerate(up_chunks):
+    column = lax.broadcasted_iota(jnp.int32, low.shape, 1)
+    low = jnp.where((column >= adapter * rank) & (column < adapter * rank + rank), low, 0.0)
+    low = sum(low[:, i : i + LANES] for i in range(LANES, low.shape[1], LANES)) + low[:, :LANES]
+    shift = LANES // 2
+    while shift >= rank:
+        low = low + pltpu.roll(low, shift, 1)
+        shift //= 2
+    lane = lax.broadcasted_iota(jnp.int32, (rows, LANES), 1)
+    numbers = jnp.concatenate([numbers] * (rows // own), axis=0)
+    store(slice(width, width + LANES), jnp.where(lane < 3 * slots, numbers, low))
+    for i, (span, copy) in enumerate(zip(spans, chunks)):
         copy.wait()
-        start(waiting[i + 3 : i + 4])
-        for tile in columns:
-            up_high, up_low = split2(up_ref[span, tile])
-            twice = jnp.dot(both[:, span], up_high, preferred_element_type=jnp.float32)
-            total = jnp.dot(high[:, span], up_low, preferred_element_type=jnp.float32)
-            total = (total + twice[rows:]) + twice[:rows]
-            total_ref[:, tile] = total if i == 0 else total_ref[:, tile] + total
-    even = lax.axis_index("kv") % PAIR == 0
-    for i, (span, copy) in enumerate(weight_chunks):
-        copy.wait()
-        start(waiting[i + len(up_chunks) + 3 : i + len(up_chunks) + 4])
-        for tile in columns:
-            total = total_ref[:, tile] + jnp.dot(
-                hidden[:, span], weight_ref[span, tile], preferred_element_type=jnp.float32
-            )
-            if i < len(weight_chunks) - 1:
+        for start in range(0, width, COLUMN_TILE):
+            tile = slice(start, start + COLUMN_TILE)
+            total = jnp.dot(hidden[:, span], weight_ref[span, tile], preferred_element_type=jnp.float32)
+            if i > 0:
+                total = total_ref[:, tile] + total
+            if i < len(chunks) - 1:
                 total_ref[:, tile] = total
             else:
-                total = total.reshape(chips, PAIR, own, COLUMN_TILE)
-                keep_ref[:, :, tile] = jnp.where(even, total[:, 0], total[:, 1])
-                send_ref[:, :, tile] = jnp.where(even, total[:, 1], total[:, 0])
-
-
-def project(tenant, tenant_adapter, holder, block, length, hidden, query_weight, down, up, rank, chips):
+                store(tile, total)
+
+
+def project(tenant, tenant_adapter, holder, block, length, hidden, query_weight, down, rank, chips):
     rows, depth = hidden.shape
     width = query_weight.shape[1]
     out = jax.ShapeDtypeStruct((chips, rows // chips // PAIR, width + LANES), jnp.float32)
-    operands = in_hbm(tenant, tenant_adapter, holder, block, length, hidden, query_weight, down, up)
+    operands = in_hbm(tenant, tenant_adapter, holder, block, length, hidden, query_weight, down)
     large = operands[5:]
     return pl.pallas_call(
         functools.partial(project_kernel, rank),
-        in_specs=[vmem_spec()] * 5 + [hbm_spec()] * 4,
+        in_specs=[vmem_spec()] * 5 + [hbm_spec()] * 3,
         out_specs=[vmem_spec()] * 2,
         out_shape=[out] * 2,
         scratch_shapes=[pltpu.VMEM(x.shape, x.dtype) for x in large]
-        + [
-            pltpu.VMEM((rows, width), jnp.float32),
-            pltpu.SemaphoreType.DMA((2 + pl.cdiv(depth, DEPTH) + pl.cdiv(down.shape[0], DEPTH),)),
-        ],
-        compiler_params=params(24),
+        + [pltpu.VMEM((rows, width), jnp.float32), pltpu.SemaphoreType.DMA((2 + pl.cdiv(depth, DEPTH),))],
+        compiler_params=params(16),
         name="project",
     )(*operands)
 
 
-def pair_kernel(keep_ref, got_ref, *out_refs):
-    width = keep_ref.shape[2] - LANES
+def gather_up_kernel(tenant_ref, adapter_ref, up_hbm, out_ref, sems):
+    own = out_ref.shape[0]
+    me = lax.axis_index("kv")
+    copies = [
+        pltpu.make_async_copy(up_hbm.at[adapter_ref[tenant_ref[me * own + r]]], out_ref.at[r], sems.at[r])
+        for r in range(own)
+    ]
+    for copy in copies:
+        copy.start()
+    for copy in copies:
+        copy.wait()
+
+
+def gather_up(tenant, tenant_adapter, up, own):
+    (up,) = in_hbm(up)
+    smem = pl.BlockSpec(memory_space=pltpu.SMEM)
+    return pl.pallas_call(
+        gather_up_kernel,
+        in_specs=[smem, smem, hbm_spec()],
+        out_specs=vmem_spec(),
+        out_shape=jax.ShapeDtypeStruct((own, *up.shape[1:]), up.dtype),
+        scratch_shapes=[pltpu.SemaphoreType.DMA((own,))],
+        compiler_params=params(16),
+        cost_estimate=pl.CostEstimate(flops=0, bytes_accessed=own * up.shape[1] * up.shape[2] * 4, transcendentals=0),
+        name="gather_up",
+    )(tenant, tenant_adapter, up)
+
+
+def pair_kernel(number_lanes, keep_ref, got_ref, *out_refs):
+    chips, own, width = keep_ref.shape
+    width = width - LANES
     chip = lax.axis_index("kv") // PAIR
+    lane = lax.broadcasted_iota(jnp.int32, (own, LANES), 1)
     for s, ref in enumerate(out_refs):
         c = jnp.bitwise_xor(chip, s)
         ref[:, :width] = keep_ref[c, :, :width] + got_ref[c, :, :width]
-        ref[:, width : width + LANES] = keep_ref[0, :, width:]
-        ref[:, width + LANES :] = got_ref[0, :, width:]
-
-
-def add_pair(keep, got):
+        keep = keep_ref[c, :, width:]
+        ref[:, width : width + LANES] = jnp.where(lane < number_lanes, keep, keep + got_ref[c, :, width:])
+        ref[:, width + LANES :] = got_ref[c, :, width:]
+
+
+def add_pair(keep, got, number_lanes):
     chips, own, width = keep.shape
     return pl.pallas_call(
-        pair_kernel,
+        functools.partial(pair_kernel, number_lanes),
         in_specs=[vmem_spec()] * 2,
         out_specs=[vmem_spec()] * chips,
         out_shape=[jax.ShapeDtypeStruct((own, width + LANES), jnp.float32)] * chips,
@@ -198,33 +201,51 @@
     )(keep, got)
 
 
-def queries_kernel(*refs):
-    parts, (cosine_ref, sine_ref, gain_ref, out_ref, turned_ref) = refs[:-5], refs[-5:]
+def queries_kernel(number_lanes, *refs):
+    parts, (up_ref, cosine_ref, sine_ref, gain_ref, out_ref, turned_ref) = refs[:-6], refs[-6:]
+    own, rank, width = up_ref.shape
     heads = turned_ref.shape[1]
+
+    def whole(columns):
+        total = parts[0][:, columns]
+        for part in parts[1:]:
+            total = total + part[:, columns]
+        return total
+
+    low = whole(slice(width, width + LANES)) * ADAPTER_SCALE
+    line = lax.broadcasted_iota(jnp.int32, (rank, LANES), 0)
+    lane = lax.broadcasted_iota(jnp.int32, (rank, LANES), 1)
+    low = [
+        jnp.sum(jnp.where(lane == line + number_lanes, low[r : r + 1], 0.0), axis=1, keepdims=True)
+        for r in range(own)
+    ]
+    row = lax.broadcasted_iota(jnp.int32, (own, LANES), 0)
     cosine, sine, gain = cosine_ref[...], sine_ref[...], gain_ref[...]
     for h in range(heads):
         columns = slice(h * LANES, (h + 1) * LANES)
-        query = parts[0][:, columns]
-        for part in parts[1:]:
-            query = query + part[:, columns]
+        query = whole(columns)
+        adapted = jnp.zeros((own, LANES), jnp.float32)
+        for r in range(own):
+            adapted = jnp.where(row == r, jnp.sum(up_ref[r, :, columns] * low[r], axis=0, keepdims=True), adapted)
+        query = query + adapted
         square = jnp.mean(query * query, axis=-1, keepdims=True)
         query = query * lax.rsqrt(square + EPSILON) * gain
         turned_ref[:, h, :] = query * cosine + pltpu.roll(query, LANES // 2, 1) * sine
     out_ref[...] = turned_ref[...].astype(jnp.bfloat16)
 
 
-def make_queries(parts, cosine, sine, gain, heads):
+def make_queries(parts, up, cosine, sine, gain, heads, number_lanes):
     own = parts[0].shape[0]
     shape = (own, heads, LANES)
     return pl.pallas_call(
-        queries_kernel,
-        in_specs=[vmem_spec()] * (len(parts) + 3),
+        functools.partial(queries_kernel, number_lanes),
+        in_specs=[vmem_spec()] * (len(parts) + 4),
         out_specs=vmem_spec(),
         out_shape=jax.ShapeDtypeStruct(shape, jnp.bfloat16),
         scratch_shapes=[pltpu.VMEM(shape, jnp.float32)],
         compiler_params=params(16),
         name="queries",
-    )(*parts, cosine, sine, gain)
+    )(*parts, up, cosine, sine, gain)
 
 
 def list_kernel(blocks, block_size, slots, *refs):
@@ -316,32 +337,26 @@
 
 def attend_kernel(scale, kv_local, count, list_vmem, bound_vmem, *refs):
     queries, refs = refs[: count // PAIR], refs[count // PAIR :]
-    (key_hbm, value_hbm, keep_ref, send_ref, list_ref, bound_ref, query_ref, key_ref, value_ref) = refs[:9]
-    (top_ref, total_ref, sum_ref, score_ref, part_top_ref, part_total_ref, part_sum_ref, number_sems, sems) = refs[9:]
+    (key_ref, value_hbm, keep_ref, send_ref, list_ref, bound_ref, query_ref, value_ref) = refs[:8]
+    (top_ref, total_ref, sum_ref, score_ref, part_top_ref, part_total_ref, part_sum_ref, number_sems, sems) = refs[8:]
     heads = query_ref.shape[1]
     rows = query_ref.shape[0] - 1
     own = rows // count
     blocks, tokens, _ = key_ref.shape
     block_size = tokens // kv_local
-    size = blocks // PHASES
     length_bits = (block_size - 1).bit_length()
     block_bits = (blocks - 1).bit_length()
-    copies = []
-    for part in range(PHASES):
-        here = pl.ds(part * size, size)
-        copies.append(
-            (
-                pltpu.make_async_copy(key_hbm.at[here], key_ref.at[here], sems.at[0, part]),
-                pltpu.make_async_copy(value_hbm.at[here], value_ref.at[here], sems.at[1, part]),
-            )
-        )
     numbers = (
         pltpu.make_async_copy(list_vmem, list_ref, number_sems.at[0]),
         pltpu.make_async_copy(bound_vmem, bound_ref, number_sems.at[1]),
     )
-    for pair in (copies[0], numbers, *copies[1:AHEAD]):
-        for copy in pair:
-            copy.start()
+    size = blocks // PHASES
+    spans = [pl.ds(part * size, size) for part in range(PHASES)]
+    copies = [
+        pltpu.make_async_copy(value_hbm.at[span], value_ref.at[span], sems.at[part]) for part, span in enumerate(spans)
+    ]
+    for copy in (copies[0], *numbers, *copies[1:AHEAD]):
+        copy.start()
 
     factor = scale * LOG2E
     for s, piece in enumerate(queries):
@@ -422,11 +437,9 @@
     for copy in numbers:
         copy.wait()
     for part in range(PHASES):
-        for copy in copies[part]:
-            copy.wait()
-        for pair in copies[part + AHEAD : part + AHEAD + 1]:
-            for copy in pair:
-                copy.start()
+        copies[part].wait()
+        for copy in copies[part + AHEAD : part + AHEAD + 1]:
+            copy.start()
         lax.fori_loop(bound_ref[0, part], bound_ref[0, part + 1], functools.partial(turn, 3), 0)
     last = bound_ref[0, PHASES]
     turn(2, last, 0)
@@ -451,19 +464,19 @@
     count = len(queries) * PAIR
     rows = count * own
     tokens = keys.shape[1]
-    keys, values = in_hbm(keys, values)
+    keys = pltpu.with_memory_space_constraint(keys, pltpu.VMEM)
+    (values,) = in_hbm(values)
     state = pltpu.VMEM((rows + 1, heads, LANES), jnp.float32)
     part = pltpu.VMEM((CHUNK, heads, LANES), jnp.float32)
     return pl.pallas_call(
         functools.partial(attend_kernel, scale, kv_local, count),
-        in_specs=[vmem_spec()] * (2 + len(queries)) + [hbm_spec()] * 2,
+        in_specs=[vmem_spec()] * (3 + len(queries)) + [hbm_spec()],
         out_specs=[vmem_spec()] * PAIR,
         out_shape=[jax.ShapeDtypeStruct((count // PAIR, own + 1, heads, LANES), jnp.float32)] * PAIR,
         scratch_shapes=[
             pltpu.SMEM(items.shape, items.dtype),
             pltpu.SMEM(bounds.shape, bounds.dtype),
             pltpu.VMEM((rows + 1, heads, LANES), jnp.bfloat16),
-            pltpu.VMEM(keys.shape, keys.dtype),
             pltpu.VMEM(values.shape, values.dtype),
             state,
             state,
@@ -473,9 +486,9 @@
             part,
             pltpu.VMEM((TASKS, GROUP * heads, LANES), jnp.float32),
             pltpu.SemaphoreType.DMA((2,)),
-            pltpu.SemaphoreType.DMA((2, PHASES)),
+            pltpu.SemaphoreType.DMA((PHASES,)),
         ],
-        compiler_params=params(40),
+        compiler_params=params(32),
         name="attend",
     )(items, bounds, *queries, keys, values)
 
@@ -638,11 +651,11 @@
         hidden,
         query_weight,
         jnp.swapaxes(adapter_down_weight, 1, 2).reshape(adapters * rank, depth),
-        adapter_up_weight.reshape(adapters * rank, width),
         rank,
         chips,
     )
-    parts = add_pair(keep, exchange(send, "kv", 1))
+    up = gather_up(tenant, tenant_adapter, adapter_up_weight, own)
+    parts = add_pair(keep, exchange(send, "kv", 1), 3 * slots)
     parts = [parts[0]] + [exchange(parts[s], "kv", PAIR * s) for s in range(1, chips)]
 
     position = (jnp.sum(block_used_length, axis=1) - 1).astype(jnp.float32)
@@ -651,7 +664,7 @@
     angles = position[:, None] * frequency[None, :]
     cosine = jnp.concatenate([jnp.cos(angles), jnp.cos(angles)], axis=-1)
     sine = jnp.concatenate([-jnp.sin(angles), jnp.sin(angles)], axis=-1)
-    queries = make_queries(parts, cosine, sine, query_norm_gain.reshape(1, head_size), heads)
+    queries = make_queries(parts, up, cosine, sine, query_norm_gain.reshape(1, head_size), heads, 3 * slots)
     queries = [q.reshape(PAIR, own, heads, head_size) for q in gather_pairs(queries)]
     items, bounds = make_list(parts, slots, blocks, block_size, kv_count)
 

time: 63.4 us -> 67.4 us (1.063)
  local copies, waits for them, and re-layouts: 0.01 us -> 4.7 us
  waiting for transfers between devices: 22.9 us -> 21.7 us
  Pallas kernels: 20.1 us -> 19.3 us
  other arithmetic: 0.95 us -> 1.64 us
    unnamed x6 -> x10, local copies, waits for them, and re-layouts: 0.01 us -> 4.7 us
    pallas_call x2 -> x3, Pallas kernels: 0.33 us -> 2.39 us  [the longest x1 1.91 us: gather_up(): pl.pallas_call(gather_up_kernel, in_specs=[smem, smem, hbm_spec()], out_s...]
    pallas_call x1, Pallas kernels: 5.14 us -> 3.1 us  [project(): pl.pallas_call(functools.partial(project_kernel, rank), in_specs=[vmem_sp...]
    ppermute x16, waiting for transfers between devices: 22.9 us -> 21.7 us  [exchange(): return lax.ppermute(x, axis, [(i, i ^ s) for i in range(count)])]
    pallas_call x1, Pallas kernels: 10.6 us -> 9.86 us  [attend(): pl.pallas_call(functools.partial(attend_kernel, scale, kv_local, count),...]
    reduce_sum x1, other arithmetic: 0.12 us -> 0.8 us  [local(): position = (jnp.sum(block_used_length, axis=1) - 1).astype(jnp.float32)]
  transfers between devices with their start and end apart: 16 -> 16, of which waited for: 13 -> 11; matrix products, arithmetic and copies ran while one was open for 1% -> 2% of each run, Pallas kernels for 4% -> 6%
where the time goes in v7:
time: 67.4 us; the launch traced here: 66.9 us
  waiting for transfers between devices  21.7 us (32%)
  starting transfers between devices  19.4 us (29%)
  Pallas kernels  19.3 us (29%)
  local copies, waits for them, and re-layouts  4.7 us (7%)
  other arithmetic  1.64 us (2%)
    ppermute x16, waiting for transfers between devices, exchange(): return lax.ppermute(x, axis, [(i, i ^ s) for i in range(count)])  21.7 us
    ppermute x16, starting transfers between devices, exchange(): return lax.ppermute(x, axis, [(i, i ^ s) for i in range(count)])  19.4 us
    pallas_call x1, Pallas kernels, attend(): pl.pallas_call(functools.partial(attend_kernel, scale, kv_local, count),...  9.86 us
    unnamed x10, local copies, waits for them, and re-layouts  4.7 us
    pallas_call x1, Pallas kernels, project(): pl.pallas_call(functools.partial(project_kernel, rank), in_specs=[vmem_sp...  3.1 us
    pallas_call x1, Pallas kernels, make_list(): pl.pallas_call(functools.partial(list_kernel, blocks, block_size, slots),...  2.44 us
    pallas_call x1, Pallas kernels, gather_up(): pl.pallas_call(gather_up_kernel, in_specs=[smem, smem, hbm_spec()], out_s...  1.91 us
  transfers between devices with their start and end apart: 16, of which 11 were waited for; matrix products, arithmetic and copies ran while one was open for 2% of the time, Pallas kernels for 6%

profile of v7, /device:TPU:0, one launch (start us, length us, event | category | flops | bytes accessed | tf_op | source)
XLA Modules:
  0.0 66.9 jit_solution(18015748143456061096)
XLA Ops:
  0.0 3.1 %project.1 = (f32[4,8,2176]{2,1,0:T(8,128)S(1)}, f32[4,8,2176]{2,1,0:T(8,128)S(1)}) custom-call(s32[1,64]{1,0:T(1,128)} %bitcast.17, s32[1,64]{1,0:T(1,128)} %bitcast.18, s32[8,32]{1,0:T(8,128)} %holder_ref.1, s32[8,32]{1,0:T(8,128)} %block_ref.1, s32[8,32]{1,0:T(8,128)} %length_ref.1, bf16[64,640]{1,0:T(8,128)(2,1)} %hidden_hbm.1, ...), custom_call_target="tpu_custom_call" | custom-call | tf_op jit(solution)/shard_map/project/pallas_call | solution.py:139
  3.1 0.5 collective-permute-start
  3.6 0.8 %reduce_sum.9 = s32[8]{0:T(128)S(1)} reduce(s32[8,32]{1,0:T(8,128)} %length_ref.1, s32[]{:T(128)} %constant.2.clone.1), dimensions={1}, to_apply=%region_0.0 | reduce | flops 248 | bytes 1060 | tf_op jit(solution)/shard_map/reduce_sum | solution.py:661
  4.5 0.7 copy-done.2
  5.1 0.7 copy-done.3
  5.8 1.9 %gather_up.1.refs_4_ = f32[8,16,2048]{2,1,0:T(8,128)S(1)} custom-call(s32[64]{0:T(128)S(1)} %copy-done.2, s32[64]{0:T(128)S(1)} %copy-done.3, f32[32,16,2048]{2,1,0:T(8,128)} %up_hbm.1), custom_call_target="tpu_custom_call" | custom-call | bytes 1048576 | tf_op jit(solution)/shard_map/gather_up/pallas_call | solution.py:167
  7.9 2.6 %collective-permute-start.1 = (f32[8,2304]{1,0:T(8,128)S(1)}, f32[8,2304]{1,0:T(8,128)S(1)}, u32[]{:S(2)}, u32[]{:S(2)}) collective-permute-start(f32[8,2304]{1,0:T(8,128)S(1)} %get-tuple-element.22), channel_id=1, source_target_pairs={{0,2},{1,3},{2,0},{3,1},{4,6},{5,7},{6,4},{7,5},{8,10},{9,11},{10,... | collective-permute-start | bytes 221192 | tf_op jit(solution)/shard_map/ppermute | solution.py:607
  10.4 1.5 %collective-permute-start.2 = (f32[8,2304]{1,0:T(8,128)S(1)}, f32[8,2304]{1,0:T(8,128)S(1)}, u32[]{:S(2)}, u32[]{:S(2)}) collective-permute-start(f32[8,2304]{1,0:T(8,128)S(1)} %get-tuple-element.23), channel_id=1, source_target_pairs={{0,4},{1,5},{2,6},{3,7},{4,0},{5,1},{6,2},{7,3},{8,12},{9,13},{10,... | collective-permute-start | bytes 221192 | tf_op jit(solution)/shard_map/ppermute | solution.py:607
  12.0 1.3 %collective-permute-done.1.refs_1_ = f32[8,2304]{1,0:T(8,128)S(1)} collective-permute-done((f32[8,2304]{1,0:T(8,128)S(1)}, f32[8,2304]{1,0:T(8,128)S(1)}, u32[]{:S(2)}, u32[]{:S(2)}) %collective-permute-start.1) | collective-permute-done | bytes 73760 | tf_op jit(solution)/shard_map/ppermute | solution.py:607
  13.4 1.6 %collective-permute-done.2.refs_2_ = f32[8,2304]{1,0:T(8,128)S(1)} collective-permute-done((f32[8,2304]{1,0:T(8,128)S(1)}, f32[8,2304]{1,0:T(8,128)S(1)}, u32[]{:S(2)}, u32[]{:S(2)}) %collective-permute-start.2) | collective-permute-done | bytes 73760 | tf_op jit(solution)/shard_map/ppermute | solution.py:607
  14.9 2.3 %collective-permute-done.3.refs_3_ = f32[8,2304]{1,0:T(8,128)S(1)} collective-permute-done((f32[8,2304]{1,0:T(8,128)S(1)}, f32[8,2304]{1,0:T(8,128)S(1)}, u32[]{:S(2)}, u32[]{:S(2)}) %collective-permute-start.3) | collective-permute-done | bytes 73760 | tf_op jit(solution)/shard_map/ppermute | solution.py:607
  17.7 1.2 %collective-permute-done.4 = bf16[8,16,128]{2,1,0:T(8,128)(2,1)S(1)} collective-permute-done((bf16[8,16,128]{2,1,0:T(8,128)(2,1)S(1)}, bf16[8,16,128]{2,1,0:T(8,128)(2,1)S(1)}, u32[]{:S(2)}, u32[]{:S(2)}) %collective-permute-start.4) | collective-permute-done | bytes 32800 | tf_op jit(solution)/shard_map/ppermute | solution.py:607
  18.9 0.6 collective-permute-start.5
  19.5 0.7 %collective-permute-start.6 = (bf16[16,16,128]{2,1,0:T(8,128)(2,1)S(1)}, bf16[16,16,128]{2,1,0:T(8,128)(2,1)S(1)}, u32[]{:S(2)}, u32[]{:S(2)}) collective-permute-start(bf16[16,16,128]{2,1,0:T(8,128)(2,1)S(1)} %pad_maximum_fusion), channel_id=1, source_target_pairs={{0,4},{1,5},{2,6},{3,7},{4,0},{5,1},{6,2},{7,3},{8,12},{9,13},{10,... | collective-permute-start | bytes 196616 | tf_op jit(solution)/shard_map/ppermute | solution.py:607
  20.2 2.2 %collective-permute-start.7 = (bf16[16,16,128]{2,1,0:T(8,128)(2,1)S(1)}, bf16[16,16,128]{2,1,0:T(8,128)(2,1)S(1)}, u32[]{:S(2)}, u32[]{:S(2)}) collective-permute-start(bf16[16,16,128]{2,1,0:T(8,128)(2,1)S(1)} %pad_maximum_fusion), channel_id=1, source_target_pairs={{0,6},{1,7},{2,4},{3,5},{4,2},{5,3},{6,0},{7,1},{8,14},{9,15},{10,... | collective-permute-start | bytes 196616 | tf_op jit(solution)/shard_map/ppermute | solution.py:607
  22.5 2.4 %slot_list.1 = (s32[1,1024]{1,0:T(1,128)S(1)}, s32[1,128]{1,0:T(1,128)S(1)}) custom-call(f32[8,2304]{1,0:T(8,128)S(1)} %get-tuple-element.21.refs_0_, f32[8,2304]{1,0:T(8,128)S(1)} %collective-permute-done.1.refs_1_, f32[8,2304]{1,0:T(8,128)S(1)} %collective-permute-done.2.refs_2_, f32[8,2304]{1,0:T(8,128)S(1)} %collective-permute-done.3.refs_3_), custom_call_target="tpu_custom_call" | custom-call | flops 100000000 | bytes 10000000 | tf_op jit(solution)/shard_map/slot_list/pallas_call | solution.py:319
  24.9 0.5 collective-permute-done.7
  25.4 3.4 %copy-done = bf16[128,128,2,128]{3,2,1,0:T(2,128)(2,1)S(1)} copy-done((bf16[128,128,2,128]{3,2,1,0:T(2,128)(2,1)S(1)}, bf16[128,128,2,128]{3,2,1,0:T(2,128)(2,1)}, u32[]{:S(2)}) %copy-start) | copy-done | bytes 8388632
  28.8 9.9 %attend.1 = (f32[4,9,16,128]{3,2,1,0:T(8,128)S(1)}, f32[4,9,16,128]{3,2,1,0:T(8,128)S(1)}) custom-call(s32[1,1024]{1,0:T(1,128)S(1)} %get-tuple-element.25.list_vmem, s32[1,128]{1,0:T(1,128)S(1)} %get-tuple-element.26.bound_vmem, bf16[2,8,16,128]{3,2,1,0:T(8,128)(2,1)S(1)} %bitcast.13, bf16[2,8,16,128]{3,2,1,0:T(8,128)(2,1)S(1)} %bitcast.14, ...), custom_call_target="tpu_custom_call" | custom-call | tf_op jit(solution)/shard_map/attend/pallas_call | solution.py:471
  38.7 3.0 %collective-permute-start.8 = (f32[4,9,16,128]{3,2,1,0:T(8,128)S(1)}, f32[4,9,16,128]{3,2,1,0:T(8,128)S(1)}, u32[]{:S(2)}, u32[]{:S(2)}) collective-permute-start(f32[4,9,16,128]{3,2,1,0:T(8,128)S(1)} %get-tuple-element.28), channel_id=1, source_target_pairs={{0,1},{1,0},{2,3},{3,2},{4,5},{5,4},{6,7},{7,6},{8,9},{9,8},{10,11... | collective-permute-start | bytes 884744 | tf_op jit(solution)/shard_map/ppermute | solution.py:607
  41.7 1.2 %collective-permute-done.8.got_ref = f32[4,9,16,128]{3,2,1,0:T(8,128)S(1)} collective-permute-done((f32[4,9,16,128]{3,2,1,0:T(8,128)S(1)}, f32[4,9,16,128]{3,2,1,0:T(8,128)S(1)}, u32[]{:S(2)}, u32[]{:S(2)}) %collective-permute-start.8) | collective-permute-done | bytes 294944 | tf_op jit(solution)/shard_map/ppermute | solution.py:607
  43.7 3.1 %collective-permute-start.9 = (bf16[4,9,16,128]{3,2,1,0:T(8,128)(2,1)S(1)}, bf16[4,9,16,128]{3,2,1,0:T(8,128)(2,1)S(1)}, u32[]{:S(2)}, u32[]{:S(2)}) collective-permute-start(bf16[4,9,16,128]{3,2,1,0:T(8,128)(2,1)S(1)} %merge_pair.1.refs_0_), channel_id=1, source_target_pairs={{0,2},{1,3},{2,0},{3,1},{4,6},{5,7},{6,4},{7,5},{8,10},{9,11},{10,... | collective-permute-start | bytes 442376 | tf_op jit(solution)/shard_map/ppermute | solution.py:607
  46.8 5.8 %collective-permute-done.10.refs_2_ = bf16[4,9,16,128]{3,2,1,0:T(8,128)(2,1)S(1)} collective-permute-done((bf16[4,9,16,128]{3,2,1,0:T(8,128)(2,1)S(1)}, bf16[4,9,16,128]{3,2,1,0:T(8,128)(2,1)S(1)}, u32[]{:S(2)}, u32[]{:S(2)}) %collective-permute-start.10) | collective-permute-done | bytes 147488 | tf_op jit(solution)/shard_map/ppermute | solution.py:607
  52.6 1.2 %collective-permute-done.9.refs_1_ = bf16[4,9,16,128]{3,2,1,0:T(8,128)(2,1)S(1)} collective-permute-done((bf16[4,9,16,128]{3,2,1,0:T(8,128)(2,1)S(1)}, bf16[4,9,16,128]{3,2,1,0:T(8,128)(2,1)S(1)}, u32[]{:S(2)}, u32[]{:S(2)}) %collective-permute-start.9) | collective-permute-done | bytes 147488 | tf_op jit(solution)/shard_map/ppermute | solution.py:607
  53.8 0.6 merge.1.refs_0_
  54.5 1.3 %collective-permute-done.12.refs_1_ = bf16[32,2048]{1,0:T(8,128)(2,1)S(1)} collective-permute-done((bf16[32,2048]{1,0:T(8,128)(2,1)S(1)}, bf16[32,2048]{1,0:T(8,128)(2,1)S(1)}, u32[]{:S(2)}, u32[]{:S(2)}) %collective-permute-start.12) | collective-permute-done | bytes 131104 | tf_op jit(solution)/shard_map/ppermute | solution.py:607
  55.8 0.6 project_out.1
  56.4 1.6 %collective-permute-start.13 = (bf16[16,640]{1,0:T(8,128)(2,1)S(1)}, bf16[16,640]{1,0:T(8,128)(2,1)S(1)}, u32[]{:S(2)}, u32[]{:S(2)}) collective-permute-start(bf16[16,640]{1,0:T(8,128)(2,1)S(1)} %get-tuple-element.30), channel_id=1, source_target_pairs={{0,8},{8,0},{16,24},{24,16},{1,9},{9,1},{17,25},{25,17},{2,10},{10... | collective-permute-start | bytes 61448 | tf_op jit(solution)/shard_map/ppermute | solution.py:607
  58.1 2.6 %collective-permute-start.14 = (bf16[16,640]{1,0:T(8,128)(2,1)S(1)}, bf16[16,640]{1,0:T(8,128)(2,1)S(1)}, u32[]{:S(2)}, u32[]{:S(2)}) collective-permute-start(bf16[16,640]{1,0:T(8,128)(2,1)S(1)} %get-tuple-element.31), channel_id=1, source_target_pairs={{0,16},{8,24},{16,0},{24,8},{1,17},{9,25},{17,1},{25,9},{2,18},{10... | collective-permute-start | bytes 61448 | tf_op jit(solution)/shard_map/ppermute | solution.py:607
  60.9 2.1 %collective-permute-done.14 = bf16[16,640]{1,0:T(8,128)(2,1)S(1)} collective-permute-done((bf16[16,640]{1,0:T(8,128)(2,1)S(1)}, bf16[16,640]{1,0:T(8,128)(2,1)S(1)}, u32[]{:S(2)}, u32[]{:S(2)}) %collective-permute-start.14) | collective-permute-done | bytes 20512 | tf_op jit(solution)/shard_map/ppermute | solution.py:607
  63.0 3.2 %collective-permute-done.15 = bf16[16,640]{1,0:T(8,128)(2,1)S(1)} collective-permute-done((bf16[16,640]{1,0:T(8,128)(2,1)S(1)}, bf16[16,640]{1,0:T(8,128)(2,1)S(1)}, u32[]{:S(2)}, u32[]{:S(2)}) %collective-permute-start.15) | collective-permute-done | bytes 20512 | tf_op jit(solution)/shard_map/ppermute | solution.py:607
  66.2 0.6 add_convert_fusion
  (26 shorter events, 2.0 us)
Async XLA Ops:
  0.0 17.2 %copy-start.4 = (f32[128]{0:T(128)S(1)}, f32[128]{0:T(128)}, u32[]{:S(2)}) copy-start(f32[128]{0:T(128)} %param.17) | copy-start | bytes 1540
  3.1 4.7 %collective-permute-start = (f32[4,8,2176]{2,1,0:T(8,128)S(1)}, f32[4,8,2176]{2,1,0:T(8,128)S(1)}, u32[]{:S(2)}, u32[]{:S(2)}) collective-permute-start(f32[4,8,2176]{2,1,0:T(8,128)S(1)} %get-tuple-element.20), channel_id=1, source_target_pairs={{0,1},{1,0},{2,3},{3,2},{4,5},{5,4},{6,7},{7,6},{8,9},{9,8},{10,11... | collective-permute-start | bytes 835592 | tf_op jit(solution)/shard_map/ppermute | solution.py:607
  4.5 0.7 copy-start.2
  5.1 0.7 copy-start.3
  7.9 5.5 %collective-permute-start.1 = (f32[8,2304]{1,0:T(8,128)S(1)}, f32[8,2304]{1,0:T(8,128)S(1)}, u32[]{:S(2)}, u32[]{:S(2)}) collective-permute-start(f32[8,2304]{1,0:T(8,128)S(1)} %get-tuple-element.22), channel_id=1, source_target_pairs={{0,2},{1,3},{2,0},{3,1},{4,6},{5,7},{6,4},{7,5},{8,10},{9,11},{10,... | collective-permute-start | bytes 221192 | tf_op jit(solution)/shard_map/ppermute | solution.py:607
  10.4 4.5 %collective-permute-start.2 = (f32[8,2304]{1,0:T(8,128)S(1)}, f32[8,2304]{1,0:T(8,128)S(1)}, u32[]{:S(2)}, u32[]{:S(2)}) collective-permute-start(f32[8,2304]{1,0:T(8,128)S(1)} %get-tuple-element.23), channel_id=1, source_target_pairs={{0,4},{1,5},{2,6},{3,7},{4,0},{5,1},{6,2},{7,3},{8,12},{9,13},{10,... | collective-permute-start | bytes 221192 | tf_op jit(solution)/shard_map/ppermute | solution.py:607
  11.9 5.3 %collective-permute-start.3 = (f32[8,2304]{1,0:T(8,128)S(1)}, f32[8,2304]{1,0:T(8,128)S(1)}, u32[]{:S(2)}, u32[]{:S(2)}) collective-permute-start(f32[8,2304]{1,0:T(8,128)S(1)} %get-tuple-element.24), channel_id=1, source_target_pairs={{0,6},{1,7},{2,4},{3,5},{4,2},{5,3},{6,0},{7,1},{8,14},{9,15},{10,... | collective-permute-start | bytes 221192 | tf_op jit(solution)/shard_map/ppermute | solution.py:607
  17.6 1.3 %collective-permute-start.4 = (bf16[8,16,128]{2,1,0:T(8,128)(2,1)S(1)}, bf16[8,16,128]{2,1,0:T(8,128)(2,1)S(1)}, u32[]{:S(2)}, u32[]{:S(2)}) collective-permute-start(bf16[8,16,128]{2,1,0:T(8,128)(2,1)S(1)} %queries.1), channel_id=1, source_target_pairs={{0,1},{1,0},{2,3},{3,2},{4,5},{5,4},{6,7},{7,6},{8,9},{9,8},{10,11... | collective-permute-start | bytes 98312 | tf_op jit(solution)/shard_map/ppermute | solution.py:607
  18.9 6.0 %collective-permute-start.5 = (bf16[16,16,128]{2,1,0:T(8,128)(2,1)S(1)}, bf16[16,16,128]{2,1,0:T(8,128)(2,1)S(1)}, u32[]{:S(2)}, u32[]{:S(2)}) collective-permute-start(bf16[16,16,128]{2,1,0:T(8,128)(2,1)S(1)} %pad_maximum_fusion), channel_id=1, source_target_pairs={{0,2},{1,3},{2,0},{3,1},{4,6},{5,7},{6,4},{7,5},{8,10},{9,11},{10,... | collective-permute-start | bytes 196616 | tf_op jit(solution)/shard_map/ppermute | solution.py:607
  19.5 5.4 %collective-permute-start.6 = (bf16[16,16,128]{2,1,0:T(8,128)(2,1)S(1)}, bf16[16,16,128]{2,1,0:T(8,128)(2,1)S(1)}, u32[]{:S(2)}, u32[]{:S(2)}) collective-permute-start(bf16[16,16,128]{2,1,0:T(8,128)(2,1)S(1)} %pad_maximum_fusion), channel_id=1, source_target_pairs={{0,4},{1,5},{2,6},{3,7},{4,0},{5,1},{6,2},{7,3},{8,12},{9,13},{10,... | collective-permute-start | bytes 196616 | tf_op jit(solution)/shard_map/ppermute | solution.py:607
  20.2 5.2 %collective-permute-start.7 = (bf16[16,16,128]{2,1,0:T(8,128)(2,1)S(1)}, bf16[16,16,128]{2,1,0:T(8,128)(2,1)S(1)}, u32[]{:S(2)}, u32[]{:S(2)}) collective-permute-start(bf16[16,16,128]{2,1,0:T(8,128)(2,1)S(1)} %pad_maximum_fusion), channel_id=1, source_target_pairs={{0,6},{1,7},{2,4},{3,5},{4,2},{5,3},{6,0},{7,1},{8,14},{9,15},{10,... | collective-permute-start | bytes 196616 | tf_op jit(solution)/shard_map/ppermute | solution.py:607
  25.4 3.4 %copy-start = (bf16[128,128,2,128]{3,2,1,0:T(2,128)(2,1)S(1)}, bf16[128,128,2,128]{3,2,1,0:T(2,128)(2,1)}, u32[]{:S(2)}) copy-start(bf16[128,128,2,128]{3,2,1,0:T(2,128)(2,1)} %param.18) | copy-start | bytes 25165828
  28.8 27.0 %copy-start.1 = (bf16[2048,640]{1,0:T(8,128)(2,1)S(1)}, bf16[2048,640]{1,0:T(8,128)(2,1)}, u32[]{:S(2)}) copy-start(bf16[2048,640]{1,0:T(8,128)(2,1)} %refs_2_.1) | copy-start | bytes 7864324
  38.7 4.2 %collective-permute-start.8 = (f32[4,9,16,128]{3,2,1,0:T(8,128)S(1)}, f32[4,9,16,128]{3,2,1,0:T(8,128)S(1)}, u32[]{:S(2)}, u32[]{:S(2)}) collective-permute-start(f32[4,9,16,128]{3,2,1,0:T(8,128)S(1)} %get-tuple-element.28), channel_id=1, source_target_pairs={{0,1},{1,0},{2,3},{3,2},{4,5},{5,4},{6,7},{7,6},{8,9},{9,8},{10,11... | collective-permute-start | bytes 884744 | tf_op jit(solution)/shard_map/ppermute | solution.py:607
  43.2 9.4 %collective-permute-start.10 = (bf16[4,9,16,128]{3,2,1,0:T(8,128)(2,1)S(1)}, bf16[4,9,16,128]{3,2,1,0:T(8,128)(2,1)S(1)}, u32[]{:S(2)}, u32[]{:S(2)}) collective-permute-start(bf16[4,9,16,128]{3,2,1,0:T(8,128)(2,1)S(1)} %merge_pair.1.refs_0_), channel_id=1, source_target_pairs={{0,4},{1,5},{2,6},{3,7},{4,0},{5,1},{6,2},{7,3},{8,12},{9,13},{10,... | collective-permute-start | bytes 442376 | tf_op jit(solution)/shard_map/ppermute | solution.py:607
  43.3 9.3 %collective-permute-start.11 = (bf16[4,9,16,128]{3,2,1,0:T(8,128)(2,1)S(1)}, bf16[4,9,16,128]{3,2,1,0:T(8,128)(2,1)S(1)}, u32[]{:S(2)}, u32[]{:S(2)}) collective-permute-start(bf16[4,9,16,128]{3,2,1,0:T(8,128)(2,1)S(1)} %merge_pair.1.refs_0_), channel_id=1, source_target_pairs={{0,6},{1,7},{2,4},{3,5},{4,2},{5,3},{6,0},{7,1},{8,14},{9,15},{10,... | collective-permute-start | bytes 442376 | tf_op jit(solution)/shard_map/ppermute | solution.py:607
  43.7 10.1 %collective-permute-start.9 = (bf16[4,9,16,128]{3,2,1,0:T(8,128)(2,1)S(1)}, bf16[4,9,16,128]{3,2,1,0:T(8,128)(2,1)S(1)}, u32[]{:S(2)}, u32[]{:S(2)}) collective-permute-start(bf16[4,9,16,128]{3,2,1,0:T(8,128)(2,1)S(1)} %merge_pair.1.refs_0_), channel_id=1, source_target_pairs={{0,2},{1,3},{2,0},{3,1},{4,6},{5,7},{6,4},{7,5},{8,10},{9,11},{10,... | collective-permute-start | bytes 442376 | tf_op jit(solution)/shard_map/ppermute | solution.py:607
  54.4 1.4 %collective-permute-start.12 = (bf16[32,2048]{1,0:T(8,128)(2,1)S(1)}, bf16[32,2048]{1,0:T(8,128)(2,1)S(1)}, u32[]{:S(2)}, u32[]{:S(2)}) collective-permute-start(bf16[32,2048]{1,0:T(8,128)(2,1)S(1)} %merge.1.refs_0_), channel_id=1, source_target_pairs={{0,1},{1,0},{2,3},{3,2},{4,5},{5,4},{6,7},{7,6},{8,9},{9,8},{10,11... | collective-permute-start | bytes 393224 | tf_op jit(solution)/shard_map/ppermute | solution.py:607
  56.4 4.5 %collective-permute-start.13 = (bf16[16,640]{1,0:T(8,128)(2,1)S(1)}, bf16[16,640]{1,0:T(8,128)(2,1)S(1)}, u32[]{:S(2)}, u32[]{:S(2)}) collective-permute-start(bf16[16,640]{1,0:T(8,128)(2,1)S(1)} %get-tuple-element.30), channel_id=1, source_target_pairs={{0,8},{8,0},{16,24},{24,16},{1,9},{9,1},{17,25},{25,17},{2,10},{10... | collective-permute-start | bytes 61448 | tf_op jit(solution)/shard_map/ppermute | solution.py:607
  58.1 4.9 %collective-permute-start.14 = (bf16[16,640]{1,0:T(8,128)(2,1)S(1)}, bf16[16,640]{1,0:T(8,128)(2,1)S(1)}, u32[]{:S(2)}, u32[]{:S(2)}) collective-permute-start(bf16[16,640]{1,0:T(8,128)(2,1)S(1)} %get-tuple-element.31), channel_id=1, source_target_pairs={{0,16},{8,24},{16,0},{24,8},{1,17},{9,25},{17,1},{25,9},{2,18},{10... | collective-permute-start | bytes 61448 | tf_op jit(solution)/shard_map/ppermute | solution.py:607
  60.6 5.6 %collective-permute-start.15 = (bf16[16,640]{1,0:T(8,128)(2,1)S(1)}, bf16[16,640]{1,0:T(8,128)(2,1)S(1)}, u32[]{:S(2)}, u32[]{:S(2)}) collective-permute-start(bf16[16,640]{1,0:T(8,128)(2,1)S(1)} %get-tuple-element.32), channel_id=1, source_target_pairs={{0,24},{8,16},{16,8},{24,0},{1,25},{9,17},{17,9},{25,1},{2,26},{10... | collective-permute-start | bytes 61448 | tf_op jit(solution)/shard_map/ppermute | solution.py:607

commit v8 on v7

--- a/solution.py
+++ b/solution.py
@@ -18,8 +18,8 @@
 GROUP = 4
 TASKS = 8
 CHUNK = GROUP * TASKS
-PHASES = 8
-AHEAD = 4
+PHASES = 16
+AHEAD = 6
 DEPTH = 256
 LOG2E = math.log2(math.e)
 MIB = 1024 * 1024
@@ -56,6 +56,8 @@
 
 def project_kernel(
     rank,
+    tenant_hbm,
+    adapter_hbm,
     tenant_ref,
     adapter_ref,
     holder_ref,
@@ -64,13 +66,18 @@
     hidden_hbm,
     weight_hbm,
     down_hbm,
+    up_hbm,
     keep_ref,
     send_ref,
+    own_up_ref,
     hidden_ref,
     weight_ref,
     down_ref,
     total_ref,
+    tenant_smem,
+    adapter_smem,
     sems,
+    up_sems,
 ):
     chips, own, _ = keep_ref.shape
     rows, depth = hidden_ref.shape
@@ -84,7 +91,11 @@
         pltpu.make_async_copy(weight_hbm.at[span], weight_ref.at[span], sems.at[2 + i])
         for i, span in enumerate(spans)
     ]
-    for copy in first + chunks:
+    scalars = [
+        pltpu.make_async_copy(tenant_hbm, tenant_smem, up_sems.at[own]),
+        pltpu.make_async_copy(adapter_hbm, adapter_smem, up_sems.at[own + 1]),
+    ]
+    for copy in scalars + first + chunks:
         copy.start()
 
     slots = holder_ref.shape[1]
@@ -96,7 +107,18 @@
     adapter = jnp.sum(jnp.where(pick, adapter_ref[...].astype(jnp.float32), 0.0), axis=1, keepdims=True).astype(
         jnp.int32
     )
-    even = lax.axis_index("kv") % PAIR == 0
+    me = lax.axis_index("kv")
+    even = me % PAIR == 0
+    for copy in scalars:
+        copy.wait()
+    ups = [
+        pltpu.make_async_copy(
+            up_hbm.at[adapter_smem[tenant_smem[me * own + r]]], own_up_ref.at[r], up_sems.at[r]
+        )
+        for r in range(own)
+    ]
+    for copy in ups:
+        copy.start()
 
     def store(columns, total):
         total = total.reshape(chips, PAIR, own, total.shape[1])
@@ -128,52 +150,34 @@
                 total_ref[:, tile] = total
             else:
                 store(tile, total)
-
-
-def project(tenant, tenant_adapter, holder, block, length, hidden, query_weight, down, rank, chips):
+    for copy in ups:
+        copy.wait()
+
+
+def project(tenant, tenant_adapter, holder, block, length, hidden, query_weight, down, up, rank, chips):
     rows, depth = hidden.shape
     width = query_weight.shape[1]
-    out = jax.ShapeDtypeStruct((chips, rows // chips // PAIR, width + LANES), jnp.float32)
-    operands = in_hbm(tenant, tenant_adapter, holder, block, length, hidden, query_weight, down)
-    large = operands[5:]
+    own = rows // chips // PAIR
+    out = jax.ShapeDtypeStruct((chips, own, width + LANES), jnp.float32)
+    tables = [x.reshape(1, -1) for x in (tenant, tenant_adapter)]
+    operands = in_hbm(tenant, tenant_adapter, *tables, holder, block, length, hidden, query_weight, down, up)
+    large = operands[7:10]
     return pl.pallas_call(
         functools.partial(project_kernel, rank),
-        in_specs=[vmem_spec()] * 5 + [hbm_spec()] * 3,
-        out_specs=[vmem_spec()] * 2,
-        out_shape=[out] * 2,
+        in_specs=[hbm_spec()] * 2 + [vmem_spec()] * 5 + [hbm_spec()] * 4,
+        out_specs=[vmem_spec()] * 3,
+        out_shape=[out, out, jax.ShapeDtypeStruct((own, *up.shape[1:]), up.dtype)],
         scratch_shapes=[pltpu.VMEM(x.shape, x.dtype) for x in large]
-        + [pltpu.VMEM((rows, width), jnp.float32), pltpu.SemaphoreType.DMA((2 + pl.cdiv(depth, DEPTH),))],
+        + [
+            pltpu.VMEM((rows, width), jnp.float32),
+            pltpu.SMEM(tenant.shape, tenant.dtype),
+            pltpu.SMEM(tenant_adapter.shape, tenant_adapter.dtype),
+            pltpu.SemaphoreType.DMA((2 + pl.cdiv(depth, DEPTH),)),
+            pltpu.SemaphoreType.DMA((own + 2,)),
+        ],
         compiler_params=params(16),
         name="project",
     )(*operands)
-
-
-def gather_up_kernel(tenant_ref, adapter_ref, up_hbm, out_ref, sems):
-    own = out_ref.shape[0]
-    me = lax.axis_index("kv")
-    copies = [
-        pltpu.make_async_copy(up_hbm.at[adapter_ref[tenant_ref[me * own + r]]], out_ref.at[r], sems.at[r])
-        for r in range(own)
-    ]
-    for copy in copies:
-        copy.start()
-    for copy in copies:
-        copy.wait()
-
-
-def gather_up(tenant, tenant_adapter, up, own):
-    (up,) = in_hbm(up)
-    smem = pl.BlockSpec(memory_space=pltpu.SMEM)
-    return pl.pallas_call(
-        gather_up_kernel,
-        in_specs=[smem, smem, hbm_spec()],
-        out_specs=vmem_spec(),
-        out_shape=jax.ShapeDtypeStruct((own, *up.shape[1:]), up.dtype),
-        scratch_shapes=[pltpu.SemaphoreType.DMA((own,))],
-        compiler_params=params(16),
-        cost_estimate=pl.CostEstimate(flops=0, bytes_accessed=own * up.shape[1] * up.shape[2] * 4, transcendentals=0),
-        name="gather_up",
-    )(tenant, tenant_adapter, up)
 
 
 def pair_kernel(number_lanes, keep_ref, got_ref, *out_refs):
@@ -337,8 +341,9 @@
 
 def attend_kernel(scale, kv_local, count, list_vmem, bound_vmem, *refs):
     queries, refs = refs[: count // PAIR], refs[count // PAIR :]
-    (key_ref, value_hbm, keep_ref, send_ref, list_ref, bound_ref, query_ref, value_ref) = refs[:8]
-    (top_ref, total_ref, sum_ref, score_ref, part_top_ref, part_total_ref, part_sum_ref, number_sems, sems) = refs[8:]
+    (key_hbm, value_hbm, keep_ref, send_ref, list_ref, bound_ref, query_ref, key_ref, value_ref) = refs[:9]
+    (score_ref, part_top_ref, part_total_ref, part_sum_ref, number_sems, sems) = refs[9:15]
+    states = [refs[15 + 3 * k : 18 + 3 * k] for k in range(GROUP)]
     heads = query_ref.shape[1]
     rows = query_ref.shape[0] - 1
     own = rows // count
@@ -353,10 +358,15 @@
     size = blocks // PHASES
     spans = [pl.ds(part * size, size) for part in range(PHASES)]
     copies = [
-        pltpu.make_async_copy(value_hbm.at[span], value_ref.at[span], sems.at[part]) for part, span in enumerate(spans)
+        (
+            pltpu.make_async_copy(key_hbm.at[span], key_ref.at[span], sems.at[0, part]),
+            pltpu.make_async_copy(value_hbm.at[span], value_ref.at[span], sems.at[1, part]),
+        )
+        for part, span in enumerate(spans)
     ]
-    for copy in (copies[0], *numbers, *copies[1:AHEAD]):
-        copy.start()
+    for pair in (copies[0], numbers, *copies[1:AHEAD]):
+        for copy in pair:
+            copy.start()
 
     factor = scale * LOG2E
     for s, piece in enumerate(queries):
@@ -364,8 +374,10 @@
             start = (PAIR * s + t) * own
             query_ref[start : start + own] = piece[t]
     query_ref[rows] = jnp.zeros((heads, LANES), jnp.bfloat16)
-    top_ref[...] = jnp.full(top_ref.shape, NEG_FILL, jnp.float32)
-    for ref in (total_ref, sum_ref, score_ref, part_top_ref, part_total_ref, part_sum_ref):
+    for state in states:
+        for ref, value in zip(state, (NEG_FILL, 0.0, 0.0)):
+            ref[...] = jnp.full(ref.shape, value, jnp.float32)
+    for ref in (score_ref, part_top_ref, part_total_ref, part_sum_ref):
         ref[...] = jnp.zeros(ref.shape, jnp.float32)
     group = heads // kv_local
     column = lax.broadcasted_iota(jnp.int32, (group, tokens), 1)
@@ -382,15 +394,25 @@
     def block_of(entry):
         return (entry >> length_bits) & (blocks - 1)
 
-    def merge_item(row, t, k):
-        j = t * GROUP + k
-        top, part_top = top_ref[row], part_top_ref[j]
-        top_ref[row] = jnp.maximum(top, part_top)
-        share = jnp.exp2(-jnp.abs(top - part_top) * factor)
-        lower = top < part_top
-        old, new = jnp.where(lower, share, 1.0), jnp.where(lower, 1.0, share)
-        total_ref[row] = total_ref[row] * old + part_total_ref[j] * new
-        sum_ref[row] = sum_ref[row] * old + part_sum_ref[t, k * heads : (k + 1) * heads] * new
+    def merge_task(row, t):
+        before = [[ref[row[k]] for ref in states[k]] for k in range(GROUP)]
+        after = []
+        for k, (top, total, acc) in enumerate(before):
+            j = t * GROUP + k
+            part_top = part_top_ref[j]
+            share = jnp.exp2(-jnp.abs(top - part_top) * factor)
+            lower = top < part_top
+            old, new = jnp.where(lower, share, 1.0), jnp.where(lower, 1.0, share)
+            after.append(
+                (
+                    jnp.maximum(top, part_top),
+                    total * old + part_total_ref[j] * new,
+                    acc * old + part_sum_ref[t, k * heads : (k + 1) * heads] * new,
+                )
+            )
+        for k in range(GROUP):
+            for ref, value in zip(states[k], after[k]):
+                ref[row[k]] = value
 
     def weigh_item(entry, t, k):
         j = t * GROUP + k
@@ -416,8 +438,7 @@
         merged, weighed, scored = (entries(jnp.maximum(i - back, 0)) for back in (2, 1, 0))
         for t in range(TASKS):
             task = slice(t * GROUP, (t + 1) * GROUP)
-            for k, entry in enumerate(merged[task]):
-                merge_item(jnp.where(i >= 2, row_of(entry), rows), t, k)
+            merge_task([jnp.where(i >= 2, row_of(entry), rows) for entry in merged[task]], t)
             if stages > 1:
                 weights = [weigh_item(entry, t, k) for k, entry in enumerate(weighed[task])]
                 part_sum_ref[t] = jnp.dot(
@@ -437,9 +458,11 @@
     for copy in numbers:
         copy.wait()
     for part in range(PHASES):
-        copies[part].wait()
-        for copy in copies[part + AHEAD : part + AHEAD + 1]:
-            copy.start()
+        for copy in copies[part]:
+            copy.wait()
+        for pair in copies[part + AHEAD : part + AHEAD + 1]:
+            for copy in pair:
+                copy.start()
         lax.fori_loop(bound_ref[0, part], bound_ref[0, part + 1], functools.partial(turn, 3), 0)
     last = bound_ref[0, PHASES]
     turn(2, last, 0)
@@ -451,12 +474,15 @@
     for q in range(count):
         ref = (keep_ref, send_ref)[q % PAIR]
         mine = slice(q * own, (q + 1) * own)
-        top, total = (
-            jnp.sum(jnp.where(eye, state[mine].reshape(square), 0.0), axis=0, keepdims=True)
-            for state in (top_ref, total_ref)
+        tops = [top_ref[mine] for top_ref, _, _ in states]
+        high = functools.reduce(jnp.maximum, tops)
+        shares = [jnp.exp2((top - high) * factor) for top in tops]
+        total = sum(total_ref[mine] * share for (_, total_ref, _), share in zip(states, shares))
+        ref[q // PAIR, :own] = sum(sum_ref[mine] * share for (_, _, sum_ref), share in zip(states, shares))
+        high, total = (
+            jnp.sum(jnp.where(eye, x.reshape(square), 0.0), axis=0, keepdims=True) for x in (high, total)
         )
-        ref[q // PAIR, :own] = sum_ref[mine]
-        ref[q // PAIR, own] = jnp.where(line == 0, top, jnp.where(line == 1, total, 0.0))
+        ref[q // PAIR, own] = jnp.where(line == 0, high, jnp.where(line == 1, total, 0.0))
 
 
 def attend(items, bounds, queries, keys, values, kv_local, scale):
@@ -464,31 +490,29 @@
     count = len(queries) * PAIR
     rows = count * own
     tokens = keys.shape[1]
-    keys = pltpu.with_memory_space_constraint(keys, pltpu.VMEM)
-    (values,) = in_hbm(values)
+    keys, values = in_hbm(keys, values)
     state = pltpu.VMEM((rows + 1, heads, LANES), jnp.float32)
     part = pltpu.VMEM((CHUNK, heads, LANES), jnp.float32)
     return pl.pallas_call(
         functools.partial(attend_kernel, scale, kv_local, count),
-        in_specs=[vmem_spec()] * (3 + len(queries)) + [hbm_spec()],
+        in_specs=[vmem_spec()] * (2 + len(queries)) + [hbm_spec()] * 2,
         out_specs=[vmem_spec()] * PAIR,
         out_shape=[jax.ShapeDtypeStruct((count // PAIR, own + 1, heads, LANES), jnp.float32)] * PAIR,
         scratch_shapes=[
             pltpu.SMEM(items.shape, items.dtype),
             pltpu.SMEM(bounds.shape, bounds.dtype),
             pltpu.VMEM((rows + 1, heads, LANES), jnp.bfloat16),
+            pltpu.VMEM(keys.shape, keys.dtype),
             pltpu.VMEM(values.shape, values.dtype),
-            state,
-            state,
-            state,
             pltpu.VMEM((TASKS, GROUP * heads, tokens), jnp.float32),
             part,
             part,
             pltpu.VMEM((TASKS, GROUP * heads, LANES), jnp.float32),
             pltpu.SemaphoreType.DMA((2,)),
-            pltpu.SemaphoreType.DMA((PHASES,)),
-        ],
-        compiler_params=params(32),
+            pltpu.SemaphoreType.DMA((2, PHASES)),
+        ]
+        + [state] * (3 * GROUP),
+        compiler_params=params(28 + 3 * GROUP * rows * heads * LANES * 4 // MIB),
         name="attend",
     )(items, bounds, *queries, keys, values)
 
@@ -642,19 +666,19 @@
     scale = 1.0 / math.sqrt(head_size)
 
     chips = kv_count // PAIR
-    keep, send = project(
-        tenant.reshape(1, rows),
-        tenant_adapter.reshape(1, -1),
+    keep, send, up = project(
+        tenant,
+        tenant_adapter,
         holder,
         holder_block_index,
         block_used_length,
         hidden,
         query_weight,
         jnp.swapaxes(adapter_down_weight, 1, 2).reshape(adapters * rank, depth),
+        adapter_up_weight,
         rank,
         chips,
     )
-    up = gather_up(tenant, tenant_adapter, adapter_up_weight, own)
     parts = add_pair(keep, exchange(send, "kv", 1), 3 * slots)
     parts = [parts[0]] + [exchange(parts[s], "kv", PAIR * s) for s in range(1, chips)]
 

time: 67.4 us -> 62.1 us (0.921)
  local copies, waits for them, and re-layouts: 4.7 us -> 0.01 us
  waiting for transfers between devices: 21.7 us -> 22.5 us
  other arithmetic: 1.64 us -> 0.95 us
    unnamed x10 -> x6, local copies, waits for them, and re-layouts: 4.7 us -> 0.01 us
    pallas_call x2 -> x1, Pallas kernels: 5 us -> 3.31 us  [project(): pl.pallas_call(functools.partial(project_kernel, rank), in_specs=[hbm_spe...]
    pallas_call x1, Pallas kernels: 9.86 us -> 11 us  [attend(): pl.pallas_call(functools.partial(attend_kernel, scale, kv_local, count),...]
    ppermute x16, waiting for transfers between devices: 21.7 us -> 22.5 us  [exchange(): return lax.ppermute(x, axis, [(i, i ^ s) for i in range(count)])]
    reduce_sum x1, other arithmetic: 0.8 us -> 0.12 us  [local(): position = (jnp.sum(block_used_length, axis=1) - 1).astype(jnp.float32)]
  transfers between devices with their start and end apart: 16 -> 16, of which waited for: 11 -> 12; matrix products, arithmetic and copies ran while one was open for 2% -> 1% of each run, Pallas kernels for 6% -> 4%
where the time goes in v8:
time: 62.1 us; the launch traced here: 62 us
  waiting for transfers between devices  22.5 us (36%)
  starting transfers between devices  19.7 us (32%)
  Pallas kernels  18.8 us (30%)
  other arithmetic  0.95 us (2%)
    ppermute x16, waiting for transfers between devices, exchange(): return lax.ppermute(x, axis, [(i, i ^ s) for i in range(count)])  22.5 us
    ppermute x16, starting transfers between devices, exchange(): return lax.ppermute(x, axis, [(i, i ^ s) for i in range(count)])  19.7 us
    pallas_call x1, Pallas kernels, attend(): pl.pallas_call(functools.partial(attend_kernel, scale, kv_local, count),...  11 us
    pallas_call x1, Pallas kernels, project(): pl.pallas_call(functools.partial(project_kernel, rank), in_specs=[hbm_spe...  3.31 us
    pallas_call x1, Pallas kernels, make_list(): pl.pallas_call(functools.partial(list_kernel, blocks, block_size, slots),...  2.44 us
  transfers between devices with their start and end apart: 16, of which 12 were waited for; matrix products, arithmetic and copies ran while one was open for 1% of the time, Pallas kernels for 4%

profile of v8, /device:TPU:0, one launch (start us, length us, event | category | flops | bytes accessed | tf_op | source)
XLA Modules:
  0.0 62.0 jit_solution(12128555426999986668)
XLA Ops:
  0.0 3.3 %project.1 = (f32[4,8,2176]{2,1,0:T(8,128)S(1)}, f32[4,8,2176]{2,1,0:T(8,128)S(1)}, f32[8,16,2048]{2,1,0:T(8,128)S(1)}) custom-call(s32[64]{0:T(128)} %tenant_hbm.1, s32[64]{0:T(128)} %adapter_hbm.1, s32[1,64]{1,0:T(1,128)} %bitcast.20, s32[1,64]{1,0:T(1,128)} %bitcast.21, s32[8,32]{1,0:T(8,128)} %holder_ref.1, s32[8,32]{1,0:T(8,128)} %block_ref.1, ...), custom_call_target="tpu_custom_call" | custom-call | tf_op jit(solution)/shard_map/project/pallas_call | solution.py:165
  3.3 0.5 collective-permute-start
  4.1 0.9 %collective-permute-done.got_ref = f32[4,8,2176]{2,1,0:T(8,128)S(1)} collective-permute-done((f32[4,8,2176]{2,1,0:T(8,128)S(1)}, f32[4,8,2176]{2,1,0:T(8,128)S(1)}, u32[]{:S(2)}, u32[]{:S(2)}) %collective-permute-start) | collective-permute-done | bytes 278560 | tf_op jit(solution)/shard_map/ppermute | solution.py:631
  5.1 2.9 %collective-permute-start.1 = (f32[8,2304]{1,0:T(8,128)S(1)}, f32[8,2304]{1,0:T(8,128)S(1)}, u32[]{:S(2)}, u32[]{:S(2)}) collective-permute-start(f32[8,2304]{1,0:T(8,128)S(1)} %get-tuple-element.23), channel_id=1, source_target_pairs={{0,2},{1,3},{2,0},{3,1},{4,6},{5,7},{6,4},{7,5},{8,10},{9,11},{10,... | collective-permute-start | bytes 221192 | tf_op jit(solution)/shard_map/ppermute | solution.py:631
  8.0 1.5 %collective-permute-start.2 = (f32[8,2304]{1,0:T(8,128)S(1)}, f32[8,2304]{1,0:T(8,128)S(1)}, u32[]{:S(2)}, u32[]{:S(2)}) collective-permute-start(f32[8,2304]{1,0:T(8,128)S(1)} %get-tuple-element.24), channel_id=1, source_target_pairs={{0,4},{1,5},{2,6},{3,7},{4,0},{5,1},{6,2},{7,3},{8,12},{9,13},{10,... | collective-permute-start | bytes 221192 | tf_op jit(solution)/shard_map/ppermute | solution.py:631
  9.6 1.0 %collective-permute-done.1.refs_1_ = f32[8,2304]{1,0:T(8,128)S(1)} collective-permute-done((f32[8,2304]{1,0:T(8,128)S(1)}, f32[8,2304]{1,0:T(8,128)S(1)}, u32[]{:S(2)}, u32[]{:S(2)}) %collective-permute-start.1) | collective-permute-done | bytes 73760 | tf_op jit(solution)/shard_map/ppermute | solution.py:631
  10.6 1.8 %collective-permute-done.2.refs_2_ = f32[8,2304]{1,0:T(8,128)S(1)} collective-permute-done((f32[8,2304]{1,0:T(8,128)S(1)}, f32[8,2304]{1,0:T(8,128)S(1)}, u32[]{:S(2)}, u32[]{:S(2)}) %collective-permute-start.2) | collective-permute-done | bytes 73760 | tf_op jit(solution)/shard_map/ppermute | solution.py:631
  12.3 2.4 %collective-permute-done.3.refs_3_ = f32[8,2304]{1,0:T(8,128)S(1)} collective-permute-done((f32[8,2304]{1,0:T(8,128)S(1)}, f32[8,2304]{1,0:T(8,128)S(1)}, u32[]{:S(2)}, u32[]{:S(2)}) %collective-permute-start.3) | collective-permute-done | bytes 73760 | tf_op jit(solution)/shard_map/ppermute | solution.py:631
  14.8 0.4 queries.1
  15.3 1.2 %collective-permute-done.4 = bf16[8,16,128]{2,1,0:T(8,128)(2,1)S(1)} collective-permute-done((bf16[8,16,128]{2,1,0:T(8,128)(2,1)S(1)}, bf16[8,16,128]{2,1,0:T(8,128)(2,1)S(1)}, u32[]{:S(2)}, u32[]{:S(2)}) %collective-permute-start.4) | collective-permute-done | bytes 32800 | tf_op jit(solution)/shard_map/ppermute | solution.py:631
  16.5 0.6 collective-permute-start.5
  17.1 0.6 collective-permute-start.6
  17.6 2.4 %collective-permute-start.7 = (bf16[16,16,128]{2,1,0:T(8,128)(2,1)S(1)}, bf16[16,16,128]{2,1,0:T(8,128)(2,1)S(1)}, u32[]{:S(2)}, u32[]{:S(2)}) collective-permute-start(bf16[16,16,128]{2,1,0:T(8,128)(2,1)S(1)} %pad_maximum_fusion), channel_id=1, source_target_pairs={{0,6},{1,7},{2,4},{3,5},{4,2},{5,3},{6,0},{7,1},{8,14},{9,15},{10,... | collective-permute-start | bytes 196616 | tf_op jit(solution)/shard_map/ppermute | solution.py:631
  20.0 2.4 %slot_list.1 = (s32[1,1024]{1,0:T(1,128)S(1)}, s32[1,128]{1,0:T(1,128)S(1)}) custom-call(f32[8,2304]{1,0:T(8,128)S(1)} %get-tuple-element.22.refs_0_, f32[8,2304]{1,0:T(8,128)S(1)} %collective-permute-done.1.refs_1_, f32[8,2304]{1,0:T(8,128)S(1)} %collective-permute-done.2.refs_2_, f32[8,2304]{1,0:T(8,128)S(1)} %collective-permute-done.3.refs_3_), custom_call_target="tpu_custom_call" | custom-call | flops 100000000 | bytes 10000000 | tf_op jit(solution)/shard_map/slot_list/pallas_call | solution.py:323
  22.5 0.3 collective-permute-done.7
  22.8 11.0 %attend.1 = (f32[4,9,16,128]{3,2,1,0:T(8,128)S(1)}, f32[4,9,16,128]{3,2,1,0:T(8,128)S(1)}) custom-call(s32[1,1024]{1,0:T(1,128)S(1)} %get-tuple-element.26.list_vmem, s32[1,128]{1,0:T(1,128)S(1)} %get-tuple-element.27.bound_vmem, bf16[2,8,16,128]{3,2,1,0:T(8,128)(2,1)S(1)} %bitcast.12, bf16[2,8,16,128]{3,2,1,0:T(8,128)(2,1)S(1)} %bitcast.13, ...), custom_call_target="tpu_custom_call" | custom-call | tf_op jit(solution)/shard_map/attend/pallas_call | solution.py:496
  33.9 3.0 %collective-permute-start.8 = (f32[4,9,16,128]{3,2,1,0:T(8,128)S(1)}, f32[4,9,16,128]{3,2,1,0:T(8,128)S(1)}, u32[]{:S(2)}, u32[]{:S(2)}) collective-permute-start(f32[4,9,16,128]{3,2,1,0:T(8,128)S(1)} %get-tuple-element.30), channel_id=1, source_target_pairs={{0,1},{1,0},{2,3},{3,2},{4,5},{5,4},{6,7},{7,6},{8,9},{9,8},{10,11... | collective-permute-start | bytes 884744 | tf_op jit(solution)/shard_map/ppermute | solution.py:631
  36.8 1.2 %collective-permute-done.8.got_ref = f32[4,9,16,128]{3,2,1,0:T(8,128)S(1)} collective-permute-done((f32[4,9,16,128]{3,2,1,0:T(8,128)S(1)}, f32[4,9,16,128]{3,2,1,0:T(8,128)S(1)}, u32[]{:S(2)}, u32[]{:S(2)}) %collective-permute-start.8) | collective-permute-done | bytes 294944 | tf_op jit(solution)/shard_map/ppermute | solution.py:631
  38.0 0.3 merge_pair.1.refs_0_
  38.5 0.9 %collective-permute-start.11 = (bf16[4,9,16,128]{3,2,1,0:T(8,128)(2,1)S(1)}, bf16[4,9,16,128]{3,2,1,0:T(8,128)(2,1)S(1)}, u32[]{:S(2)}, u32[]{:S(2)}) collective-permute-start(bf16[4,9,16,128]{3,2,1,0:T(8,128)(2,1)S(1)} %merge_pair.1.refs_0_), channel_id=1, source_target_pairs={{0,6},{1,7},{2,4},{3,5},{4,2},{5,3},{6,0},{7,1},{8,14},{9,15},{10,... | collective-permute-start | bytes 442376 | tf_op jit(solution)/shard_map/ppermute | solution.py:631
  39.4 2.6 %collective-permute-start.9 = (bf16[4,9,16,128]{3,2,1,0:T(8,128)(2,1)S(1)}, bf16[4,9,16,128]{3,2,1,0:T(8,128)(2,1)S(1)}, u32[]{:S(2)}, u32[]{:S(2)}) collective-permute-start(bf16[4,9,16,128]{3,2,1,0:T(8,128)(2,1)S(1)} %merge_pair.1.refs_0_), channel_id=1, source_target_pairs={{0,2},{1,3},{2,0},{3,1},{4,6},{5,7},{6,4},{7,5},{8,10},{9,11},{10,... | collective-permute-start | bytes 442376 | tf_op jit(solution)/shard_map/ppermute | solution.py:631
  41.9 5.8 %collective-permute-done.10.refs_2_ = bf16[4,9,16,128]{3,2,1,0:T(8,128)(2,1)S(1)} collective-permute-done((bf16[4,9,16,128]{3,2,1,0:T(8,128)(2,1)S(1)}, bf16[4,9,16,128]{3,2,1,0:T(8,128)(2,1)S(1)}, u32[]{:S(2)}, u32[]{:S(2)}) %collective-permute-start.10) | collective-permute-done | bytes 147488 | tf_op jit(solution)/shard_map/ppermute | solution.py:631
  47.7 1.2 %collective-permute-done.9.refs_1_ = bf16[4,9,16,128]{3,2,1,0:T(8,128)(2,1)S(1)} collective-permute-done((bf16[4,9,16,128]{3,2,1,0:T(8,128)(2,1)S(1)}, bf16[4,9,16,128]{3,2,1,0:T(8,128)(2,1)S(1)}, u32[]{:S(2)}, u32[]{:S(2)}) %collective-permute-start.9) | collective-permute-done | bytes 147488 | tf_op jit(solution)/shard_map/ppermute | solution.py:631
  49.0 0.6 merge.1.refs_0_
  49.6 1.3 %collective-permute-done.12.refs_1_ = bf16[32,2048]{1,0:T(8,128)(2,1)S(1)} collective-permute-done((bf16[32,2048]{1,0:T(8,128)(2,1)S(1)}, bf16[32,2048]{1,0:T(8,128)(2,1)S(1)}, u32[]{:S(2)}, u32[]{:S(2)}) %collective-permute-start.12) | collective-permute-done | bytes 131104 | tf_op jit(solution)/shard_map/ppermute | solution.py:631
  51.0 0.6 project_out.1
  51.6 1.6 %collective-permute-start.13 = (bf16[16,640]{1,0:T(8,128)(2,1)S(1)}, bf16[16,640]{1,0:T(8,128)(2,1)S(1)}, u32[]{:S(2)}, u32[]{:S(2)}) collective-permute-start(bf16[16,640]{1,0:T(8,128)(2,1)S(1)} %get-tuple-element.32), channel_id=1, source_target_pairs={{0,8},{8,0},{16,24},{24,16},{1,9},{9,1},{17,25},{25,17},{2,10},{10... | collective-permute-start | bytes 61448 | tf_op jit(solution)/shard_map/ppermute | solution.py:631
  53.2 2.6 %collective-permute-start.14 = (bf16[16,640]{1,0:T(8,128)(2,1)S(1)}, bf16[16,640]{1,0:T(8,128)(2,1)S(1)}, u32[]{:S(2)}, u32[]{:S(2)}) collective-permute-start(bf16[16,640]{1,0:T(8,128)(2,1)S(1)} %get-tuple-element.33), channel_id=1, source_target_pairs={{0,16},{8,24},{16,0},{24,8},{1,17},{9,25},{17,1},{25,9},{2,18},{10... | collective-permute-start | bytes 61448 | tf_op jit(solution)/shard_map/ppermute | solution.py:631
  55.8 0.2 collective-permute-start.15
  56.0 2.1 %collective-permute-done.14 = bf16[16,640]{1,0:T(8,128)(2,1)S(1)} collective-permute-done((bf16[16,640]{1,0:T(8,128)(2,1)S(1)}, bf16[16,640]{1,0:T(8,128)(2,1)S(1)}, u32[]{:S(2)}, u32[]{:S(2)}) %collective-permute-start.14) | collective-permute-done | bytes 20512 | tf_op jit(solution)/shard_map/ppermute | solution.py:631
  58.1 3.2 %collective-permute-done.15 = bf16[16,640]{1,0:T(8,128)(2,1)S(1)} collective-permute-done((bf16[16,640]{1,0:T(8,128)(2,1)S(1)}, bf16[16,640]{1,0:T(8,128)(2,1)S(1)}, u32[]{:S(2)}, u32[]{:S(2)}) %collective-permute-start.15) | collective-permute-done | bytes 20512 | tf_op jit(solution)/shard_map/ppermute | solution.py:631
  61.4 0.6 %add_convert_fusion = bf16[16,640]{1,0:T(8,128)(2,1)} fusion(bf16[16,640]{1,0:T(8,128)(2,1)S(1)} %collective-permute-done.15, bf16[16,640]{1,0:T(8,128)(2,1)S(1)} %collective-permute-done.14, f32[16,640]{1,0:T(8,128)S(1)} %get-tuple-element.31, bf16[16,640]{1,0:T(8,128)(2,1)S(1)} %collective-permute-done.13), kind=kLoop, calls=%fused_computation.1 | loop fusion | flops 71680 | bytes 122880 | tf_op jit(solution)/shard_map/convert_element_type | solution.py:704
  (21 shorter events, 0.6 us)
Async XLA Ops:
  0.0 3.8 %copy-start.2 = (s32[8,32]{1,0:T(8,128)S(1)}, s32[8,32]{1,0:T(8,128)}, u32[]{:S(2)}) copy-start(s32[8,32]{1,0:T(8,128)} %length_ref.1) | copy-start | bytes 3076
  0.0 14.8 %copy-start.1 = (f32[128]{0:T(128)S(1)}, f32[128]{0:T(128)}, u32[]{:S(2)}) copy-start(f32[128]{0:T(128)} %param.17) | copy-start | bytes 1540
  3.3 1.7 %collective-permute-start = (f32[4,8,2176]{2,1,0:T(8,128)S(1)}, f32[4,8,2176]{2,1,0:T(8,128)S(1)}, u32[]{:S(2)}, u32[]{:S(2)}) collective-permute-start(f32[4,8,2176]{2,1,0:T(8,128)S(1)} %get-tuple-element.21), channel_id=1, source_target_pairs={{0,1},{1,0},{2,3},{3,2},{4,5},{5,4},{6,7},{7,6},{8,9},{9,8},{10,11... | collective-permute-start | bytes 835592 | tf_op jit(solution)/shard_map/ppermute | solution.py:631
  5.1 5.5 %collective-permute-start.1 = (f32[8,2304]{1,0:T(8,128)S(1)}, f32[8,2304]{1,0:T(8,128)S(1)}, u32[]{:S(2)}, u32[]{:S(2)}) collective-permute-start(f32[8,2304]{1,0:T(8,128)S(1)} %get-tuple-element.23), channel_id=1, source_target_pairs={{0,2},{1,3},{2,0},{3,1},{4,6},{5,7},{6,4},{7,5},{8,10},{9,11},{10,... | collective-permute-start | bytes 221192 | tf_op jit(solution)/shard_map/ppermute | solution.py:631
  8.0 4.4 %collective-permute-start.2 = (f32[8,2304]{1,0:T(8,128)S(1)}, f32[8,2304]{1,0:T(8,128)S(1)}, u32[]{:S(2)}, u32[]{:S(2)}) collective-permute-start(f32[8,2304]{1,0:T(8,128)S(1)} %get-tuple-element.24), channel_id=1, source_target_pairs={{0,4},{1,5},{2,6},{3,7},{4,0},{5,1},{6,2},{7,3},{8,12},{9,13},{10,... | collective-permute-start | bytes 221192 | tf_op jit(solution)/shard_map/ppermute | solution.py:631
  9.5 5.3 %collective-permute-start.3 = (f32[8,2304]{1,0:T(8,128)S(1)}, f32[8,2304]{1,0:T(8,128)S(1)}, u32[]{:S(2)}, u32[]{:S(2)}) collective-permute-start(f32[8,2304]{1,0:T(8,128)S(1)} %get-tuple-element.25), channel_id=1, source_target_pairs={{0,6},{1,7},{2,4},{3,5},{4,2},{5,3},{6,0},{7,1},{8,14},{9,15},{10,... | collective-permute-start | bytes 221192 | tf_op jit(solution)/shard_map/ppermute | solution.py:631
  15.2 1.3 %collective-permute-start.4 = (bf16[8,16,128]{2,1,0:T(8,128)(2,1)S(1)}, bf16[8,16,128]{2,1,0:T(8,128)(2,1)S(1)}, u32[]{:S(2)}, u32[]{:S(2)}) collective-permute-start(bf16[8,16,128]{2,1,0:T(8,128)(2,1)S(1)} %queries.1), channel_id=1, source_target_pairs={{0,1},{1,0},{2,3},{3,2},{4,5},{5,4},{6,7},{7,6},{8,9},{9,8},{10,11... | collective-permute-start | bytes 98312 | tf_op jit(solution)/shard_map/ppermute | solution.py:631
  16.5 6.0 %collective-permute-start.5 = (bf16[16,16,128]{2,1,0:T(8,128)(2,1)S(1)}, bf16[16,16,128]{2,1,0:T(8,128)(2,1)S(1)}, u32[]{:S(2)}, u32[]{:S(2)}) collective-permute-start(bf16[16,16,128]{2,1,0:T(8,128)(2,1)S(1)} %pad_maximum_fusion), channel_id=1, source_target_pairs={{0,2},{1,3},{2,0},{3,1},{4,6},{5,7},{6,4},{7,5},{8,10},{9,11},{10,... | collective-permute-start | bytes 196616 | tf_op jit(solution)/shard_map/ppermute | solution.py:631
  17.1 5.4 %collective-permute-start.6 = (bf16[16,16,128]{2,1,0:T(8,128)(2,1)S(1)}, bf16[16,16,128]{2,1,0:T(8,128)(2,1)S(1)}, u32[]{:S(2)}, u32[]{:S(2)}) collective-permute-start(bf16[16,16,128]{2,1,0:T(8,128)(2,1)S(1)} %pad_maximum_fusion), channel_id=1, source_target_pairs={{0,4},{1,5},{2,6},{3,7},{4,0},{5,1},{6,2},{7,3},{8,12},{9,13},{10,... | collective-permute-start | bytes 196616 | tf_op jit(solution)/shard_map/ppermute | solution.py:631
  17.6 5.2 %collective-permute-start.7 = (bf16[16,16,128]{2,1,0:T(8,128)(2,1)S(1)}, bf16[16,16,128]{2,1,0:T(8,128)(2,1)S(1)}, u32[]{:S(2)}, u32[]{:S(2)}) collective-permute-start(bf16[16,16,128]{2,1,0:T(8,128)(2,1)S(1)} %pad_maximum_fusion), channel_id=1, source_target_pairs={{0,6},{1,7},{2,4},{3,5},{4,2},{5,3},{6,0},{7,1},{8,14},{9,15},{10,... | collective-permute-start | bytes 196616 | tf_op jit(solution)/shard_map/ppermute | solution.py:631
  22.8 28.1 %copy-start = (bf16[2048,640]{1,0:T(8,128)(2,1)S(1)}, bf16[2048,640]{1,0:T(8,128)(2,1)}, u32[]{:S(2)}) copy-start(bf16[2048,640]{1,0:T(8,128)(2,1)} %refs_2_.1) | copy-start | bytes 7864324
  33.9 4.2 %collective-permute-start.8 = (f32[4,9,16,128]{3,2,1,0:T(8,128)S(1)}, f32[4,9,16,128]{3,2,1,0:T(8,128)S(1)}, u32[]{:S(2)}, u32[]{:S(2)}) collective-permute-start(f32[4,9,16,128]{3,2,1,0:T(8,128)S(1)} %get-tuple-element.30), channel_id=1, source_target_pairs={{0,1},{1,0},{2,3},{3,2},{4,5},{5,4},{6,7},{7,6},{8,9},{9,8},{10,11... | collective-permute-start | bytes 884744 | tf_op jit(solution)/shard_map/ppermute | solution.py:631
  38.4 9.4 %collective-permute-start.10 = (bf16[4,9,16,128]{3,2,1,0:T(8,128)(2,1)S(1)}, bf16[4,9,16,128]{3,2,1,0:T(8,128)(2,1)S(1)}, u32[]{:S(2)}, u32[]{:S(2)}) collective-permute-start(bf16[4,9,16,128]{3,2,1,0:T(8,128)(2,1)S(1)} %merge_pair.1.refs_0_), channel_id=1, source_target_pairs={{0,4},{1,5},{2,6},{3,7},{4,0},{5,1},{6,2},{7,3},{8,12},{9,13},{10,... | collective-permute-start | bytes 442376 | tf_op jit(solution)/shard_map/ppermute | solution.py:631
  38.5 9.3 %collective-permute-start.11 = (bf16[4,9,16,128]{3,2,1,0:T(8,128)(2,1)S(1)}, bf16[4,9,16,128]{3,2,1,0:T(8,128)(2,1)S(1)}, u32[]{:S(2)}, u32[]{:S(2)}) collective-permute-start(bf16[4,9,16,128]{3,2,1,0:T(8,128)(2,1)S(1)} %merge_pair.1.refs_0_), channel_id=1, source_target_pairs={{0,6},{1,7},{2,4},{3,5},{4,2},{5,3},{6,0},{7,1},{8,14},{9,15},{10,... | collective-permute-start | bytes 442376 | tf_op jit(solution)/shard_map/ppermute | solution.py:631
  39.4 9.6 %collective-permute-start.9 = (bf16[4,9,16,128]{3,2,1,0:T(8,128)(2,1)S(1)}, bf16[4,9,16,128]{3,2,1,0:T(8,128)(2,1)S(1)}, u32[]{:S(2)}, u32[]{:S(2)}) collective-permute-start(bf16[4,9,16,128]{3,2,1,0:T(8,128)(2,1)S(1)} %merge_pair.1.refs_0_), channel_id=1, source_target_pairs={{0,2},{1,3},{2,0},{3,1},{4,6},{5,7},{6,4},{7,5},{8,10},{9,11},{10,... | collective-permute-start | bytes 442376 | tf_op jit(solution)/shard_map/ppermute | solution.py:631
  49.5 1.4 %collective-permute-start.12 = (bf16[32,2048]{1,0:T(8,128)(2,1)S(1)}, bf16[32,2048]{1,0:T(8,128)(2,1)S(1)}, u32[]{:S(2)}, u32[]{:S(2)}) collective-permute-start(bf16[32,2048]{1,0:T(8,128)(2,1)S(1)} %merge.1.refs_0_), channel_id=1, source_target_pairs={{0,1},{1,0},{2,3},{3,2},{4,5},{5,4},{6,7},{7,6},{8,9},{9,8},{10,11... | collective-permute-start | bytes 393224 | tf_op jit(solution)/shard_map/ppermute | solution.py:631
  51.6 4.5 %collective-permute-start.13 = (bf16[16,640]{1,0:T(8,128)(2,1)S(1)}, bf16[16,640]{1,0:T(8,128)(2,1)S(1)}, u32[]{:S(2)}, u32[]{:S(2)}) collective-permute-start(bf16[16,640]{1,0:T(8,128)(2,1)S(1)} %get-tuple-element.32), channel_id=1, source_target_pairs={{0,8},{8,0},{16,24},{24,16},{1,9},{9,1},{17,25},{25,17},{2,10},{10... | collective-permute-start | bytes 61448 | tf_op jit(solution)/shard_map/ppermute | solution.py:631
  53.2 4.9 %collective-permute-start.14 = (bf16[16,640]{1,0:T(8,128)(2,1)S(1)}, bf16[16,640]{1,0:T(8,128)(2,1)S(1)}, u32[]{:S(2)}, u32[]{:S(2)}) collective-permute-start(bf16[16,640]{1,0:T(8,128)(2,1)S(1)} %get-tuple-element.33), channel_id=1, source_target_pairs={{0,16},{8,24},{16,0},{24,8},{1,17},{9,25},{17,1},{25,9},{2,18},{10... | collective-permute-start | bytes 61448 | tf_op jit(solution)/shard_map/ppermute | solution.py:631
  55.8 5.6 %collective-permute-start.15 = (bf16[16,640]{1,0:T(8,128)(2,1)S(1)}, bf16[16,640]{1,0:T(8,128)(2,1)S(1)}, u32[]{:S(2)}, u32[]{:S(2)}) collective-permute-start(bf16[16,640]{1,0:T(8,128)(2,1)S(1)} %get-tuple-element.34), channel_id=1, source_target_pairs={{0,24},{8,16},{16,8},{24,0},{1,25},{9,17},{17,9},{25,1},{2,26},{10... | collective-permute-start | bytes 61448 | tf_op jit(solution)/shard_map/ppermute | solution.py:631

commit v9 on v8

--- a/solution.py
+++ b/solution.py
@@ -18,6 +18,7 @@
 GROUP = 4
 TASKS = 8
 CHUNK = GROUP * TASKS
+SETS = 2
 PHASES = 16
 AHEAD = 6
 DEPTH = 256
@@ -58,11 +59,11 @@
     rank,
     tenant_hbm,
     adapter_hbm,
-    tenant_ref,
-    adapter_ref,
-    holder_ref,
-    block_ref,
-    length_ref,
+    tenant_row_hbm,
+    adapter_row_hbm,
+    holder_hbm,
+    block_hbm,
+    length_hbm,
     hidden_hbm,
     weight_hbm,
     down_hbm,
@@ -70,6 +71,11 @@
     keep_ref,
     send_ref,
     own_up_ref,
+    tenant_ref,
+    adapter_ref,
+    holder_ref,
+    block_ref,
+    length_ref,
     hidden_ref,
     weight_ref,
     down_ref,
@@ -78,6 +84,7 @@
     adapter_smem,
     sems,
     up_sems,
+    small_sems,
 ):
     chips, own, _ = keep_ref.shape
     rows, depth = hidden_ref.shape
@@ -95,8 +102,22 @@
         pltpu.make_async_copy(tenant_hbm, tenant_smem, up_sems.at[own]),
         pltpu.make_async_copy(adapter_hbm, adapter_smem, up_sems.at[own + 1]),
     ]
-    for copy in scalars + first + chunks:
+    small = [
+        pltpu.make_async_copy(hbm, ref, small_sems.at[i])
+        for i, (hbm, ref) in enumerate(
+            (
+                (tenant_row_hbm, tenant_ref),
+                (adapter_row_hbm, adapter_ref),
+                (holder_hbm, holder_ref),
+                (block_hbm, block_ref),
+                (length_hbm, length_ref),
+            )
+        )
+    ]
+    for copy in scalars + small + first + chunks:
         copy.start()
+    for copy in small:
+        copy.wait()
 
     slots = holder_ref.shape[1]
     numbers = [holder_ref[...], block_ref[...], length_ref[...], jnp.zeros((own, LANES - 3 * slots), jnp.int32)]
@@ -161,19 +182,20 @@
     out = jax.ShapeDtypeStruct((chips, own, width + LANES), jnp.float32)
     tables = [x.reshape(1, -1) for x in (tenant, tenant_adapter)]
     operands = in_hbm(tenant, tenant_adapter, *tables, holder, block, length, hidden, query_weight, down, up)
-    large = operands[7:10]
+    local = operands[2:10]
     return pl.pallas_call(
         functools.partial(project_kernel, rank),
-        in_specs=[hbm_spec()] * 2 + [vmem_spec()] * 5 + [hbm_spec()] * 4,
+        in_specs=[hbm_spec()] * len(operands),
         out_specs=[vmem_spec()] * 3,
         out_shape=[out, out, jax.ShapeDtypeStruct((own, *up.shape[1:]), up.dtype)],
-        scratch_shapes=[pltpu.VMEM(x.shape, x.dtype) for x in large]
+        scratch_shapes=[pltpu.VMEM(x.shape, x.dtype) for x in local]
         + [
             pltpu.VMEM((rows, width), jnp.float32),
             pltpu.SMEM(tenant.shape, tenant.dtype),
             pltpu.SMEM(tenant_adapter.shape, tenant_adapter.dtype),
             pltpu.SemaphoreType.DMA((2 + pl.cdiv(depth, DEPTH),)),
             pltpu.SemaphoreType.DMA((own + 2,)),
+            pltpu.SemaphoreType.DMA((5,)),
         ],
         compiler_params=params(16),
         name="project",
@@ -252,10 +274,9 @@
     )(*parts, up, cosine, sine, gain)
 
 
-def list_kernel(blocks, block_size, slots, *refs):
-    pieces, (list_ref, bound_ref, place_ref, value_ref) = refs[:-4], refs[-4:]
+def place_kernel(blocks, block_size, slots, *refs):
+    pieces, (place_ref, value_ref, bound_ref) = refs[:-3], refs[-3:]
     rows = place_ref.shape[0]
-    capacity = list_ref.shape[1]
     me = lax.axis_index("kv").astype(jnp.float32)
     numbers = jnp.concatenate([p[:, i * LANES : (i + 1) * LANES] for p in pieces for i in range(PAIR)], axis=0)
     holder, block, length = (numbers[:, i * slots : (i + 1) * slots] for i in range(3))
@@ -301,6 +322,11 @@
         done = jnp.ceil(done) if part == PHASES - 1 else jnp.floor(done)
         bounds = jnp.where(bound_lane == part + 1, done, bounds)
     bound_ref[...] = bounds.astype(jnp.int32)
+
+
+def list_kernel(spare, place_ref, value_ref, list_ref):
+    rows, slots = place_ref.shape
+    capacity = list_ref.shape[1]
     target = lax.broadcasted_iota(jnp.int32, (8, capacity), 1).astype(jnp.float32)
 
     def tile(t, total):
@@ -314,36 +340,61 @@
     list_ref[...] = (jnp.sum(total, axis=0, keepdims=True) + spare).astype(jnp.int32)
 
 
-def make_list(parts, slots, blocks, block_size, count):
+def make_places(parts, slots, blocks, block_size, count):
     own, width = parts[0].shape
     rows = count * own
-    most = 2 * own * slots // count * count + (GROUP - 1) * blocks + 3 * CHUNK
-    capacity = -(-most // LANES) * LANES
     last = width // (PAIR * LANES) - 1
-    return pl.pallas_call(
-        functools.partial(list_kernel, blocks, block_size, slots),
+    table = jax.ShapeDtypeStruct((rows, slots), jnp.float32)
+    bounds = jax.ShapeDtypeStruct((1, LANES), jnp.int32)
+    return pl.pallas_call(
+        functools.partial(place_kernel, blocks, block_size, slots),
         grid=(1,),
         in_specs=[pl.BlockSpec((own, PAIR * LANES), lambda i: (0, last))] * len(parts),
-        out_specs=[
-            pl.BlockSpec((1, capacity), lambda i: (0, 0)),
-            pl.BlockSpec((1, LANES), lambda i: (0, 0)),
-        ],
-        out_shape=[
-            jax.ShapeDtypeStruct((1, capacity), jnp.int32),
-            jax.ShapeDtypeStruct((1, LANES), jnp.int32),
-        ],
-        scratch_shapes=[pltpu.VMEM((rows, slots), jnp.float32), pltpu.VMEM((rows, slots), jnp.float32)],
+        out_specs=[pl.BlockSpec(x.shape, lambda i: (0, 0)) for x in (table, table, bounds)],
+        out_shape=[table, table, bounds],
         compiler_params=params(16),
-        cost_estimate=pl.CostEstimate(flops=10**8, bytes_accessed=10**7, transcendentals=0),
+        cost_estimate=pl.CostEstimate(flops=10**8, bytes_accessed=4 * 10**6, transcendentals=0),
+        name="slot_places",
+    )(*parts)
+
+
+def make_list(places, values, blocks, block_size, count):
+    rows, slots = places.shape
+    most = 2 * rows * slots // count // count * count + (GROUP - 1) * blocks + 3 * CHUNK
+    capacity = -(-most // LANES) * LANES
+    return pl.pallas_call(
+        functools.partial(list_kernel, float(rows * blocks * block_size)),
+        in_specs=[vmem_spec()] * 2,
+        out_specs=vmem_spec(),
+        out_shape=jax.ShapeDtypeStruct((1, capacity), jnp.int32),
+        compiler_params=params(16),
+        cost_estimate=pl.CostEstimate(flops=10**8, bytes_accessed=4 * 10**6, transcendentals=0),
         name="slot_list",
-    )(*parts)
+    )(places, values)
+
+
+def join_kernel(own_ref, other_ref, places_ref, out_ref):
+    own = own_ref.shape[0]
+    out_ref[:own] = own_ref[...]
+    out_ref[own:] = other_ref[...]
+
+
+def join_pair(own, other, places):
+    return pl.pallas_call(
+        join_kernel,
+        in_specs=[vmem_spec()] * 3,
+        out_specs=vmem_spec(),
+        out_shape=jax.ShapeDtypeStruct((PAIR * own.shape[0], *own.shape[1:]), own.dtype),
+        compiler_params=params(16),
+        name="join_pair",
+    )(own, other, places)
 
 
 def attend_kernel(scale, kv_local, count, list_vmem, bound_vmem, *refs):
     queries, refs = refs[: count // PAIR], refs[count // PAIR :]
     (key_hbm, value_hbm, keep_ref, send_ref, list_ref, bound_ref, query_ref, key_ref, value_ref) = refs[:9]
     (score_ref, part_top_ref, part_total_ref, part_sum_ref, number_sems, sems) = refs[9:15]
-    states = [refs[15 + 3 * k : 18 + 3 * k] for k in range(GROUP)]
+    states = [refs[15 + 3 * k : 18 + 3 * k] for k in range(SETS)]
     heads = query_ref.shape[1]
     rows = query_ref.shape[0] - 1
     own = rows // count
@@ -394,25 +445,25 @@
     def block_of(entry):
         return (entry >> length_bits) & (blocks - 1)
 
-    def merge_task(row, t):
-        before = [[ref[row[k]] for ref in states[k]] for k in range(GROUP)]
+    def merge_slots(row, start):
+        before = [[ref[r] for ref in state] for r, state in zip(row, states)]
         after = []
         for k, (top, total, acc) in enumerate(before):
-            j = t * GROUP + k
-            part_top = part_top_ref[j]
+            t, place = divmod(start + k, GROUP)
+            part_top = part_top_ref[start + k]
             share = jnp.exp2(-jnp.abs(top - part_top) * factor)
             lower = top < part_top
             old, new = jnp.where(lower, share, 1.0), jnp.where(lower, 1.0, share)
             after.append(
                 (
                     jnp.maximum(top, part_top),
-                    total * old + part_total_ref[j] * new,
-                    acc * old + part_sum_ref[t, k * heads : (k + 1) * heads] * new,
+                    total * old + part_total_ref[start + k] * new,
+                    acc * old + part_sum_ref[t, place * heads : (place + 1) * heads] * new,
                 )
             )
-        for k in range(GROUP):
-            for ref, value in zip(states[k], after[k]):
-                ref[row[k]] = value
+        for r, state, new in zip(row, states, after):
+            for ref, value in zip(state, new):
+                ref[r] = value
 
     def weigh_item(entry, t, k):
         j = t * GROUP + k
@@ -438,7 +489,10 @@
         merged, weighed, scored = (entries(jnp.maximum(i - back, 0)) for back in (2, 1, 0))
         for t in range(TASKS):
             task = slice(t * GROUP, (t + 1) * GROUP)
-            merge_task([jnp.where(i >= 2, row_of(entry), rows) for entry in merged[task]], t)
+            for start in range(t * GROUP, (t + 1) * GROUP, SETS):
+                merge_slots(
+                    [jnp.where(i >= 2, row_of(entry), rows) for entry in merged[start : start + SETS]], start
+                )
             if stages > 1:
                 weights = [weigh_item(entry, t, k) for k, entry in enumerate(weighed[task])]
                 part_sum_ref[t] = jnp.dot(
@@ -511,8 +565,8 @@
             pltpu.SemaphoreType.DMA((2,)),
             pltpu.SemaphoreType.DMA((2, PHASES)),
         ]
-        + [state] * (3 * GROUP),
-        compiler_params=params(28 + 3 * GROUP * rows * heads * LANES * 4 // MIB),
+        + [state] * (3 * SETS),
+        compiler_params=params(28 + 3 * SETS * rows * heads * LANES * 4 // MIB),
         name="attend",
     )(items, bounds, *queries, keys, values)
 
@@ -633,10 +687,6 @@
 
 def gather_chips(x):
     return [x] + [exchange(x, "kv", s) for s in range(PAIR, lax.axis_size("kv"), PAIR)]
-
-
-def gather_pairs(x):
-    return gather_chips(jnp.concatenate([x, exchange(x, "kv", 1)], axis=0))
 
 
 def local(
@@ -689,8 +739,10 @@
     cosine = jnp.concatenate([jnp.cos(angles), jnp.cos(angles)], axis=-1)
     sine = jnp.concatenate([-jnp.sin(angles), jnp.sin(angles)], axis=-1)
     queries = make_queries(parts, up, cosine, sine, query_norm_gain.reshape(1, head_size), heads, 3 * slots)
-    queries = [q.reshape(PAIR, own, heads, head_size) for q in gather_pairs(queries)]
-    items, bounds = make_list(parts, slots, blocks, block_size, kv_count)
+    places, slot_values, bounds = make_places(parts, slots, blocks, block_size, kv_count)
+    queries = gather_chips(join_pair(queries, exchange(queries, "kv", 1), places))
+    queries = [q.reshape(PAIR, own, heads, head_size) for q in queries]
+    items = make_list(places, slot_values, blocks, block_size, kv_count)
 
     keys = paged_key_cache.reshape(blocks, block_size * kv_local, head_size)
     values = paged_value_cache.reshape(blocks, block_size * kv_local, head_size)

time: 62.1 us -> 60.9 us (0.981)
  starting transfers between devices: 19.7 us -> 18.6 us
    ppermute x16, starting transfers between devices: 19.7 us -> 18.6 us  [exchange(): return lax.ppermute(x, axis, [(i, i ^ s) for i in range(count)])]
    pallas_call x1 -> x3, Pallas kernels: 2.44 us -> 2.43 us  [the longest x1 1.42 us: make_list(): pl.pallas_call(functools.partial(list_kernel, float(rows * blocks * block...]
  transfers between devices with their start and end apart: 16 -> 16, of which waited for: 12 -> 14; matrix products, arithmetic and copies ran while one was open for 1% -> 1% of each run, Pallas kernels for 4% -> 4%
where the time goes in v9:
time: 60.9 us; the launch traced here: 60.5 us
  waiting for transfers between devices  22.4 us (37%)
  starting transfers between devices  18.6 us (31%)
  Pallas kernels  18.4 us (30%)
  other arithmetic  0.95 us (2%)
    ppermute x16, waiting for transfers between devices, exchange(): return lax.ppermute(x, axis, [(i, i ^ s) for i in range(count)])  22.4 us
    ppermute x16, starting transfers between devices, exchange(): return lax.ppermute(x, axis, [(i, i ^ s) for i in range(count)])  18.6 us
    pallas_call x1, Pallas kernels, attend(): pl.pallas_call(functools.partial(attend_kernel, scale, kv_local, count),...  10.8 us
    pallas_call x1, Pallas kernels, project(): pl.pallas_call(functools.partial(project_kernel, rank), in_specs=[hbm_spe...  3.23 us
    pallas_call x1, Pallas kernels, make_list(): pl.pallas_call(functools.partial(list_kernel, float(rows * blocks * block...  1.42 us
  transfers between devices with their start and end apart: 16, of which 14 were waited for; matrix products, arithmetic and copies ran while one was open for 1% of the time, Pallas kernels for 4%

profile of v9, /device:TPU:0, one launch (start us, length us, event | category | flops | bytes accessed | tf_op | source)
XLA Modules:
  0.0 60.5 jit_solution(2705079651600398098)
XLA Ops:
  0.0 3.2 %project.1 = (f32[4,8,2176]{2,1,0:T(8,128)S(1)}, f32[4,8,2176]{2,1,0:T(8,128)S(1)}, f32[8,16,2048]{2,1,0:T(8,128)S(1)}) custom-call(s32[64]{0:T(128)} %tenant_hbm.1, s32[64]{0:T(128)} %adapter_hbm.1, s32[1,64]{1,0:T(1,128)} %bitcast.20, s32[1,64]{1,0:T(1,128)} %bitcast.21, s32[8,32]{1,0:T(8,128)} %holder_hbm.1, s32[8,32]{1,0:T(8,128)} %block_hbm.1, ...), custom_call_target="tpu_custom_call" | custom-call | tf_op jit(solution)/shard_map/project/pallas_call | solution.py:186
  3.2 0.5 collective-permute-start
  4.0 0.9 %collective-permute-done.got_ref = f32[4,8,2176]{2,1,0:T(8,128)S(1)} collective-permute-done((f32[4,8,2176]{2,1,0:T(8,128)S(1)}, f32[4,8,2176]{2,1,0:T(8,128)S(1)}, u32[]{:S(2)}, u32[]{:S(2)}) %collective-permute-start) | collective-permute-done | bytes 278560 | tf_op jit(solution)/shard_map/ppermute | solution.py:685
  5.0 2.9 %collective-permute-start.1 = (f32[8,2304]{1,0:T(8,128)S(1)}, f32[8,2304]{1,0:T(8,128)S(1)}, u32[]{:S(2)}, u32[]{:S(2)}) collective-permute-start(f32[8,2304]{1,0:T(8,128)S(1)} %get-tuple-element.24), channel_id=1, source_target_pairs={{0,2},{1,3},{2,0},{3,1},{4,6},{5,7},{6,4},{7,5},{8,10},{9,11},{10,... | collective-permute-start | bytes 221192 | tf_op jit(solution)/shard_map/ppermute | solution.py:685
  7.9 1.5 %collective-permute-start.2 = (f32[8,2304]{1,0:T(8,128)S(1)}, f32[8,2304]{1,0:T(8,128)S(1)}, u32[]{:S(2)}, u32[]{:S(2)}) collective-permute-start(f32[8,2304]{1,0:T(8,128)S(1)} %get-tuple-element.25), channel_id=1, source_target_pairs={{0,4},{1,5},{2,6},{3,7},{4,0},{5,1},{6,2},{7,3},{8,12},{9,13},{10,... | collective-permute-start | bytes 221192 | tf_op jit(solution)/shard_map/ppermute | solution.py:685
  9.5 1.0 %collective-permute-done.1.refs_1_ = f32[8,2304]{1,0:T(8,128)S(1)} collective-permute-done((f32[8,2304]{1,0:T(8,128)S(1)}, f32[8,2304]{1,0:T(8,128)S(1)}, u32[]{:S(2)}, u32[]{:S(2)}) %collective-permute-start.1) | collective-permute-done | bytes 73760 | tf_op jit(solution)/shard_map/ppermute | solution.py:685
  10.5 1.8 %collective-permute-done.2.refs_2_ = f32[8,2304]{1,0:T(8,128)S(1)} collective-permute-done((f32[8,2304]{1,0:T(8,128)S(1)}, f32[8,2304]{1,0:T(8,128)S(1)}, u32[]{:S(2)}, u32[]{:S(2)}) %collective-permute-start.2) | collective-permute-done | bytes 73760 | tf_op jit(solution)/shard_map/ppermute | solution.py:685
  12.3 2.4 %collective-permute-done.3.refs_3_ = f32[8,2304]{1,0:T(8,128)S(1)} collective-permute-done((f32[8,2304]{1,0:T(8,128)S(1)}, f32[8,2304]{1,0:T(8,128)S(1)}, u32[]{:S(2)}, u32[]{:S(2)}) %collective-permute-start.3) | collective-permute-done | bytes 73760 | tf_op jit(solution)/shard_map/ppermute | solution.py:685
  14.7 0.4 queries.1.own_ref
  15.2 1.0 %slot_places.1 = (f32[64,32]{1,0:T(8,128)S(1)}, f32[64,32]{1,0:T(8,128)S(1)}, s32[1,128]{1,0:T(1,128)S(1)}) custom-call(f32[8,2304]{1,0:T(8,128)S(1)} %get-tuple-element.23.refs_0_, f32[8,2304]{1,0:T(8,128)S(1)} %collective-permute-done.1.refs_1_, f32[8,2304]{1,0:T(8,128)S(1)} %collective-permute-done.2.refs_2_, f32[8,2304]{1,0:T(8,128)S(1)} %collective-permute-done.3.refs_3_), custom_call_target="tpu_custom_call" | custom-call | flops 100000000 | bytes 4000000 | tf_op jit(solution)/shard_map/slot_places/pallas_call | solution.py:349
  16.4 0.5 collective-permute-start.5
  16.9 0.6 collective-permute-start.6
  17.5 2.4 %collective-permute-start.7 = (bf16[16,16,128]{2,1,0:T(8,128)(2,1)S(1)}, bf16[16,16,128]{2,1,0:T(8,128)(2,1)S(1)}, u32[]{:S(2)}, u32[]{:S(2)}) collective-permute-start(bf16[16,16,128]{2,1,0:T(8,128)(2,1)S(1)} %join_pair.1), channel_id=1, source_target_pairs={{0,6},{1,7},{2,4},{3,5},{4,2},{5,3},{6,0},{7,1},{8,14},{9,15},{10,... | collective-permute-start | bytes 196616 | tf_op jit(solution)/shard_map/ppermute | solution.py:685
  19.9 1.4 %slot_list.1.list_vmem = s32[1,1024]{1,0:T(1,128)S(1)} custom-call(f32[64,32]{1,0:T(8,128)S(1)} %get-tuple-element.27.place_ref.places_ref, f32[64,32]{1,0:T(8,128)S(1)} %get-tuple-element.28.value_ref), custom_call_target="tpu_custom_call" | custom-call | flops 100000000 | bytes 4000000 | tf_op jit(solution)/shard_map/slot_list/pallas_call | solution.py:365
  21.3 0.6 collective-permute-done.6
  21.9 0.8 %collective-permute-done.7 = bf16[16,16,128]{2,1,0:T(8,128)(2,1)S(1)} collective-permute-done((bf16[16,16,128]{2,1,0:T(8,128)(2,1)S(1)}, bf16[16,16,128]{2,1,0:T(8,128)(2,1)S(1)}, u32[]{:S(2)}, u32[]{:S(2)}) %collective-permute-start.7) | collective-permute-done | bytes 65568 | tf_op jit(solution)/shard_map/ppermute | solution.py:685
  22.7 10.8 %attend.1 = (f32[4,9,16,128]{3,2,1,0:T(8,128)S(1)}, f32[4,9,16,128]{3,2,1,0:T(8,128)S(1)}) custom-call(s32[1,1024]{1,0:T(1,128)S(1)} %slot_list.1.list_vmem, s32[1,128]{1,0:T(1,128)S(1)} %get-tuple-element.29.bound_vmem, bf16[2,8,16,128]{3,2,1,0:T(8,128)(2,1)S(1)} %bitcast.12, bf16[2,8,16,128]{3,2,1,0:T(8,128)(2,1)S(1)} %bitcast.13, ...), custom_call_target="tpu_custom_call" | custom-call | tf_op jit(solution)/shard_map/attend/pallas_call | solution.py:550
  33.5 1.6 %collective-permute-done.8.got_ref = f32[4,9,16,128]{3,2,1,0:T(8,128)S(1)} collective-permute-done((f32[4,9,16,128]{3,2,1,0:T(8,128)S(1)}, f32[4,9,16,128]{3,2,1,0:T(8,128)S(1)}, u32[]{:S(2)}, u32[]{:S(2)}) %collective-permute-start.8) | collective-permute-done | bytes 294944 | tf_op jit(solution)/shard_map/ppermute | solution.py:685
  35.1 0.3 merge_pair.1.refs_0_
  35.5 1.5 %collective-permute-start.10 = (bf16[4,9,16,128]{3,2,1,0:T(8,128)(2,1)S(1)}, bf16[4,9,16,128]{3,2,1,0:T(8,128)(2,1)S(1)}, u32[]{:S(2)}, u32[]{:S(2)}) collective-permute-start(bf16[4,9,16,128]{3,2,1,0:T(8,128)(2,1)S(1)} %merge_pair.1.refs_0_), channel_id=1, source_target_pairs={{0,4},{1,5},{2,6},{3,7},{4,0},{5,1},{6,2},{7,3},{8,12},{9,13},{10,... | collective-permute-start | bytes 442376 | tf_op jit(solution)/shard_map/ppermute | solution.py:685
  37.0 3.9 %collective-permute-start.11 = (bf16[4,9,16,128]{3,2,1,0:T(8,128)(2,1)S(1)}, bf16[4,9,16,128]{3,2,1,0:T(8,128)(2,1)S(1)}, u32[]{:S(2)}, u32[]{:S(2)}) collective-permute-start(bf16[4,9,16,128]{3,2,1,0:T(8,128)(2,1)S(1)} %merge_pair.1.refs_0_), channel_id=1, source_target_pairs={{0,6},{1,7},{2,4},{3,5},{4,2},{5,3},{6,0},{7,1},{8,14},{9,15},{10,... | collective-permute-start | bytes 442376 | tf_op jit(solution)/shard_map/ppermute | solution.py:685
  40.9 2.7 %collective-permute-done.10.refs_2_ = bf16[4,9,16,128]{3,2,1,0:T(8,128)(2,1)S(1)} collective-permute-done((bf16[4,9,16,128]{3,2,1,0:T(8,128)(2,1)S(1)}, bf16[4,9,16,128]{3,2,1,0:T(8,128)(2,1)S(1)}, u32[]{:S(2)}, u32[]{:S(2)}) %collective-permute-start.10) | collective-permute-done | bytes 147488 | tf_op jit(solution)/shard_map/ppermute | solution.py:685
  43.6 2.0 %collective-permute-done.11.refs_3_ = bf16[4,9,16,128]{3,2,1,0:T(8,128)(2,1)S(1)} collective-permute-done((bf16[4,9,16,128]{3,2,1,0:T(8,128)(2,1)S(1)}, bf16[4,9,16,128]{3,2,1,0:T(8,128)(2,1)S(1)}, u32[]{:S(2)}, u32[]{:S(2)}) %collective-permute-start.11) | collective-permute-done | bytes 147488 | tf_op jit(solution)/shard_map/ppermute | solution.py:685
  45.6 1.9 %collective-permute-done.9.refs_1_ = bf16[4,9,16,128]{3,2,1,0:T(8,128)(2,1)S(1)} collective-permute-done((bf16[4,9,16,128]{3,2,1,0:T(8,128)(2,1)S(1)}, bf16[4,9,16,128]{3,2,1,0:T(8,128)(2,1)S(1)}, u32[]{:S(2)}, u32[]{:S(2)}) %collective-permute-start.9) | collective-permute-done | bytes 147488 | tf_op jit(solution)/shard_map/ppermute | solution.py:685
  47.5 0.6 merge.1.refs_0_
  48.1 1.3 %collective-permute-done.12.refs_1_ = bf16[32,2048]{1,0:T(8,128)(2,1)S(1)} collective-permute-done((bf16[32,2048]{1,0:T(8,128)(2,1)S(1)}, bf16[32,2048]{1,0:T(8,128)(2,1)S(1)}, u32[]{:S(2)}, u32[]{:S(2)}) %collective-permute-start.12) | collective-permute-done | bytes 131104 | tf_op jit(solution)/shard_map/ppermute | solution.py:685
  49.5 0.6 project_out.1
  50.1 1.6 %collective-permute-start.13 = (bf16[16,640]{1,0:T(8,128)(2,1)S(1)}, bf16[16,640]{1,0:T(8,128)(2,1)S(1)}, u32[]{:S(2)}, u32[]{:S(2)}) collective-permute-start(bf16[16,640]{1,0:T(8,128)(2,1)S(1)} %get-tuple-element.34), channel_id=1, source_target_pairs={{0,8},{8,0},{16,24},{24,16},{1,9},{9,1},{17,25},{25,17},{2,10},{10... | collective-permute-start | bytes 61448 | tf_op jit(solution)/shard_map/ppermute | solution.py:685
  51.7 2.6 %collective-permute-start.14 = (bf16[16,640]{1,0:T(8,128)(2,1)S(1)}, bf16[16,640]{1,0:T(8,128)(2,1)S(1)}, u32[]{:S(2)}, u32[]{:S(2)}) collective-permute-start(bf16[16,640]{1,0:T(8,128)(2,1)S(1)} %get-tuple-element.35), channel_id=1, source_target_pairs={{0,16},{8,24},{16,0},{24,8},{1,17},{9,25},{17,1},{25,9},{2,18},{10... | collective-permute-start | bytes 61448 | tf_op jit(solution)/shard_map/ppermute | solution.py:685
  54.5 2.1 %collective-permute-done.14 = bf16[16,640]{1,0:T(8,128)(2,1)S(1)} collective-permute-done((bf16[16,640]{1,0:T(8,128)(2,1)S(1)}, bf16[16,640]{1,0:T(8,128)(2,1)S(1)}, u32[]{:S(2)}, u32[]{:S(2)}) %collective-permute-start.14) | collective-permute-done | bytes 20512 | tf_op jit(solution)/shard_map/ppermute | solution.py:685
  56.6 3.3 %collective-permute-done.15 = bf16[16,640]{1,0:T(8,128)(2,1)S(1)} collective-permute-done((bf16[16,640]{1,0:T(8,128)(2,1)S(1)}, bf16[16,640]{1,0:T(8,128)(2,1)S(1)}, u32[]{:S(2)}, u32[]{:S(2)}) %collective-permute-start.15) | collective-permute-done | bytes 20512 | tf_op jit(solution)/shard_map/ppermute | solution.py:685
  59.9 0.6 %add_convert_fusion = bf16[16,640]{1,0:T(8,128)(2,1)} fusion(bf16[16,640]{1,0:T(8,128)(2,1)S(1)} %collective-permute-done.15, bf16[16,640]{1,0:T(8,128)(2,1)S(1)} %collective-permute-done.14, f32[16,640]{1,0:T(8,128)S(1)} %get-tuple-element.33, bf16[16,640]{1,0:T(8,128)(2,1)S(1)} %collective-permute-done.13), kind=kLoop, calls=%fused_computation | loop fusion | flops 71680 | bytes 122880 | tf_op jit(solution)/shard_map/convert_element_type | solution.py:756
  (22 shorter events, 1.0 us)
Async XLA Ops:
  0.0 3.8 %copy-start.2 = (s32[8,32]{1,0:T(8,128)S(1)}, s32[8,32]{1,0:T(8,128)}, u32[]{:S(2)}) copy-start(s32[8,32]{1,0:T(8,128)} %length_hbm.1) | copy-start | bytes 3076
  0.0 14.7 %copy-start.1 = (f32[128]{0:T(128)S(1)}, f32[128]{0:T(128)}, u32[]{:S(2)}) copy-start(f32[128]{0:T(128)} %param.17) | copy-start | bytes 1540
  3.2 1.7 %collective-permute-start = (f32[4,8,2176]{2,1,0:T(8,128)S(1)}, f32[4,8,2176]{2,1,0:T(8,128)S(1)}, u32[]{:S(2)}, u32[]{:S(2)}) collective-permute-start(f32[4,8,2176]{2,1,0:T(8,128)S(1)} %get-tuple-element.22), channel_id=1, source_target_pairs={{0,1},{1,0},{2,3},{3,2},{4,5},{5,4},{6,7},{7,6},{8,9},{9,8},{10,11... | collective-permute-start | bytes 835592 | tf_op jit(solution)/shard_map/ppermute | solution.py:685
  5.0 5.5 %collective-permute-start.1 = (f32[8,2304]{1,0:T(8,128)S(1)}, f32[8,2304]{1,0:T(8,128)S(1)}, u32[]{:S(2)}, u32[]{:S(2)}) collective-permute-start(f32[8,2304]{1,0:T(8,128)S(1)} %get-tuple-element.24), channel_id=1, source_target_pairs={{0,2},{1,3},{2,0},{3,1},{4,6},{5,7},{6,4},{7,5},{8,10},{9,11},{10,... | collective-permute-start | bytes 221192 | tf_op jit(solution)/shard_map/ppermute | solution.py:685
  7.9 4.4 %collective-permute-start.2 = (f32[8,2304]{1,0:T(8,128)S(1)}, f32[8,2304]{1,0:T(8,128)S(1)}, u32[]{:S(2)}, u32[]{:S(2)}) collective-permute-start(f32[8,2304]{1,0:T(8,128)S(1)} %get-tuple-element.25), channel_id=1, source_target_pairs={{0,4},{1,5},{2,6},{3,7},{4,0},{5,1},{6,2},{7,3},{8,12},{9,13},{10,... | collective-permute-start | bytes 221192 | tf_op jit(solution)/shard_map/ppermute | solution.py:685
  9.4 5.3 %collective-permute-start.3 = (f32[8,2304]{1,0:T(8,128)S(1)}, f32[8,2304]{1,0:T(8,128)S(1)}, u32[]{:S(2)}, u32[]{:S(2)}) collective-permute-start(f32[8,2304]{1,0:T(8,128)S(1)} %get-tuple-element.26), channel_id=1, source_target_pairs={{0,6},{1,7},{2,4},{3,5},{4,2},{5,3},{6,0},{7,1},{8,14},{9,15},{10,... | collective-permute-start | bytes 221192 | tf_op jit(solution)/shard_map/ppermute | solution.py:685
  15.1 1.3 %collective-permute-start.4 = (bf16[8,16,128]{2,1,0:T(8,128)(2,1)S(1)}, bf16[8,16,128]{2,1,0:T(8,128)(2,1)S(1)}, u32[]{:S(2)}, u32[]{:S(2)}) collective-permute-start(bf16[8,16,128]{2,1,0:T(8,128)(2,1)S(1)} %queries.1.own_ref), channel_id=1, source_target_pairs={{0,1},{1,0},{2,3},{3,2},{4,5},{5,4},{6,7},{7,6},{8,9},{9,8},{10,11... | collective-permute-start | bytes 98312 | tf_op jit(solution)/shard_map/ppermute | solution.py:685
  16.4 4.9 %collective-permute-start.5 = (bf16[16,16,128]{2,1,0:T(8,128)(2,1)S(1)}, bf16[16,16,128]{2,1,0:T(8,128)(2,1)S(1)}, u32[]{:S(2)}, u32[]{:S(2)}) collective-permute-start(bf16[16,16,128]{2,1,0:T(8,128)(2,1)S(1)} %join_pair.1), channel_id=1, source_target_pairs={{0,2},{1,3},{2,0},{3,1},{4,6},{5,7},{6,4},{7,5},{8,10},{9,11},{10,... | collective-permute-start | bytes 196616 | tf_op jit(solution)/shard_map/ppermute | solution.py:685
  16.9 5.0 %collective-permute-start.6 = (bf16[16,16,128]{2,1,0:T(8,128)(2,1)S(1)}, bf16[16,16,128]{2,1,0:T(8,128)(2,1)S(1)}, u32[]{:S(2)}, u32[]{:S(2)}) collective-permute-start(bf16[16,16,128]{2,1,0:T(8,128)(2,1)S(1)} %join_pair.1), channel_id=1, source_target_pairs={{0,4},{1,5},{2,6},{3,7},{4,0},{5,1},{6,2},{7,3},{8,12},{9,13},{10,... | collective-permute-start | bytes 196616 | tf_op jit(solution)/shard_map/ppermute | solution.py:685
  17.5 5.2 %collective-permute-start.7 = (bf16[16,16,128]{2,1,0:T(8,128)(2,1)S(1)}, bf16[16,16,128]{2,1,0:T(8,128)(2,1)S(1)}, u32[]{:S(2)}, u32[]{:S(2)}) collective-permute-start(bf16[16,16,128]{2,1,0:T(8,128)(2,1)S(1)} %join_pair.1), channel_id=1, source_target_pairs={{0,6},{1,7},{2,4},{3,5},{4,2},{5,3},{6,0},{7,1},{8,14},{9,15},{10,... | collective-permute-start | bytes 196616 | tf_op jit(solution)/shard_map/ppermute | solution.py:685
  22.7 26.8 %copy-start = (bf16[2048,640]{1,0:T(8,128)(2,1)S(1)}, bf16[2048,640]{1,0:T(8,128)(2,1)}, u32[]{:S(2)}) copy-start(bf16[2048,640]{1,0:T(8,128)(2,1)} %refs_2_.1) | copy-start | bytes 7864324
  33.5 1.6 %collective-permute-start.8 = (f32[4,9,16,128]{3,2,1,0:T(8,128)S(1)}, f32[4,9,16,128]{3,2,1,0:T(8,128)S(1)}, u32[]{:S(2)}, u32[]{:S(2)}) collective-permute-start(f32[4,9,16,128]{3,2,1,0:T(8,128)S(1)} %get-tuple-element.32), channel_id=1, source_target_pairs={{0,1},{1,0},{2,3},{3,2},{4,5},{5,4},{6,7},{7,6},{8,9},{9,8},{10,11... | collective-permute-start | bytes 884744 | tf_op jit(solution)/shard_map/ppermute | solution.py:685
  35.5 8.1 %collective-permute-start.10 = (bf16[4,9,16,128]{3,2,1,0:T(8,128)(2,1)S(1)}, bf16[4,9,16,128]{3,2,1,0:T(8,128)(2,1)S(1)}, u32[]{:S(2)}, u32[]{:S(2)}) collective-permute-start(bf16[4,9,16,128]{3,2,1,0:T(8,128)(2,1)S(1)} %merge_pair.1.refs_0_), channel_id=1, source_target_pairs={{0,4},{1,5},{2,6},{3,7},{4,0},{5,1},{6,2},{7,3},{8,12},{9,13},{10,... | collective-permute-start | bytes 442376 | tf_op jit(solution)/shard_map/ppermute | solution.py:685
  37.0 8.6 %collective-permute-start.11 = (bf16[4,9,16,128]{3,2,1,0:T(8,128)(2,1)S(1)}, bf16[4,9,16,128]{3,2,1,0:T(8,128)(2,1)S(1)}, u32[]{:S(2)}, u32[]{:S(2)}) collective-permute-start(bf16[4,9,16,128]{3,2,1,0:T(8,128)(2,1)S(1)} %merge_pair.1.refs_0_), channel_id=1, source_target_pairs={{0,6},{1,7},{2,4},{3,5},{4,2},{5,3},{6,0},{7,1},{8,14},{9,15},{10,... | collective-permute-start | bytes 442376 | tf_op jit(solution)/shard_map/ppermute | solution.py:685
  40.9 6.6 %collective-permute-start.9 = (bf16[4,9,16,128]{3,2,1,0:T(8,128)(2,1)S(1)}, bf16[4,9,16,128]{3,2,1,0:T(8,128)(2,1)S(1)}, u32[]{:S(2)}, u32[]{:S(2)}) collective-permute-start(bf16[4,9,16,128]{3,2,1,0:T(8,128)(2,1)S(1)} %merge_pair.1.refs_0_), channel_id=1, source_target_pairs={{0,2},{1,3},{2,0},{3,1},{4,6},{5,7},{6,4},{7,5},{8,10},{9,11},{10,... | collective-permute-start | bytes 442376 | tf_op jit(solution)/shard_map/ppermute | solution.py:685
  48.0 1.4 %collective-permute-start.12 = (bf16[32,2048]{1,0:T(8,128)(2,1)S(1)}, bf16[32,2048]{1,0:T(8,128)(2,1)S(1)}, u32[]{:S(2)}, u32[]{:S(2)}) collective-permute-start(bf16[32,2048]{1,0:T(8,128)(2,1)S(1)} %merge.1.refs_0_), channel_id=1, source_target_pairs={{0,1},{1,0},{2,3},{3,2},{4,5},{5,4},{6,7},{7,6},{8,9},{9,8},{10,11... | collective-permute-start | bytes 393224 | tf_op jit(solution)/shard_map/ppermute | solution.py:685
  50.1 4.5 %collective-permute-start.13 = (bf16[16,640]{1,0:T(8,128)(2,1)S(1)}, bf16[16,640]{1,0:T(8,128)(2,1)S(1)}, u32[]{:S(2)}, u32[]{:S(2)}) collective-permute-start(bf16[16,640]{1,0:T(8,128)(2,1)S(1)} %get-tuple-element.34), channel_id=1, source_target_pairs={{0,8},{8,0},{16,24},{24,16},{1,9},{9,1},{17,25},{25,17},{2,10},{10... | collective-permute-start | bytes 61448 | tf_op jit(solution)/shard_map/ppermute | solution.py:685
  51.7 4.9 %collective-permute-start.14 = (bf16[16,640]{1,0:T(8,128)(2,1)S(1)}, bf16[16,640]{1,0:T(8,128)(2,1)S(1)}, u32[]{:S(2)}, u32[]{:S(2)}) collective-permute-start(bf16[16,640]{1,0:T(8,128)(2,1)S(1)} %get-tuple-element.35), channel_id=1, source_target_pairs={{0,16},{8,24},{16,0},{24,8},{1,17},{9,25},{17,1},{25,9},{2,18},{10... | collective-permute-start | bytes 61448 | tf_op jit(solution)/shard_map/ppermute | solution.py:685
  54.3 5.6 %collective-permute-start.15 = (bf16[16,640]{1,0:T(8,128)(2,1)S(1)}, bf16[16,640]{1,0:T(8,128)(2,1)S(1)}, u32[]{:S(2)}, u32[]{:S(2)}) collective-permute-start(bf16[16,640]{1,0:T(8,128)(2,1)S(1)} %get-tuple-element.36), channel_id=1, source_target_pairs={{0,24},{8,16},{16,8},{24,0},{1,25},{9,17},{17,9},{25,1},{2,26},{10... | collective-permute-start | bytes 61448 | tf_op jit(solution)/shard_map/ppermute | solution.py:685

commit v10 on v9

--- a/solution.py
+++ b/solution.py
@@ -324,7 +324,7 @@
     bound_ref[...] = bounds.astype(jnp.int32)
 
 
-def list_kernel(spare, place_ref, value_ref, list_ref):
+def list_kernel(spare, place_ref, value_ref, joined_ref, list_ref):
     rows, slots = place_ref.shape
     capacity = list_ref.shape[1]
     target = lax.broadcasted_iota(jnp.int32, (8, capacity), 1).astype(jnp.float32)
@@ -358,40 +358,40 @@
     )(*parts)
 
 
-def make_list(places, values, blocks, block_size, count):
+def make_list(places, values, joined, blocks, block_size, count):
     rows, slots = places.shape
     most = 2 * rows * slots // count // count * count + (GROUP - 1) * blocks + 3 * CHUNK
     capacity = -(-most // LANES) * LANES
     return pl.pallas_call(
         functools.partial(list_kernel, float(rows * blocks * block_size)),
-        in_specs=[vmem_spec()] * 2,
+        in_specs=[vmem_spec()] * 3,
         out_specs=vmem_spec(),
         out_shape=jax.ShapeDtypeStruct((1, capacity), jnp.int32),
         compiler_params=params(16),
         cost_estimate=pl.CostEstimate(flops=10**8, bytes_accessed=4 * 10**6, transcendentals=0),
         name="slot_list",
-    )(places, values)
-
-
-def join_kernel(own_ref, other_ref, places_ref, out_ref):
-    own = own_ref.shape[0]
-    out_ref[:own] = own_ref[...]
-    out_ref[own:] = other_ref[...]
-
-
-def join_pair(own, other, places):
+    )(places, values, joined)
+
+
+def join_kernel(*refs):
+    pieces, out_ref = refs[:-2], refs[-1]
+    for s, piece in enumerate(pieces):
+        out_ref[s] = piece[...]
+
+
+def join(pieces, places):
     return pl.pallas_call(
         join_kernel,
-        in_specs=[vmem_spec()] * 3,
+        in_specs=[vmem_spec()] * (len(pieces) + 1),
         out_specs=vmem_spec(),
-        out_shape=jax.ShapeDtypeStruct((PAIR * own.shape[0], *own.shape[1:]), own.dtype),
+        out_shape=jax.ShapeDtypeStruct((len(pieces), *pieces[0].shape), pieces[0].dtype),
         compiler_params=params(16),
-        name="join_pair",
-    )(own, other, places)
+        name="join",
+    )(*pieces, places)
 
 
 def attend_kernel(scale, kv_local, count, list_vmem, bound_vmem, *refs):
-    queries, refs = refs[: count // PAIR], refs[count // PAIR :]
+    queries, refs = refs[:PAIR], refs[PAIR:]
     (key_hbm, value_hbm, keep_ref, send_ref, list_ref, bound_ref, query_ref, key_ref, value_ref) = refs[:9]
     (score_ref, part_top_ref, part_total_ref, part_sum_ref, number_sems, sems) = refs[9:15]
     states = [refs[15 + 3 * k : 18 + 3 * k] for k in range(SETS)]
@@ -420,10 +420,10 @@
             copy.start()
 
     factor = scale * LOG2E
-    for s, piece in enumerate(queries):
-        for t in range(PAIR):
+    for t, piece in enumerate(queries):
+        for s in range(count // PAIR):
             start = (PAIR * s + t) * own
-            query_ref[start : start + own] = piece[t]
+            query_ref[start : start + own] = piece[s]
     query_ref[rows] = jnp.zeros((heads, LANES), jnp.bfloat16)
     for state in states:
         for ref, value in zip(state, (NEG_FILL, 0.0, 0.0)):
@@ -540,8 +540,8 @@
 
 
 def attend(items, bounds, queries, keys, values, kv_local, scale):
-    _, own, heads, _ = queries[0].shape
-    count = len(queries) * PAIR
+    chips, own, heads, _ = queries[0].shape
+    count = chips * PAIR
     rows = count * own
     tokens = keys.shape[1]
     keys, values = in_hbm(keys, values)
@@ -740,9 +740,9 @@
     sine = jnp.concatenate([-jnp.sin(angles), jnp.sin(angles)], axis=-1)
     queries = make_queries(parts, up, cosine, sine, query_norm_gain.reshape(1, head_size), heads, 3 * slots)
     places, slot_values, bounds = make_places(parts, slots, blocks, block_size, kv_count)
-    queries = gather_chips(join_pair(queries, exchange(queries, "kv", 1), places))
-    queries = [q.reshape(PAIR, own, heads, head_size) for q in queries]
-    items = make_list(places, slot_values, blocks, block_size, kv_count)
+    queries = join(gather_chips(queries), places)
+    items = make_list(places, slot_values, queries, blocks, block_size, kv_count)
+    queries = [queries, exchange(queries, "kv", 1)]
 
     keys = paged_key_cache.reshape(blocks, block_size * kv_local, head_size)
     values = paged_value_cache.reshape(blocks, block_size * kv_local, head_size)

time: 60.9 us -> 62.7 us (1.030); the launches traced: 60.5 us -> 63.4 us
  starting transfers between devices: 18.6 us -> 21.5 us
    ppermute x16, starting transfers between devices: 18.6 us -> 21.5 us  [exchange(): return lax.ppermute(x, axis, [(i, i ^ s) for i in range(count)])]
  transfers between devices with their start and end apart: 16 -> 16, of which waited for: 14 -> 12; matrix products, arithmetic and copies ran while one was open for 1% -> 1% of each run, Pallas kernels for 4% -> 4%
where the time goes in v10:
time: 62.7 us; the launch traced here: 63.4 us
  waiting for transfers between devices  22.7 us (36%)
  starting transfers between devices  21.5 us (34%)
  Pallas kernels  18.2 us (29%)
  other arithmetic  0.95 us (2%)
    ppermute x16, waiting for transfers between devices, exchange(): return lax.ppermute(x, axis, [(i, i ^ s) for i in range(count)])  22.7 us
    ppermute x16, starting transfers between devices, exchange(): return lax.ppermute(x, axis, [(i, i ^ s) for i in range(count)])  21.5 us
    pallas_call x1, Pallas kernels, attend(): pl.pallas_call(functools.partial(attend_kernel, scale, kv_local, count),...  10.5 us
    pallas_call x1, Pallas kernels, project(): pl.pallas_call(functools.partial(project_kernel, rank), in_specs=[hbm_spe...  3.23 us
    pallas_call x1, Pallas kernels, make_list(): pl.pallas_call(functools.partial(list_kernel, float(rows * blocks * block...  1.42 us
  transfers between devices with their start and end apart: 16, of which 12 were waited for; matrix products, arithmetic and copies ran while one was open for 1% of the time, Pallas kernels for 4%

profile of v10, /device:TPU:0, one launch (start us, length us, event | category | flops | bytes accessed | tf_op | source)
XLA Modules:
  0.0 63.4 jit_solution(9114736478841699589)
XLA Ops:
  0.0 3.2 %project.1 = (f32[4,8,2176]{2,1,0:T(8,128)S(1)}, f32[4,8,2176]{2,1,0:T(8,128)S(1)}, f32[8,16,2048]{2,1,0:T(8,128)S(1)}) custom-call(s32[64]{0:T(128)} %tenant_hbm.1, s32[64]{0:T(128)} %adapter_hbm.1, s32[1,64]{1,0:T(1,128)} %bitcast.12, s32[1,64]{1,0:T(1,128)} %bitcast.13, s32[8,32]{1,0:T(8,128)} %holder_hbm.1, s32[8,32]{1,0:T(8,128)} %block_hbm.1, ...), custom_call_target="tpu_custom_call" | custom-call | tf_op jit(solution)/shard_map/project/pallas_call | solution.py:186
  3.2 0.5 collective-permute-start
  4.0 0.9 %collective-permute-done.got_ref = f32[4,8,2176]{2,1,0:T(8,128)S(1)} collective-permute-done((f32[4,8,2176]{2,1,0:T(8,128)S(1)}, f32[4,8,2176]{2,1,0:T(8,128)S(1)}, u32[]{:S(2)}, u32[]{:S(2)}) %collective-permute-start) | collective-permute-done | bytes 278560 | tf_op jit(solution)/shard_map/ppermute | solution.py:685
  5.0 2.9 %collective-permute-start.1 = (f32[8,2304]{1,0:T(8,128)S(1)}, f32[8,2304]{1,0:T(8,128)S(1)}, u32[]{:S(2)}, u32[]{:S(2)}) collective-permute-start(f32[8,2304]{1,0:T(8,128)S(1)} %get-tuple-element.24), channel_id=1, source_target_pairs={{0,2},{1,3},{2,0},{3,1},{4,6},{5,7},{6,4},{7,5},{8,10},{9,11},{10,... | collective-permute-start | bytes 221192 | tf_op jit(solution)/shard_map/ppermute | solution.py:685
  7.9 1.5 %collective-permute-start.2 = (f32[8,2304]{1,0:T(8,128)S(1)}, f32[8,2304]{1,0:T(8,128)S(1)}, u32[]{:S(2)}, u32[]{:S(2)}) collective-permute-start(f32[8,2304]{1,0:T(8,128)S(1)} %get-tuple-element.25), channel_id=1, source_target_pairs={{0,4},{1,5},{2,6},{3,7},{4,0},{5,1},{6,2},{7,3},{8,12},{9,13},{10,... | collective-permute-start | bytes 221192 | tf_op jit(solution)/shard_map/ppermute | solution.py:685
  9.5 1.0 %collective-permute-done.1.refs_1_ = f32[8,2304]{1,0:T(8,128)S(1)} collective-permute-done((f32[8,2304]{1,0:T(8,128)S(1)}, f32[8,2304]{1,0:T(8,128)S(1)}, u32[]{:S(2)}, u32[]{:S(2)}) %collective-permute-start.1) | collective-permute-done | bytes 73760 | tf_op jit(solution)/shard_map/ppermute | solution.py:685
  10.5 1.8 %collective-permute-done.2.refs_2_ = f32[8,2304]{1,0:T(8,128)S(1)} collective-permute-done((f32[8,2304]{1,0:T(8,128)S(1)}, f32[8,2304]{1,0:T(8,128)S(1)}, u32[]{:S(2)}, u32[]{:S(2)}) %collective-permute-start.2) | collective-permute-done | bytes 73760 | tf_op jit(solution)/shard_map/ppermute | solution.py:685
  12.3 2.4 %collective-permute-done.3.refs_3_ = f32[8,2304]{1,0:T(8,128)S(1)} collective-permute-done((f32[8,2304]{1,0:T(8,128)S(1)}, f32[8,2304]{1,0:T(8,128)S(1)}, u32[]{:S(2)}, u32[]{:S(2)}) %collective-permute-start.3) | collective-permute-done | bytes 73760 | tf_op jit(solution)/shard_map/ppermute | solution.py:685
  14.7 0.4 queries.1.refs_0_
  15.1 0.6 collective-permute-start.4
  15.7 0.6 collective-permute-start.5
  16.3 2.4 %collective-permute-start.6 = (bf16[8,16,128]{2,1,0:T(8,128)(2,1)S(1)}, bf16[8,16,128]{2,1,0:T(8,128)(2,1)S(1)}, u32[]{:S(2)}, u32[]{:S(2)}) collective-permute-start(bf16[8,16,128]{2,1,0:T(8,128)(2,1)S(1)} %queries.1.refs_0_), channel_id=1, source_target_pairs={{0,6},{1,7},{2,4},{3,5},{4,2},{5,3},{6,0},{7,1},{8,14},{9,15},{10,... | collective-permute-start | bytes 98312 | tf_op jit(solution)/shard_map/ppermute | solution.py:685
  18.7 1.0 %slot_places.1 = (f32[64,32]{1,0:T(8,128)S(1)}, f32[64,32]{1,0:T(8,128)S(1)}, s32[1,128]{1,0:T(1,128)S(1)}) custom-call(f32[8,2304]{1,0:T(8,128)S(1)} %get-tuple-element.23.refs_0_, f32[8,2304]{1,0:T(8,128)S(1)} %collective-permute-done.1.refs_1_, f32[8,2304]{1,0:T(8,128)S(1)} %collective-permute-done.2.refs_2_, f32[8,2304]{1,0:T(8,128)S(1)} %collective-permute-done.3.refs_3_), custom_call_target="tpu_custom_call" | custom-call | flops 100000000 | bytes 4000000 | tf_op jit(solution)/shard_map/slot_places/pallas_call | solution.py:349
  19.7 1.4 %collective-permute-done.6.refs_3_ = bf16[8,16,128]{2,1,0:T(8,128)(2,1)S(1)} collective-permute-done((bf16[8,16,128]{2,1,0:T(8,128)(2,1)S(1)}, bf16[8,16,128]{2,1,0:T(8,128)(2,1)S(1)}, u32[]{:S(2)}, u32[]{:S(2)}) %collective-permute-start.6) | collective-permute-done | bytes 32800 | tf_op jit(solution)/shard_map/ppermute | solution.py:685
  21.2 1.4 %slot_list.1.list_vmem = s32[1,1024]{1,0:T(1,128)S(1)} custom-call(f32[64,32]{1,0:T(8,128)S(1)} %get-tuple-element.27.refs_4_.place_ref, f32[64,32]{1,0:T(8,128)S(1)} %get-tuple-element.28.value_ref, bf16[4,8,16,128]{3,2,1,0:T(8,128)(2,1)S(1)} %join.1.joined_ref.refs_0_), custom_call_target="tpu_custom_call" | custom-call | flops 100000000 | bytes 4000000 | tf_op jit(solution)/shard_map/slot_list/pallas_call | solution.py:365
  22.6 10.5 %attend.1 = (f32[4,9,16,128]{3,2,1,0:T(8,128)S(1)}, f32[4,9,16,128]{3,2,1,0:T(8,128)S(1)}) custom-call(s32[1,1024]{1,0:T(1,128)S(1)} %slot_list.1.list_vmem, s32[1,128]{1,0:T(1,128)S(1)} %get-tuple-element.30.bound_vmem, bf16[4,8,16,128]{3,2,1,0:T(8,128)(2,1)S(1)} %join.1.joined_ref.refs_0_, bf16[4,8,16,128]{3,2,1,0:T(8,128)(2,1)S(1)} %collective-permute-done.7.refs_1_, ...), custom_call_target="tpu_custom_call" | custom-call | tf_op jit(solution)/shard_map/attend/pallas_call | solution.py:550
  33.2 1.2 %collective-permute-start.8 = (f32[4,9,16,128]{3,2,1,0:T(8,128)S(1)}, f32[4,9,16,128]{3,2,1,0:T(8,128)S(1)}, u32[]{:S(2)}, u32[]{:S(2)}) collective-permute-start(f32[4,9,16,128]{3,2,1,0:T(8,128)S(1)} %get-tuple-element.32), channel_id=1, source_target_pairs={{0,1},{1,0},{2,3},{3,2},{4,5},{5,4},{6,7},{7,6},{8,9},{9,8},{10,11... | collective-permute-start | bytes 884744 | tf_op jit(solution)/shard_map/ppermute | solution.py:685
  34.3 1.2 %collective-permute-done.8.got_ref = f32[4,9,16,128]{3,2,1,0:T(8,128)S(1)} collective-permute-done((f32[4,9,16,128]{3,2,1,0:T(8,128)S(1)}, f32[4,9,16,128]{3,2,1,0:T(8,128)S(1)}, u32[]{:S(2)}, u32[]{:S(2)}) %collective-permute-start.8) | collective-permute-done | bytes 294944 | tf_op jit(solution)/shard_map/ppermute | solution.py:685
  35.5 0.3 merge_pair.1.refs_0_
  35.9 5.6 %collective-permute-start.10 = (bf16[4,9,16,128]{3,2,1,0:T(8,128)(2,1)S(1)}, bf16[4,9,16,128]{3,2,1,0:T(8,128)(2,1)S(1)}, u32[]{:S(2)}, u32[]{:S(2)}) collective-permute-start(bf16[4,9,16,128]{3,2,1,0:T(8,128)(2,1)S(1)} %merge_pair.1.refs_0_), channel_id=1, source_target_pairs={{0,4},{1,5},{2,6},{3,7},{4,0},{5,1},{6,2},{7,3},{8,12},{9,13},{10,... | collective-permute-start | bytes 442376 | tf_op jit(solution)/shard_map/ppermute | solution.py:685
  41.5 1.5 %collective-permute-start.9 = (bf16[4,9,16,128]{3,2,1,0:T(8,128)(2,1)S(1)}, bf16[4,9,16,128]{3,2,1,0:T(8,128)(2,1)S(1)}, u32[]{:S(2)}, u32[]{:S(2)}) collective-permute-start(bf16[4,9,16,128]{3,2,1,0:T(8,128)(2,1)S(1)} %merge_pair.1.refs_0_), channel_id=1, source_target_pairs={{0,2},{1,3},{2,0},{3,1},{4,6},{5,7},{6,4},{7,5},{8,10},{9,11},{10,... | collective-permute-start | bytes 442376 | tf_op jit(solution)/shard_map/ppermute | solution.py:685
  43.1 5.9 %collective-permute-done.10.refs_2_ = bf16[4,9,16,128]{3,2,1,0:T(8,128)(2,1)S(1)} collective-permute-done((bf16[4,9,16,128]{3,2,1,0:T(8,128)(2,1)S(1)}, bf16[4,9,16,128]{3,2,1,0:T(8,128)(2,1)S(1)}, u32[]{:S(2)}, u32[]{:S(2)}) %collective-permute-start.10) | collective-permute-done | bytes 147488 | tf_op jit(solution)/shard_map/ppermute | solution.py:685
  48.9 0.2 collective-permute-done.11.refs_3_
  49.2 1.2 %collective-permute-done.9.refs_1_ = bf16[4,9,16,128]{3,2,1,0:T(8,128)(2,1)S(1)} collective-permute-done((bf16[4,9,16,128]{3,2,1,0:T(8,128)(2,1)S(1)}, bf16[4,9,16,128]{3,2,1,0:T(8,128)(2,1)S(1)}, u32[]{:S(2)}, u32[]{:S(2)}) %collective-permute-start.9) | collective-permute-done | bytes 147488 | tf_op jit(solution)/shard_map/ppermute | solution.py:685
  50.4 0.6 merge.1.refs_0_
  51.0 1.3 %collective-permute-done.12.refs_1_ = bf16[32,2048]{1,0:T(8,128)(2,1)S(1)} collective-permute-done((bf16[32,2048]{1,0:T(8,128)(2,1)S(1)}, bf16[32,2048]{1,0:T(8,128)(2,1)S(1)}, u32[]{:S(2)}, u32[]{:S(2)}) %collective-permute-start.12) | collective-permute-done | bytes 131104 | tf_op jit(solution)/shard_map/ppermute | solution.py:685
  52.4 0.6 project_out.1
  53.0 1.6 %collective-permute-start.13 = (bf16[16,640]{1,0:T(8,128)(2,1)S(1)}, bf16[16,640]{1,0:T(8,128)(2,1)S(1)}, u32[]{:S(2)}, u32[]{:S(2)}) collective-permute-start(bf16[16,640]{1,0:T(8,128)(2,1)S(1)} %get-tuple-element.34), channel_id=1, source_target_pairs={{0,8},{8,0},{16,24},{24,16},{1,9},{9,1},{17,25},{25,17},{2,10},{10... | collective-permute-start | bytes 61448 | tf_op jit(solution)/shard_map/ppermute | solution.py:685
  54.6 2.6 %collective-permute-start.14 = (bf16[16,640]{1,0:T(8,128)(2,1)S(1)}, bf16[16,640]{1,0:T(8,128)(2,1)S(1)}, u32[]{:S(2)}, u32[]{:S(2)}) collective-permute-start(bf16[16,640]{1,0:T(8,128)(2,1)S(1)} %get-tuple-element.35), channel_id=1, source_target_pairs={{0,16},{8,24},{16,0},{24,8},{1,17},{9,25},{17,1},{25,9},{2,18},{10... | collective-permute-start | bytes 61448 | tf_op jit(solution)/shard_map/ppermute | solution.py:685
  57.4 2.1 %collective-permute-done.14 = bf16[16,640]{1,0:T(8,128)(2,1)S(1)} collective-permute-done((bf16[16,640]{1,0:T(8,128)(2,1)S(1)}, bf16[16,640]{1,0:T(8,128)(2,1)S(1)}, u32[]{:S(2)}, u32[]{:S(2)}) %collective-permute-start.14) | collective-permute-done | bytes 20512 | tf_op jit(solution)/shard_map/ppermute | solution.py:685
  59.5 3.3 %collective-permute-done.15 = bf16[16,640]{1,0:T(8,128)(2,1)S(1)} collective-permute-done((bf16[16,640]{1,0:T(8,128)(2,1)S(1)}, bf16[16,640]{1,0:T(8,128)(2,1)S(1)}, u32[]{:S(2)}, u32[]{:S(2)}) %collective-permute-start.15) | collective-permute-done | bytes 20512 | tf_op jit(solution)/shard_map/ppermute | solution.py:685
  62.8 0.6 add_convert_fusion
  (22 shorter events, 0.8 us)
Async XLA Ops:
  0.0 3.8 %copy-start.2 = (s32[8,32]{1,0:T(8,128)S(1)}, s32[8,32]{1,0:T(8,128)}, u32[]{:S(2)}) copy-start(s32[8,32]{1,0:T(8,128)} %length_hbm.1) | copy-start | bytes 3076
  0.0 14.7 %copy-start.1 = (f32[128]{0:T(128)S(1)}, f32[128]{0:T(128)}, u32[]{:S(2)}) copy-start(f32[128]{0:T(128)} %param.17) | copy-start | bytes 1540
  3.2 1.7 %collective-permute-start = (f32[4,8,2176]{2,1,0:T(8,128)S(1)}, f32[4,8,2176]{2,1,0:T(8,128)S(1)}, u32[]{:S(2)}, u32[]{:S(2)}) collective-permute-start(f32[4,8,2176]{2,1,0:T(8,128)S(1)} %get-tuple-element.22), channel_id=1, source_target_pairs={{0,1},{1,0},{2,3},{3,2},{4,5},{5,4},{6,7},{7,6},{8,9},{9,8},{10,11... | collective-permute-start | bytes 835592 | tf_op jit(solution)/shard_map/ppermute | solution.py:685
  5.0 5.5 %collective-permute-start.1 = (f32[8,2304]{1,0:T(8,128)S(1)}, f32[8,2304]{1,0:T(8,128)S(1)}, u32[]{:S(2)}, u32[]{:S(2)}) collective-permute-start(f32[8,2304]{1,0:T(8,128)S(1)} %get-tuple-element.24), channel_id=1, source_target_pairs={{0,2},{1,3},{2,0},{3,1},{4,6},{5,7},{6,4},{7,5},{8,10},{9,11},{10,... | collective-permute-start | bytes 221192 | tf_op jit(solution)/shard_map/ppermute | solution.py:685
  7.9 4.4 %collective-permute-start.2 = (f32[8,2304]{1,0:T(8,128)S(1)}, f32[8,2304]{1,0:T(8,128)S(1)}, u32[]{:S(2)}, u32[]{:S(2)}) collective-permute-start(f32[8,2304]{1,0:T(8,128)S(1)} %get-tuple-element.25), channel_id=1, source_target_pairs={{0,4},{1,5},{2,6},{3,7},{4,0},{5,1},{6,2},{7,3},{8,12},{9,13},{10,... | collective-permute-start | bytes 221192 | tf_op jit(solution)/shard_map/ppermute | solution.py:685
  9.4 5.3 %collective-permute-start.3 = (f32[8,2304]{1,0:T(8,128)S(1)}, f32[8,2304]{1,0:T(8,128)S(1)}, u32[]{:S(2)}, u32[]{:S(2)}) collective-permute-start(f32[8,2304]{1,0:T(8,128)S(1)} %get-tuple-element.26), channel_id=1, source_target_pairs={{0,6},{1,7},{2,4},{3,5},{4,2},{5,3},{6,0},{7,1},{8,14},{9,15},{10,... | collective-permute-start | bytes 221192 | tf_op jit(solution)/shard_map/ppermute | solution.py:685
  15.1 4.6 %collective-permute-start.4 = (bf16[8,16,128]{2,1,0:T(8,128)(2,1)S(1)}, bf16[8,16,128]{2,1,0:T(8,128)(2,1)S(1)}, u32[]{:S(2)}, u32[]{:S(2)}) collective-permute-start(bf16[8,16,128]{2,1,0:T(8,128)(2,1)S(1)} %queries.1.refs_0_), channel_id=1, source_target_pairs={{0,2},{1,3},{2,0},{3,1},{4,6},{5,7},{6,4},{7,5},{8,10},{9,11},{10,... | collective-permute-start | bytes 98312 | tf_op jit(solution)/shard_map/ppermute | solution.py:685
  15.7 4.0 %collective-permute-start.5 = (bf16[8,16,128]{2,1,0:T(8,128)(2,1)S(1)}, bf16[8,16,128]{2,1,0:T(8,128)(2,1)S(1)}, u32[]{:S(2)}, u32[]{:S(2)}) collective-permute-start(bf16[8,16,128]{2,1,0:T(8,128)(2,1)S(1)} %queries.1.refs_0_), channel_id=1, source_target_pairs={{0,4},{1,5},{2,6},{3,7},{4,0},{5,1},{6,2},{7,3},{8,12},{9,13},{10,... | collective-permute-start | bytes 98312 | tf_op jit(solution)/shard_map/ppermute | solution.py:685
  16.3 4.8 %collective-permute-start.6 = (bf16[8,16,128]{2,1,0:T(8,128)(2,1)S(1)}, bf16[8,16,128]{2,1,0:T(8,128)(2,1)S(1)}, u32[]{:S(2)}, u32[]{:S(2)}) collective-permute-start(bf16[8,16,128]{2,1,0:T(8,128)(2,1)S(1)} %queries.1.refs_0_), channel_id=1, source_target_pairs={{0,6},{1,7},{2,4},{3,5},{4,2},{5,3},{6,0},{7,1},{8,14},{9,15},{10,... | collective-permute-start | bytes 98312 | tf_op jit(solution)/shard_map/ppermute | solution.py:685
  21.1 1.5 %collective-permute-start.7 = (bf16[4,8,16,128]{3,2,1,0:T(8,128)(2,1)S(1)}, bf16[4,8,16,128]{3,2,1,0:T(8,128)(2,1)S(1)}, u32[]{:S(2)}, u32[]{:S(2)}) collective-permute-start(bf16[4,8,16,128]{3,2,1,0:T(8,128)(2,1)S(1)} %join.1.joined_ref.refs_0_), channel_id=1, source_target_pairs={{0,1},{1,0},{2,3},{3,2},{4,5},{5,4},{6,7},{7,6},{8,9},{9,8},{10,11... | collective-permute-start | bytes 393224 | tf_op jit(solution)/shard_map/ppermute | solution.py:685
  22.6 29.7 %copy-start = (bf16[2048,640]{1,0:T(8,128)(2,1)S(1)}, bf16[2048,640]{1,0:T(8,128)(2,1)}, u32[]{:S(2)}) copy-start(bf16[2048,640]{1,0:T(8,128)(2,1)} %refs_2_.1) | copy-start | bytes 7864324
  33.2 2.4 %collective-permute-start.8 = (f32[4,9,16,128]{3,2,1,0:T(8,128)S(1)}, f32[4,9,16,128]{3,2,1,0:T(8,128)S(1)}, u32[]{:S(2)}, u32[]{:S(2)}) collective-permute-start(f32[4,9,16,128]{3,2,1,0:T(8,128)S(1)} %get-tuple-element.32), channel_id=1, source_target_pairs={{0,1},{1,0},{2,3},{3,2},{4,5},{5,4},{6,7},{7,6},{8,9},{9,8},{10,11... | collective-permute-start | bytes 884744 | tf_op jit(solution)/shard_map/ppermute | solution.py:685
  35.9 13.1 %collective-permute-start.10 = (bf16[4,9,16,128]{3,2,1,0:T(8,128)(2,1)S(1)}, bf16[4,9,16,128]{3,2,1,0:T(8,128)(2,1)S(1)}, u32[]{:S(2)}, u32[]{:S(2)}) collective-permute-start(bf16[4,9,16,128]{3,2,1,0:T(8,128)(2,1)S(1)} %merge_pair.1.refs_0_), channel_id=1, source_target_pairs={{0,4},{1,5},{2,6},{3,7},{4,0},{5,1},{6,2},{7,3},{8,12},{9,13},{10,... | collective-permute-start | bytes 442376 | tf_op jit(solution)/shard_map/ppermute | solution.py:685
  41.5 7.7 %collective-permute-start.11 = (bf16[4,9,16,128]{3,2,1,0:T(8,128)(2,1)S(1)}, bf16[4,9,16,128]{3,2,1,0:T(8,128)(2,1)S(1)}, u32[]{:S(2)}, u32[]{:S(2)}) collective-permute-start(bf16[4,9,16,128]{3,2,1,0:T(8,128)(2,1)S(1)} %merge_pair.1.refs_0_), channel_id=1, source_target_pairs={{0,6},{1,7},{2,4},{3,5},{4,2},{5,3},{6,0},{7,1},{8,14},{9,15},{10,... | collective-permute-start | bytes 442376 | tf_op jit(solution)/shard_map/ppermute | solution.py:685
  41.5 8.8 %collective-permute-start.9 = (bf16[4,9,16,128]{3,2,1,0:T(8,128)(2,1)S(1)}, bf16[4,9,16,128]{3,2,1,0:T(8,128)(2,1)S(1)}, u32[]{:S(2)}, u32[]{:S(2)}) collective-permute-start(bf16[4,9,16,128]{3,2,1,0:T(8,128)(2,1)S(1)} %merge_pair.1.refs_0_), channel_id=1, source_target_pairs={{0,2},{1,3},{2,0},{3,1},{4,6},{5,7},{6,4},{7,5},{8,10},{9,11},{10,... | collective-permute-start | bytes 442376 | tf_op jit(solution)/shard_map/ppermute | solution.py:685
  50.9 1.4 %collective-permute-start.12 = (bf16[32,2048]{1,0:T(8,128)(2,1)S(1)}, bf16[32,2048]{1,0:T(8,128)(2,1)S(1)}, u32[]{:S(2)}, u32[]{:S(2)}) collective-permute-start(bf16[32,2048]{1,0:T(8,128)(2,1)S(1)} %merge.1.refs_0_), channel_id=1, source_target_pairs={{0,1},{1,0},{2,3},{3,2},{4,5},{5,4},{6,7},{7,6},{8,9},{9,8},{10,11... | collective-permute-start | bytes 393224 | tf_op jit(solution)/shard_map/ppermute | solution.py:685
  53.0 4.5 %collective-permute-start.13 = (bf16[16,640]{1,0:T(8,128)(2,1)S(1)}, bf16[16,640]{1,0:T(8,128)(2,1)S(1)}, u32[]{:S(2)}, u32[]{:S(2)}) collective-permute-start(bf16[16,640]{1,0:T(8,128)(2,1)S(1)} %get-tuple-element.34), channel_id=1, source_target_pairs={{0,8},{8,0},{16,24},{24,16},{1,9},{9,1},{17,25},{25,17},{2,10},{10... | collective-permute-start | bytes 61448 | tf_op jit(solution)/shard_map/ppermute | solution.py:685
  54.6 4.9 %collective-permute-start.14 = (bf16[16,640]{1,0:T(8,128)(2,1)S(1)}, bf16[16,640]{1,0:T(8,128)(2,1)S(1)}, u32[]{:S(2)}, u32[]{:S(2)}) collective-permute-start(bf16[16,640]{1,0:T(8,128)(2,1)S(1)} %get-tuple-element.35), channel_id=1, source_target_pairs={{0,16},{8,24},{16,0},{24,8},{1,17},{9,25},{17,1},{25,9},{2,18},{10... | collective-permute-start | bytes 61448 | tf_op jit(solution)/shard_map/ppermute | solution.py:685
  57.2 5.6 %collective-permute-start.15 = (bf16[16,640]{1,0:T(8,128)(2,1)S(1)}, bf16[16,640]{1,0:T(8,128)(2,1)S(1)}, u32[]{:S(2)}, u32[]{:S(2)}) collective-permute-start(bf16[16,640]{1,0:T(8,128)(2,1)S(1)} %get-tuple-element.36), channel_id=1, source_target_pairs={{0,24},{8,16},{16,8},{24,0},{1,25},{9,17},{17,9},{25,1},{2,26},{10... | collective-permute-start | bytes 61448 | tf_op jit(solution)/shard_map/ppermute | solution.py:685

commit v11 on v10

--- a/solution.py
+++ b/solution.py
@@ -19,8 +19,8 @@
 TASKS = 8
 CHUNK = GROUP * TASKS
 SETS = 2
-PHASES = 16
-AHEAD = 6
+PHASES = 8
+AHEAD = 4
 DEPTH = 256
 LOG2E = math.log2(math.e)
 MIB = 1024 * 1024
@@ -324,8 +324,17 @@
     bound_ref[...] = bounds.astype(jnp.int32)
 
 
-def list_kernel(spare, place_ref, value_ref, joined_ref, list_ref):
+def list_kernel(
+    spare, place_ref, value_ref, joined_ref, key_hbm, value_hbm, list_ref, first_key_ref, first_value_ref, sems
+):
     rows, slots = place_ref.shape
+    span = pl.ds(0, first_key_ref.shape[0])
+    copies = [
+        pltpu.make_async_copy(key_hbm.at[span], first_key_ref, sems.at[0]),
+        pltpu.make_async_copy(value_hbm.at[span], first_value_ref, sems.at[1]),
+    ]
+    for copy in copies:
+        copy.start()
     capacity = list_ref.shape[1]
     target = lax.broadcasted_iota(jnp.int32, (8, capacity), 1).astype(jnp.float32)
 
@@ -338,6 +347,8 @@
 
     total = lax.fori_loop(0, rows // 8, tile, jnp.zeros((8, capacity), jnp.float32))
     list_ref[...] = (jnp.sum(total, axis=0, keepdims=True) + spare).astype(jnp.int32)
+    for copy in copies:
+        copy.wait()
 
 
 def make_places(parts, slots, blocks, block_size, count):
@@ -358,19 +369,22 @@
     )(*parts)
 
 
-def make_list(places, values, joined, blocks, block_size, count):
+def make_list(places, slot_values, joined, keys, values, block_size, count):
+    blocks = keys.shape[0]
     rows, slots = places.shape
     most = 2 * rows * slots // count // count * count + (GROUP - 1) * blocks + 3 * CHUNK
     capacity = -(-most // LANES) * LANES
     return pl.pallas_call(
         functools.partial(list_kernel, float(rows * blocks * block_size)),
-        in_specs=[vmem_spec()] * 3,
-        out_specs=vmem_spec(),
-        out_shape=jax.ShapeDtypeStruct((1, capacity), jnp.int32),
+        in_specs=[vmem_spec()] * 3 + [hbm_spec()] * 2,
+        out_specs=[vmem_spec()] * 3,
+        out_shape=[jax.ShapeDtypeStruct((1, capacity), jnp.int32)]
+        + [jax.ShapeDtypeStruct((blocks // PHASES, *x.shape[1:]), x.dtype) for x in (keys, values)],
+        scratch_shapes=[pltpu.SemaphoreType.DMA((2,))],
         compiler_params=params(16),
         cost_estimate=pl.CostEstimate(flops=10**8, bytes_accessed=4 * 10**6, transcendentals=0),
         name="slot_list",
-    )(places, values, joined)
+    )(places, slot_values, joined, *in_hbm(keys, values))
 
 
 def join_kernel(*refs):
@@ -391,7 +405,7 @@
 
 
 def attend_kernel(scale, kv_local, count, list_vmem, bound_vmem, *refs):
-    queries, refs = refs[:PAIR], refs[PAIR:]
+    queries, first_refs, refs = refs[:PAIR], refs[PAIR : PAIR + 2], refs[PAIR + 2 :]
     (key_hbm, value_hbm, keep_ref, send_ref, list_ref, bound_ref, query_ref, key_ref, value_ref) = refs[:9]
     (score_ref, part_top_ref, part_total_ref, part_sum_ref, number_sems, sems) = refs[9:15]
     states = [refs[15 + 3 * k : 18 + 3 * k] for k in range(SETS)]
@@ -415,9 +429,11 @@
         )
         for part, span in enumerate(spans)
     ]
-    for pair in (copies[0], numbers, *copies[1:AHEAD]):
+    for pair in (numbers, *copies[1 : 1 + AHEAD]):
         for copy in pair:
             copy.start()
+    for ref, first_ref in zip((key_ref, value_ref), first_refs):
+        ref[:size] = first_ref[...]
 
     factor = scale * LOG2E
     for t, piece in enumerate(queries):
@@ -512,11 +528,12 @@
     for copy in numbers:
         copy.wait()
     for part in range(PHASES):
-        for copy in copies[part]:
-            copy.wait()
-        for pair in copies[part + AHEAD : part + AHEAD + 1]:
-            for copy in pair:
-                copy.start()
+        if part > 0:
+            for copy in copies[part]:
+                copy.wait()
+            for pair in copies[part + AHEAD : part + AHEAD + 1]:
+                for copy in pair:
+                    copy.start()
         lax.fori_loop(bound_ref[0, part], bound_ref[0, part + 1], functools.partial(turn, 3), 0)
     last = bound_ref[0, PHASES]
     turn(2, last, 0)
@@ -539,7 +556,7 @@
         ref[q // PAIR, own] = jnp.where(line == 0, high, jnp.where(line == 1, total, 0.0))
 
 
-def attend(items, bounds, queries, keys, values, kv_local, scale):
+def attend(items, bounds, queries, first, keys, values, kv_local, scale):
     chips, own, heads, _ = queries[0].shape
     count = chips * PAIR
     rows = count * own
@@ -549,7 +566,7 @@
     part = pltpu.VMEM((CHUNK, heads, LANES), jnp.float32)
     return pl.pallas_call(
         functools.partial(attend_kernel, scale, kv_local, count),
-        in_specs=[vmem_spec()] * (2 + len(queries)) + [hbm_spec()] * 2,
+        in_specs=[vmem_spec()] * (4 + len(queries)) + [hbm_spec()] * 2,
         out_specs=[vmem_spec()] * PAIR,
         out_shape=[jax.ShapeDtypeStruct((count // PAIR, own + 1, heads, LANES), jnp.float32)] * PAIR,
         scratch_shapes=[
@@ -568,7 +585,7 @@
         + [state] * (3 * SETS),
         compiler_params=params(28 + 3 * SETS * rows * heads * LANES * 4 // MIB),
         name="attend",
-    )(items, bounds, *queries, keys, values)
+    )(items, bounds, *queries, *first, keys, values)
 
 
 def merge_pair_kernel(scale, keep_ref, got_ref, out_ref):
@@ -741,12 +758,11 @@
     queries = make_queries(parts, up, cosine, sine, query_norm_gain.reshape(1, head_size), heads, 3 * slots)
     places, slot_values, bounds = make_places(parts, slots, blocks, block_size, kv_count)
     queries = join(gather_chips(queries), places)
-    items = make_list(places, slot_values, queries, blocks, block_size, kv_count)
-    queries = [queries, exchange(queries, "kv", 1)]
-
     keys = paged_key_cache.reshape(blocks, block_size * kv_local, head_size)
     values = paged_value_cache.reshape(blocks, block_size * kv_local, head_size)
-    keep, send = attend(items, bounds, queries, keys, values, kv_local, scale)
+    items, *first = make_list(places, slot_values, queries, keys, values, block_size, kv_count)
+    queries = [queries, exchange(queries, "kv", 1)]
+    keep, send = attend(items, bounds, queries, first, keys, values, kv_local, scale)
     merged = merge_pair(keep, exchange(send, "kv", 1), scale)
     attention = merge(gather_chips(merged), scale)
     terms = project_out([attention, exchange(attention, "kv", 1)], output_weight, own, row_count)

time: 62.7 us -> 61.7 us (0.984); the launches traced: 63.4 us -> 61.4 us
  starting transfers between devices: 21.5 us -> 20.3 us
    ppermute x16, starting transfers between devices: 21.5 us -> 20.3 us  [exchange(): return lax.ppermute(x, axis, [(i, i ^ s) for i in range(count)])]
where the time goes in v11:
time: 61.7 us; the launch traced here: 61.4 us
  waiting for transfers between devices  22.3 us (36%)
  starting transfers between devices  20.3 us (33%)
  Pallas kernels  17.7 us (29%)
  other arithmetic  0.95 us (2%)
    ppermute x16, waiting for transfers between devices, exchange(): return lax.ppermute(x, axis, [(i, i ^ s) for i in range(count)])  22.3 us
    ppermute x16, starting transfers between devices, exchange(): return lax.ppermute(x, axis, [(i, i ^ s) for i in range(count)])  20.3 us
    pallas_call x1, Pallas kernels, attend(): pl.pallas_call(functools.partial(attend_kernel, scale, kv_local, count),...  9.94 us
    pallas_call x1, Pallas kernels, project(): pl.pallas_call(functools.partial(project_kernel, rank), in_specs=[hbm_spe...  3.23 us
    pallas_call x1, Pallas kernels, make_list(): pl.pallas_call(functools.partial(list_kernel, float(rows * blocks * block...  1.56 us
  transfers between devices with their start and end apart: 16, of which 12 were waited for; matrix products, arithmetic and copies ran while one was open for 1% of the time, Pallas kernels for 4%

profile of v11, /device:TPU:0, one launch (start us, length us, event | category | flops | bytes accessed | tf_op | source)
XLA Modules:
  0.0 61.4 jit_solution(5128793506619922058)
XLA Ops:
  0.0 3.2 %project.1 = (f32[4,8,2176]{2,1,0:T(8,128)S(1)}, f32[4,8,2176]{2,1,0:T(8,128)S(1)}, f32[8,16,2048]{2,1,0:T(8,128)S(1)}) custom-call(s32[64]{0:T(128)} %tenant_hbm.1, s32[64]{0:T(128)} %adapter_hbm.1, s32[1,64]{1,0:T(1,128)} %bitcast.14, s32[1,64]{1,0:T(1,128)} %bitcast.15, s32[8,32]{1,0:T(8,128)} %holder_hbm.1, s32[8,32]{1,0:T(8,128)} %block_hbm.1, ...), custom_call_target="tpu_custom_call" | custom-call | tf_op jit(solution)/shard_map/project/pallas_call | solution.py:186
  3.2 0.5 collective-permute-start
  4.0 0.9 %collective-permute-done.got_ref = f32[4,8,2176]{2,1,0:T(8,128)S(1)} collective-permute-done((f32[4,8,2176]{2,1,0:T(8,128)S(1)}, f32[4,8,2176]{2,1,0:T(8,128)S(1)}, u32[]{:S(2)}, u32[]{:S(2)}) %collective-permute-start) | collective-permute-done | bytes 278560 | tf_op jit(solution)/shard_map/ppermute | solution.py:702
  5.0 2.9 %collective-permute-start.1 = (f32[8,2304]{1,0:T(8,128)S(1)}, f32[8,2304]{1,0:T(8,128)S(1)}, u32[]{:S(2)}, u32[]{:S(2)}) collective-permute-start(f32[8,2304]{1,0:T(8,128)S(1)} %get-tuple-element.27), channel_id=1, source_target_pairs={{0,2},{1,3},{2,0},{3,1},{4,6},{5,7},{6,4},{7,5},{8,10},{9,11},{10,... | collective-permute-start | bytes 221192 | tf_op jit(solution)/shard_map/ppermute | solution.py:702
  7.9 1.5 %collective-permute-start.2 = (f32[8,2304]{1,0:T(8,128)S(1)}, f32[8,2304]{1,0:T(8,128)S(1)}, u32[]{:S(2)}, u32[]{:S(2)}) collective-permute-start(f32[8,2304]{1,0:T(8,128)S(1)} %get-tuple-element.28), channel_id=1, source_target_pairs={{0,4},{1,5},{2,6},{3,7},{4,0},{5,1},{6,2},{7,3},{8,12},{9,13},{10,... | collective-permute-start | bytes 221192 | tf_op jit(solution)/shard_map/ppermute | solution.py:702
  9.5 1.0 %collective-permute-done.1.refs_1_ = f32[8,2304]{1,0:T(8,128)S(1)} collective-permute-done((f32[8,2304]{1,0:T(8,128)S(1)}, f32[8,2304]{1,0:T(8,128)S(1)}, u32[]{:S(2)}, u32[]{:S(2)}) %collective-permute-start.1) | collective-permute-done | bytes 73760 | tf_op jit(solution)/shard_map/ppermute | solution.py:702
  10.5 1.8 %collective-permute-done.2.refs_2_ = f32[8,2304]{1,0:T(8,128)S(1)} collective-permute-done((f32[8,2304]{1,0:T(8,128)S(1)}, f32[8,2304]{1,0:T(8,128)S(1)}, u32[]{:S(2)}, u32[]{:S(2)}) %collective-permute-start.2) | collective-permute-done | bytes 73760 | tf_op jit(solution)/shard_map/ppermute | solution.py:702
  12.3 2.4 %collective-permute-done.3.refs_3_ = f32[8,2304]{1,0:T(8,128)S(1)} collective-permute-done((f32[8,2304]{1,0:T(8,128)S(1)}, f32[8,2304]{1,0:T(8,128)S(1)}, u32[]{:S(2)}, u32[]{:S(2)}) %collective-permute-start.3) | collective-permute-done | bytes 73760 | tf_op jit(solution)/shard_map/ppermute | solution.py:702
  14.7 0.4 queries.1.refs_0_
  15.1 0.6 collective-permute-start.6
  15.7 1.5 %collective-permute-start.5 = (bf16[8,16,128]{2,1,0:T(8,128)(2,1)S(1)}, bf16[8,16,128]{2,1,0:T(8,128)(2,1)S(1)}, u32[]{:S(2)}, u32[]{:S(2)}) collective-permute-start(bf16[8,16,128]{2,1,0:T(8,128)(2,1)S(1)} %queries.1.refs_0_), channel_id=1, source_target_pairs={{0,4},{1,5},{2,6},{3,7},{4,0},{5,1},{6,2},{7,3},{8,12},{9,13},{10,... | collective-permute-start | bytes 98312 | tf_op jit(solution)/shard_map/ppermute | solution.py:702
  17.2 1.5 %collective-permute-start.4 = (bf16[8,16,128]{2,1,0:T(8,128)(2,1)S(1)}, bf16[8,16,128]{2,1,0:T(8,128)(2,1)S(1)}, u32[]{:S(2)}, u32[]{:S(2)}) collective-permute-start(bf16[8,16,128]{2,1,0:T(8,128)(2,1)S(1)} %queries.1.refs_0_), channel_id=1, source_target_pairs={{0,2},{1,3},{2,0},{3,1},{4,6},{5,7},{6,4},{7,5},{8,10},{9,11},{10,... | collective-permute-start | bytes 98312 | tf_op jit(solution)/shard_map/ppermute | solution.py:702
  18.7 1.0 %slot_places.1 = (f32[64,32]{1,0:T(8,128)S(1)}, f32[64,32]{1,0:T(8,128)S(1)}, s32[1,128]{1,0:T(1,128)S(1)}) custom-call(f32[8,2304]{1,0:T(8,128)S(1)} %get-tuple-element.26.refs_0_, f32[8,2304]{1,0:T(8,128)S(1)} %collective-permute-done.1.refs_1_, f32[8,2304]{1,0:T(8,128)S(1)} %collective-permute-done.2.refs_2_, f32[8,2304]{1,0:T(8,128)S(1)} %collective-permute-done.3.refs_3_), custom_call_target="tpu_custom_call" | custom-call | flops 100000000 | bytes 4000000 | tf_op jit(solution)/shard_map/slot_places/pallas_call | solution.py:360
  19.7 0.3 collective-permute-done.6.refs_3_
  20.0 1.1 %collective-permute-done.4.refs_1_ = bf16[8,16,128]{2,1,0:T(8,128)(2,1)S(1)} collective-permute-done((bf16[8,16,128]{2,1,0:T(8,128)(2,1)S(1)}, bf16[8,16,128]{2,1,0:T(8,128)(2,1)S(1)}, u32[]{:S(2)}, u32[]{:S(2)}) %collective-permute-start.4) | collective-permute-done | bytes 32800 | tf_op jit(solution)/shard_map/ppermute | solution.py:702
  21.2 1.6 %slot_list.1 = (s32[1,1024]{1,0:T(1,128)S(1)}, bf16[16,256,128]{2,1,0:T(8,128)(2,1)S(1)}, bf16[16,256,128]{2,1,0:T(8,128)(2,1)S(1)}) custom-call(f32[64,32]{1,0:T(8,128)S(1)} %get-tuple-element.30.refs_4_.place_ref, f32[64,32]{1,0:T(8,128)S(1)} %get-tuple-element.31.value_ref, bf16[4,8,16,128]{3,2,1,0:T(8,128)(2,1)S(1)} %join.1.joined_ref.refs_0_, ...), custom_call_target="tpu_custom_call" | custom-call | flops 100000000 | bytes 4000000 | tf_op jit(solution)/shard_map/slot_list/pallas_call | solution.py:377
  22.8 9.9 %attend.1 = (f32[4,9,16,128]{3,2,1,0:T(8,128)S(1)}, f32[4,9,16,128]{3,2,1,0:T(8,128)S(1)}) custom-call(s32[1,1024]{1,0:T(1,128)S(1)} %get-tuple-element.33.list_vmem, s32[1,128]{1,0:T(1,128)S(1)} %get-tuple-element.34.bound_vmem, bf16[4,8,16,128]{3,2,1,0:T(8,128)(2,1)S(1)} %join.1.joined_ref.refs_0_, ...), custom_call_target="tpu_custom_call" | custom-call | tf_op jit(solution)/shard_map/attend/pallas_call | solution.py:567
  32.7 0.5 collective-permute-start.8
  33.3 1.2 %collective-permute-done.8.got_ref = f32[4,9,16,128]{3,2,1,0:T(8,128)S(1)} collective-permute-done((f32[4,9,16,128]{3,2,1,0:T(8,128)S(1)}, f32[4,9,16,128]{3,2,1,0:T(8,128)S(1)}, u32[]{:S(2)}, u32[]{:S(2)}) %collective-permute-start.8) | collective-permute-done | bytes 294944 | tf_op jit(solution)/shard_map/ppermute | solution.py:702
  34.5 0.3 merge_pair.1.refs_0_
  34.8 5.9 %collective-permute-start.11 = (bf16[4,9,16,128]{3,2,1,0:T(8,128)(2,1)S(1)}, bf16[4,9,16,128]{3,2,1,0:T(8,128)(2,1)S(1)}, u32[]{:S(2)}, u32[]{:S(2)}) collective-permute-start(bf16[4,9,16,128]{3,2,1,0:T(8,128)(2,1)S(1)} %merge_pair.1.refs_0_), channel_id=1, source_target_pairs={{0,6},{1,7},{2,4},{3,5},{4,2},{5,3},{6,0},{7,1},{8,14},{9,15},{10,... | collective-permute-start | bytes 442376 | tf_op jit(solution)/shard_map/ppermute | solution.py:702
  40.8 0.6 %collective-permute-start.9 = (bf16[4,9,16,128]{3,2,1,0:T(8,128)(2,1)S(1)}, bf16[4,9,16,128]{3,2,1,0:T(8,128)(2,1)S(1)}, u32[]{:S(2)}, u32[]{:S(2)}) collective-permute-start(bf16[4,9,16,128]{3,2,1,0:T(8,128)(2,1)S(1)} %merge_pair.1.refs_0_), channel_id=1, source_target_pairs={{0,2},{1,3},{2,0},{3,1},{4,6},{5,7},{6,4},{7,5},{8,10},{9,11},{10,... | collective-permute-start | bytes 442376 | tf_op jit(solution)/shard_map/ppermute | solution.py:702
  41.4 4.0 %collective-permute-done.11.refs_3_ = bf16[4,9,16,128]{3,2,1,0:T(8,128)(2,1)S(1)} collective-permute-done((bf16[4,9,16,128]{3,2,1,0:T(8,128)(2,1)S(1)}, bf16[4,9,16,128]{3,2,1,0:T(8,128)(2,1)S(1)}, u32[]{:S(2)}, u32[]{:S(2)}) %collective-permute-start.11) | collective-permute-done | bytes 147488 | tf_op jit(solution)/shard_map/ppermute | solution.py:702
  45.5 2.8 %collective-permute-done.10.refs_2_ = bf16[4,9,16,128]{3,2,1,0:T(8,128)(2,1)S(1)} collective-permute-done((bf16[4,9,16,128]{3,2,1,0:T(8,128)(2,1)S(1)}, bf16[4,9,16,128]{3,2,1,0:T(8,128)(2,1)S(1)}, u32[]{:S(2)}, u32[]{:S(2)}) %collective-permute-start.10) | collective-permute-done | bytes 147488 | tf_op jit(solution)/shard_map/ppermute | solution.py:702
  48.3 0.6 merge.1.refs_0_
  49.0 1.3 %collective-permute-done.12.refs_1_ = bf16[32,2048]{1,0:T(8,128)(2,1)S(1)} collective-permute-done((bf16[32,2048]{1,0:T(8,128)(2,1)S(1)}, bf16[32,2048]{1,0:T(8,128)(2,1)S(1)}, u32[]{:S(2)}, u32[]{:S(2)}) %collective-permute-start.12) | collective-permute-done | bytes 131104 | tf_op jit(solution)/shard_map/ppermute | solution.py:702
  50.3 0.6 project_out.1
  50.9 1.6 %collective-permute-start.13 = (bf16[16,640]{1,0:T(8,128)(2,1)S(1)}, bf16[16,640]{1,0:T(8,128)(2,1)S(1)}, u32[]{:S(2)}, u32[]{:S(2)}) collective-permute-start(bf16[16,640]{1,0:T(8,128)(2,1)S(1)} %get-tuple-element.40), channel_id=1, source_target_pairs={{0,8},{8,0},{16,24},{24,16},{1,9},{9,1},{17,25},{25,17},{2,10},{10... | collective-permute-start | bytes 61448 | tf_op jit(solution)/shard_map/ppermute | solution.py:702
  52.6 2.6 %collective-permute-start.14 = (bf16[16,640]{1,0:T(8,128)(2,1)S(1)}, bf16[16,640]{1,0:T(8,128)(2,1)S(1)}, u32[]{:S(2)}, u32[]{:S(2)}) collective-permute-start(bf16[16,640]{1,0:T(8,128)(2,1)S(1)} %get-tuple-element.41), channel_id=1, source_target_pairs={{0,16},{8,24},{16,0},{24,8},{1,17},{9,25},{17,1},{25,9},{2,18},{10... | collective-permute-start | bytes 61448 | tf_op jit(solution)/shard_map/ppermute | solution.py:702
  55.4 2.1 %collective-permute-done.14 = bf16[16,640]{1,0:T(8,128)(2,1)S(1)} collective-permute-done((bf16[16,640]{1,0:T(8,128)(2,1)S(1)}, bf16[16,640]{1,0:T(8,128)(2,1)S(1)}, u32[]{:S(2)}, u32[]{:S(2)}) %collective-permute-start.14) | collective-permute-done | bytes 20512 | tf_op jit(solution)/shard_map/ppermute | solution.py:702
  57.5 3.3 %collective-permute-done.15 = bf16[16,640]{1,0:T(8,128)(2,1)S(1)} collective-permute-done((bf16[16,640]{1,0:T(8,128)(2,1)S(1)}, bf16[16,640]{1,0:T(8,128)(2,1)S(1)}, u32[]{:S(2)}, u32[]{:S(2)}) %collective-permute-start.15) | collective-permute-done | bytes 20512 | tf_op jit(solution)/shard_map/ppermute | solution.py:702
  60.7 0.6 %add_convert_fusion = bf16[16,640]{1,0:T(8,128)(2,1)} fusion(bf16[16,640]{1,0:T(8,128)(2,1)S(1)} %collective-permute-done.15, bf16[16,640]{1,0:T(8,128)(2,1)S(1)} %collective-permute-done.14, f32[16,640]{1,0:T(8,128)S(1)} %get-tuple-element.39, bf16[16,640]{1,0:T(8,128)(2,1)S(1)} %collective-permute-done.13), kind=kLoop, calls=%fused_computation | loop fusion | flops 71680 | bytes 122880 | tf_op jit(solution)/shard_map/convert_element_type | solution.py:772
  (22 shorter events, 0.8 us)
Async XLA Ops:
  0.0 3.8 %copy-start.2 = (s32[8,32]{1,0:T(8,128)S(1)}, s32[8,32]{1,0:T(8,128)}, u32[]{:S(2)}) copy-start(s32[8,32]{1,0:T(8,128)} %length_hbm.1) | copy-start | bytes 3076
  0.0 14.7 %copy-start.1 = (f32[128]{0:T(128)S(1)}, f32[128]{0:T(128)}, u32[]{:S(2)}) copy-start(f32[128]{0:T(128)} %param.17) | copy-start | bytes 1540
  3.2 1.7 %collective-permute-start = (f32[4,8,2176]{2,1,0:T(8,128)S(1)}, f32[4,8,2176]{2,1,0:T(8,128)S(1)}, u32[]{:S(2)}, u32[]{:S(2)}) collective-permute-start(f32[4,8,2176]{2,1,0:T(8,128)S(1)} %get-tuple-element.25), channel_id=1, source_target_pairs={{0,1},{1,0},{2,3},{3,2},{4,5},{5,4},{6,7},{7,6},{8,9},{9,8},{10,11... | collective-permute-start | bytes 835592 | tf_op jit(solution)/shard_map/ppermute | solution.py:702
  5.0 5.5 %collective-permute-start.1 = (f32[8,2304]{1,0:T(8,128)S(1)}, f32[8,2304]{1,0:T(8,128)S(1)}, u32[]{:S(2)}, u32[]{:S(2)}) collective-permute-start(f32[8,2304]{1,0:T(8,128)S(1)} %get-tuple-element.27), channel_id=1, source_target_pairs={{0,2},{1,3},{2,0},{3,1},{4,6},{5,7},{6,4},{7,5},{8,10},{9,11},{10,... | collective-permute-start | bytes 221192 | tf_op jit(solution)/shard_map/ppermute | solution.py:702
  7.9 4.4 %collective-permute-start.2 = (f32[8,2304]{1,0:T(8,128)S(1)}, f32[8,2304]{1,0:T(8,128)S(1)}, u32[]{:S(2)}, u32[]{:S(2)}) collective-permute-start(f32[8,2304]{1,0:T(8,128)S(1)} %get-tuple-element.28), channel_id=1, source_target_pairs={{0,4},{1,5},{2,6},{3,7},{4,0},{5,1},{6,2},{7,3},{8,12},{9,13},{10,... | collective-permute-start | bytes 221192 | tf_op jit(solution)/shard_map/ppermute | solution.py:702
  9.4 5.3 %collective-permute-start.3 = (f32[8,2304]{1,0:T(8,128)S(1)}, f32[8,2304]{1,0:T(8,128)S(1)}, u32[]{:S(2)}, u32[]{:S(2)}) collective-permute-start(f32[8,2304]{1,0:T(8,128)S(1)} %get-tuple-element.29), channel_id=1, source_target_pairs={{0,6},{1,7},{2,4},{3,5},{4,2},{5,3},{6,0},{7,1},{8,14},{9,15},{10,... | collective-permute-start | bytes 221192 | tf_op jit(solution)/shard_map/ppermute | solution.py:702
  15.1 4.9 %collective-permute-start.6 = (bf16[8,16,128]{2,1,0:T(8,128)(2,1)S(1)}, bf16[8,16,128]{2,1,0:T(8,128)(2,1)S(1)}, u32[]{:S(2)}, u32[]{:S(2)}) collective-permute-start(bf16[8,16,128]{2,1,0:T(8,128)(2,1)S(1)} %queries.1.refs_0_), channel_id=1, source_target_pairs={{0,6},{1,7},{2,4},{3,5},{4,2},{5,3},{6,0},{7,1},{8,14},{9,15},{10,... | collective-permute-start | bytes 98312 | tf_op jit(solution)/shard_map/ppermute | solution.py:702
  15.7 4.3 %collective-permute-start.5 = (bf16[8,16,128]{2,1,0:T(8,128)(2,1)S(1)}, bf16[8,16,128]{2,1,0:T(8,128)(2,1)S(1)}, u32[]{:S(2)}, u32[]{:S(2)}) collective-permute-start(bf16[8,16,128]{2,1,0:T(8,128)(2,1)S(1)} %queries.1.refs_0_), channel_id=1, source_target_pairs={{0,4},{1,5},{2,6},{3,7},{4,0},{5,1},{6,2},{7,3},{8,12},{9,13},{10,... | collective-permute-start | bytes 98312 | tf_op jit(solution)/shard_map/ppermute | solution.py:702
  17.2 3.9 %collective-permute-start.4 = (bf16[8,16,128]{2,1,0:T(8,128)(2,1)S(1)}, bf16[8,16,128]{2,1,0:T(8,128)(2,1)S(1)}, u32[]{:S(2)}, u32[]{:S(2)}) collective-permute-start(bf16[8,16,128]{2,1,0:T(8,128)(2,1)S(1)} %queries.1.refs_0_), channel_id=1, source_target_pairs={{0,2},{1,3},{2,0},{3,1},{4,6},{5,7},{6,4},{7,5},{8,10},{9,11},{10,... | collective-permute-start | bytes 98312 | tf_op jit(solution)/shard_map/ppermute | solution.py:702
  21.1 1.7 %collective-permute-start.7 = (bf16[4,8,16,128]{3,2,1,0:T(8,128)(2,1)S(1)}, bf16[4,8,16,128]{3,2,1,0:T(8,128)(2,1)S(1)}, u32[]{:S(2)}, u32[]{:S(2)}) collective-permute-start(bf16[4,8,16,128]{3,2,1,0:T(8,128)(2,1)S(1)} %join.1.joined_ref.refs_0_), channel_id=1, source_target_pairs={{0,1},{1,0},{2,3},{3,2},{4,5},{5,4},{6,7},{7,6},{8,9},{9,8},{10,11... | collective-permute-start | bytes 393224 | tf_op jit(solution)/shard_map/ppermute | solution.py:702
  22.8 27.5 %copy-start = (bf16[2048,640]{1,0:T(8,128)(2,1)S(1)}, bf16[2048,640]{1,0:T(8,128)(2,1)}, u32[]{:S(2)}) copy-start(bf16[2048,640]{1,0:T(8,128)(2,1)} %refs_2_.1) | copy-start | bytes 7864324
  32.7 1.8 %collective-permute-start.8 = (f32[4,9,16,128]{3,2,1,0:T(8,128)S(1)}, f32[4,9,16,128]{3,2,1,0:T(8,128)S(1)}, u32[]{:S(2)}, u32[]{:S(2)}) collective-permute-start(f32[4,9,16,128]{3,2,1,0:T(8,128)S(1)} %get-tuple-element.38), channel_id=1, source_target_pairs={{0,1},{1,0},{2,3},{3,2},{4,5},{5,4},{6,7},{7,6},{8,9},{9,8},{10,11... | collective-permute-start | bytes 884744 | tf_op jit(solution)/shard_map/ppermute | solution.py:702
  34.8 10.6 %collective-permute-start.11 = (bf16[4,9,16,128]{3,2,1,0:T(8,128)(2,1)S(1)}, bf16[4,9,16,128]{3,2,1,0:T(8,128)(2,1)S(1)}, u32[]{:S(2)}, u32[]{:S(2)}) collective-permute-start(bf16[4,9,16,128]{3,2,1,0:T(8,128)(2,1)S(1)} %merge_pair.1.refs_0_), channel_id=1, source_target_pairs={{0,6},{1,7},{2,4},{3,5},{4,2},{5,3},{6,0},{7,1},{8,14},{9,15},{10,... | collective-permute-start | bytes 442376 | tf_op jit(solution)/shard_map/ppermute | solution.py:702
  40.8 7.5 %collective-permute-start.10 = (bf16[4,9,16,128]{3,2,1,0:T(8,128)(2,1)S(1)}, bf16[4,9,16,128]{3,2,1,0:T(8,128)(2,1)S(1)}, u32[]{:S(2)}, u32[]{:S(2)}) collective-permute-start(bf16[4,9,16,128]{3,2,1,0:T(8,128)(2,1)S(1)} %merge_pair.1.refs_0_), channel_id=1, source_target_pairs={{0,4},{1,5},{2,6},{3,7},{4,0},{5,1},{6,2},{7,3},{8,12},{9,13},{10,... | collective-permute-start | bytes 442376 | tf_op jit(solution)/shard_map/ppermute | solution.py:702
  40.8 7.5 %collective-permute-start.9 = (bf16[4,9,16,128]{3,2,1,0:T(8,128)(2,1)S(1)}, bf16[4,9,16,128]{3,2,1,0:T(8,128)(2,1)S(1)}, u32[]{:S(2)}, u32[]{:S(2)}) collective-permute-start(bf16[4,9,16,128]{3,2,1,0:T(8,128)(2,1)S(1)} %merge_pair.1.refs_0_), channel_id=1, source_target_pairs={{0,2},{1,3},{2,0},{3,1},{4,6},{5,7},{6,4},{7,5},{8,10},{9,11},{10,... | collective-permute-start | bytes 442376 | tf_op jit(solution)/shard_map/ppermute | solution.py:702
  48.9 1.4 %collective-permute-start.12 = (bf16[32,2048]{1,0:T(8,128)(2,1)S(1)}, bf16[32,2048]{1,0:T(8,128)(2,1)S(1)}, u32[]{:S(2)}, u32[]{:S(2)}) collective-permute-start(bf16[32,2048]{1,0:T(8,128)(2,1)S(1)} %merge.1.refs_0_), channel_id=1, source_target_pairs={{0,1},{1,0},{2,3},{3,2},{4,5},{5,4},{6,7},{7,6},{8,9},{9,8},{10,11... | collective-permute-start | bytes 393224 | tf_op jit(solution)/shard_map/ppermute | solution.py:702
  50.9 4.5 %collective-permute-start.13 = (bf16[16,640]{1,0:T(8,128)(2,1)S(1)}, bf16[16,640]{1,0:T(8,128)(2,1)S(1)}, u32[]{:S(2)}, u32[]{:S(2)}) collective-permute-start(bf16[16,640]{1,0:T(8,128)(2,1)S(1)} %get-tuple-element.40), channel_id=1, source_target_pairs={{0,8},{8,0},{16,24},{24,16},{1,9},{9,1},{17,25},{25,17},{2,10},{10... | collective-permute-start | bytes 61448 | tf_op jit(solution)/shard_map/ppermute | solution.py:702
  52.6 4.9 %collective-permute-start.14 = (bf16[16,640]{1,0:T(8,128)(2,1)S(1)}, bf16[16,640]{1,0:T(8,128)(2,1)S(1)}, u32[]{:S(2)}, u32[]{:S(2)}) collective-permute-start(bf16[16,640]{1,0:T(8,128)(2,1)S(1)} %get-tuple-element.41), channel_id=1, source_target_pairs={{0,16},{8,24},{16,0},{24,8},{1,17},{9,25},{17,1},{25,9},{2,18},{10... | collective-permute-start | bytes 61448 | tf_op jit(solution)/shard_map/ppermute | solution.py:702
  55.2 5.6 %collective-permute-start.15 = (bf16[16,640]{1,0:T(8,128)(2,1)S(1)}, bf16[16,640]{1,0:T(8,128)(2,1)S(1)}, u32[]{:S(2)}, u32[]{:S(2)}) collective-permute-start(bf16[16,640]{1,0:T(8,128)(2,1)S(1)} %get-tuple-element.42), channel_id=1, source_target_pairs={{0,24},{8,16},{16,8},{24,0},{1,25},{9,17},{17,9},{25,1},{2,26},{10... | collective-permute-start | bytes 61448 | tf_op jit(solution)/shard_map/ppermute | solution.py:702

commit v12 on v11

--- a/solution.py
+++ b/solution.py
@@ -16,7 +16,7 @@
 COLUMN_TILE = 256
 PAIR = 2
 GROUP = 4
-TASKS = 8
+TASKS = 16
 CHUNK = GROUP * TASKS
 SETS = 2
 PHASES = 8
@@ -662,18 +662,18 @@
     )(*pieces)
 
 
-def output_kernel(own, *refs):
-    pieces, weight_ref = refs[:PAIR], refs[PAIR]
-    outs, (rows_ref, terms_ref) = refs[PAIR + 1 : -2], refs[-2:]
+def own_output_kernel(piece_ref, weight_ref, out_ref):
+    out_ref[...] = jnp.dot(piece_ref[...], weight_ref[...], preferred_element_type=jnp.float32)
+
+
+def output_kernel(own, done_ref, piece_ref, weight_ref, *refs):
+    outs, terms_ref = refs[:-1], refs[-1]
     me = lax.axis_index("kv")
-    for t in range(PAIR):
-        piece = pieces[t][...].astype(jnp.float32)
-        for s in range(piece.shape[0] // own):
+    products = (done_ref[...], jnp.dot(piece_ref[...], weight_ref[...], preferred_element_type=jnp.float32))
+    for t, product in enumerate(products):
+        for s in range(product.shape[0] // own):
             start = pl.multiple_of(jnp.bitwise_xor(me, PAIR * s + t) * own, own)
-            rows_ref[pl.ds(start, own), :] = piece[s * own : (s + 1) * own]
-    terms_ref[...] = jnp.dot(
-        rows_ref[...].astype(jnp.bfloat16), weight_ref[...], preferred_element_type=jnp.float32
-    )
+            terms_ref[pl.ds(start, own), :] = product[s * own : (s + 1) * own]
     me = lax.axis_index("row")
     part = outs[0].shape[0]
     for s, ref in enumerate(outs):
@@ -681,20 +681,36 @@
         ref[...] = terms_ref[pl.ds(start, part), :].astype(ref.dtype)
 
 
-def project_out(pieces, weight, own, row_count):
-    half, width = pieces[0].shape
-    rows, columns = PAIR * half, weight.shape[1]
+def project_own(piece, weight):
+    half, width = piece.shape
+    columns = weight.shape[1]
+    return pl.pallas_call(
+        own_output_kernel,
+        in_specs=[vmem_spec()] * 2,
+        out_specs=vmem_spec(),
+        out_shape=jax.ShapeDtypeStruct((half, columns), jnp.float32),
+        compiler_params=params(16),
+        cost_estimate=pl.CostEstimate(
+            flops=2 * half * width * columns, bytes_accessed=2 * width * columns, transcendentals=0
+        ),
+        name="project_own",
+    )(piece, weight)
+
+
+def project_out(done, piece, weight, own, row_count):
+    half, columns = done.shape
+    rows = PAIR * half
     shape = (rows // row_count, columns)
     send = jax.ShapeDtypeStruct(shape, jnp.bfloat16)
     return pl.pallas_call(
         functools.partial(output_kernel, own),
-        in_specs=[vmem_spec()] * (PAIR + 1),
+        in_specs=[vmem_spec()] * 3,
         out_specs=[vmem_spec()] * row_count,
         out_shape=[jax.ShapeDtypeStruct(shape, jnp.float32)] + [send] * (row_count - 1),
-        scratch_shapes=[pltpu.VMEM((rows, width), jnp.float32), pltpu.VMEM((rows, columns), jnp.float32)],
-        compiler_params=params(24),
+        scratch_shapes=[pltpu.VMEM((rows, columns), jnp.float32)],
+        compiler_params=params(16),
         name="project_out",
-    )(*pieces, weight)
+    )(done, piece, weight)
 
 
 def exchange(x, axis, s):
@@ -765,7 +781,8 @@
     keep, send = attend(items, bounds, queries, first, keys, values, kv_local, scale)
     merged = merge_pair(keep, exchange(send, "kv", 1), scale)
     attention = merge(gather_chips(merged), scale)
-    terms = project_out([attention, exchange(attention, "kv", 1)], output_weight, own, row_count)
+    done = project_own(attention, output_weight)
+    terms = project_out(done, exchange(attention, "kv", 1), output_weight, own, row_count)
     total = terms[0]
     for s in range(1, row_count):
         total = total + exchange(terms[s], "row", s).astype(jnp.float32)

time: 61.7 us -> 60.1 us (0.974)
  starting transfers between devices: 20.3 us -> 18.6 us
  Pallas kernels: 17.7 us -> 18.5 us
  waiting for transfers between devices: 22.3 us -> 21.5 us
    ppermute x16, starting transfers between devices: 20.3 us -> 18.6 us  [exchange(): return lax.ppermute(x, axis, [(i, i ^ s) for i in range(count)])]
    ppermute x16, waiting for transfers between devices: 22.3 us -> 21.5 us  [exchange(): return lax.ppermute(x, axis, [(i, i ^ s) for i in range(count)])]
  transfers between devices with their start and end apart: 16 -> 16, of which waited for: 12 -> 12; matrix products, arithmetic and copies ran while one was open for 1% -> 1% of each run, Pallas kernels for 4% -> 5%
where the time goes in v12:
time: 60.1 us; the launch traced here: 59.7 us
  waiting for transfers between devices  21.5 us (36%)
  starting transfers between devices  18.6 us (31%)
  Pallas kernels  18.5 us (31%)
  other arithmetic  0.95 us (2%)
    ppermute x16, waiting for transfers between devices, exchange(): return lax.ppermute(x, axis, [(i, i ^ s) for i in range(count)])  21.5 us
    ppermute x16, starting transfers between devices, exchange(): return lax.ppermute(x, axis, [(i, i ^ s) for i in range(count)])  18.6 us
    pallas_call x1, Pallas kernels, attend(): pl.pallas_call(functools.partial(attend_kernel, scale, kv_local, count),...  10.2 us
    pallas_call x1, Pallas kernels, project(): pl.pallas_call(functools.partial(project_kernel, rank), in_specs=[hbm_spe...  3.23 us
    pallas_call x1, Pallas kernels, make_list(): pl.pallas_call(functools.partial(list_kernel, float(rows * blocks * block...  1.56 us
  transfers between devices with their start and end apart: 16, of which 12 were waited for; matrix products, arithmetic and copies ran while one was open for 1% of the time, Pallas kernels for 5%

profile of v12, /device:TPU:0, one launch (start us, length us, event | category | flops | bytes accessed | tf_op | source)
XLA Modules:
  0.0 59.7 jit_solution(695830463167055221)
XLA Ops:
  0.0 3.2 %project.1 = (f32[4,8,2176]{2,1,0:T(8,128)S(1)}, f32[4,8,2176]{2,1,0:T(8,128)S(1)}, f32[8,16,2048]{2,1,0:T(8,128)S(1)}) custom-call(s32[64]{0:T(128)} %tenant_hbm.1, s32[64]{0:T(128)} %adapter_hbm.1, s32[1,64]{1,0:T(1,128)} %bitcast.14, s32[1,64]{1,0:T(1,128)} %bitcast.15, s32[8,32]{1,0:T(8,128)} %holder_hbm.1, s32[8,32]{1,0:T(8,128)} %block_hbm.1, ...), custom_call_target="tpu_custom_call" | custom-call | tf_op jit(solution)/shard_map/project/pallas_call | solution.py:186
  3.2 0.5 collective-permute-start
  4.0 0.9 %collective-permute-done.got_ref = f32[4,8,2176]{2,1,0:T(8,128)S(1)} collective-permute-done((f32[4,8,2176]{2,1,0:T(8,128)S(1)}, f32[4,8,2176]{2,1,0:T(8,128)S(1)}, u32[]{:S(2)}, u32[]{:S(2)}) %collective-permute-start) | collective-permute-done | bytes 278560 | tf_op jit(solution)/shard_map/ppermute | solution.py:718
  5.0 2.9 %collective-permute-start.1 = (f32[8,2304]{1,0:T(8,128)S(1)}, f32[8,2304]{1,0:T(8,128)S(1)}, u32[]{:S(2)}, u32[]{:S(2)}) collective-permute-start(f32[8,2304]{1,0:T(8,128)S(1)} %get-tuple-element.27), channel_id=1, source_target_pairs={{0,2},{1,3},{2,0},{3,1},{4,6},{5,7},{6,4},{7,5},{8,10},{9,11},{10,... | collective-permute-start | bytes 221192 | tf_op jit(solution)/shard_map/ppermute | solution.py:718
  7.9 1.5 %collective-permute-start.2 = (f32[8,2304]{1,0:T(8,128)S(1)}, f32[8,2304]{1,0:T(8,128)S(1)}, u32[]{:S(2)}, u32[]{:S(2)}) collective-permute-start(f32[8,2304]{1,0:T(8,128)S(1)} %get-tuple-element.28), channel_id=1, source_target_pairs={{0,4},{1,5},{2,6},{3,7},{4,0},{5,1},{6,2},{7,3},{8,12},{9,13},{10,... | collective-permute-start | bytes 221192 | tf_op jit(solution)/shard_map/ppermute | solution.py:718
  9.5 1.0 %collective-permute-done.1.refs_1_ = f32[8,2304]{1,0:T(8,128)S(1)} collective-permute-done((f32[8,2304]{1,0:T(8,128)S(1)}, f32[8,2304]{1,0:T(8,128)S(1)}, u32[]{:S(2)}, u32[]{:S(2)}) %collective-permute-start.1) | collective-permute-done | bytes 73760 | tf_op jit(solution)/shard_map/ppermute | solution.py:718
  10.5 1.8 %collective-permute-done.2.refs_2_ = f32[8,2304]{1,0:T(8,128)S(1)} collective-permute-done((f32[8,2304]{1,0:T(8,128)S(1)}, f32[8,2304]{1,0:T(8,128)S(1)}, u32[]{:S(2)}, u32[]{:S(2)}) %collective-permute-start.2) | collective-permute-done | bytes 73760 | tf_op jit(solution)/shard_map/ppermute | solution.py:718
  12.3 2.4 %collective-permute-done.3.refs_3_ = f32[8,2304]{1,0:T(8,128)S(1)} collective-permute-done((f32[8,2304]{1,0:T(8,128)S(1)}, f32[8,2304]{1,0:T(8,128)S(1)}, u32[]{:S(2)}, u32[]{:S(2)}) %collective-permute-start.3) | collective-permute-done | bytes 73760 | tf_op jit(solution)/shard_map/ppermute | solution.py:718
  14.7 0.4 queries.1.refs_0_
  15.1 0.6 collective-permute-start.6
  15.7 1.5 %collective-permute-start.5 = (bf16[8,16,128]{2,1,0:T(8,128)(2,1)S(1)}, bf16[8,16,128]{2,1,0:T(8,128)(2,1)S(1)}, u32[]{:S(2)}, u32[]{:S(2)}) collective-permute-start(bf16[8,16,128]{2,1,0:T(8,128)(2,1)S(1)} %queries.1.refs_0_), channel_id=1, source_target_pairs={{0,4},{1,5},{2,6},{3,7},{4,0},{5,1},{6,2},{7,3},{8,12},{9,13},{10,... | collective-permute-start | bytes 98312 | tf_op jit(solution)/shard_map/ppermute | solution.py:718
  17.2 1.5 %collective-permute-start.4 = (bf16[8,16,128]{2,1,0:T(8,128)(2,1)S(1)}, bf16[8,16,128]{2,1,0:T(8,128)(2,1)S(1)}, u32[]{:S(2)}, u32[]{:S(2)}) collective-permute-start(bf16[8,16,128]{2,1,0:T(8,128)(2,1)S(1)} %queries.1.refs_0_), channel_id=1, source_target_pairs={{0,2},{1,3},{2,0},{3,1},{4,6},{5,7},{6,4},{7,5},{8,10},{9,11},{10,... | collective-permute-start | bytes 98312 | tf_op jit(solution)/shard_map/ppermute | solution.py:718
  18.7 1.0 %slot_places.1 = (f32[64,32]{1,0:T(8,128)S(1)}, f32[64,32]{1,0:T(8,128)S(1)}, s32[1,128]{1,0:T(1,128)S(1)}) custom-call(f32[8,2304]{1,0:T(8,128)S(1)} %get-tuple-element.26.refs_0_, f32[8,2304]{1,0:T(8,128)S(1)} %collective-permute-done.1.refs_1_, f32[8,2304]{1,0:T(8,128)S(1)} %collective-permute-done.2.refs_2_, f32[8,2304]{1,0:T(8,128)S(1)} %collective-permute-done.3.refs_3_), custom_call_target="tpu_custom_call" | custom-call | flops 100000000 | bytes 4000000 | tf_op jit(solution)/shard_map/slot_places/pallas_call | solution.py:360
  20.0 1.1 %collective-permute-done.4.refs_1_ = bf16[8,16,128]{2,1,0:T(8,128)(2,1)S(1)} collective-permute-done((bf16[8,16,128]{2,1,0:T(8,128)(2,1)S(1)}, bf16[8,16,128]{2,1,0:T(8,128)(2,1)S(1)}, u32[]{:S(2)}, u32[]{:S(2)}) %collective-permute-start.4) | collective-permute-done | bytes 32800 | tf_op jit(solution)/shard_map/ppermute | solution.py:718
  21.2 1.6 %slot_list.1 = (s32[1,1152]{1,0:T(1,128)S(1)}, bf16[16,256,128]{2,1,0:T(8,128)(2,1)S(1)}, bf16[16,256,128]{2,1,0:T(8,128)(2,1)S(1)}) custom-call(f32[64,32]{1,0:T(8,128)S(1)} %get-tuple-element.30.refs_4_.place_ref, f32[64,32]{1,0:T(8,128)S(1)} %get-tuple-element.31.value_ref, bf16[4,8,16,128]{3,2,1,0:T(8,128)(2,1)S(1)} %join.1.joined_ref.refs_0_, ...), custom_call_target="tpu_custom_call" | custom-call | flops 100000000 | bytes 4000000 | tf_op jit(solution)/shard_map/slot_list/pallas_call | solution.py:377
  22.8 10.2 %attend.1 = (f32[4,9,16,128]{3,2,1,0:T(8,128)S(1)}, f32[4,9,16,128]{3,2,1,0:T(8,128)S(1)}) custom-call(s32[1,1152]{1,0:T(1,128)S(1)} %get-tuple-element.33.list_vmem, s32[1,128]{1,0:T(1,128)S(1)} %get-tuple-element.34.bound_vmem, bf16[4,8,16,128]{3,2,1,0:T(8,128)(2,1)S(1)} %join.1.joined_ref.refs_0_, ...), custom_call_target="tpu_custom_call" | custom-call | tf_op jit(solution)/shard_map/attend/pallas_call | solution.py:567
  33.0 0.6 collective-permute-start.8
  33.6 1.2 %collective-permute-done.8.got_ref = f32[4,9,16,128]{3,2,1,0:T(8,128)S(1)} collective-permute-done((f32[4,9,16,128]{3,2,1,0:T(8,128)S(1)}, f32[4,9,16,128]{3,2,1,0:T(8,128)S(1)}, u32[]{:S(2)}, u32[]{:S(2)}) %collective-permute-start.8) | collective-permute-done | bytes 294944 | tf_op jit(solution)/shard_map/ppermute | solution.py:718
  34.8 0.3 merge_pair.1.refs_0_
  35.1 4.2 %collective-permute-start.11 = (bf16[4,9,16,128]{3,2,1,0:T(8,128)(2,1)S(1)}, bf16[4,9,16,128]{3,2,1,0:T(8,128)(2,1)S(1)}, u32[]{:S(2)}, u32[]{:S(2)}) collective-permute-start(bf16[4,9,16,128]{3,2,1,0:T(8,128)(2,1)S(1)} %merge_pair.1.refs_0_), channel_id=1, source_target_pairs={{0,6},{1,7},{2,4},{3,5},{4,2},{5,3},{6,0},{7,1},{8,14},{9,15},{10,... | collective-permute-start | bytes 442376 | tf_op jit(solution)/shard_map/ppermute | solution.py:718
  39.4 0.6 %collective-permute-start.9 = (bf16[4,9,16,128]{3,2,1,0:T(8,128)(2,1)S(1)}, bf16[4,9,16,128]{3,2,1,0:T(8,128)(2,1)S(1)}, u32[]{:S(2)}, u32[]{:S(2)}) collective-permute-start(bf16[4,9,16,128]{3,2,1,0:T(8,128)(2,1)S(1)} %merge_pair.1.refs_0_), channel_id=1, source_target_pairs={{0,2},{1,3},{2,0},{3,1},{4,6},{5,7},{6,4},{7,5},{8,10},{9,11},{10,... | collective-permute-start | bytes 442376 | tf_op jit(solution)/shard_map/ppermute | solution.py:718
  40.0 4.0 %collective-permute-done.11.refs_3_ = bf16[4,9,16,128]{3,2,1,0:T(8,128)(2,1)S(1)} collective-permute-done((bf16[4,9,16,128]{3,2,1,0:T(8,128)(2,1)S(1)}, bf16[4,9,16,128]{3,2,1,0:T(8,128)(2,1)S(1)}, u32[]{:S(2)}, u32[]{:S(2)}) %collective-permute-start.11) | collective-permute-done | bytes 147488 | tf_op jit(solution)/shard_map/ppermute | solution.py:718
  44.0 2.7 %collective-permute-done.10.refs_2_ = bf16[4,9,16,128]{3,2,1,0:T(8,128)(2,1)S(1)} collective-permute-done((bf16[4,9,16,128]{3,2,1,0:T(8,128)(2,1)S(1)}, bf16[4,9,16,128]{3,2,1,0:T(8,128)(2,1)S(1)}, u32[]{:S(2)}, u32[]{:S(2)}) %collective-permute-start.10) | collective-permute-done | bytes 147488 | tf_op jit(solution)/shard_map/ppermute | solution.py:718
  46.7 0.6 merge.1.piece_ref
  47.3 0.5 project_own.1.done_ref
  47.9 0.8 %collective-permute-done.12.piece_ref = bf16[32,2048]{1,0:T(8,128)(2,1)S(1)} collective-permute-done((bf16[32,2048]{1,0:T(8,128)(2,1)S(1)}, bf16[32,2048]{1,0:T(8,128)(2,1)S(1)}, u32[]{:S(2)}, u32[]{:S(2)}) %collective-permute-start.12) | collective-permute-done | bytes 131104 | tf_op jit(solution)/shard_map/ppermute | solution.py:718
  48.7 0.6 project_out.1
  49.2 1.6 %collective-permute-start.13 = (bf16[16,640]{1,0:T(8,128)(2,1)S(1)}, bf16[16,640]{1,0:T(8,128)(2,1)S(1)}, u32[]{:S(2)}, u32[]{:S(2)}) collective-permute-start(bf16[16,640]{1,0:T(8,128)(2,1)S(1)} %get-tuple-element.40), channel_id=1, source_target_pairs={{0,8},{8,0},{16,24},{24,16},{1,9},{9,1},{17,25},{25,17},{2,10},{10... | collective-permute-start | bytes 61448 | tf_op jit(solution)/shard_map/ppermute | solution.py:718
  50.9 2.6 %collective-permute-start.14 = (bf16[16,640]{1,0:T(8,128)(2,1)S(1)}, bf16[16,640]{1,0:T(8,128)(2,1)S(1)}, u32[]{:S(2)}, u32[]{:S(2)}) collective-permute-start(bf16[16,640]{1,0:T(8,128)(2,1)S(1)} %get-tuple-element.41), channel_id=1, source_target_pairs={{0,16},{8,24},{16,0},{24,8},{1,17},{9,25},{17,1},{25,9},{2,18},{10... | collective-permute-start | bytes 61448 | tf_op jit(solution)/shard_map/ppermute | solution.py:718
  53.7 2.1 %collective-permute-done.14 = bf16[16,640]{1,0:T(8,128)(2,1)S(1)} collective-permute-done((bf16[16,640]{1,0:T(8,128)(2,1)S(1)}, bf16[16,640]{1,0:T(8,128)(2,1)S(1)}, u32[]{:S(2)}, u32[]{:S(2)}) %collective-permute-start.14) | collective-permute-done | bytes 20512 | tf_op jit(solution)/shard_map/ppermute | solution.py:718
  55.8 3.2 %collective-permute-done.15 = bf16[16,640]{1,0:T(8,128)(2,1)S(1)} collective-permute-done((bf16[16,640]{1,0:T(8,128)(2,1)S(1)}, bf16[16,640]{1,0:T(8,128)(2,1)S(1)}, u32[]{:S(2)}, u32[]{:S(2)}) %collective-permute-start.15) | collective-permute-done | bytes 20512 | tf_op jit(solution)/shard_map/ppermute | solution.py:718
  59.0 0.6 %add_convert_fusion = bf16[16,640]{1,0:T(8,128)(2,1)} fusion(bf16[16,640]{1,0:T(8,128)(2,1)S(1)} %collective-permute-done.15, bf16[16,640]{1,0:T(8,128)(2,1)S(1)} %collective-permute-done.14, f32[16,640]{1,0:T(8,128)S(1)} %get-tuple-element.39, bf16[16,640]{1,0:T(8,128)(2,1)S(1)} %collective-permute-done.13), kind=kLoop, calls=%fused_computation | loop fusion | flops 71680 | bytes 122880 | tf_op jit(solution)/shard_map/convert_element_type | solution.py:789
  (23 shorter events, 1.1 us)
Async XLA Ops:
  0.0 3.8 %copy-start.2 = (s32[8,32]{1,0:T(8,128)S(1)}, s32[8,32]{1,0:T(8,128)}, u32[]{:S(2)}) copy-start(s32[8,32]{1,0:T(8,128)} %length_hbm.1) | copy-start | bytes 3076
  0.0 14.7 %copy-start.1 = (f32[128]{0:T(128)S(1)}, f32[128]{0:T(128)}, u32[]{:S(2)}) copy-start(f32[128]{0:T(128)} %param.17) | copy-start | bytes 1540
  3.2 1.7 %collective-permute-start = (f32[4,8,2176]{2,1,0:T(8,128)S(1)}, f32[4,8,2176]{2,1,0:T(8,128)S(1)}, u32[]{:S(2)}, u32[]{:S(2)}) collective-permute-start(f32[4,8,2176]{2,1,0:T(8,128)S(1)} %get-tuple-element.25), channel_id=1, source_target_pairs={{0,1},{1,0},{2,3},{3,2},{4,5},{5,4},{6,7},{7,6},{8,9},{9,8},{10,11... | collective-permute-start | bytes 835592 | tf_op jit(solution)/shard_map/ppermute | solution.py:718
  5.0 5.5 %collective-permute-start.1 = (f32[8,2304]{1,0:T(8,128)S(1)}, f32[8,2304]{1,0:T(8,128)S(1)}, u32[]{:S(2)}, u32[]{:S(2)}) collective-permute-start(f32[8,2304]{1,0:T(8,128)S(1)} %get-tuple-element.27), channel_id=1, source_target_pairs={{0,2},{1,3},{2,0},{3,1},{4,6},{5,7},{6,4},{7,5},{8,10},{9,11},{10,... | collective-permute-start | bytes 221192 | tf_op jit(solution)/shard_map/ppermute | solution.py:718
  7.9 4.4 %collective-permute-start.2 = (f32[8,2304]{1,0:T(8,128)S(1)}, f32[8,2304]{1,0:T(8,128)S(1)}, u32[]{:S(2)}, u32[]{:S(2)}) collective-permute-start(f32[8,2304]{1,0:T(8,128)S(1)} %get-tuple-element.28), channel_id=1, source_target_pairs={{0,4},{1,5},{2,6},{3,7},{4,0},{5,1},{6,2},{7,3},{8,12},{9,13},{10,... | collective-permute-start | bytes 221192 | tf_op jit(solution)/shard_map/ppermute | solution.py:718
  9.4 5.3 %collective-permute-start.3 = (f32[8,2304]{1,0:T(8,128)S(1)}, f32[8,2304]{1,0:T(8,128)S(1)}, u32[]{:S(2)}, u32[]{:S(2)}) collective-permute-start(f32[8,2304]{1,0:T(8,128)S(1)} %get-tuple-element.29), channel_id=1, source_target_pairs={{0,6},{1,7},{2,4},{3,5},{4,2},{5,3},{6,0},{7,1},{8,14},{9,15},{10,... | collective-permute-start | bytes 221192 | tf_op jit(solution)/shard_map/ppermute | solution.py:718
  15.1 4.9 %collective-permute-start.6 = (bf16[8,16,128]{2,1,0:T(8,128)(2,1)S(1)}, bf16[8,16,128]{2,1,0:T(8,128)(2,1)S(1)}, u32[]{:S(2)}, u32[]{:S(2)}) collective-permute-start(bf16[8,16,128]{2,1,0:T(8,128)(2,1)S(1)} %queries.1.refs_0_), channel_id=1, source_target_pairs={{0,6},{1,7},{2,4},{3,5},{4,2},{5,3},{6,0},{7,1},{8,14},{9,15},{10,... | collective-permute-start | bytes 98312 | tf_op jit(solution)/shard_map/ppermute | solution.py:718
  15.7 4.3 %collective-permute-start.5 = (bf16[8,16,128]{2,1,0:T(8,128)(2,1)S(1)}, bf16[8,16,128]{2,1,0:T(8,128)(2,1)S(1)}, u32[]{:S(2)}, u32[]{:S(2)}) collective-permute-start(bf16[8,16,128]{2,1,0:T(8,128)(2,1)S(1)} %queries.1.refs_0_), channel_id=1, source_target_pairs={{0,4},{1,5},{2,6},{3,7},{4,0},{5,1},{6,2},{7,3},{8,12},{9,13},{10,... | collective-permute-start | bytes 98312 | tf_op jit(solution)/shard_map/ppermute | solution.py:718
  17.2 3.9 %collective-permute-start.4 = (bf16[8,16,128]{2,1,0:T(8,128)(2,1)S(1)}, bf16[8,16,128]{2,1,0:T(8,128)(2,1)S(1)}, u32[]{:S(2)}, u32[]{:S(2)}) collective-permute-start(bf16[8,16,128]{2,1,0:T(8,128)(2,1)S(1)} %queries.1.refs_0_), channel_id=1, source_target_pairs={{0,2},{1,3},{2,0},{3,1},{4,6},{5,7},{6,4},{7,5},{8,10},{9,11},{10,... | collective-permute-start | bytes 98312 | tf_op jit(solution)/shard_map/ppermute | solution.py:718
  21.1 1.7 %collective-permute-start.7 = (bf16[4,8,16,128]{3,2,1,0:T(8,128)(2,1)S(1)}, bf16[4,8,16,128]{3,2,1,0:T(8,128)(2,1)S(1)}, u32[]{:S(2)}, u32[]{:S(2)}) collective-permute-start(bf16[4,8,16,128]{3,2,1,0:T(8,128)(2,1)S(1)} %join.1.joined_ref.refs_0_), channel_id=1, source_target_pairs={{0,1},{1,0},{2,3},{3,2},{4,5},{5,4},{6,7},{7,6},{8,9},{9,8},{10,11... | collective-permute-start | bytes 393224 | tf_op jit(solution)/shard_map/ppermute | solution.py:718
  22.8 24.6 %copy-start = (bf16[2048,640]{1,0:T(8,128)(2,1)S(1)}, bf16[2048,640]{1,0:T(8,128)(2,1)}, u32[]{:S(2)}) copy-start(bf16[2048,640]{1,0:T(8,128)(2,1)} %weight_ref.3) | copy-start | bytes 7864324
  33.0 1.8 %collective-permute-start.8 = (f32[4,9,16,128]{3,2,1,0:T(8,128)S(1)}, f32[4,9,16,128]{3,2,1,0:T(8,128)S(1)}, u32[]{:S(2)}, u32[]{:S(2)}) collective-permute-start(f32[4,9,16,128]{3,2,1,0:T(8,128)S(1)} %get-tuple-element.38), channel_id=1, source_target_pairs={{0,1},{1,0},{2,3},{3,2},{4,5},{5,4},{6,7},{7,6},{8,9},{9,8},{10,11... | collective-permute-start | bytes 884744 | tf_op jit(solution)/shard_map/ppermute | solution.py:718
  35.1 8.8 %collective-permute-start.11 = (bf16[4,9,16,128]{3,2,1,0:T(8,128)(2,1)S(1)}, bf16[4,9,16,128]{3,2,1,0:T(8,128)(2,1)S(1)}, u32[]{:S(2)}, u32[]{:S(2)}) collective-permute-start(bf16[4,9,16,128]{3,2,1,0:T(8,128)(2,1)S(1)} %merge_pair.1.refs_0_), channel_id=1, source_target_pairs={{0,6},{1,7},{2,4},{3,5},{4,2},{5,3},{6,0},{7,1},{8,14},{9,15},{10,... | collective-permute-start | bytes 442376 | tf_op jit(solution)/shard_map/ppermute | solution.py:718
  39.4 7.3 %collective-permute-start.10 = (bf16[4,9,16,128]{3,2,1,0:T(8,128)(2,1)S(1)}, bf16[4,9,16,128]{3,2,1,0:T(8,128)(2,1)S(1)}, u32[]{:S(2)}, u32[]{:S(2)}) collective-permute-start(bf16[4,9,16,128]{3,2,1,0:T(8,128)(2,1)S(1)} %merge_pair.1.refs_0_), channel_id=1, source_target_pairs={{0,4},{1,5},{2,6},{3,7},{4,0},{5,1},{6,2},{7,3},{8,12},{9,13},{10,... | collective-permute-start | bytes 442376 | tf_op jit(solution)/shard_map/ppermute | solution.py:718
  39.4 7.3 %collective-permute-start.9 = (bf16[4,9,16,128]{3,2,1,0:T(8,128)(2,1)S(1)}, bf16[4,9,16,128]{3,2,1,0:T(8,128)(2,1)S(1)}, u32[]{:S(2)}, u32[]{:S(2)}) collective-permute-start(bf16[4,9,16,128]{3,2,1,0:T(8,128)(2,1)S(1)} %merge_pair.1.refs_0_), channel_id=1, source_target_pairs={{0,2},{1,3},{2,0},{3,1},{4,6},{5,7},{6,4},{7,5},{8,10},{9,11},{10,... | collective-permute-start | bytes 442376 | tf_op jit(solution)/shard_map/ppermute | solution.py:718
  47.2 1.4 %collective-permute-start.12 = (bf16[32,2048]{1,0:T(8,128)(2,1)S(1)}, bf16[32,2048]{1,0:T(8,128)(2,1)S(1)}, u32[]{:S(2)}, u32[]{:S(2)}) collective-permute-start(bf16[32,2048]{1,0:T(8,128)(2,1)S(1)} %merge.1.piece_ref), channel_id=1, source_target_pairs={{0,1},{1,0},{2,3},{3,2},{4,5},{5,4},{6,7},{7,6},{8,9},{9,8},{10,11... | collective-permute-start | bytes 393224 | tf_op jit(solution)/shard_map/ppermute | solution.py:718
  49.2 4.5 %collective-permute-start.13 = (bf16[16,640]{1,0:T(8,128)(2,1)S(1)}, bf16[16,640]{1,0:T(8,128)(2,1)S(1)}, u32[]{:S(2)}, u32[]{:S(2)}) collective-permute-start(bf16[16,640]{1,0:T(8,128)(2,1)S(1)} %get-tuple-element.40), channel_id=1, source_target_pairs={{0,8},{8,0},{16,24},{24,16},{1,9},{9,1},{17,25},{25,17},{2,10},{10... | collective-permute-start | bytes 61448 | tf_op jit(solution)/shard_map/ppermute | solution.py:718
  50.9 4.9 %collective-permute-start.14 = (bf16[16,640]{1,0:T(8,128)(2,1)S(1)}, bf16[16,640]{1,0:T(8,128)(2,1)S(1)}, u32[]{:S(2)}, u32[]{:S(2)}) collective-permute-start(bf16[16,640]{1,0:T(8,128)(2,1)S(1)} %get-tuple-element.41), channel_id=1, source_target_pairs={{0,16},{8,24},{16,0},{24,8},{1,17},{9,25},{17,1},{25,9},{2,18},{10... | collective-permute-start | bytes 61448 | tf_op jit(solution)/shard_map/ppermute | solution.py:718
  53.5 5.6 %collective-permute-start.15 = (bf16[16,640]{1,0:T(8,128)(2,1)S(1)}, bf16[16,640]{1,0:T(8,128)(2,1)S(1)}, u32[]{:S(2)}, u32[]{:S(2)}) collective-permute-start(bf16[16,640]{1,0:T(8,128)(2,1)S(1)} %get-tuple-element.42), channel_id=1, source_target_pairs={{0,24},{8,16},{16,8},{24,0},{1,25},{9,17},{17,9},{25,1},{2,26},{10... | collective-permute-start | bytes 61448 | tf_op jit(solution)/shard_map/ppermute | solution.py:718
